TPU v7x, 32 devices: a whole 2x2x4 slice. The times are simulated.
32 devices in a mesh: seq: 8 (over y, x, core), tp: 4 (over z).
Axes of the slice: x: 2, y: 2, z: 4, core: 2. Of those that a mesh axis runs over, the one named last changes fastest.
Arguments:
- tokens: bfloat16 [2, 4096, 2048], P(None, 'seq', 'tp'), may hold values from -6 to 6
- lengths: int32 [2, 3], replicated, may hold values from 1 to 3840, 4096 in all within a row
- pad_mask: int32 [2, 4096], P(None, 'seq'), may hold values 0 or 1
- gain_in: float32 [2048], replicated, may hold values from 0.5 to 1.5
- w_in: bfloat16 [2048, 3, 2048], P('seq', None, 'tp'), may hold values from -0.125 to 0.125
- conv_taps: float32 [3, 3, 2048], P(None, None, 'tp'), may hold values from -3 to 3
- log_rate: float32 [16, 2048], P(None, 'tp'), may hold values from -11 to -3.5
- pole_angle: float32 [16, 2048], P(None, 'tp'), may hold values from -0.3 to 0.3
- residues: float32 [2, 16, 2048], P(None, None, 'tp'), may hold values from -0.0625 to 0.0625
- skip_gain: float32 [2048], P('tp'), may hold values from -4 to 4
- w_out: bfloat16 [2048, 2048], P('tp', 'seq'), may hold values from -0.125 to 0.125
- gain_mlp: float32 [2048], replicated, may hold values from 0.5 to 1.5
- w_gu: bfloat16 [2048, 2, 5632], P('seq', None, 'tp'), may hold values from -0.125 to 0.125
- w_down: bfloat16 [5632, 2048], P('tp', 'seq'), may hold values from -0.078125 to 0.078125
- cotangent: bfloat16 [2, 4096, 2048], P(None, 'seq', 'tp'), may hold values from -6 to 6
Outputs:
- out: bfloat16 [2, 4096, 2048], P(None, 'seq', 'tp')
- d_tokens: bfloat16 [2, 4096, 2048], P(None, 'seq', 'tp')
- d_gain_in: float32 [2048], replicated
- d_w_in: float32 [2048, 3, 2048], P('seq', None, 'tp')
- d_conv_taps: float32 [3, 3, 2048], P(None, None, 'tp')
- d_log_rate: float32 [16, 2048], P(None, 'tp')
- d_pole_angle: float32 [16, 2048], P(None, 'tp')
- d_residues: float32 [2, 16, 2048], P(None, None, 'tp')
- d_skip_gain: float32 [2048], P('tp')
- d_w_out: float32 [2048, 2048], P('tp', 'seq')
- d_gain_mlp: float32 [2048], replicated
- d_w_gu: float32 [2048, 2, 5632], P('seq', None, 'tp')
- d_w_down: float32 [5632, 2048], P('tp', 'seq')
Inputs may be any that keep to these rules, and one draw needn't show every extreme that they name: In each row the 3 lengths sum to 4096, and one of them is 3840.
All inputs are finite; a program needn't handle non-finite values. No bound on the sum of `pad_mask` on one device may be relied on, other than what follows from the above.
Results may differ from a plain program's by a relative error of at most 0.024.
Values may be sent and summed in bfloat16 or wider, within the bound.
No kernel may reach another device: no remote copies, remote signals or barrier semaphores. Data moves between devices by JAX's collectives and lax.ppermute only.
A program may use at most 256 MiB of HBM per device.

v0:
```python
from functools import partial

import jax
import jax.numpy as jnp
from jax import lax
from jax.sharding import PartitionSpec as P

BLK = 64


highest = lax.Precision.HIGHEST
epsilon = 1e-06


def passed_along(block, axis, distance):
    devices = range(lax.axis_size(axis))
    route = [(i - distance, i) for i in devices if i - distance in devices]
    return lax.ppermute(block, axis, route)


def entering(value, axis, join, neutral, backward):
    count, mine = (lax.axis_size(axis), lax.axis_index(axis))
    pieces = jax.tree.map(lambda part: lax.all_gather(part, axis), value)
    if backward:
        pieces = jax.tree.map(lambda part: part[::-1], pieces)
        mine = count - 1 - mine
    subtotal = jax.tree.map(
        lambda part, zero: jnp.full_like(part, 0) + jnp.asarray(zero, part.dtype), value, neutral
    )

    def hop(position, subtotal):
        longer = join(subtotal, jax.tree.map(lambda part: part[position], pieces))
        return jax.tree.map(lambda new, old: jnp.where(position < mine, new, old), longer, subtotal)

    return lax.fori_loop(0, count - 1, hop, subtotal)


def segment_number(position, doc_lengths):
    starts_at = jnp.cumsum(doc_lengths) - doc_lengths
    hits = (starts_at[None, :] <= position[:, None]).astype(jnp.int32)
    return jnp.sum(hits, axis=1)


def pole_powers(exponent, decay_rate, pole_angle):
    magnitude = jnp.exp(-exponent[:, None, None] * decay_rate[None])
    phase = exponent[:, None, None] * pole_angle[None]
    return (magnitude * jnp.cos(phase), magnitude * jnp.sin(phase))


def conv_block(carry_state, block_inputs, decay_rate, pole_angle, res_real, res_imag):
    inject, seg_block, seg_before = block_inputs
    block_len = inject.shape[0]
    exponent = jnp.arange(block_len).astype(jnp.float32)
    ker_real, ker_imag = pole_powers(exponent, decay_rate, pole_angle)
    kernel = jnp.sum(res_real[None] * ker_real - res_imag[None] * ker_imag, axis=1)
    offset = jnp.arange(block_len)[:, None] - jnp.arange(block_len)[None, :]
    same_seg = jnp.logical_and(seg_block[:, None] == seg_block[None, :], offset >= 0)
    toeplitz = jnp.where(same_seg[:, :, None], kernel[jnp.clip(offset, 0, block_len - 1)], 0.0)
    y_inner = jnp.einsum("tsc,sc->tc", toeplitz, inject, precision=highest)
    carried = (seg_block == seg_before).astype(jnp.float32)
    next_real, next_imag = pole_powers(exponent + 1.0, decay_rate, pole_angle)
    state_real, state_imag = carry_state
    rs_real = res_real * state_real - res_imag * state_imag
    rs_imag = res_real * state_imag + res_imag * state_real
    y_cross = carried[:, None] * jnp.sum(
        next_real * rs_real[None] - next_imag * rs_imag[None], axis=1
    )
    tail_mask = (seg_block == seg_block[block_len - 1]).astype(jnp.float32)
    end_real, end_imag = pole_powers(block_len - 1.0 - exponent, decay_rate, pole_angle)
    weighted = inject * tail_mask[:, None]
    sum_real = jnp.einsum("snc,sc->nc", end_real, weighted, precision=highest)
    sum_imag = jnp.einsum("snc,sc->nc", end_imag, weighted, precision=highest)
    full_real, full_imag = pole_powers(
        jnp.full((1,), block_len).astype(jnp.float32), decay_rate, pole_angle
    )
    keep_all = carried[block_len - 1]
    mult_real = keep_all * full_real[0]
    mult_imag = keep_all * full_imag[0]
    new_real = mult_real * state_real - mult_imag * state_imag + sum_real
    new_imag = mult_real * state_imag + mult_imag * state_real + sum_imag
    return ((new_real, new_imag), y_inner + y_cross)


def local_conv(inject, seg_own, seg_before, decay_rate, pole_angle, res_real, res_imag):
    row_count, width = inject.shape
    block_count = row_count // BLK
    inject_blocks = inject.reshape(block_count, BLK, width)
    seg_blocks = seg_own.reshape(block_count, BLK)
    seg_befores = jnp.concatenate([seg_before[None], seg_blocks[:-1, BLK - 1]])

    def advance(carry_state, block_inputs):
        return conv_block(carry_state, block_inputs, decay_rate, pole_angle, res_real, res_imag)

    zero_state = jnp.zeros((decay_rate.shape[0], width), jnp.float32)
    end_state, y_blocks = lax.scan(
        jax.checkpoint(advance), (zero_state, zero_state), (inject_blocks, seg_blocks, seg_befores)
    )
    keep_all = (seg_own[row_count - 1] == seg_before).astype(jnp.float32)
    full_real, full_imag = pole_powers(
        jnp.full((1,), row_count).astype(jnp.float32), decay_rate, pole_angle
    )
    return (
        y_blocks.reshape(row_count, width),
        (keep_all * full_real[0], keep_all * full_imag[0]),
        end_state,
    )


def mixer_front(
    z_own, z_rim, conv_taps, log_rate, pole_angle, residues, skip_gain, seg_ext, mask_row
):
    row_count = z_own.shape[0]
    z_joined = jnp.concatenate([z_rim, z_own], axis=0)
    seg_own = seg_ext[2:]
    filtered = conv_taps[0][None] * z_own
    for offset in (1, 2):
        valid = (seg_ext[2 - offset : 2 - offset + row_count] == seg_own).astype(jnp.float32)
        filtered = (
            filtered
            + conv_taps[offset][None]
            * z_joined[2 - offset : 2 - offset + row_count]
            * valid[:, None, None]
        )
    query = filtered[:, 0]
    inject = filtered[:, 1] * filtered[:, 2] * mask_row[:, None]
    y_local, summary_mult, summary_sum = local_conv(
        inject, seg_own, seg_ext[1], jnp.exp(log_rate), pole_angle, residues[0], residues[1]
    )
    return (query, y_local + skip_gain[None] * inject, summary_mult, summary_sum)


def mixer_finish(
    query, y_local, state_real, state_imag, log_rate, pole_angle, residues, seg_own, seg_before
):
    row_count = query.shape[0]
    exponent = jnp.arange(1, row_count + 1).astype(jnp.float32)
    pow_real, pow_imag = pole_powers(exponent, jnp.exp(log_rate), pole_angle)
    rs_real = residues[0] * state_real - residues[1] * state_imag
    rs_imag = residues[0] * state_imag + residues[1] * state_real
    carried = (seg_own == seg_before).astype(jnp.float32)
    cross = carried[:, None] * jnp.sum(pow_real * rs_real[None] - pow_imag * rs_imag[None], axis=1)
    return query * (y_local + cross)


def compose(earlier, later):
    first_real, first_imag, first_sum_real, first_sum_imag = earlier
    second_real, second_imag, second_sum_real, second_sum_imag = later
    return (
        first_real * second_real - first_imag * second_imag,
        first_real * second_imag + first_imag * second_real,
        second_real * first_sum_real - second_imag * first_sum_imag + second_sum_real,
        second_real * first_sum_imag + second_imag * first_sum_real + second_sum_imag,
    )


def norm_scale(values):
    return lax.rsqrt(jnp.mean(values * values, axis=-1, keepdims=True) + epsilon)


def norm_back(values, gain, grad):
    scale = norm_scale(values)
    weighted = gain[None] * grad
    d_values = scale * weighted - values * scale**3 * jnp.mean(
        weighted * values, axis=-1, keepdims=True
    )
    d_gain = jnp.sum(grad * values * scale, axis=0)
    return (d_values, d_gain)


def shards(
    tokens,
    lengths,
    pad_mask,
    gain_in,
    w_in,
    conv_taps,
    log_rate,
    pole_angle,
    residues,
    skip_gain,
    w_out,
    gain_mlp,
    w_gu,
    w_down,
    cotangent,
):
    micro_count, row_count, own_width = tokens.shape
    first_col = lax.axis_index("tp") * own_width
    position = lax.axis_index("seq") * row_count + jnp.arange(-2, row_count)
    in_full, out_full, gu_full, down_full = (
        lax.all_gather(w_in, "seq", axis=0, tiled=True),
        lax.all_gather(w_out, "seq", axis=1, tiled=True),
        lax.all_gather(w_gu, "seq", axis=0, tiled=True),
        lax.all_gather(w_down, "seq", axis=1, tiled=True),
    )
    stored = []
    outputs = []
    for micro_index in range(micro_count):
        seg_ext = segment_number(position, lengths[micro_index])
        mask_row = pad_mask[micro_index].astype(jnp.float32)
        x_full = lax.all_gather(tokens[micro_index], "tp", axis=1, tiled=True)
        x_wide = x_full.astype(jnp.float32)
        h_in = (x_wide * norm_scale(x_wide) * gain_in[None]).astype(jnp.bfloat16)
        z_low = jnp.einsum("td,dkc->tkc", h_in, in_full, preferred_element_type=jnp.float32).astype(
            jnp.bfloat16
        )
        z_rim = passed_along(z_low[row_count - 2 :], "seq", 1)
        query, y_local, summary_mult, summary_sum = mixer_front(
            z_low.astype(jnp.float32),
            z_rim.astype(jnp.float32),
            conv_taps,
            log_rate,
            pole_angle,
            residues,
            skip_gain,
            seg_ext,
            mask_row,
        )
        unit_part = jnp.ones_like(summary_mult[0])
        zero_part = jnp.zeros_like(summary_mult[0])
        incoming = entering(
            (summary_mult[0], summary_mult[1], summary_sum[0], summary_sum[1]),
            "seq",
            compose,
            (unit_part, zero_part, zero_part, zero_part),
            False,
        )
        state_real, state_imag = (incoming[2], incoming[3])
        mixed = mixer_finish(
            query,
            y_local,
            state_real,
            state_imag,
            log_rate,
            pole_angle,
            residues,
            seg_ext[2:],
            seg_ext[1],
        ).astype(jnp.bfloat16)
        mixer_part = jnp.dot(mixed, out_full, preferred_element_type=jnp.float32)
        x_mid = x_wide + lax.psum(mixer_part, "tp")
        h_mlp = (x_mid * norm_scale(x_mid) * gain_mlp[None]).astype(jnp.bfloat16)
        gate_up = jnp.einsum("td,dkf->tkf", h_mlp, gu_full, preferred_element_type=jnp.float32)
        act_low = (jax.nn.silu(gate_up[:, 0]) * gate_up[:, 1]).astype(jnp.bfloat16)
        down_part = jnp.dot(act_low, down_full, preferred_element_type=jnp.float32)
        down_own = lax.psum_scatter(
            down_part.astype(jnp.bfloat16), "tp", scatter_dimension=1, tiled=True
        ).astype(jnp.float32)
        mid_own = lax.dynamic_slice_in_dim(x_mid, first_col, own_width, 1)
        outputs.append((mid_own + down_own).astype(jnp.bfloat16))
        stored.append((x_full, z_low, z_rim, state_real, state_imag, x_mid, gate_up))
    in_full, out_full, gu_full, down_full = (
        lax.all_gather(w_in, "seq", axis=0, tiled=True),
        lax.all_gather(w_out, "seq", axis=1, tiled=True),
        lax.all_gather(w_gu, "seq", axis=0, tiled=True),
        lax.all_gather(w_down, "seq", axis=1, tiled=True),
    )
    grad_w_in = jnp.zeros(in_full.shape, jnp.float32)
    grad_w_out = jnp.zeros(out_full.shape, jnp.float32)
    grad_w_gu = jnp.zeros(gu_full.shape, jnp.float32)
    grad_w_down = jnp.zeros(down_full.shape, jnp.float32)
    grad_gain_in = jnp.zeros_like(gain_in)
    grad_gain_mlp = jnp.zeros_like(gain_mlp)
    grad_taps = jnp.zeros_like(conv_taps)
    grad_rate = jnp.zeros_like(log_rate)
    grad_angle = jnp.zeros_like(pole_angle)
    grad_residues = jnp.zeros_like(residues)
    grad_skip = jnp.zeros_like(skip_gain)
    token_grads = []
    for micro_index in range(micro_count):
        x_full, z_low, z_rim, state_real, state_imag, x_mid, gate_up = stored[micro_index]
        seg_ext = segment_number(position, lengths[micro_index])
        mask_row = pad_mask[micro_index].astype(jnp.float32)
        grad_full = lax.all_gather(cotangent[micro_index], "tp", axis=1, tiled=True)
        gate_part = gate_up[:, 0]
        up_part = gate_up[:, 1]
        sig_gate = jax.nn.sigmoid(gate_part)
        act_low = (jax.nn.silu(gate_part) * up_part).astype(jnp.bfloat16)
        grad_w_down = grad_w_down + jnp.einsum(
            "tf,td->fd", act_low, grad_full, preferred_element_type=jnp.float32
        )
        d_act = jnp.einsum("td,fd->tf", grad_full, down_full, preferred_element_type=jnp.float32)
        d_gate = d_act * up_part * sig_gate * (1.0 + gate_part * (1.0 - sig_gate))
        d_up = d_act * gate_part * sig_gate
        d_gate_up = jnp.stack([d_gate, d_up], axis=1).astype(jnp.bfloat16)
        h_mlp = (x_mid * norm_scale(x_mid) * gain_mlp[None]).astype(jnp.bfloat16)
        grad_w_gu = grad_w_gu + jnp.einsum(
            "td,tkf->dkf", h_mlp, d_gate_up, preferred_element_type=jnp.float32
        )
        dh_part = jnp.einsum("tkf,dkf->td", d_gate_up, gu_full, preferred_element_type=jnp.float32)
        dh_mlp = lax.psum(dh_part, "tp")
        d_norm_mlp, d_gain_part = norm_back(x_mid, gain_mlp, dh_mlp)
        grad_gain_mlp = grad_gain_mlp + d_gain_part
        d_mid = grad_full.astype(jnp.float32) + d_norm_mlp
        d_low = d_mid.astype(jnp.bfloat16)
        front_fn = partial(mixer_front, seg_ext=seg_ext, mask_row=mask_row)
        front_out, pull_front = jax.vjp(
            front_fn,
            z_low.astype(jnp.float32),
            z_rim.astype(jnp.float32),
            conv_taps,
            log_rate,
            pole_angle,
            residues,
            skip_gain,
        )
        query, y_local, summary_mult, summary_sum = front_out
        finish_fn = partial(mixer_finish, seg_own=seg_ext[2:], seg_before=seg_ext[1])
        mixed, pull_finish = jax.vjp(
            finish_fn, query, y_local, state_real, state_imag, log_rate, pole_angle, residues
        )
        mixed_low = mixed.astype(jnp.bfloat16)
        grad_w_out = grad_w_out + jnp.einsum(
            "tc,td->cd", mixed_low, d_low, preferred_element_type=jnp.float32
        )
        d_mixed = jnp.einsum("td,cd->tc", d_low, out_full, preferred_element_type=jnp.float32)
        d_query, d_local, g_real, g_imag, rate_late, angle_late, res_late = pull_finish(d_mixed)
        unit_part = jnp.ones_like(g_real)
        zero_part = jnp.zeros_like(g_real)
        adjoint = entering(
            (summary_mult[0], -summary_mult[1], g_real, g_imag),
            "seq",
            compose,
            (unit_part, zero_part, zero_part, zero_part),
            True,
        )
        adj_real, adj_imag = (adjoint[2], adjoint[3])
        d_mult_real = adj_real * state_real + adj_imag * state_imag
        d_mult_imag = adj_imag * state_real - adj_real * state_imag
        d_z, d_rim, d_taps, rate_early, angle_early, res_early, d_skip = pull_front(
            (d_query, d_local, (d_mult_real, d_mult_imag), (adj_real, adj_imag))
        )
        rim_back = passed_along(d_rim, "seq", -1)
        d_z = jnp.concatenate([d_z[: row_count - 2], d_z[row_count - 2 :] + rim_back], axis=0)
        d_z_low = d_z.astype(jnp.bfloat16)
        grad_taps = grad_taps + d_taps
        grad_rate = grad_rate + rate_late + rate_early
        grad_angle = grad_angle + angle_late + angle_early
        grad_residues = grad_residues + res_late + res_early
        grad_skip = grad_skip + d_skip
        x_wide = x_full.astype(jnp.float32)
        h_in = (x_wide * norm_scale(x_wide) * gain_in[None]).astype(jnp.bfloat16)
        grad_w_in = grad_w_in + jnp.einsum(
            "td,tkc->dkc", h_in, d_z_low, preferred_element_type=jnp.float32
        )
        dh_in_part = jnp.einsum("tkc,dkc->td", d_z_low, in_full, preferred_element_type=jnp.float32)
        dh_in = lax.psum(dh_in_part.astype(jnp.bfloat16), "tp").astype(jnp.float32)
        d_norm_in, d_gain_first = norm_back(x_wide, gain_in, dh_in)
        grad_gain_in = grad_gain_in + d_gain_first
        d_tokens_full = d_mid + d_norm_in
        token_grads.append(
            lax.dynamic_slice_in_dim(d_tokens_full, first_col, own_width, 1).astype(jnp.bfloat16)
        )
    sum_in, sum_out, sum_gu, sum_down = (
        lax.psum_scatter(
            grad_w_in.astype(jnp.bfloat16), "seq", scatter_dimension=0, tiled=True
        ).astype(jnp.float32),
        lax.psum_scatter(
            grad_w_out.astype(jnp.bfloat16), "seq", scatter_dimension=1, tiled=True
        ).astype(jnp.float32),
        lax.psum_scatter(
            grad_w_gu.astype(jnp.bfloat16), "seq", scatter_dimension=0, tiled=True
        ).astype(jnp.float32),
        lax.psum_scatter(
            grad_w_down.astype(jnp.bfloat16), "seq", scatter_dimension=1, tiled=True
        ).astype(jnp.float32),
    )
    small_sums = (
        lax.psum(grad_gain_in.astype(jnp.bfloat16), "seq").astype(jnp.float32),
        lax.psum(grad_taps.astype(jnp.bfloat16), "seq").astype(jnp.float32),
        lax.psum(grad_rate.astype(jnp.bfloat16), "seq").astype(jnp.float32),
        lax.psum(grad_angle.astype(jnp.bfloat16), "seq").astype(jnp.float32),
        lax.psum(grad_residues.astype(jnp.bfloat16), "seq").astype(jnp.float32),
        lax.psum(grad_skip.astype(jnp.bfloat16), "seq").astype(jnp.float32),
        lax.psum(grad_gain_mlp.astype(jnp.bfloat16), "seq").astype(jnp.float32),
    )
    return (
        jnp.stack(outputs),
        jnp.stack(token_grads),
        small_sums[0],
        sum_in,
        small_sums[1],
        small_sums[2],
        small_sums[3],
        small_sums[4],
        small_sums[5],
        sum_out,
        small_sums[6],
        sum_gu,
        sum_down,
    )


def solution(mesh):
    return jax.shard_map(
        shards,
        mesh=mesh,
        in_specs=(
            P(None, "seq", "tp"),
            P(),
            P(None, "seq"),
            P(),
            P("seq", None, "tp"),
            P(None, None, "tp"),
            P(None, "tp"),
            P(None, "tp"),
            P(None, None, "tp"),
            P("tp"),
            P("tp", "seq"),
            P(),
            P("seq", None, "tp"),
            P("tp", "seq"),
            P(None, "seq", "tp"),
        ),
        out_specs=(
            P(None, "seq", "tp"),
            P(None, "seq", "tp"),
            P(),
            P("seq", None, "tp"),
            P(None, None, "tp"),
            P(None, "tp"),
            P(None, "tp"),
            P(None, None, "tp"),
            P("tp"),
            P("tp", "seq"),
            P(),
            P("seq", None, "tp"),
            P("tp", "seq"),
        ),
        check_vma=False,
    )
```

profile of v0, /device:TPU:0, one launch (start us, length us, event | category | flops | bytes accessed | tf_op | source)
XLA Modules:
  0.0 4517.1 jit_solution(99304842738812931)
XLA Ops:
  61.7 44.0 all-gather.31.cloned.1.call-done
  108.4 43.5 all-gather.23.cloned.1.call-done
  194.3 443.3 %while.194 = (s32[]{:T(128)}, f32[16,512]{1,0:T(8,128)S(1)}, f32[16,512]{1,0:T(8,128)S(1)}, f32[8,64,512]{2,1,0:T(8,128)}, s32[8,64]{1,0:T(8,128)S(1)}, /*index=...) while((s32[]{:T(128)}, f32[16,512]{1,0:T(8,128)S(1)}, ...), condition=%wide.region_19.20_spmd.clone, body=%wide.region_16.19_spmd.clone.sunk | while | flops 19080068 | bytes 28882332 | solution.py:95
  209.1 17.5 fusion.462
  264.5 17.5 fusion.462
  319.9 17.5 fusion.462
  375.4 17.5 fusion.462
  430.8 17.5 fusion.462
  486.2 17.5 fusion.462
  541.6 17.5 fusion.462
  597.0 17.5 fusion.462
  670.4 443.4 %while.192 = (s32[]{:T(128)}, f32[16,512]{1,0:T(8,128)S(1)}, f32[16,512]{1,0:T(8,128)S(1)}, f32[8,64,512]{2,1,0:T(8,128)}, s32[8,64]{1,0:T(8,128)}, /*index=5*/s...) while((s32[]{:T(128)}, f32[16,512]{1,0:T(8,128)S(1)}, ...), condition=%wide.region_6.7_spmd.clone, body=%wide.region_3.6_spmd.clone.sunk | while | flops 19080068 | bytes 28882496 | solution.py:95
  685.2 17.5 fusion.456
  740.6 17.5 fusion.456
  1145.0 71.5 %subtract_reduce_fusion.3 = (f32[512,512]{1,0:T(8,128)S(1)}, f32[512,512]{1,0:T(8,128)S(1)}) fusion(f32[16,512]{1,0:T(8,128)S(1)} %get-tuple-element.3153, f32[16,512]{1,0:T(8,128)S(1)} %get-tuple-element.3154, f32[16,512]{1,0:T(8,128)S(1)} %get-tuple-element.4977, f32[512]{0:T(512)S(1)} %copy-done.201, f32[16,512]{1,0:T(8,128)S(1)} %get-tuple-element.4976, ...), kind=kLoop, calls=%fused_computation.493 | loop fusion | flops 49807360 | bytes 2297856 | tf_op jit(solution)/shard_map/reduce_sum | solution.py:141
  1281.4 235.6 %while.201 = (s32[]{:T(128)}, f32[16,512]{1,0:T(8,128)S(1)}, f32[16,512]{1,0:T(8,128)S(1)}, f32[8,64,512]{2,1,0:T(8,128)}, f32[8,16,512]{2,1,0:T(8,128)S(1)}, /*...) while((s32[]{:T(128)}, f32[16,512]{1,0:T(8,128)S(1)}, ...), condition=%wide.region_60.61_spmd.clone.clone.clone, body=%wide.region_58.60_spmd.clone.clone.clone.sunk | while | flops 14876931 | bytes 10628372 | solution.py:95
  1527.6 61.7 %all-gather.27.cloned.1.call-done = bf16[2048,2,1408]{2,0,1:T(8,128)(2,1)} async-done(((bf16[256,2,1408]{2,0,1:T(8,128)(2,1)}), bf16[2048,2,1408]{2,0,1:T(8,128)(2,1)}) %all-gather.27.cloned.1.call-update) | async-done | bytes 11534352 | tf_op jit(solution)/shard_map/all_gather | solution.py:193
  1602.7 34.2 all-gather.37.cloned.1.call-done
  1636.8 45.0 all-gather.29.cloned.1.call-done
  1704.6 25.4 all-gather.35.cloned.1.call-done
  1761.6 230.4 %while.200 = (s32[]{:T(128)}, f32[16,512]{1,0:T(8,128)S(1)}, f32[16,512]{1,0:T(8,128)S(1)}, f32[8,64,512]{2,1,0:T(8,128)S(1)}, f32[8,16,512]{2,1,0:T(8,128)}, /*...) while((s32[]{:T(128)}, f32[16,512]{1,0:T(8,128)S(1)}, ...), condition=%wide.region_35.36_spmd.clone.clone.clone, body=%wide.region_33.35_spmd.clone.clone.clone.sunk | while | flops 14876931 | bytes 10628628 | solution.py:95
  1992.1 58.3 %all-reduce.37.cloned.1.call-done = (f32[512,2048]{1,0:T(8,128)}, f32[512,2048]{1,0:T(8,128)}) async-done(((f32[512,2048]{1,0:T(8,128)}, f32[512,2048]{1,0:T(8,128)}), (f32[512,2048]{1,0:T(8,128)}, f32[512,2048]{1,0:T(8,128)})) %all-reduce.37.cloned.1.call-update) | async-done | bytes 8388624 | tf_op jit(solution)/shard_map/psum | solution.py:291
  2076.9 85.8 %fusion.240 = (f32[16,512]{1,0:T(8,128)}, f32[16,512]{1,0:T(8,128)}, f32[16,512]{1,0:T(8,128)S(1)}, f32[16,512]{1,0:T(8,128)S(1)}, f32[16,512]{1,0:T(8,128)S(1)}...) fusion(f32[512,512]{1,0:T(8,128)S(1)} %get-tuple-element.3024, ...), kind=kLoop, calls=%fused_computation.474 | loop fusion | flops 184483840 | bytes 4657152 | tf_op jit(solution)/shard_map/transpose(jvp())/reduce_sum | solution.py:46
  2188.5 794.1 %while.197 = (s32[]{:T(128)}, f32[16,512]{1,0:T(8,128)}, f32[16,512]{1,0:T(8,128)S(1)}, f32[16,512]{1,0:T(8,128)}, f32[16,512]{1,0:T(8,128)}, /*index=5*/f32[16,...) while((s32[]{:T(128)}, f32[16,512]{1,0:T(8,128)}, ...), condition=%wide.region_49.50_spmd.clone, body=%wide.region_36.49_spmd.clone.sunk | while | flops 54125504 | bytes 41472192 | solution.py:95
  2200.3 26.8 scatter_custom_fusion.11
  2227.2 29.1 fusion.472
  2299.5 26.8 scatter_custom_fusion.11
  2326.4 29.1 fusion.472
  2398.7 26.8 scatter_custom_fusion.11
  2425.6 29.1 fusion.472
  2497.9 26.8 scatter_custom_fusion.11
  2524.9 29.1 fusion.472
  2597.2 26.8 scatter_custom_fusion.11
  2624.1 29.1 fusion.472
  2696.4 26.8 scatter_custom_fusion.11
  2723.3 29.1 fusion.472
  2795.6 26.8 scatter_custom_fusion.11
  2822.5 29.1 fusion.472
  2894.8 26.8 scatter_custom_fusion.11
  2921.7 29.1 fusion.472
  3008.6 902.1 %while.199 = (s32[]{:T(128)}, f32[16,512]{1,0:T(8,128)}, f32[16,512]{1,0:T(8,128)}, f32[16,512]{1,0:T(8,128)}, f32[16,512]{1,0:T(8,128)}, /*index=5*/f32[16,512]...) while((s32[]{:T(128)}, f32[16,512]{1,0:T(8,128)}, ...), condition=%wide.region_74.75_spmd.clone, body=%wide.region_61.74_spmd.clone.sunk | while | flops 54125504 | bytes 41296804 | solution.py:95
  3025.0 27.4 scatter_custom_fusion.13
  3054.0 29.5 fusion.481
  3137.7 27.4 scatter_custom_fusion.13
  3166.7 29.5 fusion.481
  3250.3 27.4 scatter_custom_fusion.13
  3279.4 29.5 fusion.481
  3363.0 27.4 scatter_custom_fusion.13
  3392.0 29.5 fusion.481
  3475.8 27.4 scatter_custom_fusion.13
  3504.8 29.5 fusion.481
  3588.5 27.4 scatter_custom_fusion.13
  3617.5 29.5 fusion.481
  3701.2 27.4 scatter_custom_fusion.13
  3730.2 29.5 fusion.481
  3813.9 27.4 scatter_custom_fusion.13
  3842.9 29.5 fusion.481
  3994.0 102.0 %all-reduce.43.cloned.1.call-done = (bf16[512,2048]{1,0:T(8,128)(2,1)}, bf16[512,2048]{1,0:T(8,128)(2,1)}) async-done(((bf16[512,2048]{1,0:T(8,128)(2,1)}, bf16[512,2048]{1,0:T(8,128)(2,1)}), (bf16[512,2048]{1,0:T(8,128)(2,1)}, bf16[512,2048]{1,0:T(8,128)(2,1)})) %all-reduce.43.cloned.1.call-update) | async-done | bytes 4194320 | tf_op jit(solution)/shard_map/psum | solution.py:347
  4143.3 44.0 reduce-scatter.7.cloned.1.call-done
  4189.9 59.4 %reduce-scatter.17.cloned.1.call-done = bf16[1408,256]{1,0:T(8,128)(2,1)} async-done(((bf16[1408,2048]{1,0:T(8,128)(2,1)}), bf16[1408,256]{1,0:T(8,128)(2,1)}) %reduce-scatter.17.cloned.1.call-update) | async-done | bytes 720912 | tf_op jit(solution)/shard_map/reduce_scatter | solution.py:364
  4251.6 42.1 reduce-scatter.13.cloned.1.call-done
  4300.9 50.7 %all-reduce.41.cloned.1.call-done = (bf16[2048]{0:T(1024)(128)(2,1)}, bf16[3,3,512]{2,1,0:T(4,128)(2,1)}, bf16[16,512]{1,0:T(8,128)(2,1)}, bf16[16,512]{1,0:T(8,...) async-done(((bf16[2048]{0:T(1024)(128)(2,1)}, bf16[3,3,512]{2,1,0:T(4,128)(2,1)}, bf16[16,512]{1,0:T(8,128)(2,1)}, ...) | async-done | bytes 83984 | tf_op jit(solution)/shard_map/psum | solution.py:369
  4360.7 81.8 %reduce-scatter.15.cloned.1.call-done = bf16[256,2,1408]{2,0,1:T(8,128)(2,1)} async-done(((bf16[2048,2,1408]{2,0,1:T(8,128)(2,1)}), bf16[256,2,1408]{2,0,1:T(8,128)(2,1)}) %reduce-scatter.15.cloned.1.call-update) | async-done | bytes 1441808 | tf_op jit(solution)/shard_map/reduce_scatter | solution.py:361
  4446.9 60.6 %reduce-scatter.11.cloned.1.call-done = bf16[256,3,512]{2,0,1:T(8,128)(2,1)} async-done(((bf16[2048,3,512]{2,0,1:T(8,128)(2,1)}), bf16[256,3,512]{2,0,1:T(8,128)(2,1)}) %reduce-scatter.11.cloned.1.call-update) | async-done | bytes 786448 | tf_op jit(solution)/shard_map/reduce_scatter | solution.py:355
  (2312 shorter events, 2535.7 us)
Async XLA Ops:
  7.2 51.7 %all-gather.33.cloned.1.call-start = ((), (), s32[]{:S(2)}) async-start(), calls=%async_computation.17 | async-start | bytes 2621440 | tf_op jit(solution)/shard_map/all_gather | solution.py:201
  9.5 96.2 %all-gather.31.cloned.1.call-start = ((), (), s32[]{:S(2)}) async-start(), calls=%async_computation.16 | async-start | bytes 2621440 | tf_op jit(solution)/shard_map/all_gather | solution.py:201
  10.3 141.6 %all-gather.23.cloned.1.call-start = ((), (), s32[]{:S(2)}) async-start(), calls=%async_computation.6 | async-start | bytes 7077888 | tf_op jit(solution)/shard_map/all_gather | solution.py:191
  11.0 1209.2 %all-gather.25.cloned.1.call-start = ((), (), s32[]{:S(2)}) async-start(), calls=%async_computation.7 | async-start | bytes 2359296 | tf_op jit(solution)/shard_map/all_gather | solution.py:192
  11.6 1508.6 %all-reduce.39.cloned.1.call-start = ((), (), s32[]{:S(2)}) async-start(), calls=%async_computation.21 | async-start | bytes 16777216 | tf_op jit(solution)/shard_map/psum | solution.py:241
  15.6 136.4 %copy-start.194 = (f32[2048]{0:T(1024)S(1)}, f32[2048]{0:T(1024)}, u32[]{:S(2)}) copy-start(f32[2048]{0:T(1024)} %param.38) | copy-start | bytes 24580
  19.0 163.0 %copy-start.185 = (f32[512]{0:T(512)}, f32[512]{0:T(512)S(1)}, u32[]{:S(2)}) copy-start(f32[512]{0:T(512)S(1)} %get-tuple-element.3224) | copy-start | bytes 6148
  19.0 163.0 %copy-start.187 = (f32[512]{0:T(512)}, f32[512]{0:T(512)S(1)}, u32[]{:S(2)}) copy-start(f32[512]{0:T(512)S(1)} %get-tuple-element.3225) | copy-start | bytes 6148
  19.0 163.0 %copy-start.189 = (f32[512]{0:T(512)}, f32[512]{0:T(512)S(1)}, u32[]{:S(2)}) copy-start(f32[512]{0:T(512)S(1)} %get-tuple-element.3189) | copy-start | bytes 6148
  19.0 163.0 %copy-start.191 = (f32[512]{0:T(512)}, f32[512]{0:T(512)S(1)}, u32[]{:S(2)}) copy-start(f32[512]{0:T(512)S(1)} %get-tuple-element.3190) | copy-start | bytes 6148
  20.4 161.7 %copy-start.132 = (f32[3,512]{1,0:T(4,128)}, f32[3,512]{1,0:T(4,128)S(1)}, u32[]{:S(2)}) copy-start(f32[3,512]{1,0:T(4,128)S(1)} %get-tuple-element.3175) | copy-start | bytes 18436
  20.4 161.7 %copy-start.134 = (f32[3,512]{1,0:T(4,128)}, f32[3,512]{1,0:T(4,128)S(1)}, u32[]{:S(2)}) copy-start(f32[3,512]{1,0:T(4,128)S(1)} %get-tuple-element.3176) | copy-start | bytes 18436
  20.4 161.7 %copy-start.142 = (f32[3,512]{1,0:T(4,128)}, f32[3,512]{1,0:T(4,128)S(1)}, u32[]{:S(2)}) copy-start(f32[3,512]{1,0:T(4,128)S(1)} %get-tuple-element.3174) | copy-start | bytes 18436
  58.9 93.0 %copy-start.8 = (bf16[1,512,2048]{2,1,0:T(8,128)(2,1)S(1)}, bf16[1,512,2048]{2,1,0:T(8,128)(2,1)}, u32[]{:S(2)}) copy-start(bf16[1,512,2048]{2,1,0:T(8,128)(2,1)} %all-gather.33.cloned.1.call-done) | copy-start | bytes 6291460
  61.7 98.3 %copy-start.175 = (f32[512]{0:T(512)}, f32[512]{0:T(512)S(1)}, u32[]{:S(2)}) copy-start(f32[512]{0:T(512)S(1)} %get-tuple-element.3205) | copy-start | bytes 6148
  160.0 21.9 collective-permute-start.1
  167.4 14.5 collective-permute-start
  191.0 1025.7 %copy-start = (f32[512,3,512]{2,0,1:T(8,128)}, f32[512,3,512]{2,0,1:T(8,128)S(1)}, u32[]{:S(2)}) copy-start(f32[512,3,512]{2,0,1:T(8,128)S(1)} %get-tuple-element.3173) | copy-start | bytes 9437188
  670.3 474.6 %copy-start.201 = (f32[512]{0:T(512)S(1)}, f32[512]{0:T(512)}, u32[]{:S(2)}) copy-start(f32[512]{0:T(512)} %add_convert_fusion.12) | copy-start | bytes 6148
  670.3 474.6 %copy-start.203 = (f32[512]{0:T(512)S(1)}, f32[512]{0:T(512)}, u32[]{:S(2)}) copy-start(f32[512]{0:T(512)} %fusion.354) | copy-start | bytes 6148
  1144.9 71.7 %copy-start.154 = (f32[16,512]{1,0:T(8,128)}, f32[16,512]{1,0:T(8,128)S(1)}, u32[]{:S(2)}) copy-start(f32[16,512]{1,0:T(8,128)S(1)} %get-tuple-element.3145) | copy-start | bytes 98308
  1144.9 71.7 %copy-start.156 = (f32[16,512]{1,0:T(8,128)}, f32[16,512]{1,0:T(8,128)S(1)}, u32[]{:S(2)}) copy-start(f32[16,512]{1,0:T(8,128)S(1)} %get-tuple-element.3146) | copy-start | bytes 98308
  1144.9 71.7 %copy-start.158 = (f32[16,512]{1,0:T(8,128)}, f32[16,512]{1,0:T(8,128)S(1)}, u32[]{:S(2)}) copy-start(f32[16,512]{1,0:T(8,128)S(1)} %get-tuple-element.3153) | copy-start | bytes 98308
  1144.9 71.7 %copy-start.160 = (f32[16,512]{1,0:T(8,128)}, f32[16,512]{1,0:T(8,128)S(1)}, u32[]{:S(2)}) copy-start(f32[16,512]{1,0:T(8,128)S(1)} %get-tuple-element.3154) | copy-start | bytes 98308
  1145.0 73.0 %copy-start.3 = (f32[512,3,512]{2,0,1:T(8,128)S(1)}, f32[512,3,512]{2,0,1:T(8,128)}, u32[]{:S(2)}) copy-start(f32[512,3,512]{2,0,1:T(8,128)} %copy-done.2) | copy-start | bytes 9437188
  1145.0 73.0 %copy-start.40 = (f32[8,64,512]{2,1,0:T(8,128)S(1)}, f32[8,64,512]{2,1,0:T(8,128)}, u32[]{:S(2)}) copy-start(f32[8,64,512]{2,1,0:T(8,128)} %get-tuple-element.1770) | copy-start | bytes 3145732
  1145.0 73.0 %copy-start.41 = (f32[8,64,512]{2,1,0:T(8,128)S(1)}, f32[8,64,512]{2,1,0:T(8,128)}, u32[]{:S(2)}) copy-start(f32[8,64,512]{2,1,0:T(8,128)} %get-tuple-element.4973) | copy-start | bytes 3145732
  1145.0 73.0 %copy-start.168 = (f32[512]{0:T(512)S(1)}, f32[512]{0:T(512)}, u32[]{:S(2)}) copy-start(f32[512]{0:T(512)} %get-tuple-element.3188) | copy-start | bytes 6148
  1145.0 72.9 %copy-start.170 = (f32[512]{0:T(512)S(1)}, f32[512]{0:T(512)}, u32[]{:S(2)}) copy-start(f32[512]{0:T(512)} %get-tuple-element.3226) | copy-start | bytes 6148
  1145.0 72.9 %copy-start.173 = (f32[512]{0:T(512)S(1)}, f32[512]{0:T(512)}, u32[]{:S(2)}) copy-start(f32[512]{0:T(512)} %param.44) | copy-start | bytes 6148
  1145.0 72.9 %copy-start.183 = (f32[1,512]{1,0:T(1,128)S(1)}, f32[1,512]{1,0:T(1,128)}, u32[]{:S(2)}) copy-start(f32[1,512]{1,0:T(1,128)} %get-tuple-element.3186) | copy-start | bytes 6148
  1145.0 72.9 %copy-start.184 = (f32[1,512]{1,0:T(1,128)S(1)}, f32[1,512]{1,0:T(1,128)}, u32[]{:S(2)}) copy-start(f32[1,512]{1,0:T(1,128)} %get-tuple-element.3187) | copy-start | bytes 6148
  1228.6 360.8 %all-gather.27.cloned.1.call-start = ((), (), s32[]{:S(2)}) async-start(), calls=%async_computation.8 | async-start | bytes 12976128 | tf_op jit(solution)/shard_map/all_gather | solution.py:193
  1231.2 405.7 %all-gather.37.cloned.1.call-start = ((), (), s32[]{:S(2)}) async-start(), calls=%async_computation.19 | async-start | bytes 2621440 | tf_op jit(solution)/shard_map/all_gather | solution.py:274
  1232.3 449.5 %all-gather.29.cloned.1.call-start = ((), (), s32[]{:S(2)}) async-start(), calls=%async_computation.9 | async-start | bytes 6488064 | tf_op jit(solution)/shard_map/all_gather | solution.py:194
  1233.1 496.9 %all-gather.35.cloned.1.call-start = ((), (), s32[]{:S(2)}) async-start(), calls=%async_computation.18 | async-start | bytes 2621440 | tf_op jit(solution)/shard_map/all_gather | solution.py:274
  1233.8 816.6 %all-reduce.37.cloned.1.call-start = ((), (), s32[]{:S(2)}) async-start(), calls=%async_computation.20 | async-start | bytes 16777216 | tf_op jit(solution)/shard_map/psum | solution.py:291
  1281.4 238.8 %copy-start.9 = (bf16[1,512,2048]{2,1,0:T(8,128)(2,1)S(1)}, bf16[1,512,2048]{2,1,0:T(8,128)(2,1)}, u32[]{:S(2)}) copy-start(bf16[1,512,2048]{2,1,0:T(8,128)(2,1)} %all-gather.33.cloned.1.call-done) | copy-start | bytes 6291460
  1525.1 533.1 %copy-start.179 = (f32[512]{0:T(512)}, f32[512]{0:T(512)S(1)}, u32[]{:S(2)}) copy-start(f32[512]{0:T(512)S(1)} %get-tuple-element.3211) | copy-start | bytes 6148
  1525.1 64.2 %copy-start.148 = (f32[2048]{0:T(1024)S(1)}, f32[2048]{0:T(1024)}, u32[]{:S(2)}) copy-start(f32[2048]{0:T(1024)} %param.46) | copy-start | bytes 24580
  1527.6 530.6 %copy-start.181 = (f32[512]{0:T(512)}, f32[512]{0:T(512)S(1)}, u32[]{:S(2)}) copy-start(f32[512]{0:T(512)S(1)} %get-tuple-element.3209) | copy-start | bytes 6148
  1760.0 2336.0 %all-reduce.43.cloned.1.call-start = ((), (), s32[]{:S(2)}) async-start(), calls=%async_computation.23 | async-start | bytes 8388608 | tf_op jit(solution)/shard_map/psum | solution.py:347
  1992.0 66.1 %copy-start.38 = (f32[8,64,512]{2,1,0:T(8,128)}, f32[8,64,512]{2,1,0:T(8,128)S(1)}, u32[]{:S(2)}) copy-start(f32[8,64,512]{2,1,0:T(8,128)S(1)} %get-tuple-element.1780) | copy-start | bytes 3145732
  2076.9 85.9 %copy-start.119 = (f32[2,16,512]{2,1,0:T(8,128)S(1)}, f32[2,16,512]{2,1,0:T(8,128)}, u32[]{:S(2)}) copy-start(f32[2,16,512]{2,1,0:T(8,128)} %param.43) | copy-start | bytes 196612
  2076.9 105.1 %copy-start.63 = (f32[16,512]{1,0:T(8,128)S(1)}, f32[16,512]{1,0:T(8,128)}, u32[]{:S(2)}) copy-start(f32[16,512]{1,0:T(8,128)} %custom-call.8) | copy-start | bytes 98308
  2076.9 105.1 %copy-start.66 = (f32[16,512]{1,0:T(8,128)S(1)}, f32[16,512]{1,0:T(8,128)}, u32[]{:S(2)}) copy-start(f32[16,512]{1,0:T(8,128)} %custom-call.9) | copy-start | bytes 98308
  2188.0 812.3 %copy-start.57 = (f32[16,512]{1,0:T(8,128)S(1)}, f32[16,512]{1,0:T(8,128)}, u32[]{:S(2)}) copy-start(f32[16,512]{1,0:T(8,128)} %custom-call.16) | copy-start | bytes 98308
  2188.0 812.3 %copy-start.60 = (f32[16,512]{1,0:T(8,128)S(1)}, f32[16,512]{1,0:T(8,128)}, u32[]{:S(2)}) copy-start(f32[16,512]{1,0:T(8,128)} %custom-call.17) | copy-start | bytes 98308
  3008.6 902.1 %copy-start.1 = (f32[512,3,512]{2,0,1:T(8,128)S(1)}, f32[512,3,512]{2,0,1:T(8,128)}, u32[]{:S(2)}) copy-start(f32[512,3,512]{2,0,1:T(8,128)} %copy-done) | copy-start | bytes 9437188
  3917.3 8.9 collective-permute-start.3
  3924.6 3.1 collective-permute-start.2
  3940.3 201.4 %reduce-scatter.9.cloned.1.call-start = ((), (), s32[]{:S(2)}) async-start(), calls=%async_computation.11 | async-start | bytes 2621440 | tf_op jit(solution)/shard_map/reduce_scatter | solution.py:246
  3948.2 239.0 %reduce-scatter.7.cloned.1.call-start = ((), (), s32[]{:S(2)}) async-start(), calls=%async_computation.10 | async-start | bytes 2621440 | tf_op jit(solution)/shard_map/reduce_scatter | solution.py:246
  3956.1 293.2 %reduce-scatter.17.cloned.1.call-start = ((), (), s32[]{:S(2)}) async-start(), calls=%async_computation.15 | async-start | bytes 6488064 | tf_op jit(solution)/shard_map/reduce_scatter | solution.py:364
  3967.3 326.4 %reduce-scatter.13.cloned.1.call-start = ((), (), s32[]{:S(2)}) async-start(), calls=%async_computation.13 | async-start | bytes 2359296 | tf_op jit(solution)/shard_map/reduce_scatter | solution.py:358
  3975.9 120.1 %copy-start.176 = (f32[512]{0:T(512)S(1)}, f32[512]{0:T(512)}, u32[]{:S(2)}) copy-start(f32[512]{0:T(512)} %copy-done.175) | copy-start | bytes 6148
  3975.9 120.1 %copy-start.178 = (f32[512]{0:T(512)S(1)}, f32[512]{0:T(512)}, u32[]{:S(2)}) copy-start(f32[512]{0:T(512)} %copy-done.177) | copy-start | bytes 6148
  3975.9 120.1 %copy-start.195 = (f32[2048]{0:T(1024)S(1)}, f32[2048]{0:T(1024)}, u32[]{:S(2)}) copy-start(f32[2048]{0:T(1024)} %param.38) | copy-start | bytes 24580
  3975.9 375.7 %all-reduce.41.cloned.1.call-start = ((), (), s32[]{:S(2)}) async-start(), calls=%async_computation.22 | async-start | bytes 174080 | tf_op jit(solution)/shard_map/psum | solution.py:369
  3976.2 119.8 %copy-start.10 = (bf16[1,512,2048]{2,1,0:T(8,128)(2,1)S(1)}, bf16[1,512,2048]{2,1,0:T(8,128)(2,1)}, u32[]{:S(2)}) copy-start(bf16[1,512,2048]{2,1,0:T(8,128)(2,1)} %all-gather.33.cloned.1.call-done) | copy-start | bytes 6291460
  4103.5 339.0 %reduce-scatter.15.cloned.1.call-start = ((), (), s32[]{:S(2)}) async-start(), calls=%async_computation.14 | async-start | bytes 12976128 | tf_op jit(solution)/shard_map/reduce_scatter | solution.py:361
  4119.2 388.4 %reduce-scatter.11.cloned.1.call-start = ((), (), s32[]{:S(2)}) async-start(), calls=%async_computation.12 | async-start | bytes 7077888 | tf_op jit(solution)/shard_map/reduce_scatter | solution.py:355
  4188.8 106.7 %copy-start.196 = (f32[512]{0:T(512)S(1)}, f32[512]{0:T(512)}, u32[]{:S(2)}) copy-start(f32[512]{0:T(512)} %get-tuple-element.3204) | copy-start | bytes 6148
  4189.9 107.8 %copy-start.197 = (f32[512]{0:T(512)S(1)}, f32[512]{0:T(512)}, u32[]{:S(2)}) copy-start(f32[512]{0:T(512)} %get-tuple-element.3202) | copy-start | bytes 6148
  (488 other events, 4996.4 us)
Sparse Core Ops, SparseCore 0:
  10.2 48.6 all-gather.32
  61.1 44.6 all-gather.30
  107.7 44.2 all-gather.22
  153.7 29.2 all-gather.24
  1228.7 291.5 all-reduce.38
  1522.6 66.7 all-gather.26
  1590.9 45.9 all-gather.36
  1638.7 43.0 all-gather.28
  1684.0 45.9 all-gather.34
  1760.1 290.2 all-reduce.36
  3940.4 155.5 all-reduce.42
  4098.8 42.8 reduce-scatter.8
  4144.0 43.1 reduce-scatter.6
  4190.9 58.3 reduce-scatter.16
  4252.4 41.2 reduce-scatter.12
  4299.2 52.3 all-reduce.40
  4354.9 87.5 reduce-scatter.14
  4445.8 61.7 reduce-scatter.10
where the time goes:
time: 4540 us; the launch traced here: 4520 us
  other arithmetic  2620 us (58%)
  local copies, waits for them, and re-layouts  780 us (17%)
  waiting for transfers between devices  765 us (17%)
  matrix products  183 us (4%)
  blocking collectives  136 us (3%)
    gather x33, local copies, waits for them, and re-layouts, conv_block(): kernel[jnp.clip(offset, 0, block_len - 1)]  556 us
    reduce_sum x17, other arithmetic, pole_powers(): phase = exponent[:, None, None] * pole_angle[None]  555 us
    scatter-add x16, other arithmetic, conv_block(): kernel[jnp.clip(offset, 0, block_len - 1)]  433 us
    reduce_sum x32, other arithmetic, conv_block(): jnp.sum(next_real * rs_real[None] - next_imag * rs_imag[None], axis=1)  417 us
    dot_general x32, other arithmetic, conv_block(): sum_imag = jnp.einsum('snc,sc->nc', end_imag, weighted, precision=highest)  274 us
    dot_general x48, other arithmetic, conv_block(): y_inner = jnp.einsum('tsc,sc->tc', toeplitz, inject, precision=highest)  206 us
    dot_general x16, other arithmetic, conv_block(): sum_real = jnp.einsum('snc,sc->nc', end_real, weighted, precision=highest)  150 us
    all_gather x14, blocking collectives, entering(): pieces = jax.tree.map(lambda part: lax.all_gather(part, axis), value)  136 us
  transfers between devices with their start and end apart: 22, of which 18 were waited for; matrix products, arithmetic and copies ran while one was open for 37% of the time, Pallas kernels for 0%

commit v1 on v0

v1 whole, which is shorter than its diff:
```python
import functools

import jax
import jax.numpy as jnp
from jax import lax
from jax.experimental import pallas as pl
from jax.experimental.pallas import tpu as pltpu
from jax.sharding import PartitionSpec as P

EPS = 1e-06
SPAN = 64
STEP = 8
ROWS = 16
SUB, LANE = 8, 128
BF, F32 = jnp.bfloat16, jnp.float32
VMEM_LIMIT = 56 * 1024 * 1024


def keep_rows(z_ref, rim_ref, zs_ref):
    zs_ref[0:SUB, :] = rim_ref[...]

    def body(i, _):
        rows = pl.ds(pl.multiple_of(i * ROWS, ROWS), ROWS)
        zs_ref[pl.ds(pl.multiple_of(i * ROWS + SUB, SUB), ROWS), :] = z_ref[rows, :].astype(F32)
        return 0

    lax.fori_loop(0, z_ref.shape[0] // ROWS, body, 0)


def window(zs_ref, i, stream, width):
    rows = pl.ds(pl.multiple_of(i * ROWS, ROWS), ROWS + SUB)
    wide = zs_ref[rows, stream * width : (stream + 1) * width]
    return wide[8 : 8 + ROWS], wide[7 : 7 + ROWS], wide[6 : 6 + ROWS]


def filtered(zs_ref, taps_ref, cols, i, stream, width):
    z0, z1, z2 = window(zs_ref, i, stream, width)
    t0, t1, t2 = (taps_ref[lag * 3 + stream : lag * 3 + stream + 1, :] for lag in range(3))
    return t0 * z0 + (t1 * z1) * cols[:, 0:1] + (t2 * z2) * cols[:, 1:2]


def spread(ref, i, value):
    parts = value.shape[1] // LANE
    for c in range(parts):
        piece = value[:, c * LANE : (c + 1) * LANE]
        for half in range(SUB // parts):
            ref[pl.ds(i * (ROWS * SUB) + half * parts + c, ROWS, stride=SUB), :] = piece


def collect(ref, i, width):
    parts = width // LANE
    pieces = []
    for c in range(parts):
        piece = ref[pl.ds(i * (ROWS * SUB) + c, ROWS, stride=SUB), :]
        for half in range(1, SUB // parts):
            piece = piece + ref[pl.ds(i * (ROWS * SUB) + half * parts + c, ROWS, stride=SUB), :]
        pieces.append(piece)
    return jnp.concatenate(pieces, axis=1)


def chunk_cols(cols_ref, i):
    return cols_ref[pl.ds(pl.multiple_of(i * ROWS, ROWS), ROWS), :]


def at(group, j):
    return pl.ds(pl.multiple_of((group * STEP + j) * SUB, SUB), SUB)


def by_flag(flag, step):
    @pl.when(flag == 0)
    def _():
        step(False)

    @pl.when(flag != 0)
    def _():
        step(True)


def front_kernel(keep_ref, flag_ref, z_ref, rim_ref, taps_ref, cols_ref, lam_ref,
                 u_ref, end_ref, zs_ref):
    count, width = z_ref.shape[0], z_ref.shape[1] // 3
    poles = lam_ref.shape[0] // 2
    keep_rows(z_ref, rim_ref, zs_ref)

    def natural(i, _):
        cols = chunk_cols(cols_ref, i)
        key = filtered(zs_ref, taps_ref, cols, i, 1, width)
        value = filtered(zs_ref, taps_ref, cols, i, 2, width)
        spread(u_ref, i, key * value * cols[:, 2:3])
        return 0

    lax.fori_loop(0, count // ROWS, natural, 0)
    end_ref[...] = jnp.zeros_like(end_ref)

    def scan(group, _):
        def step(masked):
            us = [u_ref[at(group, j), :] for j in range(STEP)]
            for k in range(poles):
                lr, li = lam_ref[k], lam_ref[poles + k]
                sr, si = end_ref[k], end_ref[poles + k]
                for j in range(STEP):
                    if masked:
                        keep = keep_ref[group * STEP + j]
                        sr, si = sr * keep, si * keep
                    sr, si = lr * sr - li * si + us[j], lr * si + li * sr
                end_ref[k], end_ref[poles + k] = sr, si

        by_flag(flag_ref[group], step)
        return 0

    lax.fori_loop(0, count // STEP, scan, 0)


def joined(all_ref, full_ref, carry_ref, spans_ref, me, count, conj):
    poles = full_ref.shape[0] // 2
    carry_ref[...] = jnp.zeros_like(carry_ref)

    def hop(order, _):
        j = count - 1 - order if conj else order
        span = spans_ref[j]
        for k in range(poles):
            lr, li = full_ref[k] * span, full_ref[poles + k] * (-span if conj else span)
            sr, si = carry_ref[k], carry_ref[poles + k]
            carry_ref[k] = lr * sr - li * si + all_ref[j, k]
            carry_ref[poles + k] = lr * si + li * sr + all_ref[j, poles + k]
        return 0

    lax.fori_loop(0, count - 1 - me if conj else me, hop, 0)


def finish_kernel(keep_ref, flag_ref, spans_ref, me_ref, z_ref, rim_ref, taps_ref, cols_ref,
                  lam_ref, full_ref, res_ref, skip_ref, u_ref, ends_ref,
                  mixed_ref, conv_ref, marks_ref, zs_ref, y_ref, st_ref):
    count, width = z_ref.shape[0], z_ref.shape[1] // 3
    poles = lam_ref.shape[0] // 2
    keep_rows(z_ref, rim_ref, zs_ref)
    joined(ends_ref, full_ref, st_ref, spans_ref, me_ref[0], ends_ref.shape[0], False)

    def scan(group, _):
        @pl.when(group % (SPAN // STEP) == 0)
        def _():
            marks_ref[group // (SPAN // STEP)] = st_ref[...]

        def step(masked):
            us = [u_ref[at(group, j), :] for j in range(STEP)]
            ys = [None] * STEP
            for k in range(poles):
                lr, li = lam_ref[k], lam_ref[poles + k]
                rr, ri = res_ref[k], res_ref[poles + k]
                sr, si = st_ref[k], st_ref[poles + k]
                for j in range(STEP):
                    if masked:
                        keep = keep_ref[group * STEP + j]
                        sr, si = sr * keep, si * keep
                    sr, si = lr * sr - li * si + us[j], lr * si + li * sr
                    part = rr * sr - ri * si
                    ys[j] = part if ys[j] is None else ys[j] + part
                st_ref[k], st_ref[poles + k] = sr, si
            for j in range(STEP):
                y_ref[at(group, j), :] = ys[j]

        by_flag(flag_ref[group], step)
        return 0

    lax.fori_loop(0, count // STEP, scan, 0)

    def natural(i, _):
        rows = pl.ds(pl.multiple_of(i * ROWS, ROWS), ROWS)
        cols = chunk_cols(cols_ref, i)
        query = filtered(zs_ref, taps_ref, cols, i, 0, width)
        key = filtered(zs_ref, taps_ref, cols, i, 1, width)
        value = filtered(zs_ref, taps_ref, cols, i, 2, width)
        conv = collect(y_ref, i, width) + skip_ref[...] * (key * value * cols[:, 2:3])
        conv_ref[rows, :] = conv
        mixed_ref[rows, :] = (query * conv).astype(BF)
        return 0

    lax.fori_loop(0, count // ROWS, natural, 0)


def adjoint_kernel(keep_ref, flag_ref, z_ref, rim_ref, taps_ref, cols_ref, lam_ref, dmix_ref,
                   e_ref, end_ref, zs_ref):
    count, width = z_ref.shape[0], z_ref.shape[1] // 3
    poles = lam_ref.shape[0] // 2
    keep_rows(z_ref, rim_ref, zs_ref)

    def natural(i, _):
        rows = pl.ds(pl.multiple_of(i * ROWS, ROWS), ROWS)
        query = filtered(zs_ref, taps_ref, chunk_cols(cols_ref, i), i, 0, width)
        spread(e_ref, i, dmix_ref[rows, :].astype(F32) * query)
        return 0

    lax.fori_loop(0, count // ROWS, natural, 0)
    end_ref[...] = jnp.zeros_like(end_ref)

    def scan(order, _):
        group = count // STEP - 1 - order

        def step(masked):
            es = [e_ref[at(group, j), :] for j in range(STEP)]
            for k in range(poles):
                lr, li = lam_ref[k], lam_ref[poles + k]
                br, bi = end_ref[k], end_ref[poles + k]
                for j in reversed(range(STEP)):
                    if masked:
                        keep = keep_ref[group * STEP + j + 1]
                        br, bi = br * keep, bi * keep
                    br, bi = lr * br + li * bi + es[j], lr * bi - li * br
                end_ref[k], end_ref[poles + k] = br, bi

        by_flag(flag_ref[group] + flag_ref[group + 1], step)
        return 0

    lax.fori_loop(0, count // STEP, scan, 0)


def back_kernel(keep_ref, flag_ref, spans_ref, me_ref, z_ref, rim_ref, taps_ref, cols_ref,
                lam_ref, full_ref, res_ref, skip_ref, u_ref, e_ref, dmix_ref, conv_ref,
                marks_ref, ends_ref,
                dz_ref, rimback_ref, tail_ref, dtaps_ref, dskip_ref, dres_ref, g_ref,
                zs_ref, dc_ref, di_ref, ss_ref, bt_ref):
    count, width = z_ref.shape[0], z_ref.shape[1] // 3
    poles = lam_ref.shape[0] // 2
    state_rows = 2 * poles * SUB
    keep_rows(z_ref, rim_ref, zs_ref)
    joined(ends_ref, full_ref, bt_ref, spans_ref, me_ref[0], ends_ref.shape[0], True)
    bt_ref[...] = bt_ref[...] * keep_ref[count]
    for ref in (dtaps_ref, dskip_ref, dres_ref, g_ref):
        ref[...] = jnp.zeros_like(ref)

    def held(slot, k):
        return pl.ds(pl.multiple_of(slot * state_rows + k * SUB, SUB), SUB)

    def block(order, _):
        number = count // SPAN - 1 - order
        for k in range(2 * poles):
            ss_ref[held(0, k), :] = marks_ref[number, k]

        def forward(inner, _):
            group = number * (SPAN // STEP) + inner

            def step(masked):
                us = [u_ref[at(group, j), :] for j in range(STEP)]
                es = [e_ref[at(group, j), :] for j in range(STEP)]
                for k in range(poles):
                    lr, li = lam_ref[k], lam_ref[poles + k]
                    sr = ss_ref[held(inner * STEP, k), :]
                    si = ss_ref[held(inner * STEP, poles + k), :]
                    ar = ai = None
                    for j in range(STEP):
                        if masked:
                            keep = keep_ref[group * STEP + j]
                            sr, si = sr * keep, si * keep
                        sr, si = lr * sr - li * si + us[j], lr * si + li * sr
                        ss_ref[held(inner * STEP + j + 1, k), :] = sr
                        ss_ref[held(inner * STEP + j + 1, poles + k), :] = si
                        ar = es[j] * sr if ar is None else ar + es[j] * sr
                        ai = es[j] * si if ai is None else ai + es[j] * si
                    dres_ref[k] = dres_ref[k] + ar
                    dres_ref[poles + k] = dres_ref[poles + k] + ai

            by_flag(flag_ref[group], step)
            return 0

        lax.fori_loop(0, SPAN // STEP, forward, 0)

        def backward(outer, _):
            inner = SPAN // STEP - 1 - outer
            group = number * (SPAN // STEP) + inner

            def step(masked):
                es = [e_ref[at(group, j), :] for j in range(STEP)]
                ds = [None] * STEP
                for k in range(poles):
                    lr, li = lam_ref[k], lam_ref[poles + k]
                    rr, ri = res_ref[k], res_ref[poles + k]
                    tr, ti = bt_ref[k], bt_ref[poles + k]
                    gr, gi = g_ref[k], g_ref[poles + k]
                    for j in reversed(range(STEP)):
                        tr, ti = lr * tr + li * ti + es[j], lr * ti - li * tr
                        part = rr * tr + ri * ti
                        ds[j] = part if ds[j] is None else ds[j] + part
                        if masked:
                            keep = keep_ref[group * STEP + j]
                            tr, ti = tr * keep, ti * keep
                        sr = ss_ref[held(inner * STEP + j, k), :]
                        si = ss_ref[held(inner * STEP + j, poles + k), :]
                        gr = gr + (sr * tr + si * ti)
                        gi = gi + (sr * ti - si * tr)
                    bt_ref[k], bt_ref[poles + k] = tr, ti
                    g_ref[k], g_ref[poles + k] = gr, gi
                for j in range(STEP):
                    di_ref[at(group, j), :] = ds[j]

            by_flag(flag_ref[group], step)
            return 0

        lax.fori_loop(0, SPAN // STEP, backward, 0)
        return 0

    lax.fori_loop(0, count // SPAN, block, 0)

    def eighths(value):
        total = value[0:SUB]
        for start in range(SUB, ROWS, SUB):
            total = total + value[start : start + SUB]
        return total

    def natural(i, _):
        rows = pl.ds(pl.multiple_of(i * ROWS, ROWS), ROWS)
        cols = chunk_cols(cols_ref, i)
        query = filtered(zs_ref, taps_ref, cols, i, 0, width)
        key = filtered(zs_ref, taps_ref, cols, i, 1, width)
        value = filtered(zs_ref, taps_ref, cols, i, 2, width)
        mask = cols[:, 2:3]
        d_mixed = dmix_ref[rows, :].astype(F32)
        e = d_mixed * query
        dskip_ref[...] = dskip_ref[...] + eighths(e * (key * value * mask))
        d_inject = (collect(di_ref, i, width) + skip_ref[...] * e) * mask
        for stream, grad in enumerate((d_mixed * conv_ref[rows, :], d_inject * value, d_inject * key)):
            lanes = slice(stream * width, (stream + 1) * width)
            dc_ref[rows, lanes] = grad
            shifted = window(zs_ref, i, stream, width)
            for lag in range(3):
                product = grad * shifted[lag]
                if lag:
                    product = product * cols[:, lag - 1 : lag]
                slot = slice((lag * 3 + stream) * SUB, (lag * 3 + stream + 1) * SUB)
                dtaps_ref[slot, :] = dtaps_ref[slot, :] + eighths(product)
        return 0

    lax.fori_loop(0, count // ROWS, natural, 0)
    dc_ref[count : count + SUB, :] = jnp.zeros((SUB, 3 * width), F32)

    def spread_back(i, _):
        rows = pl.ds(pl.multiple_of(i * ROWS, ROWS), ROWS)
        beyond = pl.ds(pl.multiple_of(i * ROWS, ROWS), ROWS + SUB)
        cols = cols_ref[beyond, :]
        v1, v2 = cols[1 : 1 + ROWS, 0:1], cols[2 : 2 + ROWS, 1:2]
        for stream in range(3):
            lanes = slice(stream * width, (stream + 1) * width)
            wide = dc_ref[beyond, lanes]
            t0, t1, t2 = (taps_ref[lag * 3 + stream : lag * 3 + stream + 1, :] for lag in range(3))
            total = t0 * wide[0:ROWS] + (t1 * wide[1 : 1 + ROWS]) * v1 + (t2 * wide[2 : 2 + ROWS]) * v2
            dz_ref[rows, lanes] = total.astype(BF)

            @pl.when(i == count // ROWS - 1)
            def _():
                tail_ref[:, lanes] = total

        return 0

    lax.fori_loop(0, count // ROWS, spread_back, 0)
    first = cols_ref[0:SUB, :]
    for stream in range(3):
        lanes = slice(stream * width, (stream + 1) * width)
        dc = dc_ref[0:SUB, lanes]
        t1, t2 = (taps_ref[lag * 3 + stream : lag * 3 + stream + 1, :] for lag in (1, 2))
        one, two = t1 * (dc * first[:, 0:1]), t2 * (dc * first[:, 1:2])
        rimback_ref[...] = rimback_ref[...] if stream else jnp.zeros_like(rimback_ref)
        rimback_ref[0:1, lanes] = two[0:1]
        rimback_ref[1:2, lanes] = one[0:1] + two[1:2]


def call(kernel, ins, outs, scratch, smem, name, flops):
    vmem = pl.BlockSpec(memory_space=pltpu.VMEM)
    scalar = pl.BlockSpec(memory_space=pltpu.SMEM)
    moved = sum(a.size * a.dtype.itemsize for a in ins) + sum(
        functools.reduce(lambda x, y: x * y, s) * jnp.dtype(d).itemsize for s, d in outs
    )
    return pl.pallas_call(
        kernel,
        out_shape=[jax.ShapeDtypeStruct(s, d) for s, d in outs],
        in_specs=[scalar] * smem + [vmem] * (len(ins) - smem),
        out_specs=[vmem] * len(outs),
        scratch_shapes=[pltpu.VMEM(s, d) for s, d in scratch],
        compiler_params=pltpu.CompilerParams(vmem_limit_bytes=VMEM_LIMIT),
        cost_estimate=pl.CostEstimate(flops=flops, bytes_accessed=moved, transcendentals=0),
        name=name,
    )(*ins)


def segment_number(position, doc_lengths):
    starts_at = jnp.cumsum(doc_lengths) - doc_lengths
    hits = (starts_at[None, :] <= position[:, None]).astype(jnp.int32)
    return jnp.sum(hits, axis=1)


def norm_scale(values):
    return lax.rsqrt(jnp.mean(values * values, axis=-1, keepdims=True) + EPS)


def norm_back(values, scale, gain, grad):
    weighted = gain[None] * grad
    d_values = scale * weighted - values * scale**3 * jnp.mean(
        weighted * values, axis=-1, keepdims=True
    )
    return d_values, jnp.sum(grad * values * scale, axis=0)


def polar(exponent, decay_rate, pole_angle):
    magnitude = jnp.exp(-exponent * decay_rate)
    phase = exponent * pole_angle
    return magnitude * jnp.cos(phase), magnitude * jnp.sin(phase)


def packed(real, imag):
    rows = real.size // (SUB * LANE)
    return jnp.concatenate([real.reshape(rows, SUB, LANE), imag.reshape(rows, SUB, LANE)])


def unpacked(pair, shape):
    half = pair.shape[0] // 2
    return pair[:half].reshape(shape), pair[half:].reshape(shape)


def gather(block, axis, dim):
    return lax.all_gather(block, axis, axis=dim, tiled=True)


def scatter(block, axis, dim):
    return lax.psum_scatter(block, axis, scatter_dimension=dim, tiled=True)


def dot(a, b, dims):
    return lax.dot_general(a, b, (dims, ((), ())), preferred_element_type=F32)


def shards(tokens, lengths, pad_mask, gain_in, w_in, conv_taps, log_rate, pole_angle, residues,
           skip_gain, w_out, gain_mlp, w_gu, w_down, cotangent):
    micros, count, width = tokens.shape
    n_seq, n_tp = lax.axis_size("seq"), lax.axis_size("tp")
    me = lax.axis_index("seq")
    hidden = w_gu.shape[2]
    x_own = [tokens[m] for m in range(micros)]
    x_full = [gather(x, "tp", 1) for x in x_own]
    in_full = gather(w_in.reshape(w_in.shape[0], -1), "seq", 0)
    out_full = gather(gather(w_out, "seq", 1), "tp", 0)
    gu_full = gather(w_gu.reshape(w_gu.shape[0], -1), "seq", 0)
    down_full = gather(w_down, "seq", 1)
    cot_full = gather(cotangent, "tp", 2)

    rate = jnp.exp(log_rate)
    lam_real, lam_imag = polar(1.0, rate, pole_angle)
    lam = packed(lam_real, lam_imag)
    lam_all = packed(*polar(float(count), rate, pole_angle))
    res = packed(residues[0], residues[1])
    taps = conv_taps.reshape(9, width)
    skip = skip_gain.reshape(1, width)
    me_word = me.astype(jnp.int32).reshape(1)
    edges = jnp.arange(n_seq + 1) * count
    seq_shape = (count * SUB, LANE)
    st_shape = lam.shape
    work = lam.shape[0] * SUB * LANE * count

    kept = []
    outputs = []
    for m in range(micros):
        position = me * count + jnp.arange(-2, count + 1)
        seg = segment_number(position, lengths[m])
        valid1 = (seg[2:] == seg[1:-1]).astype(F32)
        valid1 = valid1.at[count].multiply((me < n_seq - 1).astype(F32))
        valid2 = (seg[2:-1] == seg[:-3]).astype(F32)
        mask = pad_mask[m].astype(F32)
        cols = jnp.zeros((count + SUB, SUB), F32)
        cols = cols.at[:count, 0].set(valid1[:count]).at[:count, 1].set(valid2).at[:count, 2].set(mask)
        keep = jnp.concatenate([valid1, jnp.zeros((SUB - 1,), F32)])
        flags = jnp.any(keep.reshape(-1, STEP) == 0, axis=1).astype(jnp.int32)
        last, first = segment_number(edges - 1, lengths[m]), segment_number(edges, lengths[m])
        spans = (last[1:] == last[:-1]).astype(F32)
        spans_back = (first[1:] == first[:-1]).astype(F32)

        x_wide = x_full[m].astype(F32)
        h_in = (x_wide * norm_scale(x_wide) * gain_in[None]).astype(BF)
        z_low = dot(h_in, in_full, ((1,), (0,))).astype(BF)
        rim = lax.ppermute(z_low[count - 2 :], "seq", [(i, i + 1) for i in range(n_seq - 1)])
        rim = jnp.concatenate([jnp.zeros((SUB - 2, 3 * width), F32), rim.astype(F32)])
        base = (z_low, rim, taps, cols, lam)
        zs = ((count + SUB, 3 * width), F32)
        u, end = call(front_kernel, (keep, flags, *base), [(seq_shape, F32), (st_shape, F32)],
                      [zs], 2, "mixer_front", 4 * work)
        ends = lax.all_gather(end, "seq")
        mixed, conv_out, marks = call(
            finish_kernel,
            (keep, flags, spans, me_word, *base, lam_all, res, skip, u, ends),
            [((count, width), BF), ((count, width), F32), ((count // SPAN, *st_shape), F32)],
            [zs, (seq_shape, F32), (st_shape, F32)], 4, "mixer_finish", 6 * work,
        )
        mixed_full = gather(mixed, "tp", 1)
        x_mid = x_wide + dot(mixed_full, out_full, ((1,), (0,)))
        scale_mid = norm_scale(x_mid)
        h_mlp = (x_mid * scale_mid * gain_mlp[None]).astype(BF)
        gate_up = dot(h_mlp, gu_full, ((1,), (0,)))
        gate, up = gate_up[:, :hidden], gate_up[:, hidden:]
        sig = jax.nn.sigmoid(gate)
        act = (gate * sig * up).astype(BF)
        down_own = scatter(dot(act, down_full, ((1,), (0,))).astype(BF), "tp", 1)
        mid_own = lax.dynamic_slice_in_dim(x_mid, lax.axis_index("tp") * width, width, 1)
        outputs.append((mid_own + down_own.astype(F32)).astype(BF))

        cot = cot_full[m]
        d_act = dot(cot, down_full, ((1,), (1,)))
        d_gu = jnp.concatenate(
            [d_act * up * sig * (1.0 + gate * (1.0 - sig)), d_act * gate * sig], axis=1
        ).astype(BF)
        d_h = dot(d_gu, gu_full, ((1,), (1,)))
        d_norm, d_gain_mlp = norm_back(x_mid, scale_mid, gain_mlp, d_h)
        d_mid = d_norm + cot.astype(F32) * (1.0 / n_tp)
        d_low = d_mid.astype(BF)
        d_mixed = scatter(dot(d_low, out_full, ((1,), (1,))).astype(BF), "tp", 1)
        kept.append(dict(
            base=base, zs=zs, keep=keep, flags=flags, spans=spans_back, u=u, conv=conv_out,
            marks=marks, mixed=mixed_full, h_mlp=h_mlp, act=act, d_gu=d_gu, d_mid=d_mid,
            d_low=d_low, d_mixed=d_mixed, x_wide=x_wide, h_in=h_in, d_gain_mlp=d_gain_mlp,
        ))

    token_grads = []
    smalls = []
    for m in range(micros):
        c = kept[m]
        base, zs, u, d_mixed = c["base"], c["zs"], c["u"], c["d_mixed"]
        e, end = call(adjoint_kernel, (c["keep"], c["flags"], *base, d_mixed),
                      [(seq_shape, F32), (st_shape, F32)], [zs], 2, "mixer_adjoint", 4 * work)
        ends = lax.all_gather(end, "seq")
        d_z, rim_back, tail, d_taps, d_skip, d_res, d_lam = call(
            back_kernel,
            (c["keep"], c["flags"], c["spans"], me_word, *base, lam_all, res, skip, u, e, d_mixed,
             c["conv"], c["marks"], ends),
            [((count, 3 * width), BF), ((SUB, 3 * width), F32), ((ROWS, 3 * width), F32),
             ((9 * SUB, width), F32), ((SUB, width), F32), (st_shape, F32), (st_shape, F32)],
            [zs, ((count + SUB, 3 * width), F32), (seq_shape, F32),
             (((SPAN + 1) * st_shape[0] * SUB, LANE), F32), (st_shape, F32)],
            4, "mixer_back", 16 * work,
        )
        rim_back = lax.ppermute(rim_back[:2], "seq", [(i + 1, i) for i in range(n_seq - 1)])
        tail = (tail + jnp.concatenate([jnp.zeros((ROWS - 2, 3 * width), F32), rim_back])).astype(BF)
        d_z = lax.dynamic_update_slice(d_z, tail, (count - ROWS, 0))
        d_h_in = dot(d_z, in_full, ((1,), (1,)))
        d_norm, d_gain_in = norm_back(c["x_wide"], norm_scale(c["x_wide"]), gain_in, d_h_in)
        token_grads.append(scatter((c["d_mid"] + d_norm).astype(BF), "tp", 1))
        g_real, g_imag = unpacked(d_lam, log_rate.shape)
        s_real, s_imag = unpacked(d_res, log_rate.shape)
        h_real = residues[0] * g_real + residues[1] * g_imag
        h_imag = residues[0] * g_imag - residues[1] * g_real
        c["d_z"] = d_z
        smalls.append(jnp.concatenate([
            jnp.sum(d_taps.reshape(9, SUB, width), axis=1),
            -rate * (lam_real * h_real + lam_imag * h_imag),
            lam_real * h_imag - lam_imag * h_real,
            s_real, -s_imag,
            jnp.sum(d_skip, axis=0, keepdims=True),
            d_gain_in.reshape(-1, width), c["d_gain_mlp"].reshape(-1, width),
        ]))

    def both(name):
        return jnp.concatenate([c[name] for c in kept])

    rows = ((0,), (0,))
    g_down = scatter(dot(both("act"), cot_full.reshape(micros * count, -1), rows).astype(BF), "seq", 1)
    g_gu = scatter(dot(both("h_mlp"), both("d_gu"), rows).astype(BF), "seq", 0)
    g_out = scatter(dot(both("mixed"), both("d_low"), rows).astype(BF), "seq", 1)
    g_out = scatter(g_out, "tp", 0)
    g_in = scatter(dot(both("h_in"), both("d_z"), rows).astype(BF), "seq", 0)

    small = sum(smalls)
    small = jnp.sum(lax.all_gather(small.astype(BF), "seq").astype(F32), axis=0)
    n_gain = 2 * (gain_in.shape[0] // width)
    n_pole = log_rate.shape[0]
    gains = jnp.sum(lax.all_gather(small[-n_gain:].astype(BF), "tp").astype(F32), axis=0)
    cuts = [9, 9 + n_pole, 9 + 2 * n_pole, 9 + 3 * n_pole, 9 + 4 * n_pole]
    return (
        jnp.stack(outputs),
        jnp.stack(token_grads),
        gains[: n_gain // 2].reshape(-1),
        g_in.astype(F32).reshape(w_in.shape),
        small[: cuts[0]].reshape(conv_taps.shape),
        small[cuts[0] : cuts[1]],
        small[cuts[1] : cuts[2]],
        small[cuts[2] : cuts[4]].reshape(residues.shape),
        small[cuts[4]],
        g_out.astype(F32),
        gains[n_gain // 2 :].reshape(-1),
        g_gu.astype(F32).reshape(w_gu.shape),
        g_down.astype(F32),
    )


def solution(mesh):
    wide, deep, flat = P(None, "seq", "tp"), P("seq", None, "tp"), P("tp", "seq")
    poles, taps = P(None, "tp"), P(None, None, "tp")
    return jax.shard_map(
        shards,
        mesh=mesh,
        in_specs=(wide, P(), P(None, "seq"), P(), deep, taps, poles, poles, taps, P("tp"), flat,
                  P(), deep, flat, wide),
        out_specs=(wide, wide, P(), deep, taps, poles, poles, taps, P("tp"), flat, P(), deep, flat),
        check_vma=False,
    )
```

time: 4540 us -> 1340 us (0.30)
  other arithmetic: 2620 us -> 47 us
  local copies, waits for them, and re-layouts: 780 us -> 43.6 us
  Pallas kernels: 0 us -> 148 us
  blocking collectives: 136 us -> 72 us
    reduce_sum x60 -> x8, other arithmetic: 1090 us -> 4.52 us  [the longest x2 4.3 us: norm_scale(): return lax.rsqrt(jnp.mean(values * values, axis=-1, keepdims=True) + EPS)]
    dot_general x96 -> x0, other arithmetic: 631 us -> none  [the longest x32 274 us: conv_block(): sum_imag = jnp.einsum('snc,sc->nc', end_imag, weighted, precision=highest)]
    gather x33 -> x0, local copies, waits for them, and re-layouts: 556 us -> none  [conv_block(): kernel[jnp.clip(offset, 0, block_len - 1)]]
    scatter-add x16 -> x0, other arithmetic: 433 us -> none  [conv_block(): kernel[jnp.clip(offset, 0, block_len - 1)]]
    psum x4 -> x0, waiting for transfers between devices: 214 us -> none  [the longest x1 102 us: shards(): dh_in = lax.psum(dh_in_part.astype(jnp.bfloat16), 'tp').astype(jnp.float32)]
    all_gather x8 -> x10, waiting for transfers between devices: 258 us -> 458 us  [gather(): return lax.all_gather(block, axis, axis=dim, tiled=True)]
    pallas_call x0 -> x8, Pallas kernels: none -> 148 us  [call(): pl.pallas_call(kernel, out_shape=[jax.ShapeDtypeStruct(s, d) for s, d in...]
    select_n x77 -> x0, other arithmetic: 101 us -> none  [the longest x16 63.8 us: conv_block(): jnp.where(same_seg[:, :, None], kernel[jnp.clip(offset, 0, block_len - 1)...]
  transfers between devices with their start and end apart: 22 -> 25, of which waited for: 18 -> 17; matrix products, arithmetic and copies ran while one was open for 37% -> 16% of each run, Pallas kernels for 0% -> 11%
where the time goes in v1:
time: 1340 us; the launch traced here: 1330 us
  waiting for transfers between devices  789 us (59%)
  matrix products  203 us (15%)
  Pallas kernels  148 us (11%)
  blocking collectives  72 us (5%)
  other arithmetic  47 us (4%)
  local copies, waits for them, and re-layouts  43.6 us (3%)
  between operations  15.8 us (1%)
    all_gather x10, waiting for transfers between devices, gather(): return lax.all_gather(block, axis, axis=dim, tiled=True)  458 us
    reduce_scatter x11, waiting for transfers between devices, scatter(): return lax.psum_scatter(block, axis, scatter_dimension=dim, tiled=True)  326 us
    dot_general x20, matrix products, dot(): return lax.dot_general(a, b, (dims, ((), ())), preferred_element_type=F32)  203 us
    pallas_call x8, Pallas kernels, call(): pl.pallas_call(kernel, out_shape=[jax.ShapeDtypeStruct(s, d) for s, d in...  148 us
    all_gather x4, blocking collectives, shards(): ends = lax.all_gather(end, 'seq')  48.2 us
  transfers between devices with their start and end apart: 25, of which 17 were waited for; matrix products, arithmetic and copies ran while one was open for 16% of the time, Pallas kernels for 11%

profile of v1, /device:TPU:0, one launch (start us, length us, event | category | flops | bytes accessed | tf_op | source)
XLA Modules:
  0.0 1326.6 jit_solution(3627986653167329922)
XLA Ops:
  7.3 2.2 fusion.79
  10.3 2.3 copy.47
  16.9 3.2 scatter.21
  23.4 35.5 %all-gather.34.cloned.1.call-done = bf16[1,512,2048]{2,1,0:T(8,128)(2,1)} async-done(((bf16[1,512,512]{2,1,0:T(8,128)(2,1)}), bf16[1,512,2048]{2,1,0:T(8,128)(2,1)}) %all-gather.34.cloned.1.call-update) | async-done | bytes 2097168 | tf_op jit(solution)/shard_map/all_gather | solution.py:418
  61.7 44.0 %all-gather.36.cloned.1.call-done = bf16[1,512,2048]{2,1,0:T(8,128)(2,1)} async-done(((bf16[1,512,512]{2,1,0:T(8,128)(2,1)}), bf16[1,512,2048]{2,1,0:T(8,128)(2,1)}) %all-gather.36.cloned.1.call-update) | async-done | bytes 2097168 | tf_op jit(solution)/shard_map/all_gather | solution.py:418
  109.0 4.6 fusion.9
  113.6 40.0 %all-gather.18.cloned.1.call-done = bf16[2048,1536]{0,1:T(8,128)(2,1)} async-done(((bf16[256,1536]{0,1:T(8,128)(2,1)}), bf16[2048,1536]{0,1:T(8,128)(2,1)}) %all-gather.18.cloned.1.call-update) | async-done | bytes 6291472 | tf_op jit(solution)/shard_map/all_gather | solution.py:418
  153.6 6.9 convolution_convert_fusion.7.z_ref
  164.7 3.3 scatter.24.cols_ref
  168.7 12.0 mixer_front.2
  180.7 11.2 all-gather.1
  191.8 15.8 %mixer_finish.2 = (bf16[512,512]{1,0:T(8,128)(2,1)}, f32[512,512]{1,0:T(8,128)}, f32[8,16,8,128]{3,2,1,0:T(8,128)}) custom-call(f32[520]{0:T(1024)} %concatenate.128.keep_ref, s32[65]{0:T(128)} %convert_element_type.190.flag_ref, f32[8]{0:T(128)} %compare_convert_fusion.3.spans_ref, s32[1]{0:T(128)} %bitcast.3.me_ref, bf16[512,1536]{1,0:T(8,128)(2,1)} %copy-done, ...), custom_call_target="tpu_custom_call" | custom-call | flops 50331648 | bytes 6576712 | tf_op jit(solution)/shard_map/mixer_finish/pallas_call | solution.py:371
  209.1 3.2 scatter.26
  212.8 2.7 dynamic-slice_select_fusion
  215.6 7.0 convolution_convert_fusion.6.z_ref
  222.6 2.2 collective-permute-start.1
  226.3 3.8 scatter.29.cols_ref
  230.9 12.0 mixer_front.3
  242.9 11.2 all-gather.3
  254.1 15.9 %mixer_finish.3 = (bf16[512,512]{1,0:T(8,128)(2,1)}, f32[512,512]{1,0:T(8,128)}, f32[8,16,8,128]{3,2,1,0:T(8,128)}) custom-call(f32[520]{0:T(1024)} %concatenate.134.keep_ref, s32[65]{0:T(128)} %convert_element_type.205.flag_ref, f32[8]{0:T(128)} %compare_convert_fusion.2.spans_ref, s32[1]{0:T(128)} %bitcast.3.me_ref, bf16[512,1536]{1,0:T(8,128)(2,1)} %copy-done.1, ...), custom_call_target="tpu_custom_call" | custom-call | flops 50331648 | bytes 6576712 | tf_op jit(solution)/shard_map/mixer_finish/pallas_call | solution.py:371
  273.1 130.7 %all-gather.24.cloned.1.call-done = bf16[2048,2048]{1,0:T(8,128)(2,1)} async-done(((bf16[512,2048]{1,0:T(8,128)(2,1)}), bf16[2048,2048]{1,0:T(8,128)(2,1)}) %all-gather.24.cloned.1.call-update) | async-done | bytes 8388624 | tf_op jit(solution)/shard_map/all_gather | solution.py:418
  403.8 10.6 multiply_reduce_fusion.5
  414.3 35.1 %all-gather.30.cloned.1.call-done = bf16[512,2048]{1,0:T(8,128)(2,1)} async-done(((bf16[512,512]{1,0:T(8,128)(2,1)}), bf16[512,2048]{1,0:T(8,128)(2,1)}) %all-gather.30.cloned.1.call-update) | async-done | bytes 2097168 | tf_op jit(solution)/shard_map/all_gather | solution.py:418
  449.5 11.3 multiply_reduce_fusion.4
  461.2 57.2 %all-gather.26.cloned.1.call-done = bf16[2048,2816]{1,0:T(8,128)(2,1)} async-done(((bf16[256,2816]{1,0:T(8,128)(2,1)}), bf16[2048,2816]{1,0:T(8,128)(2,1)}) %all-gather.26.cloned.1.call-update) | async-done | bytes 11534352 | tf_op jit(solution)/shard_map/all_gather | solution.py:418
  518.4 11.6 fusion.87
  530.0 70.8 %all-gather.32.cloned.1.call-done = bf16[2,512,2048]{2,1,0:T(8,128)(2,1)} async-done(((bf16[2,512,512]{2,1,0:T(8,128)(2,1)}), bf16[2,512,2048]{2,1,0:T(8,128)(2,1)}) %all-gather.32.cloned.1.call-update) | async-done | bytes 4194320 | tf_op jit(solution)/shard_map/all_gather | solution.py:418
  600.8 44.6 %all-gather.28.cloned.1.call-done = bf16[1408,2048]{1,0:T(8,128)(2,1)} async-done(((bf16[1408,256]{1,0:T(8,128)(2,1)}), bf16[1408,2048]{1,0:T(8,128)(2,1)}) %all-gather.28.cloned.1.call-update) | async-done | bytes 5767184 | tf_op jit(solution)/shard_map/all_gather | solution.py:418
  645.5 11.3 multiply_convert_fusion.5
  656.8 14.9 %multiply_reduce_fusion.1 = (f32[2048]{0:T(1024)}, f32[512]{0:T(512)S(1)}, bf16[512,2048]{1,0:T(8,128)(2,1)S(1)}, f32[512,2048]{1,0:T(8,128)}) fusion(f32[512,2048]{1,0:T(8,128)} %get-tuple-element.300, f32[512]{0:T(512)S(1)} %get-tuple-element.286, f32[2048]{0:T(1024)S(1)} %copy-done.42, f32[512,2048]{1,0:T(8,128)} %get-tuple-element.302, ...), kind=kOutput, calls=%fused_computation.56 | convolution fusion | flops 5920781824 | bytes 29120512 | tf_op jit(solution)/shard_map/dot_general | solution.py:426
  671.7 11.9 fusion.88
  683.6 8.1 multiply_convert_fusion.3
  691.8 11.8 multiply_reduce_fusion
  703.5 7.2 fusion.77
  712.1 9.3 convolution_convert_fusion.4
  721.5 9.1 convolution_convert_fusion.5
  730.7 14.0 %convolution_convert_fusion.2 = bf16[2048,2048]{1,0:T(8,128)(2,1)} fusion(bf16[512,2048]{1,0:T(8,128)(2,1)} %all-gather.30.cloned.1.call-done, bf16[512,2048]{1,0:T(8,128)(2,1)} %all-gather.20.cloned.1.call-done, bf16[512,2048]{1,0:T(8,128)(2,1)} %copy-done.20, bf16[512,2048]{1,0:T(8,128)(2,1)S(1)} %copy-done.19), kind=kOutput, calls=%fused_computation.14 | convolution fusion | flops 8610906112 | bytes 16777216 | tf_op jit(solution)/shard_map/dot_general | solution.py:426
  744.9 8.0 convolution_convert_fusion.8
  754.2 7.4 convolution_convert_fusion.9
  761.7 3.8 reduce-scatter.20.cloned.1.call-done.dmix_ref
  765.5 11.9 mixer_adjoint.3
  777.4 11.5 all-gather.5
  788.9 33.6 %mixer_back.3 = (bf16[512,1536]{1,0:T(8,128)(2,1)}, f32[8,1536]{1,0:T(8,128)}, f32[16,1536]{1,0:T(8,128)}, f32[72,512]{1,0:T(8,128)}, f32[8,512]{1,0:T(8,128)}, ...) custom-call(f32[520]{0:T(1024)} %concatenate.134.keep_ref, s32[65]{0:T(128)} %convert_element_type.205.flag_ref, ...), custom_call_target="tpu_custom_call" | custom-call | flops 134217728 | bytes 10689096 | tf_op jit(solution)/shard_map/mixer_back/pallas_call | solution.py:371
  824.6 12.3 mixer_adjoint.2
  836.9 14.2 %all-gather.4 = f32[128,8,128]{2,1,0:T(8,128)} all-gather(f32[16,8,128]{2,1,0:T(8,128)} %get-tuple-element.146), channel_id=6, replica_groups=mesh['seq'=8,'tp'=4] {'seq'}, dimensions={0}, use_global_device_ids=true | all-gather | bytes 589824 | tf_op jit(solution)/shard_map/all_gather | solution.py:524
  851.1 34.2 %mixer_back.2 = (bf16[512,1536]{1,0:T(8,128)(2,1)}, f32[8,1536]{1,0:T(8,128)}, f32[16,1536]{1,0:T(8,128)}, f32[72,512]{1,0:T(8,128)}, f32[8,512]{1,0:T(8,128)}, ...) custom-call(f32[520]{0:T(1024)} %concatenate.128.keep_ref, s32[65]{0:T(128)} %convert_element_type.190.flag_ref, ...), custom_call_target="tpu_custom_call" | custom-call | flops 134217728 | bytes 10689096 | tf_op jit(solution)/shard_map/mixer_back/pallas_call | solution.py:371
  890.8 6.1 fusion.89
  897.1 5.0 fusion.16
  902.1 3.9 fusion.13
  907.4 10.0 convolution_convert_fusion.1
  919.0 11.0 convolution_convert_fusion.3
  931.6 18.0 %convolution_convert_fusion = bf16[2048,2816]{1,0:T(8,128)(2,1)} fusion(bf16[512,1408]{1,0:T(8,128)(2,1)} %get-tuple-element.244, bf16[512,1408]{1,0:T(8,128)(2,1)} %get-tuple-element.243, bf16[512,1408]{1,0:T(8,128)(2,1)} %get-tuple-element.242, bf16[512,1408]{1,0:T(8,128)(2,1)} %get-tuple-element.241, bf16[512,2048]{1,0:T(8,128)(2,1)} %copy-done.62, ...), kind=kOutput, calls=%fused_computation | convolution fusion | flops 11848384512 | bytes 21495808 | tf_op jit(solution)/shard_map/dot_general | solution.py:426
  952.4 25.8 %reduce-scatter.12.cloned.1.call-done = bf16[512,512]{1,0:T(8,128)(2,1)} async-done(((bf16[512,2048]{1,0:T(8,128)(2,1)}), bf16[512,512]{1,0:T(8,128)(2,1)}) %reduce-scatter.12.cloned.1.call-update) | async-done | bytes 524304 | tf_op jit(solution)/shard_map/reduce_scatter | solution.py:422
  982.3 10.2 all_gather.82
  993.9 13.6 %all-gather.6 = bf16[32,512]{1,0:T(8,128)(2,1)S(1)} all-gather(bf16[8,512]{1,0:T(8,128)(2,1)S(1)} %slice.443), channel_id=8, replica_groups=mesh['seq'=8,'tp'=4] {'tp'}, dimensions={0}, use_global_device_ids=true | all-gather | bytes 40960 | tf_op jit(solution)/shard_map/all_gather | solution.py:569
  1009.9 14.3 %reduce-scatter.22.cloned.1.call-done = bf16[512,512]{1,0:T(8,128)(2,1)} async-done(((bf16[512,2048]{1,0:T(8,128)(2,1)}), bf16[512,512]{1,0:T(8,128)(2,1)}) %reduce-scatter.22.cloned.1.call-update) | async-done | bytes 524304 | tf_op jit(solution)/shard_map/reduce_scatter | solution.py:422
  1024.2 45.4 %reduce-scatter.18.cloned.1.call-done = bf16[512,512]{1,0:T(8,128)(2,1)} async-done(((bf16[512,2048]{1,0:T(8,128)(2,1)}), bf16[512,512]{1,0:T(8,128)(2,1)}) %reduce-scatter.18.cloned.1.call-update) | async-done | bytes 524304 | tf_op jit(solution)/shard_map/reduce_scatter | solution.py:422
  1069.6 2.3 pad_maximum_fusion.1
  1071.9 59.8 %reduce-scatter.32.cloned.1.call-done = bf16[1408,256]{1,0:T(8,128)(2,1)} async-done(((bf16[1408,2048]{1,0:T(8,128)(2,1)}), bf16[1408,256]{1,0:T(8,128)(2,1)}) %reduce-scatter.32.cloned.1.call-update) | async-done | bytes 720912 | tf_op jit(solution)/shard_map/reduce_scatter | solution.py:422
  1131.6 2.3 convert_element_type.239
  1134.0 62.8 %reduce-scatter.24.cloned.1.call-done = bf16[256,1536]{1,0:T(8,128)(2,1)} async-done(((bf16[2048,1536]{1,0:T(8,128)(2,1)}), bf16[256,1536]{1,0:T(8,128)(2,1)}) %reduce-scatter.24.cloned.1.call-update) | async-done | bytes 786448 | tf_op jit(solution)/shard_map/reduce_scatter | solution.py:422
  1199.8 26.4 %reduce-scatter.28.cloned.1.call-done = bf16[512,256]{1,0:T(8,128)(2,1)} async-done(((bf16[2048,256]{1,0:T(8,128)(2,1)}), bf16[512,256]{1,0:T(8,128)(2,1)}) %reduce-scatter.28.cloned.1.call-update) | async-done | bytes 262160 | tf_op jit(solution)/shard_map/reduce_scatter | solution.py:422
  1228.0 87.2 %reduce-scatter.30.cloned.1.call-done = bf16[256,2816]{1,0:T(8,128)(2,1)} async-done(((bf16[2048,2816]{1,0:T(8,128)(2,1)}), bf16[256,2816]{1,0:T(8,128)(2,1)}) %reduce-scatter.30.cloned.1.call-update) | async-done | bytes 1441808 | tf_op jit(solution)/shard_map/reduce_scatter | solution.py:422
  1315.2 4.3 reshape.697
  (304 shorter events, 56.6 us)
Async XLA Ops:
  7.2 8.1 copy-start.59
  7.2 7.4 copy-start.54
  7.2 8.7 copy-start.41
  7.2 8.7 copy-start.32
  7.2 9.0 copy-start.28
  7.2 51.6 %all-gather.34.cloned.1.call-start = ((), (), s32[]{:S(2)}) async-start(), calls=%async_computation.30 | async-start | bytes 2621440 | tf_op jit(solution)/shard_map/all_gather | solution.py:418
  9.6 96.2 %all-gather.36.cloned.1.call-start = ((), (), s32[]{:S(2)}) async-start(), calls=%async_computation.31 | async-start | bytes 2621440 | tf_op jit(solution)/shard_map/all_gather | solution.py:418
  10.3 143.3 %all-gather.18.cloned.1.call-start = ((), (), s32[]{:S(2)}) async-start(), calls=%async_computation.11 | async-start | bytes 7077888 | tf_op jit(solution)/shard_map/all_gather | solution.py:418
  12.7 96.3 %copy-start.39 = (f32[2048]{0:T(1024)S(1)}, f32[2048]{0:T(1024)}, u32[]{:S(2)}) copy-start(f32[2048]{0:T(1024)} %param.34) | copy-start | bytes 24580
  12.7 195.1 %all-gather.22.cloned.1.call-start = ((), (), s32[]{:S(2)}) async-start(), calls=%async_computation.13 | async-start | bytes 2359296 | tf_op jit(solution)/shard_map/all_gather | solution.py:418
  13.3 259.8 %all-gather.20.cloned.1.call-start = ((), (), s32[]{:S(2)}) async-start(), calls=%async_computation.12 | async-start | bytes 2621440 | tf_op jit(solution)/shard_map/all_gather | solution.py:418
  16.3 97.3 %copy-start.13 = (f32[16,8,128]{2,1,0:T(8,128)}, f32[16,8,128]{2,1,0:T(8,128)S(1)}, u32[]{:S(2)}) copy-start(f32[16,8,128]{2,1,0:T(8,128)S(1)} %constant_dynamic-update-slice_fusion.lam_ref) | copy-start | bytes 196612
  20.1 93.5 %copy-start.22 = (f32[16,8,128]{2,1,0:T(8,128)}, f32[16,8,128]{2,1,0:T(8,128)S(1)}, u32[]{:S(2)}) copy-start(f32[16,8,128]{2,1,0:T(8,128)S(1)} %get-tuple-element.312.full_ref) | copy-start | bytes 196612
  20.1 93.5 %copy-start.23 = (f32[16,8,128]{2,1,0:T(8,128)}, f32[16,8,128]{2,1,0:T(8,128)S(1)}, u32[]{:S(2)}) copy-start(f32[16,8,128]{2,1,0:T(8,128)S(1)} %get-tuple-element.313.res_ref) | copy-start | bytes 196612
  58.9 50.1 %copy-start.4 = (bf16[1,512,2048]{2,1,0:T(8,128)(2,1)S(1)}, bf16[1,512,2048]{2,1,0:T(8,128)(2,1)}, u32[]{:S(2)}) copy-start(bf16[1,512,2048]{2,1,0:T(8,128)(2,1)} %all-gather.34.cloned.1.call-done) | copy-start | bytes 6291460
  61.7 51.9 %copy-start.44 = (f32[512]{0:T(512)}, f32[512]{0:T(512)S(1)}, u32[]{:S(2)}) copy-start(f32[512]{0:T(512)S(1)} %get-tuple-element.284) | copy-start | bytes 6148
  153.6 10.4 copy-start.43
  160.5 8.2 copy-start
  160.5 7.4 collective-permute-start
  207.7 196.1 %all-gather.24.cloned.1.call-start = ((), (), s32[]{:S(2)}) async-start(), calls=%async_computation.14 | async-start | bytes 10485760 | tf_op jit(solution)/shard_map/all_gather | solution.py:418
  208.2 241.2 %all-gather.30.cloned.1.call-start = ((), (), s32[]{:S(2)}) async-start(), calls=%async_computation.18 | async-start | bytes 2621440 | tf_op jit(solution)/shard_map/all_gather | solution.py:418
  222.6 8.3 copy-start.1
  222.6 7.5 collective-permute-start.1
  226.3 43.8 %copy-start.21 = (bf16[256,2,1408]{2,1,0:T(2,128)(2,1)S(1)}, bf16[256,2,1408]{2,1,0:T(2,128)(2,1)}, u32[]{:S(2)}) copy-start(bf16[256,2,1408]{2,1,0:T(2,128)(2,1)} %param.43) | copy-start | bytes 4325380
  270.0 133.7 %copy-start.5 = (bf16[1,512,2048]{2,1,0:T(8,128)(2,1)S(1)}, bf16[1,512,2048]{2,1,0:T(8,128)(2,1)}, u32[]{:S(2)}) copy-start(bf16[1,512,2048]{2,1,0:T(8,128)(2,1)} %all-gather.34.cloned.1.call-done) | copy-start | bytes 6291460
  270.0 248.4 %all-gather.26.cloned.1.call-start = ((), (), s32[]{:S(2)}) async-start(), calls=%async_computation.15 | async-start | bytes 12976128 | tf_op jit(solution)/shard_map/all_gather | solution.py:418
  271.4 329.4 %all-gather.32.cloned.1.call-start = ((), (), s32[]{:S(2)}) async-start(), calls=%async_computation.20 | async-start | bytes 5242880 | tf_op jit(solution)/shard_map/all_gather | solution.py:418
  272.1 373.3 %all-gather.28.cloned.1.call-start = ((), (), s32[]{:S(2)}) async-start(), calls=%async_computation.16 | async-start | bytes 6488064 | tf_op jit(solution)/shard_map/all_gather | solution.py:418
  272.7 492.8 %reduce-scatter.20.cloned.1.call-start = ((), (), s32[]{:S(2)}) async-start(), calls=%async_computation.23 | async-start | bytes 2621440 | tf_op jit(solution)/shard_map/reduce_scatter | solution.py:422
  414.3 46.5 %copy-start.42 = (f32[2048]{0:T(1024)S(1)}, f32[2048]{0:T(1024)}, u32[]{:S(2)}) copy-start(f32[2048]{0:T(1024)} %param.42) | copy-start | bytes 24580
  449.5 11.3 copy-start.2
  461.2 68.8 %copy-start.17 = (bf16[512,2048]{1,0:T(8,128)(2,1)}, bf16[512,2048]{1,0:T(8,128)(2,1)S(1)}, u32[]{:S(2)}) copy-start(bf16[512,2048]{1,0:T(8,128)(2,1)S(1)} %multiply_convert_fusion.1) | copy-start | bytes 6291460
  671.7 11.9 copy-start.62
  671.7 11.9 copy-start.14
  671.7 11.9 copy-start.57
  683.6 8.1 copy-start.12
  691.8 11.8 copy-start.3
  691.8 11.8 copy-start.15
  712.1 9.4 copy-start.19
  721.5 103.2 %reduce-scatter.16.cloned.1.call-start = ((), (), s32[]{:S(2)}) async-start(), calls=%async_computation.21 | async-start | bytes 2621440 | tf_op jit(solution)/shard_map/reduce_scatter | solution.py:422
  730.7 199.4 %reduce-scatter.26.cloned.1.call-start = ((), (), s32[]{:S(2)}) async-start(), calls=%async_computation.26 | async-start | bytes 9437184 | tf_op jit(solution)/shard_map/reduce_scatter | solution.py:422
  744.8 206.1 %reduce-scatter.14.cloned.1.call-start = ((), (), s32[]{:S(2)}) async-start(), calls=%async_computation.19 | async-start | bytes 2621440 | tf_op jit(solution)/shard_map/reduce_scatter | solution.py:422
  744.8 8.1 copy-start.56
  744.8 8.7 copy-start.55
  744.9 9.4 copy-start.60
  752.9 225.4 %reduce-scatter.12.cloned.1.call-start = ((), (), s32[]{:S(2)}) async-start(), calls=%async_computation.17 | async-start | bytes 2621440 | tf_op jit(solution)/shard_map/reduce_scatter | solution.py:422
  761.6 262.6 %reduce-scatter.22.cloned.1.call-start = ((), (), s32[]{:S(2)}) async-start(), calls=%async_computation.24 | async-start | bytes 2621440 | tf_op jit(solution)/shard_map/reduce_scatter | solution.py:422
  823.3 64.2 %collective-permute-start.3 = (f32[2,1536]{1,0:T(2,128)S(1)}, f32[2,1536]{1,0:T(2,128)S(1)}, u32[]{:S(2)}, u32[]{:S(2)}) collective-permute-start(f32[2,1536]{1,0:T(2,128)S(1)} %slice.341), channel_id=1, source_target_pairs={{4,0},{8,4},{12,8},{16,12},{20,16},{24,20},{28,24},{5,1},{9,5},{13... | collective-permute-start | bytes 36872 | tf_op jit(solution)/shard_map/ppermute | solution.py:535
  851.1 36.4 %copy-start.34 = (f32[16,1536]{1,0:T(8,128)S(1)}, f32[16,1536]{1,0:T(8,128)}, u32[]{:S(2)}) copy-start(f32[16,1536]{1,0:T(8,128)} %get-tuple-element.155) | copy-start | bytes 294916
  851.1 45.8 %slice-start = ((s8[6291456]{0:T(1024)(128)(4,1)}), s8[4194304]{0:T(1024)(128)(4,1)S(1)}, s32[]{:S(2)}) async-start(s8[6291456]{0:T(1024)(128)(4,1)} %bitcast.183), calls=%async_computation.32 | async-start | bytes 8388608
  886.2 3.1 collective-permute-start.2
  890.8 6.2 copy-start.45
  890.8 6.2 copy-start.47
  890.8 6.2 slice-start.1
  890.8 6.2 copy-start.58
  906.1 163.5 %reduce-scatter.18.cloned.1.call-start = ((), (), s32[]{:S(2)}) async-start(), calls=%async_computation.22 | async-start | bytes 2621440 | tf_op jit(solution)/shard_map/reduce_scatter | solution.py:422
  906.7 225.0 %reduce-scatter.32.cloned.1.call-start = ((), (), s32[]{:S(2)}) async-start(), calls=%async_computation.29 | async-start | bytes 6488064 | tf_op jit(solution)/shard_map/reduce_scatter | solution.py:422
  917.5 279.3 %reduce-scatter.24.cloned.1.call-start = ((), (), s32[]{:S(2)}) async-start(), calls=%async_computation.25 | async-start | bytes 7077888 | tf_op jit(solution)/shard_map/reduce_scatter | solution.py:422
  930.1 296.2 %reduce-scatter.28.cloned.1.call-start = ((), (), s32[]{:S(2)}) async-start(), calls=%async_computation.27 | async-start | bytes 1310720 | tf_op jit(solution)/shard_map/reduce_scatter | solution.py:422
  930.6 384.6 %reduce-scatter.30.cloned.1.call-start = ((), (), s32[]{:S(2)}) async-start(), calls=%async_computation.28 | async-start | bytes 12976128 | tf_op jit(solution)/shard_map/reduce_scatter | solution.py:422
  949.7 31.2 %copy-start.25 = (f32[16,512]{1,0:T(8,128)S(1)}, f32[16,512]{1,0:T(8,128)}, u32[]{:S(2)}) copy-start(f32[16,512]{1,0:T(8,128)} %copy-done.24) | copy-start | bytes 98308
  949.7 31.2 %copy-start.27 = (f32[16,512]{1,0:T(8,128)S(1)}, f32[16,512]{1,0:T(8,128)}, u32[]{:S(2)}) copy-start(f32[16,512]{1,0:T(8,128)} %copy-done.26) | copy-start | bytes 98308
  949.7 31.2 %copy-start.29 = (f32[2,16,512]{2,1,0:T(8,128)S(1)}, f32[2,16,512]{2,1,0:T(8,128)}, u32[]{:S(2)}) copy-start(f32[2,16,512]{2,1,0:T(8,128)} %param.39) | copy-start | bytes 196612
  949.8 31.2 %copy-start.33 = (f32[16,512]{1,0:T(8,128)S(1)}, f32[16,512]{1,0:T(8,128)}, u32[]{:S(2)}) copy-start(f32[16,512]{1,0:T(8,128)} %param.37) | copy-start | bytes 98308
  (26 other events, 62.9 us)
Sparse Core Ops, SparseCore 0:
  10.2 48.6 all-gather.33
  61.0 44.6 all-gather.35
  108.2 45.3 all-gather.17
  155.3 28.2 all-gather.21
  207.8 46.0 all-gather.19
  255.3 148.3 all-gather.23
  405.3 44.0 all-gather.29
  451.9 66.4 all-gather.25
  520.0 80.7 all-gather.31
  602.5 42.8 all-gather.27
  721.6 43.8 reduce-scatter.19
  767.7 43.2 reduce-scatter.15
  814.5 72.3 reduce-scatter.25
  889.1 43.8 reduce-scatter.13
  935.2 43.0 reduce-scatter.11
  980.5 43.6 reduce-scatter.21
  1026.3 43.1 reduce-scatter.17
  1073.3 58.3 reduce-scatter.31
  1135.0 61.7 reduce-scatter.23
  1199.0 27.1 reduce-scatter.27
  1229.7 85.4 reduce-scatter.29

commit v2 on v1

--- a/solution.py
+++ b/solution.py
@@ -111,7 +111,7 @@
     lax.fori_loop(0, count // STEP, scan, 0)
 
 
-def joined(all_ref, full_ref, carry_ref, spans_ref, me, count, conj):
+def joined(all_ref, micro, full_ref, carry_ref, spans_ref, me, count, conj):
     poles = full_ref.shape[0] // 2
     carry_ref[...] = jnp.zeros_like(carry_ref)
 
@@ -121,20 +121,20 @@
         for k in range(poles):
             lr, li = full_ref[k] * span, full_ref[poles + k] * (-span if conj else span)
             sr, si = carry_ref[k], carry_ref[poles + k]
-            carry_ref[k] = lr * sr - li * si + all_ref[j, k]
-            carry_ref[poles + k] = lr * si + li * sr + all_ref[j, poles + k]
+            carry_ref[k] = lr * sr - li * si + all_ref[j, micro, k]
+            carry_ref[poles + k] = lr * si + li * sr + all_ref[j, micro, poles + k]
         return 0
 
     lax.fori_loop(0, count - 1 - me if conj else me, hop, 0)
 
 
-def finish_kernel(keep_ref, flag_ref, spans_ref, me_ref, z_ref, rim_ref, taps_ref, cols_ref,
+def finish_kernel(micro, keep_ref, flag_ref, spans_ref, me_ref, z_ref, rim_ref, taps_ref, cols_ref,
                   lam_ref, full_ref, res_ref, skip_ref, u_ref, ends_ref,
                   mixed_ref, conv_ref, marks_ref, zs_ref, y_ref, st_ref):
     count, width = z_ref.shape[0], z_ref.shape[1] // 3
     poles = lam_ref.shape[0] // 2
     keep_rows(z_ref, rim_ref, zs_ref)
-    joined(ends_ref, full_ref, st_ref, spans_ref, me_ref[0], ends_ref.shape[0], False)
+    joined(ends_ref, micro, full_ref, st_ref, spans_ref, me_ref[0], ends_ref.shape[0], False)
 
     def scan(group, _):
         @pl.when(group % (SPAN // STEP) == 0)
@@ -214,7 +214,7 @@
     lax.fori_loop(0, count // STEP, scan, 0)
 
 
-def back_kernel(keep_ref, flag_ref, spans_ref, me_ref, z_ref, rim_ref, taps_ref, cols_ref,
+def back_kernel(micro, keep_ref, flag_ref, spans_ref, me_ref, z_ref, rim_ref, taps_ref, cols_ref,
                 lam_ref, full_ref, res_ref, skip_ref, u_ref, e_ref, dmix_ref, conv_ref,
                 marks_ref, ends_ref,
                 dz_ref, rimback_ref, tail_ref, dtaps_ref, dskip_ref, dres_ref, g_ref,
@@ -223,7 +223,7 @@
     poles = lam_ref.shape[0] // 2
     state_rows = 2 * poles * SUB
     keep_rows(z_ref, rim_ref, zs_ref)
-    joined(ends_ref, full_ref, bt_ref, spans_ref, me_ref[0], ends_ref.shape[0], True)
+    joined(ends_ref, micro, full_ref, bt_ref, spans_ref, me_ref[0], ends_ref.shape[0], True)
     bt_ref[...] = bt_ref[...] * keep_ref[count]
     for ref in (dtaps_ref, dskip_ref, dres_ref, g_ref):
         ref[...] = jnp.zeros_like(ref)
@@ -362,22 +362,28 @@
         rimback_ref[1:2, lanes] = one[0:1] + two[1:2]
 
 
-def call(kernel, ins, outs, scratch, smem, name, flops):
+def call(kernel, ins, outs, scratch, smem, name, flops, after=()):
+    count = len(ins)
+
+    def without(*refs):
+        kernel(*refs[:count], *refs[count + len(after) :])
+
     vmem = pl.BlockSpec(memory_space=pltpu.VMEM)
     scalar = pl.BlockSpec(memory_space=pltpu.SMEM)
     moved = sum(a.size * a.dtype.itemsize for a in ins) + sum(
         functools.reduce(lambda x, y: x * y, s) * jnp.dtype(d).itemsize for s, d in outs
     )
     return pl.pallas_call(
-        kernel,
+        without,
         out_shape=[jax.ShapeDtypeStruct(s, d) for s, d in outs],
-        in_specs=[scalar] * smem + [vmem] * (len(ins) - smem),
+        in_specs=[scalar] * smem + [vmem] * (count - smem)
+        + [pl.BlockSpec(memory_space=pl.ANY)] * len(after),
         out_specs=[vmem] * len(outs),
         scratch_shapes=[pltpu.VMEM(s, d) for s, d in scratch],
         compiler_params=pltpu.CompilerParams(vmem_limit_bytes=VMEM_LIMIT),
         cost_estimate=pl.CostEstimate(flops=flops, bytes_accessed=moved, transcendentals=0),
         name=name,
-    )(*ins)
+    )(*ins, *after)
 
 
 def segment_number(position, doc_lengths):
@@ -422,6 +428,165 @@
     return lax.psum_scatter(block, axis, scatter_dimension=dim, tiled=True)
 
 
+CORE, X, Y = 1, 2, 4
+
+
+def over(value, bit):
+    return lax.ppermute(value, "seq", [(i, i ^ bit) for i in range(8)])
+
+
+def place_kernel(spots, me_ref, *refs):
+    count = len(spots)
+    pieces, out_ref, held, sems = refs[:count], refs[count], refs[count + 1 : -1], refs[-1]
+    arrive = [pltpu.make_async_copy(pieces[i], held[i], sems.at[0, i]) for i in range(count)]
+    leave = [
+        pltpu.make_async_copy(held[i], out_ref.at[spots[i](me_ref[0])], sems.at[1, i])
+        for i in range(count)
+    ]
+    for copy in arrive:
+        copy.start()
+    for i in range(count):
+        arrive[i].wait()
+        leave[i].start()
+    for copy in leave:
+        copy.wait()
+
+
+def place(me, pieces, spots, shape, name):
+    anywhere = pl.BlockSpec(memory_space=pl.ANY)
+    moved = 4 * shape[0] * shape[1]
+    return pl.pallas_call(
+        functools.partial(place_kernel, spots),
+        out_shape=jax.ShapeDtypeStruct(shape, pieces[0].dtype),
+        in_specs=[pl.BlockSpec(memory_space=pltpu.SMEM)] + [anywhere] * len(pieces),
+        out_specs=anywhere,
+        scratch_shapes=[pltpu.VMEM(piece.shape, piece.dtype) for piece in pieces]
+        + [pltpu.SemaphoreType.DMA((2, len(pieces)))],
+        compiler_params=pltpu.CompilerParams(vmem_limit_bytes=VMEM_LIMIT),
+        cost_estimate=pl.CostEstimate(flops=0, bytes_accessed=moved, transcendentals=0),
+        name=name,
+    )(me.astype(jnp.int32).reshape(1), *pieces)
+
+
+def rows_of(bits, rows):
+    return lambda me: pl.ds(pl.multiple_of((me ^ bits) * rows, 16), rows)
+
+
+def seq_links(block, relay):
+    if lax.axis_size("seq") != 8:
+        return (block,)
+    from_x, from_y = over(block, X), over(block, Y)
+    return block, from_x, from_y, over(from_x if relay == Y else from_y, relay)
+
+
+def seq_gather(blocks):
+    if lax.axis_size("seq") != 8:
+        return gather(blocks[0], "seq", 0)
+    rows, width = blocks[0].shape
+    others = [over(block, CORE) for block in blocks]
+    spots = [rows_of(bits + core, rows) for core in (0, CORE) for bits in (0, X, Y, X + Y)]
+    return place(lax.axis_index("seq"), [*blocks, *others], spots, (8 * rows, width), "place_rows")
+
+
+def plus(*terms):
+    total = terms[0].astype(F32)
+    for term in terms[1:]:
+        total = total + term.astype(F32)
+    return total
+
+
+def half_kernel(micros, me_ref, *refs):
+    lefts, rights, out_ref = refs[:micros], refs[micros : 2 * micros], refs[-1]
+    total = None
+    for left, right in zip(lefts, rights):
+        part = lax.dot_general(left[...], right[...], (((0,), (0,)), ((), ())), preferred_element_type=F32)
+        total = part if total is None else total + part
+    out_ref[...] = total.astype(BF)
+
+
+def grad_half(lefts, rights, own, name, after):
+    count, wide = lefts[0].shape
+    rows, width = wide // 8, rights[0].shape[1]
+    core = (lax.axis_index("seq") & CORE).astype(jnp.int32)
+    core = (core if own else 1 - core).reshape(1)
+    steps, pick = (8, lambda i, c: (0, i)) if own is None else (4, lambda i, c: (0, 2 * i + c[0]))
+    n = len(lefts)
+    return pl.pallas_call(
+        functools.partial(half_kernel, n),
+        out_shape=jax.ShapeDtypeStruct((steps * rows, width), BF),
+        grid_spec=pltpu.PrefetchScalarGridSpec(
+            num_scalar_prefetch=1,
+            grid=(steps,),
+            in_specs=[pl.BlockSpec((count, rows), pick)] * n
+            + [pl.BlockSpec((count, width), lambda i, c: (0, 0))] * n
+            + [pl.BlockSpec(memory_space=pl.ANY)] * len(after),
+            out_specs=pl.BlockSpec((rows, width), lambda i, c: (i, 0)),
+        ),
+        compiler_params=pltpu.CompilerParams(vmem_limit_bytes=VMEM_LIMIT),
+        cost_estimate=pl.CostEstimate(
+            flops=2 * n * count * rows * steps * width,
+            bytes_accessed=n * count * (wide + 2 * width) + wide * width,
+            transcendentals=0,
+        ),
+        name=name,
+    )(core, *lefts, *rights, *after)
+
+
+def grad_halves(lefts, rights, name, after=()):
+    if lax.axis_size("seq") != 8:
+        return (dot(jnp.concatenate(lefts), jnp.concatenate(rights), ((0,), (0,))).astype(BF),)
+    return tuple(grad_half(lefts, rights, own, name, after) for own in (False, True))
+
+
+def grad_chip(halves):
+    if len(halves) == 1:
+        return halves[0]
+    send, keep = halves
+    four = plus(keep, over(send, CORE)).astype(BF)
+    return four.reshape(4, keep.shape[0] // 4, keep.shape[1])
+
+
+def owner(four, bits):
+    return lax.dynamic_index_in_dim(four, (lax.axis_index("seq") // 2) ^ (bits // 2), 0, keepdims=False)
+
+
+def grad_far(four, relay):
+    if four.ndim == 2:
+        return four
+    return over(owner(four, X + Y), relay)
+
+
+def grad_own(four, far, relay):
+    if four.ndim == 2:
+        return scatter(four, "seq", 0).astype(F32)
+    to_x, to_y = owner(four, X), owner(four, Y)
+    if relay == Y:
+        to_x = plus(to_x, far).astype(BF)
+    else:
+        to_y = plus(to_y, far).astype(BF)
+    return plus(owner(four, 0), over(to_x, X), over(to_y, Y))
+
+
+def grad_sum(halves, relay):
+    four = grad_chip(halves)
+    return grad_own(four, grad_far(four, relay), relay)
+
+
+def tp_sum(block):
+    count = lax.axis_size("tp")
+    return plus(block, *[
+        lax.ppermute(block, "tp", [(i, (i + hop) % count) for i in range(count)])
+        for hop in range(1, count)
+    ])
+
+
+def tied(value, *others):
+    if not others:
+        return value
+    nothing = sum(other[(0,) * other.ndim].astype(F32) * 0.0 for other in others)
+    return value + nothing.astype(value.dtype)
+
+
 def dot(a, b, dims):
     return lax.dot_general(a, b, (dims, ((), ())), preferred_element_type=F32)
 
@@ -432,13 +597,17 @@
     n_seq, n_tp = lax.axis_size("seq"), lax.axis_size("tp")
     me = lax.axis_index("seq")
     hidden = w_gu.shape[2]
-    x_own = [tokens[m] for m in range(micros)]
-    x_full = [gather(x, "tp", 1) for x in x_own]
-    in_full = gather(w_in.reshape(w_in.shape[0], -1), "seq", 0)
-    out_full = gather(gather(w_out, "seq", 1), "tp", 0)
-    gu_full = gather(w_gu.reshape(w_gu.shape[0], -1), "seq", 0)
-    down_full = gather(w_down, "seq", 1)
-    cot_full = gather(cotangent, "tp", 2)
+    joint = jnp.concatenate([tokens.reshape(micros * count, width), w_out.T])
+    joint = gather(joint, "tp", 1)
+    x_full = joint[: micros * count].reshape(micros, count, -1)
+    out_lanes = joint[micros * count :]
+    in_links = seq_links(w_in.reshape(w_in.shape[0], -1), Y)
+    gu_links = seq_links(tied(w_gu.reshape(w_gu.shape[0], -1), *in_links[1:2]), X)
+    down_links = seq_links(tied(w_down.T, gu_links[-1]), Y)
+    in_full, gu_full, down_full = seq_gather(in_links), seq_gather(gu_links), seq_gather(down_links)
+    cot_full = [gather(cotangent[0], "tp", 1)]
+    out_links = seq_links(out_lanes, X)
+    out_full = seq_gather(out_links)
 
     rate = jnp.exp(log_rate)
     lam_real, lam_imag = polar(1.0, rate, pole_angle)
@@ -453,53 +622,65 @@
     st_shape = lam.shape
     work = lam.shape[0] * SUB * LANE * count
 
+    position = me * count + jnp.arange(-2, count + 1)
+    seg = jnp.stack([segment_number(position, lengths[m]) for m in range(micros)])
+    valid1 = (seg[:, 2:] == seg[:, 1:-1]).astype(F32)
+    valid2 = (seg[:, 2:] == seg[:, :-2]).astype(F32)
+    inside = (jnp.arange(count + 1) < count) | (me < n_seq - 1)
+    keeps = jnp.pad(valid1 * inside[None].astype(F32), ((0, 0), (0, SUB - 1)))
+    group_flags = jnp.any(keeps.reshape(micros, -1, STEP) == 0, axis=2).astype(jnp.int32)
+    columns = jnp.stack([valid1[:, :count], valid2[:, :count], pad_mask.astype(F32)], axis=2)
+    columns = jnp.pad(columns, ((0, 0), (0, SUB), (0, SUB - 3)))
+
+    x_wide = x_full.astype(F32)
+    scale_in = norm_scale(x_wide)
+    h_in = (x_wide * scale_in * tied(gain_in, gu_full)).astype(BF)
+    z_low = dot(h_in, in_full, ((2,), (0,))).astype(BF)
+    rims = lax.ppermute(z_low[:, count - 2 :], "seq", [(i, i + 1) for i in range(n_seq - 1)])
+    rims = jnp.pad(rims.astype(F32), ((0, 0), (SUB - 2, 0), (0, 0)))
+    zs = ((count + SUB, 3 * width), F32)
+    bases = [(z_low[m], rims[m], taps, columns[m], lam) for m in range(micros)]
+    masks = [(keeps[m], group_flags[m]) for m in range(micros)]
+    last = [segment_number(edges - 1, lengths[m]) for m in range(micros)]
+    first = [segment_number(edges, lengths[m]) for m in range(micros)]
+    spans = [(v[1:] == v[:-1]).astype(F32) for v in last]
+    spans_back = [(v[1:] == v[:-1]).astype(F32) for v in first]
+    injects, ends = zip(*[
+        call(front_kernel, (*masks[m], *bases[m]), [(seq_shape, F32), (st_shape, F32)],
+             [zs], 2, "mixer_front", 4 * work)
+        for m in range(micros)
+    ])
+    ends = lax.all_gather(jnp.stack(ends).astype(BF), "seq").astype(F32)
+
     kept = []
     outputs = []
     for m in range(micros):
-        position = me * count + jnp.arange(-2, count + 1)
-        seg = segment_number(position, lengths[m])
-        valid1 = (seg[2:] == seg[1:-1]).astype(F32)
-        valid1 = valid1.at[count].multiply((me < n_seq - 1).astype(F32))
-        valid2 = (seg[2:-1] == seg[:-3]).astype(F32)
-        mask = pad_mask[m].astype(F32)
-        cols = jnp.zeros((count + SUB, SUB), F32)
-        cols = cols.at[:count, 0].set(valid1[:count]).at[:count, 1].set(valid2).at[:count, 2].set(mask)
-        keep = jnp.concatenate([valid1, jnp.zeros((SUB - 1,), F32)])
-        flags = jnp.any(keep.reshape(-1, STEP) == 0, axis=1).astype(jnp.int32)
-        last, first = segment_number(edges - 1, lengths[m]), segment_number(edges, lengths[m])
-        spans = (last[1:] == last[:-1]).astype(F32)
-        spans_back = (first[1:] == first[:-1]).astype(F32)
-
-        x_wide = x_full[m].astype(F32)
-        h_in = (x_wide * norm_scale(x_wide) * gain_in[None]).astype(BF)
-        z_low = dot(h_in, in_full, ((1,), (0,))).astype(BF)
-        rim = lax.ppermute(z_low[count - 2 :], "seq", [(i, i + 1) for i in range(n_seq - 1)])
-        rim = jnp.concatenate([jnp.zeros((SUB - 2, 3 * width), F32), rim.astype(F32)])
-        base = (z_low, rim, taps, cols, lam)
-        zs = ((count + SUB, 3 * width), F32)
-        u, end = call(front_kernel, (keep, flags, *base), [(seq_shape, F32), (st_shape, F32)],
-                      [zs], 2, "mixer_front", 4 * work)
-        ends = lax.all_gather(end, "seq")
         mixed, conv_out, marks = call(
-            finish_kernel,
-            (keep, flags, spans, me_word, *base, lam_all, res, skip, u, ends),
+            functools.partial(finish_kernel, m),
+            (*masks[m], spans[m], me_word, *bases[m], lam_all, res, skip, injects[m], ends),
             [((count, width), BF), ((count, width), F32), ((count // SPAN, *st_shape), F32)],
             [zs, (seq_shape, F32), (st_shape, F32)], 4, "mixer_finish", 6 * work,
+            (out_links[-1], *down_links[1:3]) if m else (*cot_full, *out_links[1:3]),
         )
-        mixed_full = gather(mixed, "tp", 1)
-        x_mid = x_wide + dot(mixed_full, out_full, ((1,), (0,)))
+        kept.append(dict(mixed=mixed, conv=conv_out, marks=marks))
+
+    for m in range(micros):
+        mixed_full = gather(kept[m]["mixed"], "tp", 1)
+        if m + 1 < micros:
+            cot_full.append(gather(tied(cotangent[m + 1], mixed_full), "tp", 1))
+        x_mid = x_full[m].astype(F32) + dot(mixed_full, out_full, ((1,), (1,)))
         scale_mid = norm_scale(x_mid)
         h_mlp = (x_mid * scale_mid * gain_mlp[None]).astype(BF)
         gate_up = dot(h_mlp, gu_full, ((1,), (0,)))
         gate, up = gate_up[:, :hidden], gate_up[:, hidden:]
         sig = jax.nn.sigmoid(gate)
         act = (gate * sig * up).astype(BF)
-        down_own = scatter(dot(act, down_full, ((1,), (0,))).astype(BF), "tp", 1)
+        down_own = scatter(dot(act, down_full, ((1,), (1,))).astype(BF), "tp", 1)
         mid_own = lax.dynamic_slice_in_dim(x_mid, lax.axis_index("tp") * width, width, 1)
         outputs.append((mid_own + down_own.astype(F32)).astype(BF))
 
         cot = cot_full[m]
-        d_act = dot(cot, down_full, ((1,), (1,)))
+        d_act = dot(cot, down_full, ((1,), (0,)))
         d_gu = jnp.concatenate(
             [d_act * up * sig * (1.0 + gate * (1.0 - sig)), d_act * gate * sig], axis=1
         ).astype(BF)
@@ -507,42 +688,62 @@
         d_norm, d_gain_mlp = norm_back(x_mid, scale_mid, gain_mlp, d_h)
         d_mid = d_norm + cot.astype(F32) * (1.0 / n_tp)
         d_low = d_mid.astype(BF)
-        d_mixed = scatter(dot(d_low, out_full, ((1,), (1,))).astype(BF), "tp", 1)
-        kept.append(dict(
-            base=base, zs=zs, keep=keep, flags=flags, spans=spans_back, u=u, conv=conv_out,
-            marks=marks, mixed=mixed_full, h_mlp=h_mlp, act=act, d_gu=d_gu, d_mid=d_mid,
-            d_low=d_low, d_mixed=d_mixed, x_wide=x_wide, h_in=h_in, d_gain_mlp=d_gain_mlp,
-        ))
+        d_mixed = scatter(dot(d_low, out_full, ((1,), (0,))).astype(BF), "tp", 1)
+        kept[m].update(
+            mixed=mixed_full, h_mlp=h_mlp, act=act, d_gu=d_gu, d_mid=d_mid, d_low=d_low,
+            d_mixed=d_mixed, d_gain_mlp=d_gain_mlp,
+        )
+
+    def each(name):
+        return [c[name] for c in kept]
+
+    down_halves = grad_halves(cot_full, each("act"), "grad_down")
+    out_halves = grad_halves(each("d_low"), each("mixed"), "grad_out")
+    g_down = grad_sum(down_halves, Y)
+    g_out = scatter(grad_sum(out_halves, X).astype(BF), "tp", 1)
+    adjoints, ends = zip(*[
+        call(adjoint_kernel, (*masks[m], *bases[m], kept[m]["d_mixed"]),
+             [(seq_shape, F32), (st_shape, F32)], [zs], 2, "mixer_adjoint", 4 * work,
+             (*down_halves, *out_halves))
+        for m in range(micros)
+    ])
+    ends = lax.all_gather(jnp.stack(ends).astype(BF), "seq").astype(F32)
+    gu_halves = grad_halves(each("h_mlp"), each("d_gu"), "grad_gu", (ends,))
+    gu_chip = grad_chip(gu_halves)
+    gu_far = grad_far(gu_chip, X)
+    g_gu = grad_own(gu_chip, gu_far, X)
 
     token_grads = []
+    partial_grads = []
     smalls = []
     for m in range(micros):
         c = kept[m]
-        base, zs, u, d_mixed = c["base"], c["zs"], c["u"], c["d_mixed"]
-        e, end = call(adjoint_kernel, (c["keep"], c["flags"], *base, d_mixed),
-                      [(seq_shape, F32), (st_shape, F32)], [zs], 2, "mixer_adjoint", 4 * work)
-        ends = lax.all_gather(end, "seq")
         d_z, rim_back, tail, d_taps, d_skip, d_res, d_lam = call(
-            back_kernel,
-            (c["keep"], c["flags"], c["spans"], me_word, *base, lam_all, res, skip, u, e, d_mixed,
-             c["conv"], c["marks"], ends),
+            functools.partial(back_kernel, m),
+            (*masks[m], spans_back[m], me_word, *bases[m], lam_all, res, skip, injects[m],
+             adjoints[m], c["d_mixed"], c["conv"], c["marks"], ends),
             [((count, 3 * width), BF), ((SUB, 3 * width), F32), ((ROWS, 3 * width), F32),
              ((9 * SUB, width), F32), ((SUB, width), F32), (st_shape, F32), (st_shape, F32)],
             [zs, ((count + SUB, 3 * width), F32), (seq_shape, F32),
              (((SPAN + 1) * st_shape[0] * SUB, LANE), F32), (st_shape, F32)],
-            4, "mixer_back", 16 * work,
+            4, "mixer_back", 16 * work, (*partial_grads, g_down, gu_far) if m else (*gu_halves, gu_chip),
         )
         rim_back = lax.ppermute(rim_back[:2], "seq", [(i + 1, i) for i in range(n_seq - 1)])
         tail = (tail + jnp.concatenate([jnp.zeros((ROWS - 2, 3 * width), F32), rim_back])).astype(BF)
         d_z = lax.dynamic_update_slice(d_z, tail, (count - ROWS, 0))
+        c["d_z"] = d_z
+        gain = gain_in
+        if m == micros - 1:
+            in_halves = grad_halves([h_in[i] for i in range(micros)], each("d_z"), "grad_in")
+            gain = tied(gain_in, in_halves[0])
         d_h_in = dot(d_z, in_full, ((1,), (1,)))
-        d_norm, d_gain_in = norm_back(c["x_wide"], norm_scale(c["x_wide"]), gain_in, d_h_in)
-        token_grads.append(scatter((c["d_mid"] + d_norm).astype(BF), "tp", 1))
+        d_norm, d_gain_in = norm_back(x_full[m].astype(F32), scale_in[m], gain, d_h_in)
+        partial_grads.append((c["d_mid"] + d_norm).astype(BF))
+        token_grads.append(scatter(partial_grads[m], "tp", 1))
         g_real, g_imag = unpacked(d_lam, log_rate.shape)
         s_real, s_imag = unpacked(d_res, log_rate.shape)
         h_real = residues[0] * g_real + residues[1] * g_imag
         h_imag = residues[0] * g_imag - residues[1] * g_real
-        c["d_z"] = d_z
         smalls.append(jnp.concatenate([
             jnp.sum(d_taps.reshape(9, SUB, width), axis=1),
             -rate * (lam_real * h_real + lam_imag * h_imag),
@@ -552,36 +753,28 @@
             d_gain_in.reshape(-1, width), c["d_gain_mlp"].reshape(-1, width),
         ]))
 
-    def both(name):
-        return jnp.concatenate([c[name] for c in kept])
-
-    rows = ((0,), (0,))
-    g_down = scatter(dot(both("act"), cot_full.reshape(micros * count, -1), rows).astype(BF), "seq", 1)
-    g_gu = scatter(dot(both("h_mlp"), both("d_gu"), rows).astype(BF), "seq", 0)
-    g_out = scatter(dot(both("mixed"), both("d_low"), rows).astype(BF), "seq", 1)
-    g_out = scatter(g_out, "tp", 0)
-    g_in = scatter(dot(both("h_in"), both("d_z"), rows).astype(BF), "seq", 0)
-
+    g_in = grad_sum(in_halves, Y)
+    n_gain = 2 * (gain_in.shape[0] // width)
     small = sum(smalls)
-    small = jnp.sum(lax.all_gather(small.astype(BF), "seq").astype(F32), axis=0)
-    n_gain = 2 * (gain_in.shape[0] // width)
+    gains = tp_sum(small[-n_gain:].astype(BF))
+    small = jnp.sum(lax.all_gather(tied(small[:-n_gain], partial_grads[-1]).astype(BF), "seq").astype(F32), axis=0)
+    gains = jnp.sum(lax.all_gather(tied(gains, g_in).astype(BF), "seq").astype(F32), axis=0)
     n_pole = log_rate.shape[0]
-    gains = jnp.sum(lax.all_gather(small[-n_gain:].astype(BF), "tp").astype(F32), axis=0)
     cuts = [9, 9 + n_pole, 9 + 2 * n_pole, 9 + 3 * n_pole, 9 + 4 * n_pole]
     return (
         jnp.stack(outputs),
         jnp.stack(token_grads),
         gains[: n_gain // 2].reshape(-1),
-        g_in.astype(F32).reshape(w_in.shape),
+        g_in.reshape(w_in.shape),
         small[: cuts[0]].reshape(conv_taps.shape),
         small[cuts[0] : cuts[1]],
         small[cuts[1] : cuts[2]],
         small[cuts[2] : cuts[4]].reshape(residues.shape),
         small[cuts[4]],
-        g_out.astype(F32),
+        g_out.T.astype(F32),
         gains[n_gain // 2 :].reshape(-1),
-        g_gu.astype(F32).reshape(w_gu.shape),
-        g_down.astype(F32),
+        g_gu.reshape(w_gu.shape),
+        g_down.T,
     )
 
 

time: 1340 us -> 842 us (0.63)
  waiting for transfers between devices: 789 us -> 181 us
  Pallas kernels: 148 us -> 244 us
  matrix products: 203 us -> 124 us
  other arithmetic: 47 us -> 94.9 us
  local copies, waits for them, and re-layouts: 43.6 us -> 80.5 us
  starting transfers between devices: 8.36 us -> 43.8 us
  blocking collectives: 72 us -> 43.4 us
    all_gather x10 -> x5, waiting for transfers between devices: 458 us -> 15.5 us  [gather(): return lax.all_gather(block, axis, axis=dim, tiled=True)]
    reduce_scatter x11 -> x7, waiting for transfers between devices: 326 us -> 0.03 us  [scatter(): return lax.psum_scatter(block, axis, scatter_dimension=dim, tiled=True)]
    ppermute x2 -> x48, waiting for transfers between devices: 0.01 us -> 164 us  [the longest x44 164 us: over(): return lax.ppermute(value, 'seq', [(i, i ^ bit) for i in range(8)])]
    pallas_call x8 -> x20, Pallas kernels: 148 us -> 244 us  [the longest x8 147 us: call(): pl.pallas_call(without, out_shape=[jax.ShapeDtypeStruct(s, d) for s, d in...]
    dot_general x20 -> x15, matrix products: 203 us -> 124 us  [dot(): return lax.dot_general(a, b, (dims, ((), ())), preferred_element_type=F32)]
    ppermute x2 -> x48, starting transfers between devices: 4.41 us -> 40.3 us  [the longest x44 36.5 us: over(): return lax.ppermute(value, 'seq', [(i, i ^ bit) for i in range(8)])]
    convert_element_type x13 -> x23, other arithmetic: 16.3 us -> 47.5 us  [the longest x4 16.1 us: grad_chip(): four = plus(keep, over(send, CORE)).astype(BF)]
    all_gather x6 -> x4, blocking collectives: 72 us -> 43.4 us  [the longest x2 23.5 us: shards(): ends = lax.all_gather(jnp.stack(ends).astype(BF), 'seq').astype(F32)]
  transfers between devices with their start and end apart: 25 -> 62, of which waited for: 17 -> 20; matrix products, arithmetic and copies ran while one was open for 16% -> 33% of each run, Pallas kernels for 11% -> 23%
where the time goes in v2:
time: 842 us; the launch traced here: 832 us
  Pallas kernels  244 us (29%)
  waiting for transfers between devices  181 us (21%)
  matrix products  124 us (15%)
  other arithmetic  94.9 us (11%)
  local copies, waits for them, and re-layouts  80.5 us (10%)
  starting transfers between devices  43.8 us (5%)
  blocking collectives  43.4 us (5%)
  between operations  20.8 us (2%)
    ppermute x44, waiting for transfers between devices, over(): return lax.ppermute(value, 'seq', [(i, i ^ bit) for i in range(8)])  164 us
    pallas_call x8, Pallas kernels, call(): pl.pallas_call(without, out_shape=[jax.ShapeDtypeStruct(s, d) for s, d in...  147 us
    dot_general x15, matrix products, dot(): return lax.dot_general(a, b, (dims, ((), ())), preferred_element_type=F32)  124 us
    pallas_call x8, Pallas kernels, grad_half(): pl.pallas_call(functools.partial(half_kernel, n), out_shape=jax.ShapeDtyp...  70.3 us
    ppermute x44, starting transfers between devices, over(): return lax.ppermute(value, 'seq', [(i, i ^ bit) for i in range(8)])  36.5 us
    pallas_call x4, Pallas kernels, place(): pl.pallas_call(functools.partial(place_kernel, spots), out_shape=jax.Shap...  26.2 us
    unnamed x210, local copies, waits for them, and re-layouts  25.1 us
    all_gather x2, blocking collectives, shards(): ends = lax.all_gather(jnp.stack(ends).astype(BF), 'seq').astype(F32)  23.5 us
  transfers between devices with their start and end apart: 62, of which 20 were waited for; matrix products, arithmetic and copies ran while one was open for 33% of the time, Pallas kernels for 23%

profile of v2, /device:TPU:0, one launch (start us, length us, event | category | flops | bytes accessed | tf_op | source)
XLA Modules:
  0.0 831.7 jit_solution(14410650670830229547)
XLA Ops:
  14.4 17.6 %collective-permute-done.refs_1_ = bf16[256,1536]{1,0:T(8,128)(2,1)} collective-permute-done((bf16[256,1536]{1,0:T(8,128)(2,1)S(1)}, bf16[256,1536]{1,0:T(8,128)(2,1)}, u32[]{:S(2)}, u32[]{:S(2)}) %collective-permute-start) | collective-permute-done | bytes 786464 | tf_op jit(solution)/shard_map/ppermute | solution.py:435
  40.9 29.5 %collective-permute-done.2.refs_2_ = bf16[256,2816]{1,0:T(8,128)(2,1)} collective-permute-done((bf16[256,2816]{1,0:T(8,128)(2,1)S(1)}, bf16[256,2816]{1,0:T(8,128)(2,1)}, u32[]{:S(2)}, u32[]{:S(2)}) %collective-permute-start.2) | collective-permute-done | bytes 1441824 | tf_op jit(solution)/shard_map/ppermute | solution.py:435
  72.5 13.0 %collective-permute-done.8.refs_2_ = bf16[256,1536]{1,0:T(8,128)(2,1)} collective-permute-done((bf16[256,1536]{1,0:T(8,128)(2,1)S(1)}, bf16[256,1536]{1,0:T(8,128)(2,1)}, u32[]{:S(2)}, u32[]{:S(2)}) %collective-permute-start.8) | collective-permute-done | bytes 786464 | tf_op jit(solution)/shard_map/ppermute | solution.py:435
  92.7 11.3 %collective-permute-done.3.refs_3_ = bf16[256,2816]{1,0:T(8,128)(2,1)} collective-permute-done((bf16[256,2816]{1,0:T(8,128)(2,1)}, bf16[256,2816]{1,0:T(8,128)(2,1)}, u32[]{:S(2)}, u32[]{:S(2)}) %collective-permute-start.3) | collective-permute-done | bytes 1441824 | tf_op jit(solution)/shard_map/ppermute | solution.py:435
  113.3 5.5 place_rows.5
  119.9 8.9 %place_rows.4 = bf16[2048,2816]{1,0:T(8,128)(2,1)} custom-call(s32[1]{0:T(128)} %bitcast.5.me_ref.refs_3_, bf16[256,2816]{1,0:T(8,128)(2,1)} %bitcast.241, bf16[256,2816]{1,0:T(8,128)(2,1)} %collective-permute-done.1.refs_1_, bf16[256,2816]{1,0:T(8,128)(2,1)} %collective-permute-done.2.refs_2_, bf16[256,2816]{1,0:T(8,128)(2,1)} %collective-permute-done.3.refs_3_, ...), custom_call_target="tpu_custom_call" | custom-call | bytes 23068672 | tf_op jit(solution)/shard_map/place_rows/pallas_call | solution.py:458
  138.5 3.4 slice_convert_fusion
  143.6 6.9 fusion.16
  154.4 11.9 %mixer_front.2 = (f32[4096,128]{1,0:T(8,128)}, f32[16,8,128]{2,1,0:T(8,128)}) custom-call(f32[520]{0:T(1024)} %get-tuple-element.142.refs_0_, s32[65]{0:T(128)} %get-tuple-element.219.refs_1_, bf16[512,1536]{1,0:T(8,128)(2,1)} %get-tuple-element.179.refs_2_.refs_4_, f32[8,1536]{1,0:T(8,128)} %get-tuple-element.192.refs_3_.refs_5_, ...), custom_call_target="tpu_custom_call" | custom-call | flops 33554432 | bytes 3887652 | tf_op jit(solution)/shard_map/mixer_front/pallas_call | solution.py:376
  166.4 12.0 %mixer_front.3 = (f32[4096,128]{1,0:T(8,128)}, f32[16,8,128]{2,1,0:T(8,128)}) custom-call(f32[520]{0:T(1024)} %get-tuple-element.143.refs_0_, s32[65]{0:T(128)} %get-tuple-element.220.refs_1_, bf16[512,1536]{1,0:T(8,128)(2,1)} %get-tuple-element.180.refs_2_.refs_4_, f32[8,1536]{1,0:T(8,128)} %get-tuple-element.193.refs_3_.refs_5_, ...), custom_call_target="tpu_custom_call" | custom-call | flops 33554432 | bytes 3887652 | tf_op jit(solution)/shard_map/mixer_front/pallas_call | solution.py:376
  180.1 13.7 %all_gather.36 = bf16[8,2,16,8,128]{4,3,2,1,0:T(8,128)(2,1)S(1)} all-gather(bf16[1,2,16,8,128]{4,3,2,1,0:T(8,128)(2,1)S(1)} %pad_maximum_fusion.5), channel_id=1, replica_groups=mesh['seq'=8,'tp'=4] {'seq'}, dimensions={0}, use_global_device_ids=true | all-gather | bytes 589824 | tf_op jit(solution)/shard_map/all_gather | solution.py:653
  196.1 16.0 %mixer_finish.2 = (bf16[512,512]{1,0:T(8,128)(2,1)}, f32[512,512]{1,0:T(8,128)}, f32[8,16,8,128]{3,2,1,0:T(8,128)}) custom-call(f32[520]{0:T(1024)} %get-tuple-element.142.refs_0_, s32[65]{0:T(128)} %get-tuple-element.219.refs_1_, f32[8]{0:T(128)} %compare_convert_fusion.4.refs_2_, s32[1]{0:T(128)} %bitcast.5.me_ref.refs_3_, ...), custom_call_target="tpu_custom_call" | custom-call | flops 50331648 | bytes 7101000 | tf_op jit(solution)/shard_map/mixer_finish/pallas_call | solution.py:376
  217.9 15.5 %collective-permute-done.23.refs_2_.refs_16_ = bf16[256,1408]{1,0:T(8,128)(2,1)S(1)} collective-permute-done((bf16[256,1408]{1,0:T(8,128)(2,1)S(1)}, bf16[256,1408]{1,0:T(8,128)(2,1)S(1)}, u32[]{:S(2)}, u32[]{:S(2)}) %collective-permute-start.23) | collective-permute-done | bytes 720928 | tf_op jit(solution)/shard_map/ppermute | solution.py:435
  237.2 19.3 %collective-permute-done.17.refs_3_.refs_14_ = bf16[256,2048]{1,0:T(8,128)(2,1)S(1)} collective-permute-done((bf16[256,2048]{1,0:T(8,128)(2,1)S(1)}, bf16[256,2048]{1,0:T(8,128)(2,1)S(1)}, u32[]{:S(2)}, u32[]{:S(2)}) %collective-permute-start.17) | collective-permute-done | bytes 1048608 | tf_op jit(solution)/shard_map/ppermute | solution.py:435
  260.4 5.2 place_rows.7
  265.5 16.1 %mixer_finish.3 = (bf16[512,512]{1,0:T(8,128)(2,1)}, f32[512,512]{1,0:T(8,128)}, f32[8,16,8,128]{3,2,1,0:T(8,128)}) custom-call(f32[520]{0:T(1024)} %get-tuple-element.143.refs_0_, s32[65]{0:T(128)} %get-tuple-element.220.refs_1_, f32[8]{0:T(128)} %compare_convert_fusion.3.refs_2_, s32[1]{0:T(128)} %bitcast.5.me_ref.refs_3_, ...), custom_call_target="tpu_custom_call" | custom-call | flops 50331648 | bytes 7101000 | tf_op jit(solution)/shard_map/mixer_finish/pallas_call | solution.py:376
  281.7 6.6 place_rows.6
  290.2 9.4 %multiply_reduce_fusion.6 = (f32[512]{0:T(512)S(1)}, f32[512,2048]{1,0:T(8,128)S(1)}) fusion(bf16[512,2048]{1,0:T(8,128)(2,1)} %all-gather.13.cloned.1.call-done.refs_2_, bf16[2048,2048]{1,0:T(8,128)(2,1)} %place_rows.6, bf16[1280,2048]{1,0:T(8,128)(2,1)} %all-gather.11.cloned.1.call-done), kind=kOutput, calls=%fused_computation.40 | convolution fusion | flops 4299161088 | bytes 16779264 | tf_op jit(solution)/shard_map/dot_general | solution.py:591
  300.2 6.1 fusion.67
  306.4 5.8 multiply_convert_fusion.6
  312.2 9.7 %multiply_reduce_fusion.2 = (f32[2048]{0:T(1024)S(1)}, f32[512]{0:T(512)S(1)}, f32[512,2048]{1,0:T(8,128)}) fusion(f32[512,2048]{1,0:T(8,128)S(1)} %get-tuple-element.226, f32[512]{0:T(512)S(1)} %get-tuple-element.216, f32[2048]{0:T(1024)S(1)} %copy-done.64, bf16[2048,2816]{1,0:T(8,128)(2,1)S(1)} %bitcast.221, bf16[512,1408]{1,0:T(8,128)(2,1)} %get-tuple-element.164, ...), kind=kOutput, calls=%fused_computation.32 | convolution fusion | flops 5917636096 | bytes 22827008 | tf_op jit(solution)/shard_map/dot_general | solution.py:591
  323.9 4.2 all-gather.15.cloned.1.call-done.refs_3_
  328.0 9.4 %multiply_reduce_fusion.5 = (f32[512]{0:T(512)S(1)}, f32[512,2048]{1,0:T(8,128)S(1)}) fusion(bf16[512,2048]{1,0:T(8,128)(2,1)} %all-gather.15.cloned.1.call-done.refs_3_, bf16[2048,2048]{1,0:T(8,128)(2,1)} %place_rows.6, bf16[1280,2048]{1,0:T(8,128)(2,1)} %all-gather.11.cloned.1.call-done), kind=kOutput, calls=%fused_computation.38 | convolution fusion | flops 4299161088 | bytes 16779264 | tf_op jit(solution)/shard_map/dot_general | solution.py:591
  337.5 3.9 fusion.58
  342.8 9.3 %convolution_convert_fusion.1 = bf16[512,2048]{1,0:T(8,128)(2,1)} fusion(bf16[512,2048]{1,0:T(8,128)(2,1)S(1)} %get-tuple-element.156.refs_0_, bf16[2048,2048]{1,0:T(8,128)(2,1)} %place_rows.6), kind=kOutput, calls=%fused_computation.44 | convolution fusion | flops 4296015872 | bytes 12582912 | tf_op jit(solution)/shard_map/dot_general | solution.py:591
  352.1 11.2 %fusion.68 = f32[512,2816]{1,0:T(8,128)} fusion(bf16[512,2048]{1,0:T(8,128)(2,1)S(1)} %copy-done.31, bf16[2048,2816]{1,0:T(8,128)(2,1)} %place_rows.4), kind=kOutput, calls=%fused_computation.223 | convolution fusion | flops 5905580032 | bytes 19398656 | tf_op jit(solution)/shard_map/dot_general | solution.py:591
  363.4 11.3 %all-gather.19.cloned.1.call-done = bf16[1,512,2048]{2,1,0:T(8,128)(2,1)} async-done(((bf16[1,512,512]{2,1,0:T(8,128)(2,1)}), bf16[1,512,2048]{2,1,0:T(8,128)(2,1)}) %all-gather.19.cloned.1.call-update) | async-done | bytes 2097168 | tf_op jit(solution)/shard_map/all_gather | solution.py:424
  374.7 11.5 %multiply_convert_fusion.4 = (bf16[512,1408]{1,0:T(8,128)(2,1)}, bf16[512,1408]{1,0:T(8,128)(2,1)}, bf16[512,1408]{1,0:T(8,128)(2,1)}) fusion(f32[512,2816]{1,0:T(8,128)} %fusion.68, bf16[2048,1408]{1,0:T(8,128)(2,1)} %place_rows.7, bf16[1,512,2048]{2,1,0:T(8,128)(2,1)} %all-gather.19.cloned.1.call-done), kind=kOutput, calls=%fused_computation.54 | convolution fusion | flops 2964324352 | bytes 17956864 | tf_op jit(solution)/shard_map/dot_general | solution.py:591
  386.2 11.0 %multiply_reduce_fusion.1 = (f32[2048]{0:T(1024)S(1)}, f32[512]{0:T(512)S(1)}, f32[512,2048]{1,0:T(8,128)S(1)}) fusion(f32[512,2048]{1,0:T(8,128)S(1)} %copy-done.4, f32[512]{0:T(512)S(1)} %get-tuple-element.218, f32[2048]{0:T(1024)S(1)} %copy-done.64, bf16[2048,2816]{1,0:T(8,128)(2,1)} %place_rows.4, bf16[512,1408]{1,0:T(8,128)(2,1)} %get-tuple-element.166, ...), kind=kOutput, calls=%fused_computation.31 | convolution fusion | flops 5917636096 | bytes 22827008 | tf_op jit(solution)/shard_map/dot_general | solution.py:591
  397.2 4.3 fusion.59
  402.8 5.8 convolution_convert_fusion
  408.7 7.3 convolution_convert_fusion.3
  416.1 8.8 %grad_out.2.refs_10_ = bf16[1024,2048]{1,0:T(8,128)(2,1)} custom-call(s32[1]{0:T(128)} %bitcast.30.me_ref, bf16[512,2048]{1,0:T(8,128)(2,1)} %copy-done.32, bf16[512,2048]{1,0:T(8,128)(2,1)} %copy-done.33, bf16[512,2048]{1,0:T(8,128)(2,1)} %all-gather.13.cloned.1.call-done.refs_2_, bf16[512,2048]{1,0:T(8,128)(2,1)} %all-gather.15.cloned.1.call-done.refs_3_), custom_call_target="tpu_custom_call" | custom-call | flops 4294967296 | bytes 10485760 | tf_op jit(solution)/shard_map/grad_out/pallas_call | solution.py:514
  426.8 8.0 grad_down.2.refs_8_
  435.2 4.7 convolution_convert_fusion.2
  440.0 7.5 grad_down.3.refs_9_
  447.5 8.9 %grad_out.3.refs_11_ = bf16[1024,2048]{1,0:T(8,128)(2,1)} custom-call(s32[1]{0:T(128)} %bitcast.33.me_ref, bf16[512,2048]{1,0:T(8,128)(2,1)} %copy-done.32, bf16[512,2048]{1,0:T(8,128)(2,1)} %copy-done.33, bf16[512,2048]{1,0:T(8,128)(2,1)} %all-gather.13.cloned.1.call-done.refs_2_, bf16[512,2048]{1,0:T(8,128)(2,1)} %all-gather.15.cloned.1.call-done.refs_3_), custom_call_target="tpu_custom_call" | custom-call | flops 4294967296 | bytes 10485760 | tf_op jit(solution)/shard_map/grad_out/pallas_call | solution.py:514
  458.1 11.9 %mixer_adjoint.2 = (f32[4096,128]{1,0:T(8,128)}, f32[16,8,128]{2,1,0:T(8,128)}) custom-call(f32[520]{0:T(1024)} %get-tuple-element.142.refs_0_, s32[65]{0:T(128)} %get-tuple-element.219.refs_1_, bf16[512,1536]{1,0:T(8,128)(2,1)} %get-tuple-element.179.refs_2_.refs_4_, f32[8,1536]{1,0:T(8,128)} %get-tuple-element.192.refs_3_.refs_5_, ...), custom_call_target="tpu_custom_call" | custom-call | flops 33554432 | bytes 4411940 | tf_op jit(solution)/shard_map/mixer_adjoint/pallas_call | solution.py:376
  470.9 12.0 %mixer_adjoint.3 = (f32[4096,128]{1,0:T(8,128)}, f32[16,8,128]{2,1,0:T(8,128)}) custom-call(f32[520]{0:T(1024)} %get-tuple-element.143.refs_0_, s32[65]{0:T(128)} %get-tuple-element.220.refs_1_, bf16[512,1536]{1,0:T(8,128)(2,1)} %get-tuple-element.180.refs_2_.refs_4_, f32[8,1536]{1,0:T(8,128)} %get-tuple-element.193.refs_3_.refs_5_, ...), custom_call_target="tpu_custom_call" | custom-call | flops 33554432 | bytes 4411940 | tf_op jit(solution)/shard_map/mixer_adjoint/pallas_call | solution.py:376
  483.7 4.2 add_convert_fusion.1
  487.9 9.8 %all_gather.41 = bf16[8,2,16,8,128]{4,3,2,1,0:T(8,128)(2,1)S(1)} all-gather(bf16[1,2,16,8,128]{4,3,2,1,0:T(8,128)(2,1)S(1)} %pad_maximum_fusion.6), channel_id=1, replica_groups=mesh['seq'=8,'tp'=4] {'seq'}, dimensions={0}, use_global_device_ids=true | all-gather | bytes 589824 | tf_op jit(solution)/shard_map/all_gather | solution.py:710
  503.3 11.0 %grad_gu.2.refs_18_ = bf16[1024,2816]{1,0:T(8,128)(2,1)} custom-call(s32[1]{0:T(128)} %bitcast.30.me_ref, bf16[512,2048]{1,0:T(8,128)(2,1)} %copy-done.30, bf16[512,2048]{1,0:T(8,128)(2,1)} %get-tuple-element.210.refs_1_, bf16[512,2816]{1,0:T(8,128)(2,1)} %pad_maximum_fusion.refs_2_, bf16[512,2816]{1,0:T(8,128)(2,1)} %pad_maximum_fusion.1.refs_3_, ...), custom_call_target="tpu_custom_call" | custom-call | flops 5905580032 | bytes 13631488 | tf_op jit(solution)/shard_map/grad_gu/pallas_call | solution.py:514
  515.6 4.8 slice_bitcast_fusion
  538.7 11.3 %collective-permute-done.45 = bf16[256,2048]{0,1:T(8,128)(2,1)} collective-permute-done((bf16[256,2048]{0,1:T(8,128)(2,1)}, bf16[256,2048]{0,1:T(8,128)(2,1)}, u32[]{:S(2)}, u32[]{:S(2)}) %collective-permute-start.45) | collective-permute-done | bytes 1048608 | tf_op jit(solution)/shard_map/ppermute | solution.py:435
  550.0 6.7 collective-permute-done.47
  563.4 8.7 %collective-permute-done.32 = bf16[256,1408]{1,0:T(8,128)(2,1)S(1)} collective-permute-done((bf16[256,1408]{1,0:T(8,128)(2,1)}, bf16[256,1408]{1,0:T(8,128)(2,1)S(1)}, u32[]{:S(2)}, u32[]{:S(2)}) %collective-permute-start.32) | collective-permute-done | bytes 720928 | tf_op jit(solution)/shard_map/ppermute | solution.py:435
  578.1 11.1 %grad_gu.3.refs_19_ = bf16[1024,2816]{1,0:T(8,128)(2,1)} custom-call(s32[1]{0:T(128)} %bitcast.33.me_ref, bf16[512,2048]{1,0:T(8,128)(2,1)} %copy-done.30, bf16[512,2048]{1,0:T(8,128)(2,1)} %get-tuple-element.210.refs_1_, bf16[512,2816]{1,0:T(8,128)(2,1)} %pad_maximum_fusion.refs_2_, bf16[512,2816]{1,0:T(8,128)(2,1)} %pad_maximum_fusion.1.refs_3_, ...), custom_call_target="tpu_custom_call" | custom-call | flops 5905580032 | bytes 13631488 | tf_op jit(solution)/shard_map/grad_gu/pallas_call | solution.py:514
  595.1 5.7 add_convert_fusion
  603.8 33.6 %mixer_back.2 = (bf16[512,1536]{1,0:T(8,128)(2,1)}, f32[8,1536]{1,0:T(8,128)}, f32[16,1536]{1,0:T(8,128)}, f32[72,512]{1,0:T(8,128)}, f32[8,512]{1,0:T(8,128)}, ...) custom-call(f32[520]{0:T(1024)} %get-tuple-element.142.refs_0_, s32[65]{0:T(128)} %get-tuple-element.219.refs_1_, ...), custom_call_target="tpu_custom_call" | custom-call | flops 134217728 | bytes 11213384 | tf_op jit(solution)/shard_map/mixer_back/pallas_call | solution.py:376
  642.8 7.9 fusion.8
  650.7 3.7 fusion.5.refs_18_
  658.2 16.5 %collective-permute-done.35.refs_20_ = bf16[256,2816]{1,0:T(8,128)(2,1)S(1)} collective-permute-done((bf16[256,2816]{1,0:T(8,128)(2,1)S(1)}, bf16[256,2816]{1,0:T(8,128)(2,1)S(1)}, u32[]{:S(2)}, u32[]{:S(2)}) %collective-permute-start.35) | collective-permute-done | bytes 1441824 | tf_op jit(solution)/shard_map/ppermute | solution.py:435
  678.7 33.7 %mixer_back.3 = (bf16[512,1536]{1,0:T(8,128)(2,1)}, f32[8,1536]{1,0:T(8,128)}, f32[16,1536]{1,0:T(8,128)}, f32[72,512]{1,0:T(8,128)}, f32[8,512]{1,0:T(8,128)}, ...) custom-call(f32[520]{0:T(1024)} %get-tuple-element.143.refs_0_, s32[65]{0:T(128)} %get-tuple-element.220.refs_1_, ...), custom_call_target="tpu_custom_call" | custom-call | flops 134217728 | bytes 11213384 | tf_op jit(solution)/shard_map/mixer_back/pallas_call | solution.py:376
  717.8 7.7 grad_in.2
  729.5 8.0 fusion.15
  737.5 3.7 fusion.12
  742.0 7.4 grad_in.3
  749.4 3.7 add_convert_fusion.2
  762.0 4.2 concatenate.57
  768.4 11.5 %all-gather.4 = bf16[8,74,512]{2,1,0:T(8,128)(2,1)S(1)} all-gather(bf16[1,74,512]{2,1,0:T(8,128)(2,1)S(1)} %fusion.33), channel_id=5, replica_groups=mesh['seq'=8,'tp'=4] {'seq'}, dimensions={0}, use_global_device_ids=true | all-gather | bytes 681984 | tf_op jit(solution)/shard_map/all_gather | solution.py:760
  787.6 4.4 fusion.20
  792.0 4.7 reshape.436
  799.0 6.5 collective-permute-done.43
  814.7 8.4 %all-gather.2 = bf16[64,512]{1,0:T(8,128)(2,1)S(1)} all-gather(bf16[8,512]{1,0:T(8,128)(2,1)S(1)} %add_convert_fusion.8), channel_id=4, replica_groups=mesh['seq'=8,'tp'=4] {'seq'}, dimensions={0}, use_global_device_ids=true | all-gather | bytes 73728 | tf_op jit(solution)/shard_map/all_gather | solution.py:761
  (476 shorter events, 177.7 us)
Async XLA Ops:
  7.2 123.6 %all-gather.11.cloned.1.call-start = ((), (), s32[]{:S(2)}) async-start(), calls=%async_computation.7 | async-start | bytes 6553600 | tf_op jit(solution)/shard_map/all_gather | solution.py:424
  10.8 184.0 %all-gather.17.cloned.1.call-start = ((), (), s32[]{:S(2)}) async-start(), calls=%async_computation.17 | async-start | bytes 2621440 | tf_op jit(solution)/shard_map/all_gather | solution.py:424
  11.4 20.7 %collective-permute-start = (bf16[256,1536]{1,0:T(8,128)(2,1)S(1)}, bf16[256,1536]{1,0:T(8,128)(2,1)}, u32[]{:S(2)}, u32[]{:S(2)}) collective-permute-start(bf16[256,1536]{1,0:T(8,128)(2,1)S(1)} %copy.92.refs_0_), channel_id=1, source_target_pairs={{0,8},{4,12},{8,0},{12,4},{16,24},{20,28},{24,16},{28,20},{1,9},{5... | collective-permute-start | bytes 2359304 | tf_op jit(solution)/shard_map/ppermute | solution.py:435
  35.5 52.1 %copy-start.72 = (f32[3,3,512]{2,1,0:T(4,128)S(1)}, f32[3,3,512]{2,1,0:T(4,128)}, u32[]{:S(2)}) copy-start(f32[3,3,512]{2,1,0:T(4,128)} %param.20) | copy-start | bytes 55300
  35.7 83.1 %copy-start.16 = (bf16[32,8,2,1408]{3,1,2,0:T(8,128)(2,1)}, bf16[32,8,2,1408]{3,1,2,0:T(8,128)(2,1)S(1)}, u32[]{:S(2)}) copy-start(bf16[32,8,2,1408]{3,1,2,0:T(8,128)(2,1)S(1)} %copy.109) | copy-start | bytes 4325380
  35.7 34.7 %collective-permute-start.2 = (bf16[256,2816]{1,0:T(8,128)(2,1)S(1)}, bf16[256,2816]{1,0:T(8,128)(2,1)}, u32[]{:S(2)}, u32[]{:S(2)}) collective-permute-start(bf16[256,2816]{1,0:T(8,128)(2,1)S(1)} %bitcast.238), channel_id=1, source_target_pairs={{0,16},{4,20},{8,24},{12,28},{16,0},{20,4},{24,8},{28,12},{1,17},{... | collective-permute-start | bytes 4325384 | tf_op jit(solution)/shard_map/ppermute | solution.py:435
  37.6 48.3 %collective-permute-start.10 = (bf16[256,1536]{1,0:T(8,128)(2,1)S(1)}, bf16[256,1536]{1,0:T(8,128)(2,1)S(1)}, u32[]{:S(2)}, u32[]{:S(2)}) collective-permute-start(bf16[256,1536]{1,0:T(8,128)(2,1)S(1)} %copy.92.refs_0_), channel_id=1, source_target_pairs={{0,4},{4,0},{8,12},{12,8},{16,20},{20,16},{24,28},{28,24},{1,5},{5... | collective-permute-start | bytes 2359304 | tf_op jit(solution)/shard_map/ppermute | solution.py:435
  37.6 47.9 %collective-permute-start.8 = (bf16[256,1536]{1,0:T(8,128)(2,1)S(1)}, bf16[256,1536]{1,0:T(8,128)(2,1)}, u32[]{:S(2)}, u32[]{:S(2)}) collective-permute-start(bf16[256,1536]{1,0:T(8,128)(2,1)S(1)} %copy.92.refs_0_), channel_id=1, source_target_pairs={{0,16},{4,20},{8,24},{12,28},{16,0},{20,4},{24,8},{28,12},{1,17},{... | collective-permute-start | bytes 2359304 | tf_op jit(solution)/shard_map/ppermute | solution.py:435
  38.7 249.7 %all-gather.13.cloned.1.call-start = ((), (), s32[]{:S(2)}) async-start(), calls=%async_computation.8 | async-start | bytes 2621440 | tf_op jit(solution)/shard_map/all_gather | solution.py:424
  39.1 53.3 %collective-permute-start.1 = (bf16[256,2816]{1,0:T(8,128)(2,1)S(1)}, bf16[256,2816]{1,0:T(8,128)(2,1)}, u32[]{:S(2)}, u32[]{:S(2)}) collective-permute-start(bf16[256,2816]{1,0:T(8,128)(2,1)S(1)} %bitcast.239), channel_id=1, source_target_pairs={{0,8},{4,12},{8,0},{12,4},{16,24},{20,28},{24,16},{28,20},{1,9},{5... | collective-permute-start | bytes 4325384 | tf_op jit(solution)/shard_map/ppermute | solution.py:435
  70.4 33.5 %collective-permute-start.3 = (bf16[256,2816]{1,0:T(8,128)(2,1)}, bf16[256,2816]{1,0:T(8,128)(2,1)}, u32[]{:S(2)}, u32[]{:S(2)}) collective-permute-start(bf16[256,2816]{1,0:T(8,128)(2,1)} %collective-permute-done.2.refs_2_), channel_id=1, source_target_pairs={{0,8},{4,12},{8,0},{12,4},{16,24},{20,28},{24,16},{28,20},{1,9},{5... | collective-permute-start | bytes 4325384 | tf_op jit(solution)/shard_map/ppermute | solution.py:435
  72.4 19.8 %collective-permute-start.11 = (bf16[256,1536]{1,0:T(8,128)(2,1)}, bf16[256,1536]{1,0:T(8,128)(2,1)}, u32[]{:S(2)}, u32[]{:S(2)}) collective-permute-start(bf16[256,1536]{1,0:T(8,128)(2,1)} %collective-permute-done.refs_1_), channel_id=1, source_target_pairs={{0,4},{4,0},{8,12},{12,8},{16,20},{20,16},{24,28},{28,24},{1,5},{5... | collective-permute-start | bytes 2359304 | tf_op jit(solution)/shard_map/ppermute | solution.py:435
  85.5 6.4 collective-permute-start.12
  85.9 23.4 %collective-permute-start.9 = (bf16[256,1536]{1,0:T(8,128)(2,1)}, bf16[256,1536]{1,0:T(8,128)(2,1)}, u32[]{:S(2)}, u32[]{:S(2)}) collective-permute-start(bf16[256,1536]{1,0:T(8,128)(2,1)} %collective-permute-done.refs_1_), channel_id=1, source_target_pairs={{0,16},{4,20},{8,24},{12,28},{16,0},{20,4},{24,8},{28,12},{1,17},{... | collective-permute-start | bytes 2359304 | tf_op jit(solution)/shard_map/ppermute | solution.py:435
  91.9 26.9 %collective-permute-start.4 = (bf16[256,2816]{1,0:T(8,128)(2,1)S(1)}, bf16[256,2816]{1,0:T(8,128)(2,1)S(1)}, u32[]{:S(2)}, u32[]{:S(2)}) collective-permute-start(bf16[256,2816]{1,0:T(8,128)(2,1)S(1)} %bitcast.240), channel_id=1, source_target_pairs={{0,4},{4,0},{8,12},{12,8},{16,20},{20,16},{24,28},{28,24},{1,5},{5... | collective-permute-start | bytes 4325384 | tf_op jit(solution)/shard_map/ppermute | solution.py:435
  92.2 26.7 %collective-permute-start.6 = (bf16[256,2816]{1,0:T(8,128)(2,1)}, bf16[256,2816]{1,0:T(8,128)(2,1)}, u32[]{:S(2)}, u32[]{:S(2)}) collective-permute-start(bf16[256,2816]{1,0:T(8,128)(2,1)} %collective-permute-done.2.refs_2_), channel_id=1, source_target_pairs={{0,4},{4,0},{8,12},{12,8},{16,20},{20,16},{24,28},{28,24},{1,5},{5... | collective-permute-start | bytes 4325384 | tf_op jit(solution)/shard_map/ppermute | solution.py:435
  92.5 26.4 %collective-permute-start.5 = (bf16[256,2816]{1,0:T(8,128)(2,1)}, bf16[256,2816]{1,0:T(8,128)(2,1)}, u32[]{:S(2)}, u32[]{:S(2)}) collective-permute-start(bf16[256,2816]{1,0:T(8,128)(2,1)} %collective-permute-done.1.refs_1_), channel_id=1, source_target_pairs={{0,4},{4,0},{8,12},{12,8},{16,20},{20,16},{24,28},{28,24},{1,5},{5... | collective-permute-start | bytes 4325384 | tf_op jit(solution)/shard_map/ppermute | solution.py:435
  103.9 14.9 %collective-permute-start.7 = (bf16[256,2816]{1,0:T(8,128)(2,1)}, bf16[256,2816]{1,0:T(8,128)(2,1)}, u32[]{:S(2)}, u32[]{:S(2)}) collective-permute-start(bf16[256,2816]{1,0:T(8,128)(2,1)} %collective-permute-done.3.refs_3_), channel_id=1, source_target_pairs={{0,4},{4,0},{8,12},{12,8},{16,20},{20,16},{24,28},{28,24},{1,5},{5... | collective-permute-start | bytes 4325384 | tf_op jit(solution)/shard_map/ppermute | solution.py:435
  109.3 3.1 collective-permute-start.13
  132.1 62.7 %collective-permute-start.16 = (bf16[256,2048]{1,0:T(8,128)(2,1)S(1)}, bf16[256,2048]{1,0:T(8,128)(2,1)S(1)}, u32[]{:S(2)}, u32[]{:S(2)}) collective-permute-start(bf16[256,2048]{1,0:T(8,128)(2,1)S(1)} %slice.311.refs_0_), channel_id=1, source_target_pairs={{0,16},{4,20},{8,24},{12,28},{16,0},{20,4},{24,8},{28,12},{1,17},{... | collective-permute-start | bytes 3145736 | tf_op jit(solution)/shard_map/ppermute | solution.py:435
  133.9 61.0 %collective-permute-start.15 = (bf16[256,2048]{1,0:T(8,128)(2,1)S(1)}, bf16[256,2048]{1,0:T(8,128)(2,1)S(1)}, u32[]{:S(2)}, u32[]{:S(2)}) collective-permute-start(bf16[256,2048]{1,0:T(8,128)(2,1)S(1)} %slice.311.refs_0_), channel_id=1, source_target_pairs={{0,8},{4,12},{8,0},{12,4},{16,24},{20,28},{24,16},{28,20},{1,9},{5... | collective-permute-start | bytes 3145736 | tf_op jit(solution)/shard_map/ppermute | solution.py:435
  150.5 3.3 collective-permute-start.14
  212.2 115.8 %all-gather.15.cloned.1.call-start = ((), (), s32[]{:S(2)}) async-start(), calls=%async_computation.10 | async-start | bytes 2621440 | tf_op jit(solution)/shard_map/all_gather | solution.py:424
  215.0 18.4 %collective-permute-start.23 = (bf16[256,1408]{1,0:T(8,128)(2,1)S(1)}, bf16[256,1408]{1,0:T(8,128)(2,1)S(1)}, u32[]{:S(2)}, u32[]{:S(2)}) collective-permute-start(bf16[256,1408]{1,0:T(8,128)(2,1)S(1)} %add_bitcast_fusion.refs_0_), channel_id=1, source_target_pairs={{0,16},{4,20},{8,24},{12,28},{16,0},{20,4},{24,8},{28,12},{1,17},{... | collective-permute-start | bytes 2162696 | tf_op jit(solution)/shard_map/ppermute | solution.py:435
  215.9 19.0 %collective-permute-start.22 = (bf16[256,1408]{1,0:T(8,128)(2,1)S(1)}, bf16[256,1408]{1,0:T(8,128)(2,1)S(1)}, u32[]{:S(2)}, u32[]{:S(2)}) collective-permute-start(bf16[256,1408]{1,0:T(8,128)(2,1)S(1)} %add_bitcast_fusion.refs_0_), channel_id=1, source_target_pairs={{0,8},{4,12},{8,0},{12,4},{16,24},{20,28},{24,16},{28,20},{1,9},{5... | collective-permute-start | bytes 2162696 | tf_op jit(solution)/shard_map/ppermute | solution.py:435
  217.2 39.3 %collective-permute-start.17 = (bf16[256,2048]{1,0:T(8,128)(2,1)S(1)}, bf16[256,2048]{1,0:T(8,128)(2,1)S(1)}, u32[]{:S(2)}, u32[]{:S(2)}) collective-permute-start(bf16[256,2048]{1,0:T(8,128)(2,1)S(1)} %copy-done.20), channel_id=1, source_target_pairs={{0,8},{4,12},{8,0},{12,4},{16,24},{20,28},{24,16},{28,20},{1,9},{5... | collective-permute-start | bytes 3145736 | tf_op jit(solution)/shard_map/ppermute | solution.py:435
  217.9 18.2 %collective-permute-start.25 = (bf16[256,1408]{1,0:T(8,128)(2,1)S(1)}, bf16[256,1408]{1,0:T(8,128)(2,1)S(1)}, u32[]{:S(2)}, u32[]{:S(2)}) collective-permute-start(bf16[256,1408]{1,0:T(8,128)(2,1)S(1)} %add_bitcast_fusion.refs_0_), channel_id=1, source_target_pairs={{0,4},{4,0},{8,12},{12,8},{16,20},{20,16},{24,28},{28,24},{1,5},{5... | collective-permute-start | bytes 2162696 | tf_op jit(solution)/shard_map/ppermute | solution.py:435
  233.5 2.9 collective-permute-start.27
  234.9 2.2 collective-permute-start.26
  234.9 21.6 %collective-permute-start.24 = (bf16[256,1408]{1,0:T(8,128)(2,1)S(1)}, bf16[256,1408]{1,0:T(8,128)(2,1)S(1)}, u32[]{:S(2)}, u32[]{:S(2)}) collective-permute-start(bf16[256,1408]{1,0:T(8,128)(2,1)S(1)} %collective-permute-done.22.refs_1_.refs_15_), channel_id=1, source_target_pairs={{0,16},{4,20},{8,24},{12,28},{16,0},{20,4},{24,8},{28,12},{1,17},{... | collective-permute-start | bytes 2162696 | tf_op jit(solution)/shard_map/ppermute | solution.py:435
  236.1 45.5 %collective-permute-start.18 = (bf16[256,2048]{1,0:T(8,128)(2,1)}, bf16[256,2048]{1,0:T(8,128)(2,1)}, u32[]{:S(2)}, u32[]{:S(2)}) collective-permute-start(bf16[256,2048]{1,0:T(8,128)(2,1)} %copy-done.24), channel_id=1, source_target_pairs={{0,4},{4,0},{8,12},{12,8},{16,20},{20,16},{24,28},{28,24},{1,5},{5... | collective-permute-start | bytes 3145736 | tf_op jit(solution)/shard_map/ppermute | solution.py:435
  236.4 45.3 %collective-permute-start.20 = (bf16[256,2048]{1,0:T(8,128)(2,1)S(1)}, bf16[256,2048]{1,0:T(8,128)(2,1)}, u32[]{:S(2)}, u32[]{:S(2)}) collective-permute-start(bf16[256,2048]{1,0:T(8,128)(2,1)S(1)} %copy-done.20), channel_id=1, source_target_pairs={{0,4},{4,0},{8,12},{12,8},{16,20},{20,16},{24,28},{28,24},{1,5},{5... | collective-permute-start | bytes 3145736 | tf_op jit(solution)/shard_map/ppermute | solution.py:435
  237.1 44.6 %collective-permute-start.19 = (bf16[256,2048]{1,0:T(8,128)(2,1)S(1)}, bf16[256,2048]{1,0:T(8,128)(2,1)}, u32[]{:S(2)}, u32[]{:S(2)}) collective-permute-start(bf16[256,2048]{1,0:T(8,128)(2,1)S(1)} %copy-done.22), channel_id=1, source_target_pairs={{0,4},{4,0},{8,12},{12,8},{16,20},{20,16},{24,28},{28,24},{1,5},{5... | collective-permute-start | bytes 3145736 | tf_op jit(solution)/shard_map/ppermute | solution.py:435
  256.5 25.2 %collective-permute-start.21 = (bf16[256,2048]{1,0:T(8,128)(2,1)S(1)}, bf16[256,2048]{1,0:T(8,128)(2,1)}, u32[]{:S(2)}, u32[]{:S(2)}) collective-permute-start(bf16[256,2048]{1,0:T(8,128)(2,1)S(1)} %collective-permute-done.17.refs_3_.refs_14_), channel_id=1, source_target_pairs={{0,4},{4,0},{8,12},{12,8},{16,20},{20,16},{24,28},{28,24},{1,5},{5... | collective-permute-start | bytes 3145736 | tf_op jit(solution)/shard_map/ppermute | solution.py:435
  257.4 2.9 collective-permute-start.28
  281.6 93.1 %all-gather.19.cloned.1.call-start = ((), (), s32[]{:S(2)}) async-start(), calls=%async_computation.18 | async-start | bytes 2621440 | tf_op jit(solution)/shard_map/all_gather | solution.py:424
  323.8 134.3 %reduce-scatter.12.cloned.1.call-start = ((), (), s32[]{:S(2)}) async-start(), calls=%async_computation.12 | async-start | bytes 2621440 | tf_op jit(solution)/shard_map/reduce_scatter | solution.py:428
  363.3 107.5 %reduce-scatter.14.cloned.1.call-start = ((), (), s32[]{:S(2)}) async-start(), calls=%async_computation.13 | async-start | bytes 2621440 | tf_op jit(solution)/shard_map/reduce_scatter | solution.py:428
  408.6 151.1 %reduce-scatter.8.cloned.1.call-start = ((), (), s32[]{:S(2)}) async-start(), calls=%async_computation.9 | async-start | bytes 2621440 | tf_op jit(solution)/shard_map/reduce_scatter | solution.py:428
  416.0 159.4 %reduce-scatter.10.cloned.1.call-start = ((), (), s32[]{:S(2)}) async-start(), calls=%async_computation.11 | async-start | bytes 2621440 | tf_op jit(solution)/shard_map/reduce_scatter | solution.py:428
  424.9 58.8 %collective-permute-start.44 = (bf16[1024,2048]{1,0:T(8,128)(2,1)}, bf16[1024,2048]{1,0:T(8,128)(2,1)}, u32[]{:S(2)}, u32[]{:S(2)}) collective-permute-start(bf16[1024,2048]{1,0:T(8,128)(2,1)} %grad_out.2.refs_10_), channel_id=1, source_target_pairs={{0,4},{4,0},{8,12},{12,8},{16,20},{20,16},{24,28},{28,24},{1,5},{5... | collective-permute-start | bytes 12582920 | tf_op jit(solution)/shard_map/ppermute | solution.py:435
  434.8 98.2 %collective-permute-start.31 = (bf16[1024,1408]{1,0:T(8,128)(2,1)}, bf16[1024,1408]{1,0:T(8,128)(2,1)}, u32[]{:S(2)}, u32[]{:S(2)}) collective-permute-start(bf16[1024,1408]{1,0:T(8,128)(2,1)} %grad_down.2.refs_8_), channel_id=1, source_target_pairs={{0,4},{4,0},{8,12},{12,8},{16,20},{20,16},{24,28},{28,24},{1,5},{5... | collective-permute-start | bytes 8650760 | tf_op jit(solution)/shard_map/ppermute | solution.py:435
  440.0 153.4 %reduce-scatter.20.cloned.1.call-start = ((), (), s32[]{:S(2)}) async-start(), calls=%async_computation.16 | async-start | bytes 1310720 | tf_op jit(solution)/shard_map/reduce_scatter | solution.py:428
  501.8 25.7 %collective-permute-start.46 = (bf16[256,2048]{0,1:T(8,128)(2,1)}, bf16[256,2048]{0,1:T(8,128)(2,1)}, u32[]{:S(2)}, u32[]{:S(2)}) collective-permute-start(bf16[256,2048]{0,1:T(8,128)(2,1)} %bitcast.70), channel_id=1, source_target_pairs={{0,8},{4,12},{8,0},{12,4},{16,24},{20,28},{24,16},{28,20},{1,9},{5... | collective-permute-start | bytes 3145736 | tf_op jit(solution)/shard_map/ppermute | solution.py:435
  514.2 80.9 %collective-permute-start.29 = (bf16[1024,2816]{1,0:T(8,128)(2,1)}, bf16[1024,2816]{1,0:T(8,128)(2,1)}, u32[]{:S(2)}, u32[]{:S(2)}) collective-permute-start(bf16[1024,2816]{1,0:T(8,128)(2,1)} %grad_gu.2.refs_18_), channel_id=1, source_target_pairs={{0,4},{4,0},{8,12},{12,8},{16,20},{20,16},{24,28},{28,24},{1,5},{5... | collective-permute-start | bytes 17301512 | tf_op jit(solution)/shard_map/ppermute | solution.py:435
  524.1 25.9 %collective-permute-start.45 = (bf16[256,2048]{0,1:T(8,128)(2,1)}, bf16[256,2048]{0,1:T(8,128)(2,1)}, u32[]{:S(2)}, u32[]{:S(2)}) collective-permute-start(bf16[256,2048]{0,1:T(8,128)(2,1)} %bitcast.248), channel_id=1, source_target_pairs={{0,8},{4,12},{8,0},{12,4},{16,24},{20,28},{24,16},{28,20},{1,9},{5... | collective-permute-start | bytes 3145736 | tf_op jit(solution)/shard_map/ppermute | solution.py:435
  530.3 26.4 %collective-permute-start.47 = (bf16[256,2048]{0,1:T(8,128)(2,1)}, bf16[256,2048]{0,1:T(8,128)(2,1)}, u32[]{:S(2)}, u32[]{:S(2)}) collective-permute-start(bf16[256,2048]{0,1:T(8,128)(2,1)} %fusion.21), channel_id=1, source_target_pairs={{0,16},{4,20},{8,24},{12,28},{16,0},{20,4},{24,8},{28,12},{1,17},{... | collective-permute-start | bytes 3145736 | tf_op jit(solution)/shard_map/ppermute | solution.py:435
  538.1 34.0 %collective-permute-start.32 = (bf16[256,1408]{1,0:T(8,128)(2,1)}, bf16[256,1408]{1,0:T(8,128)(2,1)S(1)}, u32[]{:S(2)}, u32[]{:S(2)}) collective-permute-start(bf16[256,1408]{1,0:T(8,128)(2,1)} %get-tuple-element.181), channel_id=1, source_target_pairs={{0,16},{4,20},{8,24},{12,28},{16,0},{20,4},{24,8},{28,12},{1,17},{... | collective-permute-start | bytes 2162696 | tf_op jit(solution)/shard_map/ppermute | solution.py:435
  559.7 237.0 %reduce-scatter.16.cloned.1.call-start = ((), (), s32[]{:S(2)}) async-start(), calls=%async_computation.14 | async-start | bytes 2621440 | tf_op jit(solution)/shard_map/reduce_scatter | solution.py:428
  561.3 27.8 %collective-permute-start.34 = (bf16[256,1408]{1,0:T(8,128)(2,1)S(1)}, bf16[256,1408]{1,0:T(8,128)(2,1)S(1)}, u32[]{:S(2)}, u32[]{:S(2)}) collective-permute-start(bf16[256,1408]{1,0:T(8,128)(2,1)S(1)} %get-tuple-element.182), channel_id=1, source_target_pairs={{0,16},{4,20},{8,24},{12,28},{16,0},{20,4},{24,8},{28,12},{1,17},{... | collective-permute-start | bytes 2162696 | tf_op jit(solution)/shard_map/ppermute | solution.py:435
  573.4 16.6 %collective-permute-start.33 = (bf16[256,1408]{1,0:T(8,128)(2,1)S(1)}, bf16[256,1408]{1,0:T(8,128)(2,1)}, u32[]{:S(2)}, u32[]{:S(2)}) collective-permute-start(bf16[256,1408]{1,0:T(8,128)(2,1)S(1)} %fusion.26), channel_id=1, source_target_pairs={{0,8},{4,12},{8,0},{12,4},{16,24},{20,28},{24,16},{28,20},{1,9},{5... | collective-permute-start | bytes 2162696 | tf_op jit(solution)/shard_map/ppermute | solution.py:435
  638.2 3.1 collective-permute-start.30
  640.3 34.4 %collective-permute-start.35 = (bf16[256,2816]{1,0:T(8,128)(2,1)S(1)}, bf16[256,2816]{1,0:T(8,128)(2,1)S(1)}, u32[]{:S(2)}, u32[]{:S(2)}) collective-permute-start(bf16[256,2816]{1,0:T(8,128)(2,1)S(1)} %get-tuple-element.168), channel_id=1, source_target_pairs={{0,8},{4,12},{8,0},{12,4},{16,24},{20,28},{24,16},{28,20},{1,9},{5... | collective-permute-start | bytes 4325384 | tf_op jit(solution)/shard_map/ppermute | solution.py:435
  654.5 142.2 %reduce-scatter.18.cloned.1.call-start = ((), (), s32[]{:S(2)}) async-start(), calls=%async_computation.15 | async-start | bytes 2621440 | tf_op jit(solution)/shard_map/reduce_scatter | solution.py:428
  655.8 129.8 %collective-permute-start.48 = (bf16[256,2816]{1,0:T(8,128)(2,1)}, bf16[256,2816]{1,0:T(8,128)(2,1)}, u32[]{:S(2)}, u32[]{:S(2)}) collective-permute-start(bf16[256,2816]{1,0:T(8,128)(2,1)} %get-tuple-element.167), channel_id=1, source_target_pairs={{0,8},{4,12},{8,0},{12,4},{16,24},{20,28},{24,16},{28,20},{1,9},{5... | collective-permute-start | bytes 4325384 | tf_op jit(solution)/shard_map/ppermute | solution.py:435
  678.0 109.0 %collective-permute-start.49 = (bf16[256,2816]{1,0:T(8,128)(2,1)}, bf16[256,2816]{1,0:T(8,128)(2,1)}, u32[]{:S(2)}, u32[]{:S(2)}) collective-permute-start(bf16[256,2816]{1,0:T(8,128)(2,1)} %fusion.19), channel_id=1, source_target_pairs={{0,16},{4,20},{8,24},{12,28},{16,0},{20,4},{24,8},{28,12},{1,17},{... | collective-permute-start | bytes 4325384 | tf_op jit(solution)/shard_map/ppermute | solution.py:435
  713.2 3.1 collective-permute-start.36
  726.7 22.7 %collective-permute-start.40 = (bf16[1024,1536]{1,0:T(8,128)(2,1)}, bf16[1024,1536]{1,0:T(8,128)(2,1)}, u32[]{:S(2)}, u32[]{:S(2)}) collective-permute-start(bf16[1024,1536]{1,0:T(8,128)(2,1)} %grad_in.2), channel_id=1, source_target_pairs={{0,4},{4,0},{8,12},{12,8},{16,20},{20,16},{24,28},{28,24},{1,5},{5... | collective-permute-start | bytes 9437192 | tf_op jit(solution)/shard_map/ppermute | solution.py:435
  754.4 28.1 %collective-permute-start.41 = (bf16[256,1536]{1,0:T(8,128)(2,1)}, bf16[256,1536]{1,0:T(8,128)(2,1)}, u32[]{:S(2)}, u32[]{:S(2)}) collective-permute-start(bf16[256,1536]{1,0:T(8,128)(2,1)} %get-tuple-element.177), channel_id=1, source_target_pairs={{0,16},{4,20},{8,24},{12,28},{16,0},{20,4},{24,8},{28,12},{1,17},{... | collective-permute-start | bytes 2359304 | tf_op jit(solution)/shard_map/ppermute | solution.py:435
  766.3 47.7 %collective-permute-start.37 = (bf16[8,512]{1,0:T(8,128)(2,1)S(1)}, bf16[8,512]{1,0:T(8,128)(2,1)S(1)}, u32[]{:S(2)}, u32[]{:S(2)}) collective-permute-start(bf16[8,512]{1,0:T(8,128)(2,1)S(1)} %slice.423), channel_id=1, source_target_pairs={{0,1},{1,2},{2,3},{3,0},{4,5},{5,6},{6,7},{7,4},{8,9},{9,10},{10,1... | collective-permute-start | bytes 24584 | tf_op jit(solution)/shard_map/ppermute | solution.py:578
  766.3 47.6 %collective-permute-start.38 = (bf16[8,512]{1,0:T(8,128)(2,1)S(1)}, bf16[8,512]{1,0:T(8,128)(2,1)S(1)}, u32[]{:S(2)}, u32[]{:S(2)}) collective-permute-start(bf16[8,512]{1,0:T(8,128)(2,1)S(1)} %slice.423), channel_id=1, source_target_pairs={{0,2},{1,3},{2,0},{3,1},{4,6},{5,7},{6,4},{7,5},{8,10},{9,11},{10,... | collective-permute-start | bytes 24584 | tf_op jit(solution)/shard_map/ppermute | solution.py:578
  782.5 31.5 %collective-permute-start.39 = (bf16[8,512]{1,0:T(8,128)(2,1)S(1)}, bf16[8,512]{1,0:T(8,128)(2,1)S(1)}, u32[]{:S(2)}, u32[]{:S(2)}) collective-permute-start(bf16[8,512]{1,0:T(8,128)(2,1)S(1)} %slice.423), channel_id=1, source_target_pairs={{0,3},{1,0},{2,1},{3,2},{4,7},{5,4},{6,5},{7,6},{8,11},{9,8},{10,9... | collective-permute-start | bytes 24584 | tf_op jit(solution)/shard_map/ppermute | solution.py:578
  785.6 19.8 %collective-permute-start.43 = (bf16[256,1536]{1,0:T(8,128)(2,1)}, bf16[256,1536]{1,0:T(8,128)(2,1)}, u32[]{:S(2)}, u32[]{:S(2)}) collective-permute-start(bf16[256,1536]{1,0:T(8,128)(2,1)} %get-tuple-element.178), channel_id=1, source_target_pairs={{0,16},{4,20},{8,24},{12,28},{16,0},{20,4},{24,8},{28,12},{1,17},{... | collective-permute-start | bytes 2359304 | tf_op jit(solution)/shard_map/ppermute | solution.py:435
  787.0 19.5 %collective-permute-start.42 = (bf16[256,1536]{1,0:T(8,128)(2,1)}, bf16[256,1536]{1,0:T(8,128)(2,1)}, u32[]{:S(2)}, u32[]{:S(2)}) collective-permute-start(bf16[256,1536]{1,0:T(8,128)(2,1)} %fusion.24), channel_id=1, source_target_pairs={{0,8},{4,12},{8,0},{12,4},{16,24},{20,28},{24,16},{28,20},{1,9},{5... | collective-permute-start | bytes 2359304 | tf_op jit(solution)/shard_map/ppermute | solution.py:435
  (96 other events, 1141.0 us)
Sparse Core Ops, SparseCore 0:
  10.9 100.7 all-gather.10
  113.8 44.2 all-gather.16
  212.3 46.0 all-gather.12
  281.7 46.2 all-gather.14
  330.0 44.6 all-gather.18
  376.8 42.5 reduce-scatter.11
  421.8 43.1 reduce-scatter.13
  467.4 42.8 reduce-scatter.7
  512.7 43.4 reduce-scatter.9
  559.8 25.5 reduce-scatter.19
  654.6 42.0 reduce-scatter.15
  741.4 42.2 reduce-scatter.17

commit v3 on v2

--- a/solution.py
+++ b/solution.py
@@ -435,57 +435,67 @@
     return lax.ppermute(value, "seq", [(i, i ^ bit) for i in range(8)])
 
 
-def place_kernel(spots, me_ref, *refs):
-    count = len(spots)
-    pieces, out_ref, held, sems = refs[:count], refs[count], refs[count + 1 : -1], refs[-1]
-    arrive = [pltpu.make_async_copy(pieces[i], held[i], sems.at[0, i]) for i in range(count)]
-    leave = [
-        pltpu.make_async_copy(held[i], out_ref.at[spots[i](me_ref[0])], sems.at[1, i])
-        for i in range(count)
-    ]
+def place_kernel(plan, count, me_ref, *refs):
+    pieces, whole, held, arrive_sem, leave_sem = refs[:count], refs[count], refs[count + 1 : -2], refs[-2], refs[-1]
+    arrive, leave = [], []
+    for n, (i, lanes, bits, there) in enumerate(plan):
+        rows = pieces[i].shape[0]
+        spot = pl.ds(pl.multiple_of((me_ref[0] ^ bits) * rows, 16), rows)
+        arrive.append(pltpu.make_async_copy(pieces[i].at[:, lanes], held[n], arrive_sem.at[n]))
+        leave.append(pltpu.make_async_copy(held[n], whole.at[spot, there], leave_sem.at[n]))
     for copy in arrive:
         copy.start()
-    for i in range(count):
-        arrive[i].wait()
-        leave[i].start()
+    for come, go in zip(arrive, leave):
+        come.wait()
+        go.start()
     for copy in leave:
         copy.wait()
 
 
-def place(me, pieces, spots, shape, name):
+def place(pieces, spans, start, width, name):
+    plan = []
+    for i, (bits, low) in enumerate(spans):
+        first, last = max(low, start), min(low + pieces[i].shape[1], start + width)
+        if first < last:
+            plan.append((i, pl.ds(first - low, last - first), bits, pl.ds(first - start, last - first)))
+    used = sorted({entry[0] for entry in plan})
+    plan = [(used.index(i), *entry) for i, *entry in plan]
+    pieces = [pieces[i] for i in used]
+    rows, count, dtype = pieces[0].shape[0], len(pieces), pieces[0].dtype
     anywhere = pl.BlockSpec(memory_space=pl.ANY)
-    moved = 4 * shape[0] * shape[1]
     return pl.pallas_call(
-        functools.partial(place_kernel, spots),
-        out_shape=jax.ShapeDtypeStruct(shape, pieces[0].dtype),
-        in_specs=[pl.BlockSpec(memory_space=pltpu.SMEM)] + [anywhere] * len(pieces),
+        functools.partial(place_kernel, plan, count),
+        out_shape=jax.ShapeDtypeStruct((8 * rows, width), dtype),
+        in_specs=[pl.BlockSpec(memory_space=pltpu.SMEM)] + [anywhere] * count,
         out_specs=anywhere,
-        scratch_shapes=[pltpu.VMEM(piece.shape, piece.dtype) for piece in pieces]
-        + [pltpu.SemaphoreType.DMA((2, len(pieces)))],
+        scratch_shapes=[pltpu.VMEM((rows, lanes.size), dtype) for _, lanes, _, _ in plan]
+        + [pltpu.SemaphoreType.DMA((len(plan),)) for _ in range(2)],
         compiler_params=pltpu.CompilerParams(vmem_limit_bytes=VMEM_LIMIT),
-        cost_estimate=pl.CostEstimate(flops=0, bytes_accessed=moved, transcendentals=0),
+        cost_estimate=pl.CostEstimate(flops=0, bytes_accessed=32 * rows * width, transcendentals=0),
         name=name,
-    )(me.astype(jnp.int32).reshape(1), *pieces)
-
-
-def rows_of(bits, rows):
-    return lambda me: pl.ds(pl.multiple_of((me ^ bits) * rows, 16), rows)
-
-
-def seq_links(block, relay):
+    )(lax.axis_index("seq").astype(jnp.int32).reshape(1), *pieces)
+
+
+def seq_links(block, half):
     if lax.axis_size("seq") != 8:
         return (block,)
     from_x, from_y = over(block, X), over(block, Y)
-    return block, from_x, from_y, over(from_x if relay == Y else from_y, relay)
-
-
-def seq_gather(blocks):
+    return block, from_x, from_y, over(from_x[:, :half], Y), over(from_y[:, half:], X)
+
+
+def seq_gather(blocks, widths, names):
+    starts = [sum(widths[:i]) for i in range(len(widths))]
     if lax.axis_size("seq") != 8:
-        return gather(blocks[0], "seq", 0)
-    rows, width = blocks[0].shape
-    others = [over(block, CORE) for block in blocks]
-    spots = [rows_of(bits + core, rows) for core in (0, CORE) for bits in (0, X, Y, X + Y)]
-    return place(lax.axis_index("seq"), [*blocks, *others], spots, (8 * rows, width), "place_rows")
+        whole = gather(blocks[0], "seq", 0)
+        return [whole[:, start : start + width] for start, width in zip(starts, widths)]
+    pieces = [*blocks, *[over(block, CORE) for block in blocks]]
+    half = blocks[3].shape[1]
+    spans = [
+        (bits + core, low)
+        for core in (0, CORE)
+        for bits, low in ((0, 0), (X, 0), (Y, 0), (X + Y, 0), (X + Y, half))
+    ]
+    return [place(pieces, spans, *cut) for cut in zip(starts, widths, names)]
 
 
 def plus(*terms):
@@ -495,54 +505,59 @@
     return total
 
 
-def half_kernel(micros, me_ref, *refs):
-    lefts, rights, out_ref = refs[:micros], refs[micros : 2 * micros], refs[-1]
+def halves_kernel(micros, core_ref, *refs):
+    lefts, rights, send_ref, keep_ref = refs[:micros], refs[micros : 2 * micros], refs[-2], refs[-1]
     total = None
     for left, right in zip(lefts, rights):
         part = lax.dot_general(left[...], right[...], (((0,), (0,)), ((), ())), preferred_element_type=F32)
         total = part if total is None else total + part
-    out_ref[...] = total.astype(BF)
-
-
-def grad_half(lefts, rights, own, name, after):
+
+    @pl.when(pl.program_id(0) < 4)
+    def _():
+        send_ref[...] = total.astype(BF)
+
+    @pl.when(pl.program_id(0) >= 4)
+    def _():
+        keep_ref[...] = total.astype(BF)
+
+
+def grad_halves(lefts, rights, name, after=()):
+    if lax.axis_size("seq") != 8:
+        return (dot(jnp.concatenate(lefts), jnp.concatenate(rights), ((0,), (0,))).astype(BF),)
     count, wide = lefts[0].shape
-    rows, width = wide // 8, rights[0].shape[1]
-    core = (lax.axis_index("seq") & CORE).astype(jnp.int32)
-    core = (core if own else 1 - core).reshape(1)
-    steps, pick = (8, lambda i, c: (0, i)) if own is None else (4, lambda i, c: (0, 2 * i + c[0]))
-    n = len(lefts)
+    rows, width, n = wide // 8, rights[0].shape[1], len(lefts)
+    core = (lax.axis_index("seq") & CORE).astype(jnp.int32).reshape(1)
     return pl.pallas_call(
-        functools.partial(half_kernel, n),
-        out_shape=jax.ShapeDtypeStruct((steps * rows, width), BF),
+        functools.partial(halves_kernel, n),
+        out_shape=[jax.ShapeDtypeStruct((wide // 2, width), BF)] * 2,
         grid_spec=pltpu.PrefetchScalarGridSpec(
             num_scalar_prefetch=1,
-            grid=(steps,),
-            in_specs=[pl.BlockSpec((count, rows), pick)] * n
+            grid=(8,),
+            in_specs=[
+                pl.BlockSpec((count, rows), lambda i, c: (0, 2 * (i % 4) + jnp.where(i < 4, 1 - c[0], c[0])))
+            ] * n
             + [pl.BlockSpec((count, width), lambda i, c: (0, 0))] * n
             + [pl.BlockSpec(memory_space=pl.ANY)] * len(after),
-            out_specs=pl.BlockSpec((rows, width), lambda i, c: (i, 0)),
+            out_specs=[
+                pl.BlockSpec((rows, width), lambda i, c: (jnp.minimum(i, 3), 0)),
+                pl.BlockSpec((rows, width), lambda i, c: (jnp.maximum(i, 4) - 4, 0)),
+            ],
         ),
         compiler_params=pltpu.CompilerParams(vmem_limit_bytes=VMEM_LIMIT),
         cost_estimate=pl.CostEstimate(
-            flops=2 * n * count * rows * steps * width,
-            bytes_accessed=n * count * (wide + 2 * width) + wide * width,
+            flops=2 * n * count * wide * width,
+            bytes_accessed=2 * n * count * (wide + width) + 2 * wide * width,
             transcendentals=0,
         ),
         name=name,
     )(core, *lefts, *rights, *after)
 
 
-def grad_halves(lefts, rights, name, after=()):
-    if lax.axis_size("seq") != 8:
-        return (dot(jnp.concatenate(lefts), jnp.concatenate(rights), ((0,), (0,))).astype(BF),)
-    return tuple(grad_half(lefts, rights, own, name, after) for own in (False, True))
-
-
-def grad_chip(halves):
+def grad_chip(halves, after=()):
     if len(halves) == 1:
         return halves[0]
     send, keep = halves
-    four = plus(keep, over(send, CORE)).astype(BF)
+    four = plus(keep, over(send, CORE), nothing_of(after)).astype(BF)
     return four.reshape(4, keep.shape[0] // 4, keep.shape[1])
 
 
@@ -550,26 +565,28 @@
     return lax.dynamic_index_in_dim(four, (lax.axis_index("seq") // 2) ^ (bits // 2), 0, keepdims=False)
 
 
-def grad_far(four, relay):
+def grad_far(four, relay, after=()):
     if four.ndim == 2:
         return four
-    return over(owner(four, X + Y), relay)
-
-
-def grad_own(four, far, relay):
+    return over(tied(owner(four, X + Y), *after), relay)
+
+
+def grad_turn(four, far, relay, after=()):
+    if four.ndim == 2:
+        return (four,)
+    nothing = nothing_of(after)
+    to_x, to_y = owner(four, X).astype(F32) + nothing, owner(four, Y).astype(F32) + nothing
+    if relay == Y:
+        to_x = plus(to_x, far)
+    else:
+        to_y = plus(to_y, far)
+    return to_x.astype(BF), to_y.astype(BF)
+
+
+def grad_own(four, turn, after=()):
     if four.ndim == 2:
         return scatter(four, "seq", 0).astype(F32)
-    to_x, to_y = owner(four, X), owner(four, Y)
-    if relay == Y:
-        to_x = plus(to_x, far).astype(BF)
-    else:
-        to_y = plus(to_y, far).astype(BF)
-    return plus(owner(four, 0), over(to_x, X), over(to_y, Y))
-
-
-def grad_sum(halves, relay):
-    four = grad_chip(halves)
-    return grad_own(four, grad_far(four, relay), relay)
+    return plus(owner(four, 0), over(turn[0], X), over(turn[1], Y), nothing_of(after))
 
 
 def tp_sum(block):
@@ -580,11 +597,12 @@
     ])
 
 
+def nothing_of(others):
+    return sum([other[(0,) * other.ndim].astype(F32) * 0.0 for other in others], jnp.zeros((), F32))
+
+
 def tied(value, *others):
-    if not others:
-        return value
-    nothing = sum(other[(0,) * other.ndim].astype(F32) * 0.0 for other in others)
-    return value + nothing.astype(value.dtype)
+    return value + nothing_of(others).astype(value.dtype) if others else value
 
 
 def dot(a, b, dims):
@@ -601,13 +619,13 @@
     joint = gather(joint, "tp", 1)
     x_full = joint[: micros * count].reshape(micros, count, -1)
     out_lanes = joint[micros * count :]
-    in_links = seq_links(w_in.reshape(w_in.shape[0], -1), Y)
-    gu_links = seq_links(tied(w_gu.reshape(w_gu.shape[0], -1), *in_links[1:2]), X)
-    down_links = seq_links(tied(w_down.T, gu_links[-1]), Y)
-    in_full, gu_full, down_full = seq_gather(in_links), seq_gather(gu_links), seq_gather(down_links)
+    rows_in = w_in.shape[0]
+    first_links = seq_links(jnp.concatenate([w_in.reshape(rows_in, -1), w_gu.reshape(rows_in, -1)], axis=1), 3 * width)
+    in_full, gu_full = seq_gather(first_links, (3 * width, 2 * hidden), ("place_in", "place_gu"))
     cot_full = [gather(cotangent[0], "tp", 1)]
-    out_links = seq_links(out_lanes, X)
-    out_full = seq_gather(out_links)
+    down_full = gather(tied(w_down.T, *first_links[-2:]), "seq", 0)
+    out_links = seq_links(out_lanes, out_lanes.shape[1] // 2)
+    (out_full,) = seq_gather(out_links, (n_tp * width,), ("place_out",))
 
     rate = jnp.exp(log_rate)
     lam_real, lam_imag = polar(1.0, rate, pole_angle)
@@ -620,7 +638,7 @@
     edges = jnp.arange(n_seq + 1) * count
     seq_shape = (count * SUB, LANE)
     st_shape = lam.shape
-    work = lam.shape[0] * SUB * LANE * count
+    work = 400 * lam.shape[0] * SUB * LANE * count
 
     position = me * count + jnp.arange(-2, count + 1)
     seg = jnp.stack([segment_number(position, lengths[m]) for m in range(micros)])
@@ -634,7 +652,7 @@
 
     x_wide = x_full.astype(F32)
     scale_in = norm_scale(x_wide)
-    h_in = (x_wide * scale_in * tied(gain_in, gu_full)).astype(BF)
+    h_in = (x_wide * scale_in * gain_in).astype(BF)
     z_low = dot(h_in, in_full, ((2,), (0,))).astype(BF)
     rims = lax.ppermute(z_low[:, count - 2 :], "seq", [(i, i + 1) for i in range(n_seq - 1)])
     rims = jnp.pad(rims.astype(F32), ((0, 0), (SUB - 2, 0), (0, 0)))
@@ -650,7 +668,7 @@
              [zs], 2, "mixer_front", 4 * work)
         for m in range(micros)
     ])
-    ends = lax.all_gather(jnp.stack(ends).astype(BF), "seq").astype(F32)
+    ends = lax.all_gather(tied(jnp.stack(ends), *out_links[1:3]).astype(BF), "seq").astype(F32)
 
     kept = []
     outputs = []
@@ -659,16 +677,17 @@
             functools.partial(finish_kernel, m),
             (*masks[m], spans[m], me_word, *bases[m], lam_all, res, skip, injects[m], ends),
             [((count, width), BF), ((count, width), F32), ((count // SPAN, *st_shape), F32)],
-            [zs, (seq_shape, F32), (st_shape, F32)], 4, "mixer_finish", 6 * work,
-            (out_links[-1], *down_links[1:3]) if m else (*cot_full, *out_links[1:3]),
+            [zs, (seq_shape, F32), (st_shape, F32)], 4, "mixer_finish", 5 * work,
+            (kept[0]["mixed"], down_full) if m else cot_full,
         )
         kept.append(dict(mixed=mixed, conv=conv_out, marks=marks))
 
+    order = ()
     for m in range(micros):
         mixed_full = gather(kept[m]["mixed"], "tp", 1)
         if m + 1 < micros:
             cot_full.append(gather(tied(cotangent[m + 1], mixed_full), "tp", 1))
-        x_mid = x_full[m].astype(F32) + dot(mixed_full, out_full, ((1,), (1,)))
+        x_mid = tied(x_full[m].astype(F32), *order) + dot(mixed_full, out_full, ((1,), (1,)))
         scale_mid = norm_scale(x_mid)
         h_mlp = (x_mid * scale_mid * gain_mlp[None]).astype(BF)
         gate_up = dot(h_mlp, gu_full, ((1,), (0,)))
@@ -677,7 +696,7 @@
         act = (gate * sig * up).astype(BF)
         down_own = scatter(dot(act, down_full, ((1,), (1,))).astype(BF), "tp", 1)
         mid_own = lax.dynamic_slice_in_dim(x_mid, lax.axis_index("tp") * width, width, 1)
-        outputs.append((mid_own + down_own.astype(F32)).astype(BF))
+        outputs.append((mid_own, down_own))
 
         cot = cot_full[m]
         d_act = dot(cot, down_full, ((1,), (0,)))
@@ -688,7 +707,9 @@
         d_norm, d_gain_mlp = norm_back(x_mid, scale_mid, gain_mlp, d_h)
         d_mid = d_norm + cot.astype(F32) * (1.0 / n_tp)
         d_low = d_mid.astype(BF)
-        d_mixed = scatter(dot(d_low, out_full, ((1,), (0,))).astype(BF), "tp", 1)
+        d_mixed = dot(d_low, out_full, ((1,), (0,))).astype(BF)
+        order = (d_mixed,)
+        d_mixed = scatter(d_mixed, "tp", 1)
         kept[m].update(
             mixed=mixed_full, h_mlp=h_mlp, act=act, d_gu=d_gu, d_mid=d_mid, d_low=d_low,
             d_mixed=d_mixed, d_gain_mlp=d_gain_mlp,
@@ -697,21 +718,23 @@
     def each(name):
         return [c[name] for c in kept]
 
-    down_halves = grad_halves(cot_full, each("act"), "grad_down")
-    out_halves = grad_halves(each("d_low"), each("mixed"), "grad_out")
-    g_down = grad_sum(down_halves, Y)
-    g_out = scatter(grad_sum(out_halves, X).astype(BF), "tp", 1)
+    down_halves = grad_halves(cot_full, each("act"), "grad_down", order)
+    out_halves = grad_halves(each("d_low"), each("mixed"), "grad_out", order)
+    down_chip, out_chip = grad_chip(down_halves), grad_chip(out_halves)
+    down_far, out_far = grad_far(down_chip, Y), grad_far(out_chip, X)
     adjoints, ends = zip(*[
         call(adjoint_kernel, (*masks[m], *bases[m], kept[m]["d_mixed"]),
              [(seq_shape, F32), (st_shape, F32)], [zs], 2, "mixer_adjoint", 4 * work,
-             (*down_halves, *out_halves))
+             (down_chip, out_chip) if m else (*down_halves, *out_halves))
         for m in range(micros)
     ])
-    ends = lax.all_gather(jnp.stack(ends).astype(BF), "seq").astype(F32)
+    ends = lax.all_gather(tied(jnp.stack(ends), down_far, out_far).astype(BF), "seq").astype(F32)
     gu_halves = grad_halves(each("h_mlp"), each("d_gu"), "grad_gu", (ends,))
     gu_chip = grad_chip(gu_halves)
     gu_far = grad_far(gu_chip, X)
-    g_gu = grad_own(gu_chip, gu_far, X)
+    down_turn = grad_turn(down_chip, down_far, Y, (ends,))
+    g_out = grad_own(out_chip, grad_turn(out_chip, out_far, X, (ends,)))
+    g_out = scatter(tied(g_out, *gu_halves).astype(BF), "tp", 1)
 
     token_grads = []
     partial_grads = []
@@ -726,9 +749,13 @@
              ((9 * SUB, width), F32), ((SUB, width), F32), (st_shape, F32), (st_shape, F32)],
             [zs, ((count + SUB, 3 * width), F32), (seq_shape, F32),
              (((SPAN + 1) * st_shape[0] * SUB, LANE), F32), (st_shape, F32)],
-            4, "mixer_back", 16 * work, (*partial_grads, g_down, gu_far) if m else (*gu_halves, gu_chip),
+            4, "mixer_back", 12 * work, (*partial_grads, *gu_turn) if m else (*gu_halves, gu_chip),
         )
         rim_back = lax.ppermute(rim_back[:2], "seq", [(i + 1, i) for i in range(n_seq - 1)])
+        if m == 0:
+            gu_turn = grad_turn(gu_chip, gu_far, X, (rim_back,))
+            g_gu = grad_own(gu_chip, gu_turn)
+        tail = tied(tail, g_gu if m else gu_far)
         tail = (tail + jnp.concatenate([jnp.zeros((ROWS - 2, 3 * width), F32), rim_back])).astype(BF)
         d_z = lax.dynamic_update_slice(d_z, tail, (count - ROWS, 0))
         c["d_z"] = d_z
@@ -738,31 +765,38 @@
             gain = tied(gain_in, in_halves[0])
         d_h_in = dot(d_z, in_full, ((1,), (1,)))
         d_norm, d_gain_in = norm_back(x_full[m].astype(F32), scale_in[m], gain, d_h_in)
+        gains = [d_gain_in, c["d_gain_mlp"]] if m == 0 else [gains[0] + d_gain_in, gains[1] + c["d_gain_mlp"]]
+        if m == micros - 1:
+            gains = tp_sum(jnp.concatenate(gains).reshape(-1, width).astype(BF))
+            d_norm = tied(d_norm, gains)
         partial_grads.append((c["d_mid"] + d_norm).astype(BF))
         token_grads.append(scatter(partial_grads[m], "tp", 1))
-        g_real, g_imag = unpacked(d_lam, log_rate.shape)
-        s_real, s_imag = unpacked(d_res, log_rate.shape)
-        h_real = residues[0] * g_real + residues[1] * g_imag
-        h_imag = residues[0] * g_imag - residues[1] * g_real
-        smalls.append(jnp.concatenate([
-            jnp.sum(d_taps.reshape(9, SUB, width), axis=1),
-            -rate * (lam_real * h_real + lam_imag * h_imag),
-            lam_real * h_imag - lam_imag * h_real,
-            s_real, -s_imag,
-            jnp.sum(d_skip, axis=0, keepdims=True),
-            d_gain_in.reshape(-1, width), c["d_gain_mlp"].reshape(-1, width),
-        ]))
-
-    g_in = grad_sum(in_halves, Y)
-    n_gain = 2 * (gain_in.shape[0] // width)
-    small = sum(smalls)
-    gains = tp_sum(small[-n_gain:].astype(BF))
-    small = jnp.sum(lax.all_gather(tied(small[:-n_gain], partial_grads[-1]).astype(BF), "seq").astype(F32), axis=0)
-    gains = jnp.sum(lax.all_gather(tied(gains, g_in).astype(BF), "seq").astype(F32), axis=0)
+        smalls.append((d_taps, d_lam, d_res, d_skip))
+
+    in_chip = grad_chip(in_halves)
+    d_taps, d_lam, d_res, d_skip = (sum(parts) for parts in zip(*smalls))
+    g_real, g_imag = unpacked(d_lam, log_rate.shape)
+    s_real, s_imag = unpacked(d_res, log_rate.shape)
+    h_real = residues[0] * g_real + residues[1] * g_imag
+    h_imag = residues[0] * g_imag - residues[1] * g_real
+    small = jnp.concatenate([
+        jnp.sum(d_taps.reshape(9, SUB, width), axis=1),
+        -rate * (lam_real * h_real + lam_imag * h_imag),
+        lam_real * h_imag - lam_imag * h_real,
+        s_real, -s_imag,
+        jnp.sum(d_skip, axis=0, keepdims=True),
+        gains,
+    ])
+    small = jnp.sum(lax.all_gather(small.astype(BF), "seq").astype(F32), axis=0)
+    in_far = grad_far(in_chip, Y, (small,))
+    g_in = grad_own(in_chip, grad_turn(in_chip, in_far, Y, (small,)))
+    g_down = grad_own(down_chip, down_turn, (in_far,))
+    gains = small[-gains.shape[0] :]
+    n_gain = gains.shape[0]
     n_pole = log_rate.shape[0]
     cuts = [9, 9 + n_pole, 9 + 2 * n_pole, 9 + 3 * n_pole, 9 + 4 * n_pole]
     return (
-        jnp.stack(outputs),
+        jnp.stack([(mid + tied(down.astype(F32), in_far)).astype(BF) for mid, down in outputs]),
         jnp.stack(token_grads),
         gains[: n_gain // 2].reshape(-1),
         g_in.reshape(w_in.shape),
@@ -771,9 +805,9 @@
         small[cuts[1] : cuts[2]],
         small[cuts[2] : cuts[4]].reshape(residues.shape),
         small[cuts[4]],
-        g_out.T.astype(F32),
+        tied(g_out.astype(F32), in_far).T,
         gains[n_gain // 2 :].reshape(-1),
-        g_gu.reshape(w_gu.shape),
+        tied(g_gu, in_far).reshape(w_gu.shape),
         g_down.T,
     )
 

time: 842 us -> 786 us (0.933)
  waiting for transfers between devices: 181 us -> 122 us
  Pallas kernels: 244 us -> 229 us
  blocking collectives: 43.4 us -> 33.2 us
  other arithmetic: 94.9 us -> 105 us
  matrix products: 124 us -> 133 us
    ppermute x44 -> x34, waiting for transfers between devices: 164 us -> 108 us  [over(): return lax.ppermute(value, 'seq', [(i, i ^ bit) for i in range(8)])]
    pallas_call x12 -> x7, Pallas kernels: 96.5 us -> 81.5 us  [the longest x4 60.4 us: grad_halves(): pl.pallas_call(functools.partial(halves_kernel, n), out_shape=[jax.ShapeD...]
    slice x8 -> x22, local copies, waits for them, and re-layouts: 7.6 us -> 19.4 us  [the longest x18 14.7 us: nothing_of(): other[(0,) * other.ndim].astype(F32) * 0.0]
    reduce_scatter x7, starting transfers between devices: 0.29 us -> 11.2 us  [scatter(): return lax.psum_scatter(block, axis, scatter_dimension=dim, tiled=True)]
    all_gather x4 -> x3, blocking collectives: 43.4 us -> 33.2 us  [the longest x1 14.8 us: shards(): lax.all_gather(tied(jnp.stack(ends), *out_links[1:3]).astype(BF), 'seq')]
    all_gather x5 -> x6, waiting for transfers between devices: 15.5 us -> 5.71 us  [gather(): return lax.all_gather(block, axis, axis=dim, tiled=True)]
    dot_general x15, matrix products: 124 us -> 133 us  [dot(): return lax.dot_general(a, b, (dims, ((), ())), preferred_element_type=F32)]
    ppermute x44 -> x34, starting transfers between devices: 36.5 us -> 28.8 us  [over(): return lax.ppermute(value, 'seq', [(i, i ^ bit) for i in range(8)])]
  transfers between devices with their start and end apart: 62 -> 53, of which waited for: 20 -> 13; matrix products, arithmetic and copies ran while one was open for 33% -> 36% of each run, Pallas kernels for 23% -> 30%
where the time goes in v3:
time: 786 us; the launch traced here: 776 us
  Pallas kernels  229 us (29%)
  matrix products  133 us (17%)
  waiting for transfers between devices  122 us (16%)
  other arithmetic  105 us (13%)
  local copies, waits for them, and re-layouts  75 us (10%)
  starting transfers between devices  51 us (6%)
  blocking collectives  33.2 us (4%)
  between operations  27.5 us (3%)
    pallas_call x8, Pallas kernels, call(): pl.pallas_call(without, out_shape=[jax.ShapeDtypeStruct(s, d) for s, d in...  148 us
    dot_general x15, matrix products, dot(): return lax.dot_general(a, b, (dims, ((), ())), preferred_element_type=F32)  133 us
    ppermute x34, waiting for transfers between devices, over(): return lax.ppermute(value, 'seq', [(i, i ^ bit) for i in range(8)])  108 us
    pallas_call x4, Pallas kernels, grad_halves(): pl.pallas_call(functools.partial(halves_kernel, n), out_shape=[jax.ShapeD...  60.4 us
    ppermute x34, starting transfers between devices, over(): return lax.ppermute(value, 'seq', [(i, i ^ bit) for i in range(8)])  28.8 us
    unnamed x171, local copies, waits for them, and re-layouts  27.5 us
    pallas_call x3, Pallas kernels, place(): pl.pallas_call(functools.partial(place_kernel, plan, count), out_shape=ja...  21.1 us
    convert_element_type x4, other arithmetic, grad_chip(): four = plus(keep, over(send, CORE), nothing_of(after)).astype(BF)  18.8 us
  transfers between devices with their start and end apart: 53, of which 13 were waited for; matrix products, arithmetic and copies ran while one was open for 36% of the time, Pallas kernels for 30%

profile of v3, /device:TPU:0, one launch (start us, length us, event | category | flops | bytes accessed | tf_op | source)
XLA Modules:
  0.0 775.7 jit_solution(15734748347729129343)
XLA Ops:
  12.5 3.0 collective-permute-start.1
  18.6 45.4 %collective-permute-done.1.refs_2_ = bf16[256,4352]{1,0:T(8,128)(2,1)} collective-permute-done((bf16[256,4352]{1,0:T(8,128)(2,1)S(1)}, bf16[256,4352]{1,0:T(8,128)(2,1)}, u32[]{:S(2)}, u32[]{:S(2)}) %collective-permute-start.1) | collective-permute-done | bytes 2228256 | tf_op jit(solution)/shard_map/ppermute | solution.py:435
  64.1 2.6 slice.356
  74.5 14.7 %collective-permute-done.2.refs_3_ = bf16[256,1536]{1,0:T(8,128)(2,1)} collective-permute-done((bf16[256,1536]{1,0:T(8,128)(2,1)}, bf16[256,1536]{1,0:T(8,128)(2,1)}, u32[]{:S(2)}, u32[]{:S(2)}) %collective-permute-start.2) | collective-permute-done | bytes 786464 | tf_op jit(solution)/shard_map/ppermute | solution.py:435
  90.4 9.3 %collective-permute-done.17.refs_3_ = bf16[256,2816]{1,0:T(8,128)(2,1)} collective-permute-done((bf16[256,2816]{1,0:T(8,128)(2,1)}, bf16[256,2816]{1,0:T(8,128)(2,1)}, u32[]{:S(2)}, u32[]{:S(2)}) %collective-permute-start.17) | collective-permute-done | bytes 1441824 | tf_op jit(solution)/shard_map/ppermute | solution.py:435
  108.4 5.5 place_in.1
  118.3 3.3 multiply_reduce_fusion
  121.7 3.4 slice_convert_fusion
  126.7 6.9 fusion.18
  138.1 11.9 %mixer_front.2 = (f32[4096,128]{1,0:T(8,128)}, f32[16,8,128]{2,1,0:T(8,128)}) custom-call(f32[520]{0:T(1024)} %get-tuple-element.158.refs_0_, s32[65]{0:T(128)} %get-tuple-element.212.refs_1_, bf16[512,1536]{1,0:T(8,128)(2,1)} %get-tuple-element.186.refs_2_.refs_4_, f32[8,1536]{1,0:T(8,128)} %get-tuple-element.194.refs_3_.refs_5_, ...), custom_call_target="tpu_custom_call" | custom-call | flops 13421772800 | bytes 3887652 | tf_op jit(solution)/shard_map/mixer_front/pallas_call | solution.py:376
  150.0 12.1 %mixer_front.3 = (f32[4096,128]{1,0:T(8,128)}, f32[16,8,128]{2,1,0:T(8,128)}) custom-call(f32[520]{0:T(1024)} %get-tuple-element.159.refs_0_, s32[65]{0:T(128)} %get-tuple-element.213.refs_1_, bf16[512,1536]{1,0:T(8,128)(2,1)} %get-tuple-element.187.refs_2_.refs_4_, f32[8,1536]{1,0:T(8,128)} %get-tuple-element.195.refs_3_.refs_5_, ...), custom_call_target="tpu_custom_call" | custom-call | flops 13421772800 | bytes 3887652 | tf_op jit(solution)/shard_map/mixer_front/pallas_call | solution.py:376
  165.3 14.8 %all_gather.31 = bf16[8,2,16,8,128]{4,3,2,1,0:T(8,128)(2,1)S(1)} all-gather(bf16[1,2,16,8,128]{4,3,2,1,0:T(8,128)(2,1)S(1)} %fusion.41), channel_id=1, replica_groups=mesh['seq'=8,'tp'=4] {'seq'}, dimensions={0}, use_global_device_ids=true | all-gather | bytes 589824 | tf_op jit(solution)/shard_map/all_gather | solution.py:671
  181.2 16.0 %mixer_finish.2 = (bf16[512,512]{1,0:T(8,128)(2,1)}, f32[512,512]{1,0:T(8,128)}, f32[8,16,8,128]{3,2,1,0:T(8,128)}) custom-call(f32[520]{0:T(1024)} %get-tuple-element.158.refs_0_, s32[65]{0:T(128)} %get-tuple-element.212.refs_1_, f32[8]{0:T(128)} %compare_convert_fusion.4.refs_2_, s32[1]{0:T(128)} %bitcast.5.me_ref.refs_3_, ...), custom_call_target="tpu_custom_call" | custom-call | flops 16777216000 | bytes 7101000 | tf_op jit(solution)/shard_map/mixer_finish/pallas_call | solution.py:376
  198.2 5.6 all-gather.13.cloned.1.call-done.refs_15_
  203.8 16.2 %mixer_finish.3 = (bf16[512,512]{1,0:T(8,128)(2,1)}, f32[512,512]{1,0:T(8,128)}, f32[8,16,8,128]{3,2,1,0:T(8,128)}) custom-call(f32[520]{0:T(1024)} %get-tuple-element.159.refs_0_, s32[65]{0:T(128)} %get-tuple-element.213.refs_1_, f32[8]{0:T(128)} %compare_convert_fusion.2.refs_2_, s32[1]{0:T(128)} %bitcast.5.me_ref.refs_3_, ...), custom_call_target="tpu_custom_call" | custom-call | flops 16777216000 | bytes 7101000 | tf_op jit(solution)/shard_map/mixer_finish/pallas_call | solution.py:376
  223.6 11.5 %collective-permute-done.11.refs_4_ = bf16[256,1024]{1,0:T(8,128)(2,1)} collective-permute-done((bf16[256,1024]{1,0:T(8,128)(2,1)S(1)}, bf16[256,1024]{1,0:T(8,128)(2,1)}, u32[]{:S(2)}, u32[]{:S(2)}) %collective-permute-start.11) | collective-permute-done | bytes 524320 | tf_op jit(solution)/shard_map/ppermute | solution.py:435
  236.9 9.1 %place_gu.1 = bf16[2048,2816]{1,0:T(8,128)(2,1)} custom-call(s32[1]{0:T(128)} %bitcast.5.me_ref.refs_3_, bf16[256,4352]{1,0:T(8,128)(2,1)} %copy-done.3, bf16[256,4352]{1,0:T(8,128)(2,1)} %collective-permute-done.refs_1_, bf16[256,4352]{1,0:T(8,128)(2,1)} %collective-permute-done.1.refs_2_, bf16[256,2816]{1,0:T(8,128)(2,1)} %collective-permute-done.17.refs_3_, ...), custom_call_target="tpu_custom_call" | custom-call | bytes 23068672 | tf_op jit(solution)/shard_map/place_gu/pallas_call | solution.py:466
  246.1 6.5 place_out.1
  254.5 11.5 %multiply_reduce_fusion.6 = (f32[512]{0:T(512)S(1)}, f32[512,2048]{1,0:T(8,128)}) fusion(bf16[512,2048]{1,0:T(8,128)(2,1)} %all-gather.11.cloned.1.call-done.refs_2_, bf16[2048,2048]{1,0:T(8,128)(2,1)} %place_out.1, bf16[1280,2048]{1,0:T(8,128)(2,1)} %all-gather.9.cloned.1.call-done), kind=kOutput, calls=%fused_computation.42 | convolution fusion | flops 4299161088 | bytes 16779264 | tf_op jit(solution)/shard_map/dot_general | solution.py:609
  267.5 2.8 multiply_convert_fusion.2.refs_0_
  271.8 9.7 %fusion.74 = f32[512,2816]{1,0:T(8,128)S(1)} fusion(bf16[512,2048]{1,0:T(8,128)(2,1)S(1)} %multiply_convert_fusion.2.refs_0_, bf16[2048,2816]{1,0:T(8,128)(2,1)} %place_gu.1), kind=kOutput, calls=%fused_computation.221 | convolution fusion | flops 5905580032 | bytes 19398656 | tf_op jit(solution)/shard_map/dot_general | solution.py:609
  281.6 5.9 multiply_convert_fusion.7
  287.5 10.1 %multiply_reduce_fusion.2 = (f32[2048]{0:T(1024)}, f32[512]{0:T(512)}, f32[512,2048]{1,0:T(8,128)}) fusion(f32[512,2048]{1,0:T(8,128)S(1)} %copy-done, f32[512]{0:T(512)S(1)} %get-tuple-element.211, f32[2048]{0:T(1024)S(1)} %copy-done.39, bf16[2048,2816]{1,0:T(8,128)(2,1)S(1)} %bitcast.219, bf16[512,1408]{1,0:T(8,128)(2,1)} %get-tuple-element.181, ...), kind=kOutput, calls=%fused_computation.34 | convolution fusion | flops 5917636096 | bytes 22827008 | tf_op jit(solution)/shard_map/dot_general | solution.py:609
  298.3 4.6 fusion.67
  304.2 8.6 %convolution_convert_fusion.1 = bf16[512,2048]{1,0:T(8,128)(2,1)S(1)} fusion(bf16[512,2048]{1,0:T(8,128)(2,1)S(1)} %get-tuple-element.173.refs_0_, bf16[2048,2048]{1,0:T(8,128)(2,1)} %place_out.1), kind=kOutput, calls=%fused_computation.46 | convolution fusion | flops 4296015872 | bytes 12582912 | tf_op jit(solution)/shard_map/dot_general | solution.py:609
  314.2 11.0 %reduce-scatter.12.cloned.1.call-start = ((), (), s32[]{:S(2)}) async-start(), calls=%async_computation.13 | async-start | bytes 2621440 | tf_op jit(solution)/shard_map/reduce_scatter | solution.py:428
  325.2 9.3 %multiply_reduce_fusion.4 = (f32[512]{0:T(512)S(1)}, f32[512,2048]{1,0:T(8,128)S(1)}) fusion(bf16[512,2048]{1,0:T(8,128)(2,1)} %all-gather.15.cloned.1.call-done.refs_3_, bf16[2048,2048]{1,0:T(8,128)(2,1)} %place_out.1, f32[]{:T(128)} %bitcast.32, bf16[1280,2048]{1,0:T(8,128)(2,1)} %all-gather.9.cloned.1.call-done), kind=kOutput, calls=%fused_computation.38 | convolution fusion | flops 4300209664 | bytes 16779268 | tf_op jit(solution)/shard_map/dot_general | solution.py:609
  337.8 11.1 %fusion.75 = f32[512,2816]{1,0:T(8,128)} fusion(bf16[512,2048]{1,0:T(8,128)(2,1)S(1)} %multiply_convert_fusion.1.refs_1_, bf16[2048,2816]{1,0:T(8,128)(2,1)} %place_gu.1), kind=kOutput, calls=%fused_computation.222 | convolution fusion | flops 5905580032 | bytes 19398656 | tf_op jit(solution)/shard_map/dot_general | solution.py:609
  348.9 11.8 %multiply_convert_fusion.4 = (bf16[512,1408]{1,0:T(8,128)(2,1)}, bf16[512,1408]{1,0:T(8,128)(2,1)}, bf16[512,1408]{1,0:T(8,128)(2,1)}) fusion(f32[512,2816]{1,0:T(8,128)} %fusion.75, bf16[2048,1408]{1,0:T(8,128)(2,1)} %all-gather.13.cloned.1.call-done.refs_15_, bf16[1,512,2048]{2,1,0:T(8,128)(2,1)} %all-gather.19.cloned.1.call-done), kind=kOutput, calls=%fused_computation.57 | convolution fusion | flops 2964324352 | bytes 17956864 | tf_op jit(solution)/shard_map/dot_general | solution.py:609
  360.7 10.5 %multiply_reduce_fusion.1 = (f32[2048]{0:T(1024)S(1)}, f32[512]{0:T(512)S(1)}, f32[512,2048]{1,0:T(8,128)S(1)}) fusion(f32[512,2048]{1,0:T(8,128)S(1)} %copy-done.2, f32[512]{0:T(512)S(1)} %get-tuple-element.209, f32[2048]{0:T(1024)S(1)} %copy-done.39, bf16[2048,2816]{1,0:T(8,128)(2,1)} %place_gu.1, bf16[512,1408]{1,0:T(8,128)(2,1)} %get-tuple-element.179, ...), kind=kOutput, calls=%fused_computation.33 | convolution fusion | flops 5917636096 | bytes 22827008 | tf_op jit(solution)/shard_map/dot_general | solution.py:609
  371.2 4.3 fusion.66
  376.8 5.7 convolution_convert_fusion.refs_4_
  382.5 12.5 %grad_down.1 = (bf16[1024,1408]{1,0:T(8,128)(2,1)}, bf16[1024,1408]{1,0:T(8,128)(2,1)}) custom-call(s32[1]{0:T(128)} %bitcast.26.core_ref, bf16[512,2048]{1,0:T(8,128)(2,1)} %bitcast.233, bf16[512,2048]{1,0:T(8,128)(2,1)} %bitcast.234, bf16[512,1408]{1,0:T(8,128)(2,1)} %get-tuple-element.183.refs_2_, bf16[512,1408]{1,0:T(8,128)(2,1)} %get-tuple-element.182.refs_3_, ...), custom_call_target="tpu_custom_call" | custom-call | flops 5905580032 | bytes 12845056 | tf_op jit(solution)/shard_map/grad_down/pallas_call | solution.py:530
  395.6 15.4 %grad_out.1 = (bf16[1024,2048]{1,0:T(8,128)(2,1)}, bf16[1024,2048]{1,0:T(8,128)(2,1)}) custom-call(s32[1]{0:T(128)} %bitcast.26.core_ref, bf16[512,2048]{1,0:T(8,128)(2,1)} %copy-done.21, bf16[512,2048]{1,0:T(8,128)(2,1)} %copy-done.22, bf16[512,2048]{1,0:T(8,128)(2,1)} %all-gather.11.cloned.1.call-done.refs_2_, ...), custom_call_target="tpu_custom_call" | custom-call | flops 8589934592 | bytes 16777216 | tf_op jit(solution)/shard_map/grad_out/pallas_call | solution.py:530
  411.1 3.7 pad_maximum_fusion.refs_2_
  422.0 11.9 %mixer_adjoint.2 = (f32[4096,128]{1,0:T(8,128)}, f32[16,8,128]{2,1,0:T(8,128)}) custom-call(f32[520]{0:T(1024)} %get-tuple-element.158.refs_0_, s32[65]{0:T(128)} %get-tuple-element.212.refs_1_, bf16[512,1536]{1,0:T(8,128)(2,1)} %get-tuple-element.186.refs_2_.refs_4_, f32[8,1536]{1,0:T(8,128)} %get-tuple-element.194.refs_3_.refs_5_, ...), custom_call_target="tpu_custom_call" | custom-call | flops 13421772800 | bytes 4411940 | tf_op jit(solution)/shard_map/mixer_adjoint/pallas_call | solution.py:376
  434.0 6.7 collective-permute-done.21
  441.9 4.1 add_convert_fusion.1
  448.3 5.7 reduce-scatter.12.cloned.1.call-done.refs_7_.refs_14_
  454.0 12.0 %mixer_adjoint.3 = (f32[4096,128]{1,0:T(8,128)}, f32[16,8,128]{2,1,0:T(8,128)}) custom-call(f32[520]{0:T(1024)} %get-tuple-element.159.refs_0_, s32[65]{0:T(128)} %get-tuple-element.213.refs_1_, bf16[512,1536]{1,0:T(8,128)(2,1)} %get-tuple-element.187.refs_2_.refs_4_, f32[8,1536]{1,0:T(8,128)} %get-tuple-element.195.refs_3_.refs_5_, ...), custom_call_target="tpu_custom_call" | custom-call | flops 13421772800 | bytes 4411940 | tf_op jit(solution)/shard_map/mixer_adjoint/pallas_call | solution.py:376
  466.1 7.1 collective-permute-done.22
  475.8 8.7 %all_gather.37 = bf16[8,2,16,8,128]{4,3,2,1,0:T(8,128)(2,1)S(1)} all-gather(bf16[1,2,16,8,128]{4,3,2,1,0:T(8,128)(2,1)S(1)} %fusion.42), channel_id=1, replica_groups=mesh['seq'=8,'tp'=4] {'seq'}, dimensions={0}, use_global_device_ids=true | all-gather | bytes 589824 | tf_op jit(solution)/shard_map/all_gather | solution.py:731
  490.4 19.5 %grad_gu.1 = (bf16[1024,2816]{1,0:T(8,128)(2,1)}, bf16[1024,2816]{1,0:T(8,128)(2,1)}) custom-call(s32[1]{0:T(128)} %bitcast.26.core_ref, bf16[512,2048]{1,0:T(8,128)(2,1)} %copy-done.19, bf16[512,2048]{1,0:T(8,128)(2,1)} %copy-done.20, bf16[512,2816]{1,0:T(8,128)(2,1)} %pad_maximum_fusion.refs_2_, bf16[512,2816]{1,0:T(8,128)(2,1)} %pad_maximum_fusion.1.refs_3_, ...), custom_call_target="tpu_custom_call" | custom-call | flops 11811160064 | bytes 21495808 | tf_op jit(solution)/shard_map/grad_gu/pallas_call | solution.py:530
  517.0 7.3 convolution_convert_fusion.2
  525.6 5.1 slice_bitcast_fusion
  530.7 7.8 %convolution_convert_fusion.3 = bf16[512,2048]{1,0:T(8,128)(2,1)} fusion(bf16[512,1408]{1,0:T(8,128)(2,1)S(1)} %copy-done.66, bf16[2048,1408]{1,0:T(8,128)(2,1)} %all-gather.13.cloned.1.call-done.refs_15_), kind=kOutput, calls=%fused_computation.48 | convolution fusion | flops 2953838592 | bytes 9306112 | tf_op jit(solution)/shard_map/dot_general | solution.py:609
  538.6 8.4 %add_convert_fusion = bf16[1024,2816]{1,0:T(8,128)(2,1)} fusion(bf16[1024,2816]{1,0:T(8,128)(2,1)} %collective-permute-done.23, bf16[1024,2816]{1,0:T(8,128)(2,1)} %get-tuple-element.65.refs_19_), kind=kLoop, calls=%fused_computation | loop fusion | flops 11534336 | bytes 17301504 | tf_op jit(solution)/shard_map/convert_element_type | solution.py:560
  547.0 2.6 dynamic-slice_bitcast_fusion
  549.8 33.9 %mixer_back.2 = (bf16[512,1536]{1,0:T(8,128)(2,1)}, f32[8,1536]{1,0:T(8,128)}, f32[16,1536]{1,0:T(8,128)}, f32[72,512]{1,0:T(8,128)}, f32[8,512]{1,0:T(8,128)}, ...) custom-call(f32[520]{0:T(1024)} %get-tuple-element.158.refs_0_, s32[65]{0:T(128)} %get-tuple-element.212.refs_1_, ...), custom_call_target="tpu_custom_call" | custom-call | flops 40265318400 | bytes 11213384 | tf_op jit(solution)/shard_map/mixer_back/pallas_call | solution.py:376
  587.9 3.5 collective-permute-start.39
  592.7 2.8 fusion.29.refs_19_
  597.1 2.9 fusion.22.refs_20_
  600.6 6.7 fusion.8
  609.8 33.9 %mixer_back.3 = (bf16[512,1536]{1,0:T(8,128)(2,1)}, f32[8,1536]{1,0:T(8,128)}, f32[16,1536]{1,0:T(8,128)}, f32[72,512]{1,0:T(8,128)}, f32[8,512]{1,0:T(8,128)}, ...) custom-call(f32[520]{0:T(1024)} %get-tuple-element.159.refs_0_, s32[65]{0:T(128)} %get-tuple-element.213.refs_1_, ...), custom_call_target="tpu_custom_call" | custom-call | flops 40265318400 | bytes 11213384 | tf_op jit(solution)/shard_map/mixer_back/pallas_call | solution.py:376
  653.1 12.9 %grad_in.1 = (bf16[1024,1536]{1,0:T(8,128)(2,1)}, bf16[1024,1536]{1,0:T(8,128)(2,1)}) custom-call(s32[1]{0:T(128)} %bitcast.26.core_ref, bf16[512,2048]{1,0:T(8,128)(2,1)} %get-tuple-element.185.refs_0_, bf16[512,2048]{1,0:T(8,128)(2,1)} %get-tuple-element.184.refs_1_, bf16[512,1536]{1,0:T(8,128)(2,1)} %copy-done.65, bf16[512,1536]{1,0:T(8,128)(2,1)} %fusion.44.refs_3_), custom_call_target="tpu_custom_call" | custom-call | flops 6442450944 | bytes 13631488 | tf_op jit(solution)/shard_map/grad_in/pallas_call | solution.py:530
  669.2 9.7 %fusion.17 = (f32[512]{0:T(512)S(1)}, f32[2048]{0:T(1024)S(1)}, f32[512,2048]{1,0:T(8,128)}) fusion(f32[2048]{0:T(1024)S(1)} %broadcast_add_fusion.1, bf16[1280,2048]{1,0:T(8,128)(2,1)} %all-gather.9.cloned.1.call-done, f32[512]{0:T(512)S(1)} %get-tuple-element.206, bf16[512,1536]{1,0:T(8,128)(2,1)} %fusion.44.refs_3_, bf16[2048,1536]{1,0:T(8,128)(2,1)} %place_in.1), kind=kOutput, calls=%fused_computation.31 | convolution fusion | flops 3228562944 | bytes 14176256 | tf_op jit(solution)/shard_map/dot_general | solution.py:609
  688.8 9.7 %all_gather.38 = bf16[8,82,512]{2,1,0:T(8,128)(2,1)S(1)} all-gather(bf16[1,82,512]{2,1,0:T(8,128)(2,1)S(1)} %concatenate.90), channel_id=1, replica_groups=mesh['seq'=8,'tp'=4] {'seq'}, dimensions={0}, use_global_device_ids=true | all-gather | bytes 755712 | tf_op jit(solution)/shard_map/all_gather | solution.py:790
  699.7 5.7 fusion.16
  707.2 3.7 add_convert_fusion.2
  722.5 10.0 %collective-permute-done.33 = bf16[256,1536]{1,0:T(8,128)(2,1)} collective-permute-done((bf16[256,1536]{1,0:T(8,128)(2,1)}, bf16[256,1536]{1,0:T(8,128)(2,1)}, u32[]{:S(2)}, u32[]{:S(2)}) %collective-permute-start.33) | collective-permute-done | bytes 786464 | tf_op jit(solution)/shard_map/ppermute | solution.py:435
  738.3 2.9 fusion.32
  744.8 2.9 copy.78
  747.7 4.7 reshape.563
  762.7 2.8 fusion.27
  (420 shorter events, 146.2 us)
Async XLA Ops:
  7.2 106.8 %all-gather.9.cloned.1.call-start = ((), (), s32[]{:S(2)}) async-start(), calls=%async_computation.7 | async-start | bytes 6553600 | tf_op jit(solution)/shard_map/all_gather | solution.py:424
  10.8 170.4 %all-gather.17.cloned.1.call-start = ((), (), s32[]{:S(2)}) async-start(), calls=%async_computation.18 | async-start | bytes 2621440 | tf_op jit(solution)/shard_map/all_gather | solution.py:424
  12.5 58.3 %copy-start.3 = (bf16[256,4352]{1,0:T(8,128)(2,1)}, bf16[256,4352]{1,0:T(8,128)(2,1)S(1)}, u32[]{:S(2)}) copy-start(bf16[256,4352]{1,0:T(8,128)(2,1)S(1)} %pad_maximum_fusion.2.refs_0_) | copy-start | bytes 6684676
  12.5 55.9 %copy-start.35 = (f32[2,16,512]{2,1,0:T(8,128)S(1)}, f32[2,16,512]{2,1,0:T(8,128)}, u32[]{:S(2)}) copy-start(f32[2,16,512]{2,1,0:T(8,128)} %param.23) | copy-start | bytes 196612
  12.5 55.9 %copy-start.40 = (f32[16,512]{1,0:T(8,128)S(1)}, f32[16,512]{1,0:T(8,128)}, u32[]{:S(2)}) copy-start(f32[16,512]{1,0:T(8,128)} %param.21) | copy-start | bytes 98308
  12.5 55.9 %copy-start.52 = (f32[16,512]{1,0:T(8,128)S(1)}, f32[16,512]{1,0:T(8,128)}, u32[]{:S(2)}) copy-start(f32[16,512]{1,0:T(8,128)} %param.22) | copy-start | bytes 98308
  12.5 51.6 %collective-permute-start.1 = (bf16[256,4352]{1,0:T(8,128)(2,1)S(1)}, bf16[256,4352]{1,0:T(8,128)(2,1)}, u32[]{:S(2)}, u32[]{:S(2)}) collective-permute-start(bf16[256,4352]{1,0:T(8,128)(2,1)S(1)} %pad_maximum_fusion.2.refs_0_), channel_id=1, source_target_pairs={{0,16},{4,20},{8,24},{12,28},{16,0},{20,4},{24,8},{28,12},{1,17},{... | collective-permute-start | bytes 6684680 | tf_op jit(solution)/shard_map/ppermute | solution.py:435
  15.5 53.2 %collective-permute-start = (bf16[256,4352]{1,0:T(8,128)(2,1)S(1)}, bf16[256,4352]{1,0:T(8,128)(2,1)}, u32[]{:S(2)}, u32[]{:S(2)}) collective-permute-start(bf16[256,4352]{1,0:T(8,128)(2,1)S(1)} %pad_maximum_fusion.2.refs_0_), channel_id=1, source_target_pairs={{0,8},{4,12},{8,0},{12,4},{16,24},{20,28},{24,16},{28,20},{1,9},{5... | collective-permute-start | bytes 6684680 | tf_op jit(solution)/shard_map/ppermute | solution.py:435
  17.9 55.0 %copy-start.61 = (s32[2,512]{1,0:T(2,128)S(1)}, s32[2,512]{1,0:T(2,128)}, u32[]{:S(2)}) copy-start(s32[2,512]{1,0:T(2,128)} %param.17) | copy-start | bytes 12292
  17.9 186.0 %all-gather.13.cloned.1.call-start = ((), (), s32[]{:S(2)}) async-start(), calls=%async_computation.9 | async-start | bytes 6488064 | tf_op jit(solution)/shard_map/all_gather | solution.py:424
  17.9 89.6 %collective-permute-start.3 = (bf16[256,4352]{1,0:T(8,128)(2,1)S(1)}, bf16[256,4352]{1,0:T(8,128)(2,1)}, u32[]{:S(2)}, u32[]{:S(2)}) collective-permute-start(bf16[256,4352]{1,0:T(8,128)(2,1)S(1)} %pad_maximum_fusion.2.refs_0_), channel_id=1, source_target_pairs={{0,4},{4,0},{8,12},{12,8},{16,20},{20,16},{24,28},{28,24},{1,5},{5... | collective-permute-start | bytes 6684680 | tf_op jit(solution)/shard_map/ppermute | solution.py:435
  66.7 33.1 %collective-permute-start.17 = (bf16[256,2816]{1,0:T(8,128)(2,1)}, bf16[256,2816]{1,0:T(8,128)(2,1)}, u32[]{:S(2)}, u32[]{:S(2)}) collective-permute-start(bf16[256,2816]{1,0:T(8,128)(2,1)} %slice.356), channel_id=1, source_target_pairs={{0,8},{4,12},{8,0},{12,4},{16,24},{20,28},{24,16},{28,20},{1,9},{5... | collective-permute-start | bytes 4325384 | tf_op jit(solution)/shard_map/ppermute | solution.py:435
  70.8 18.4 %collective-permute-start.2 = (bf16[256,1536]{1,0:T(8,128)(2,1)}, bf16[256,1536]{1,0:T(8,128)(2,1)}, u32[]{:S(2)}, u32[]{:S(2)}) collective-permute-start(bf16[256,1536]{1,0:T(8,128)(2,1)} %slice.343), channel_id=1, source_target_pairs={{0,16},{4,20},{8,24},{12,28},{16,0},{20,4},{24,8},{28,12},{1,17},{... | collective-permute-start | bytes 2359304 | tf_op jit(solution)/shard_map/ppermute | solution.py:435
  72.3 35.3 %collective-permute-start.5 = (bf16[256,4352]{1,0:T(8,128)(2,1)}, bf16[256,4352]{1,0:T(8,128)(2,1)}, u32[]{:S(2)}, u32[]{:S(2)}) collective-permute-start(bf16[256,4352]{1,0:T(8,128)(2,1)} %collective-permute-done.1.refs_2_), channel_id=1, source_target_pairs={{0,4},{4,0},{8,12},{12,8},{16,20},{20,16},{24,28},{28,24},{1,5},{5... | collective-permute-start | bytes 6684680 | tf_op jit(solution)/shard_map/ppermute | solution.py:435
  72.3 35.3 %collective-permute-start.4 = (bf16[256,4352]{1,0:T(8,128)(2,1)}, bf16[256,4352]{1,0:T(8,128)(2,1)}, u32[]{:S(2)}, u32[]{:S(2)}) collective-permute-start(bf16[256,4352]{1,0:T(8,128)(2,1)} %collective-permute-done.refs_1_), channel_id=1, source_target_pairs={{0,4},{4,0},{8,12},{12,8},{16,20},{20,16},{24,28},{28,24},{1,5},{5... | collective-permute-start | bytes 6684680 | tf_op jit(solution)/shard_map/ppermute | solution.py:435
  74.4 39.5 %copy-start.56 = (f32[16,8,128]{2,1,0:T(8,128)}, f32[16,8,128]{2,1,0:T(8,128)S(1)}, u32[]{:S(2)}) copy-start(f32[16,8,128]{2,1,0:T(8,128)S(1)} %constant_dynamic-update-slice_fusion.refs_6_.refs_8_) | copy-start | bytes 196612
  103.2 149.4 %all-gather.11.cloned.1.call-start = ((), (), s32[]{:S(2)}) async-start(), calls=%async_computation.8 | async-start | bytes 2621440 | tf_op jit(solution)/shard_map/all_gather | solution.py:424
  105.0 2.6 collective-permute-start.6
  115.3 105.1 %copy-start.12 = (bf16[256,2048]{1,0:T(8,128)(2,1)}, bf16[256,2048]{1,0:T(8,128)(2,1)S(1)}, u32[]{:S(2)}) copy-start(bf16[256,2048]{1,0:T(8,128)(2,1)S(1)} %slice.351.refs_0_) | copy-start | bytes 3145732
  115.3 46.7 %collective-permute-start.9 = (bf16[256,2048]{1,0:T(8,128)(2,1)S(1)}, bf16[256,2048]{1,0:T(8,128)(2,1)S(1)}, u32[]{:S(2)}, u32[]{:S(2)}) collective-permute-start(bf16[256,2048]{1,0:T(8,128)(2,1)S(1)} %slice.351.refs_0_), channel_id=1, source_target_pairs={{0,16},{4,20},{8,24},{12,28},{16,0},{20,4},{24,8},{28,12},{1,17},{... | collective-permute-start | bytes 3145736 | tf_op jit(solution)/shard_map/ppermute | solution.py:435
  116.8 45.8 %collective-permute-start.8 = (bf16[256,2048]{1,0:T(8,128)(2,1)S(1)}, bf16[256,2048]{1,0:T(8,128)(2,1)S(1)}, u32[]{:S(2)}, u32[]{:S(2)}) collective-permute-start(bf16[256,2048]{1,0:T(8,128)(2,1)S(1)} %slice.351.refs_0_), channel_id=1, source_target_pairs={{0,8},{4,12},{8,0},{12,4},{16,24},{20,28},{24,16},{28,20},{1,9},{5... | collective-permute-start | bytes 3145736 | tf_op jit(solution)/shard_map/ppermute | solution.py:435
  133.7 3.7 collective-permute-start.7
  162.0 60.2 %copy-start.16 = (bf16[256,2048]{1,0:T(8,128)(2,1)}, bf16[256,2048]{1,0:T(8,128)(2,1)S(1)}, u32[]{:S(2)}) copy-start(bf16[256,2048]{1,0:T(8,128)(2,1)S(1)} %collective-permute-done.9.refs_2_) | copy-start | bytes 3145732
  162.6 59.7 %copy-start.17 = (bf16[256,2048]{1,0:T(8,128)(2,1)}, bf16[256,2048]{1,0:T(8,128)(2,1)S(1)}, u32[]{:S(2)}) copy-start(bf16[256,2048]{1,0:T(8,128)(2,1)S(1)} %collective-permute-done.8.refs_1_) | copy-start | bytes 3145732
  197.2 127.9 %all-gather.15.cloned.1.call-start = ((), (), s32[]{:S(2)}) async-start(), calls=%async_computation.12 | async-start | bytes 2621440 | tf_op jit(solution)/shard_map/all_gather | solution.py:424
  197.9 25.1 %collective-permute-start.18 = (bf16[256,2816]{1,0:T(8,128)(2,1)}, bf16[256,2816]{1,0:T(8,128)(2,1)}, u32[]{:S(2)}, u32[]{:S(2)}) collective-permute-start(bf16[256,2816]{1,0:T(8,128)(2,1)} %collective-permute-done.17.refs_3_), channel_id=1, source_target_pairs={{0,4},{4,0},{8,12},{12,8},{16,20},{20,16},{24,28},{28,24},{1,5},{5... | collective-permute-start | bytes 4325384 | tf_op jit(solution)/shard_map/ppermute | solution.py:435
  220.1 128.8 %all-gather.19.cloned.1.call-start = ((), (), s32[]{:S(2)}) async-start(), calls=%async_computation.19 | async-start | bytes 2621440 | tf_op jit(solution)/shard_map/all_gather | solution.py:424
  220.4 25.6 %collective-permute-start.12 = (bf16[256,2048]{1,0:T(8,128)(2,1)S(1)}, bf16[256,2048]{1,0:T(8,128)(2,1)}, u32[]{:S(2)}, u32[]{:S(2)}) collective-permute-start(bf16[256,2048]{1,0:T(8,128)(2,1)S(1)} %slice.351.refs_0_), channel_id=1, source_target_pairs={{0,4},{4,0},{8,12},{12,8},{16,20},{20,16},{24,28},{28,24},{1,5},{5... | collective-permute-start | bytes 3145736 | tf_op jit(solution)/shard_map/ppermute | solution.py:435
  220.7 14.3 %collective-permute-start.11 = (bf16[256,1024]{1,0:T(8,128)(2,1)S(1)}, bf16[256,1024]{1,0:T(8,128)(2,1)}, u32[]{:S(2)}, u32[]{:S(2)}) collective-permute-start(bf16[256,1024]{1,0:T(8,128)(2,1)S(1)} %slice.355), channel_id=1, source_target_pairs={{0,8},{4,12},{8,0},{12,4},{16,24},{20,28},{24,16},{28,20},{1,9},{5... | collective-permute-start | bytes 1572872 | tf_op jit(solution)/shard_map/ppermute | solution.py:435
  222.3 23.8 %collective-permute-start.14 = (bf16[256,2048]{1,0:T(8,128)(2,1)S(1)}, bf16[256,2048]{1,0:T(8,128)(2,1)}, u32[]{:S(2)}, u32[]{:S(2)}) collective-permute-start(bf16[256,2048]{1,0:T(8,128)(2,1)S(1)} %collective-permute-done.9.refs_2_), channel_id=1, source_target_pairs={{0,4},{4,0},{8,12},{12,8},{16,20},{20,16},{24,28},{28,24},{1,5},{5... | collective-permute-start | bytes 3145736 | tf_op jit(solution)/shard_map/ppermute | solution.py:435
  222.3 23.7 %collective-permute-start.13 = (bf16[256,2048]{1,0:T(8,128)(2,1)S(1)}, bf16[256,2048]{1,0:T(8,128)(2,1)}, u32[]{:S(2)}, u32[]{:S(2)}) collective-permute-start(bf16[256,2048]{1,0:T(8,128)(2,1)S(1)} %collective-permute-done.8.refs_1_), channel_id=1, source_target_pairs={{0,4},{4,0},{8,12},{12,8},{16,20},{20,16},{24,28},{28,24},{1,5},{5... | collective-permute-start | bytes 3145736 | tf_op jit(solution)/shard_map/ppermute | solution.py:435
  222.9 14.0 %collective-permute-start.10 = (bf16[256,1024]{1,0:T(8,128)(2,1)S(1)}, bf16[256,1024]{1,0:T(8,128)(2,1)}, u32[]{:S(2)}, u32[]{:S(2)}) collective-permute-start(bf16[256,1024]{1,0:T(8,128)(2,1)S(1)} %slice.354), channel_id=1, source_target_pairs={{0,16},{4,20},{8,24},{12,28},{16,0},{20,4},{24,8},{28,12},{1,17},{... | collective-permute-start | bytes 1572872 | tf_op jit(solution)/shard_map/ppermute | solution.py:435
  235.0 11.0 %collective-permute-start.16 = (bf16[256,1024]{1,0:T(8,128)(2,1)}, bf16[256,1024]{1,0:T(8,128)(2,1)}, u32[]{:S(2)}, u32[]{:S(2)}) collective-permute-start(bf16[256,1024]{1,0:T(8,128)(2,1)} %collective-permute-done.11.refs_4_), channel_id=1, source_target_pairs={{0,4},{4,0},{8,12},{12,8},{16,20},{20,16},{24,28},{28,24},{1,5},{5... | collective-permute-start | bytes 1572872 | tf_op jit(solution)/shard_map/ppermute | solution.py:435
  236.9 9.1 %collective-permute-start.15 = (bf16[256,1024]{1,0:T(8,128)(2,1)}, bf16[256,1024]{1,0:T(8,128)(2,1)}, u32[]{:S(2)}, u32[]{:S(2)}) collective-permute-start(bf16[256,1024]{1,0:T(8,128)(2,1)} %collective-permute-done.10.refs_3_), channel_id=1, source_target_pairs={{0,4},{4,0},{8,12},{12,8},{16,20},{20,16},{24,28},{28,24},{1,5},{5... | collective-permute-start | bytes 1572872 | tf_op jit(solution)/shard_map/ppermute | solution.py:435
  267.4 154.6 %reduce-scatter.10.cloned.1.call-start = ((), (), s32[]{:S(2)}) async-start(), calls=%async_computation.11 | async-start | bytes 2621440 | tf_op jit(solution)/shard_map/reduce_scatter | solution.py:428
  314.2 139.9 %reduce-scatter.12.cloned.1.call-start = ((), (), s32[]{:S(2)}) async-start(), calls=%async_computation.13 | async-start | bytes 2621440 | tf_op jit(solution)/shard_map/reduce_scatter | solution.py:428
  395.1 21.6 %collective-permute-start.19 = (bf16[1024,1408]{1,0:T(8,128)(2,1)}, bf16[1024,1408]{1,0:T(8,128)(2,1)S(1)}, u32[]{:S(2)}, u32[]{:S(2)}) collective-permute-start(bf16[1024,1408]{1,0:T(8,128)(2,1)} %get-tuple-element.55.refs_8_), channel_id=1, source_target_pairs={{0,4},{4,0},{8,12},{12,8},{16,20},{20,16},{24,28},{28,24},{1,5},{5... | collective-permute-start | bytes 8650760 | tf_op jit(solution)/shard_map/ppermute | solution.py:435
  411.0 30.9 %collective-permute-start.20 = (bf16[1024,2048]{1,0:T(8,128)(2,1)}, bf16[1024,2048]{1,0:T(8,128)(2,1)}, u32[]{:S(2)}, u32[]{:S(2)}) collective-permute-start(bf16[1024,2048]{1,0:T(8,128)(2,1)} %get-tuple-element.57.refs_10_), channel_id=1, source_target_pairs={{0,4},{4,0},{8,12},{12,8},{16,20},{20,16},{24,28},{28,24},{1,5},{5... | collective-permute-start | bytes 12582920 | tf_op jit(solution)/shard_map/ppermute | solution.py:435
  411.0 331.9 %reduce-scatter.20.cloned.1.call-start = ((), (), s32[]{:S(2)}) async-start(), calls=%async_computation.17 | async-start | bytes 1310720 | tf_op jit(solution)/shard_map/reduce_scatter | solution.py:428
  421.8 18.9 %collective-permute-start.21 = (bf16[256,1408]{1,0:T(8,128)(2,1)}, bf16[256,1408]{1,0:T(8,128)(2,1)}, u32[]{:S(2)}, u32[]{:S(2)}) collective-permute-start(bf16[256,1408]{1,0:T(8,128)(2,1)} %dynamic-slice_bitcast_fusion.2), channel_id=1, source_target_pairs={{0,16},{4,20},{8,24},{12,28},{16,0},{20,4},{24,8},{28,12},{1,17},{... | collective-permute-start | bytes 2162696 | tf_op jit(solution)/shard_map/ppermute | solution.py:435
  448.2 24.9 %collective-permute-start.22 = (bf16[256,2048]{1,0:T(8,128)(2,1)S(1)}, bf16[256,2048]{1,0:T(8,128)(2,1)S(1)}, u32[]{:S(2)}, u32[]{:S(2)}) collective-permute-start(bf16[256,2048]{1,0:T(8,128)(2,1)S(1)} %dynamic-slice_bitcast_fusion.1), channel_id=1, source_target_pairs={{0,8},{4,12},{8,0},{12,4},{16,24},{20,28},{24,16},{28,20},{1,9},{5... | collective-permute-start | bytes 3145736 | tf_op jit(solution)/shard_map/ppermute | solution.py:435
  487.9 25.7 %collective-permute-start.36 = (bf16[256,2048]{1,0:T(8,128)(2,1)}, bf16[256,2048]{1,0:T(8,128)(2,1)S(1)}, u32[]{:S(2)}, u32[]{:S(2)}) collective-permute-start(bf16[256,2048]{1,0:T(8,128)(2,1)} %fusion.34), channel_id=1, source_target_pairs={{0,8},{4,12},{8,0},{12,4},{16,24},{20,28},{24,16},{28,20},{1,9},{5... | collective-permute-start | bytes 3145736 | tf_op jit(solution)/shard_map/ppermute | solution.py:435
  490.1 25.2 %collective-permute-start.37 = (bf16[256,2048]{1,0:T(8,128)(2,1)S(1)}, bf16[256,2048]{1,0:T(8,128)(2,1)S(1)}, u32[]{:S(2)}, u32[]{:S(2)}) collective-permute-start(bf16[256,2048]{1,0:T(8,128)(2,1)S(1)} %fusion.26), channel_id=1, source_target_pairs={{0,16},{4,20},{8,24},{12,28},{16,0},{20,4},{24,8},{28,12},{1,17},{... | collective-permute-start | bytes 3145736 | tf_op jit(solution)/shard_map/ppermute | solution.py:435
  516.9 237.5 %reduce-scatter.14.cloned.1.call-start = ((), (), s32[]{:S(2)}) async-start(), calls=%async_computation.14 | async-start | bytes 2621440 | tf_op jit(solution)/shard_map/reduce_scatter | solution.py:428
  516.9 21.6 %collective-permute-start.23 = (bf16[1024,2816]{1,0:T(8,128)(2,1)}, bf16[1024,2816]{1,0:T(8,128)(2,1)}, u32[]{:S(2)}, u32[]{:S(2)}) collective-permute-start(bf16[1024,2816]{1,0:T(8,128)(2,1)} %get-tuple-element.64.refs_18_), channel_id=1, source_target_pairs={{0,4},{4,0},{8,12},{12,8},{16,20},{20,16},{24,28},{28,24},{1,5},{5... | collective-permute-start | bytes 17301512 | tf_op jit(solution)/shard_map/ppermute | solution.py:435
  524.3 232.4 %reduce-scatter.8.cloned.1.call-start = ((), (), s32[]{:S(2)}) async-start(), calls=%async_computation.10 | async-start | bytes 2621440 | tf_op jit(solution)/shard_map/reduce_scatter | solution.py:428
  538.5 222.0 %reduce-scatter.16.cloned.1.call-start = ((), (), s32[]{:S(2)}) async-start(), calls=%async_computation.15 | async-start | bytes 2621440 | tf_op jit(solution)/shard_map/reduce_scatter | solution.py:428
  538.5 62.0 %slice-start = ((s8[5242880]{0:T(1024)(128)(4,1)}), s8[4194304]{0:T(1024)(128)(4,1)S(1)}, s32[]{:S(2)}) async-start(s8[5242880]{0:T(1024)(128)(4,1)} %bitcast.201), calls=%async_computation.20 | async-start | bytes 8388608
  549.5 46.4 %collective-permute-start.24 = (bf16[256,2816]{1,0:T(8,128)(2,1)}, bf16[256,2816]{1,0:T(8,128)(2,1)S(1)}, u32[]{:S(2)}, u32[]{:S(2)}) collective-permute-start(bf16[256,2816]{1,0:T(8,128)(2,1)} %dynamic-slice_bitcast_fusion), channel_id=1, source_target_pairs={{0,8},{4,12},{8,0},{12,4},{16,24},{20,28},{24,16},{28,20},{1,9},{5... | collective-permute-start | bytes 4325384 | tf_op jit(solution)/shard_map/ppermute | solution.py:435
  549.8 50.7 %slice-start.1 = ((s8[5242880]{0:T(1024)(128)(4,1)}), s8[1048576]{0:T(1024)(128)(4,1)S(1)}, s32[]{:S(2)}) async-start(s8[5242880]{0:T(1024)(128)(4,1)} %bitcast.201), calls=%async_computation.21 | async-start | bytes 2097152
  584.6 6.9 collective-permute-start.25
  587.9 150.3 %collective-permute-start.39 = (bf16[256,1408]{1,0:T(8,128)(2,1)}, bf16[256,1408]{1,0:T(8,128)(2,1)}, u32[]{:S(2)}, u32[]{:S(2)}) collective-permute-start(bf16[256,1408]{1,0:T(8,128)(2,1)} %fusion.36), channel_id=1, source_target_pairs={{0,16},{4,20},{8,24},{12,28},{16,0},{20,4},{24,8},{28,12},{1,17},{... | collective-permute-start | bytes 2162696 | tf_op jit(solution)/shard_map/ppermute | solution.py:435
  595.4 52.4 %collective-permute-start.26 = (bf16[256,2816]{1,0:T(8,128)(2,1)}, bf16[256,2816]{1,0:T(8,128)(2,1)S(1)}, u32[]{:S(2)}, u32[]{:S(2)}) collective-permute-start(bf16[256,2816]{1,0:T(8,128)(2,1)} %fusion.29.refs_19_), channel_id=1, source_target_pairs={{0,8},{4,12},{8,0},{12,4},{16,24},{20,28},{24,16},{28,20},{1,9},{5... | collective-permute-start | bytes 4325384 | tf_op jit(solution)/shard_map/ppermute | solution.py:435
  600.0 47.8 %collective-permute-start.27 = (bf16[256,2816]{1,0:T(8,128)(2,1)}, bf16[256,2816]{1,0:T(8,128)(2,1)S(1)}, u32[]{:S(2)}, u32[]{:S(2)}) collective-permute-start(bf16[256,2816]{1,0:T(8,128)(2,1)} %fusion.22.refs_20_), channel_id=1, source_target_pairs={{0,16},{4,20},{8,24},{12,28},{16,0},{20,4},{24,8},{28,12},{1,17},{... | collective-permute-start | bytes 4325384 | tf_op jit(solution)/shard_map/ppermute | solution.py:435
  644.7 115.7 %reduce-scatter.18.cloned.1.call-start = ((), (), s32[]{:S(2)}) async-start(), calls=%async_computation.16 | async-start | bytes 2621440 | tf_op jit(solution)/shard_map/reduce_scatter | solution.py:428
  645.5 6.9 collective-permute-start.28
  666.0 39.4 %collective-permute-start.29 = (bf16[1024,1536]{1,0:T(8,128)(2,1)}, bf16[1024,1536]{1,0:T(8,128)(2,1)S(1)}, u32[]{:S(2)}, u32[]{:S(2)}) collective-permute-start(bf16[1024,1536]{1,0:T(8,128)(2,1)} %get-tuple-element.76), channel_id=1, source_target_pairs={{0,4},{4,0},{8,12},{12,8},{16,20},{20,16},{24,28},{28,24},{1,5},{5... | collective-permute-start | bytes 9437192 | tf_op jit(solution)/shard_map/ppermute | solution.py:435
  678.9 6.5 collective-permute-start.31
  681.1 5.8 collective-permute-start.30
  682.7 4.3 collective-permute-start.32
  711.8 20.7 %collective-permute-start.33 = (bf16[256,1536]{1,0:T(8,128)(2,1)}, bf16[256,1536]{1,0:T(8,128)(2,1)}, u32[]{:S(2)}, u32[]{:S(2)}) collective-permute-start(bf16[256,1536]{1,0:T(8,128)(2,1)} %add_bitcast_fusion), channel_id=1, source_target_pairs={{0,16},{4,20},{8,24},{12,28},{16,0},{20,4},{24,8},{28,12},{1,17},{... | collective-permute-start | bytes 2359304 | tf_op jit(solution)/shard_map/ppermute | solution.py:435
  715.7 22.6 %collective-permute-start.38 = (bf16[256,1408]{1,0:T(8,128)(2,1)}, bf16[256,1408]{1,0:T(8,128)(2,1)}, u32[]{:S(2)}, u32[]{:S(2)}) collective-permute-start(bf16[256,1408]{1,0:T(8,128)(2,1)} %fusion.33), channel_id=1, source_target_pairs={{0,8},{4,12},{8,0},{12,4},{16,24},{20,28},{24,16},{28,20},{1,9},{5... | collective-permute-start | bytes 2162696 | tf_op jit(solution)/shard_map/ppermute | solution.py:435
  721.0 41.7 %collective-permute-start.35 = (bf16[256,1536]{1,0:T(8,128)(2,1)}, bf16[256,1536]{1,0:T(8,128)(2,1)}, u32[]{:S(2)}, u32[]{:S(2)}) collective-permute-start(bf16[256,1536]{1,0:T(8,128)(2,1)} %fusion.35), channel_id=1, source_target_pairs={{0,16},{4,20},{8,24},{12,28},{16,0},{20,4},{24,8},{28,12},{1,17},{... | collective-permute-start | bytes 2359304 | tf_op jit(solution)/shard_map/ppermute | solution.py:435
  736.8 25.9 %collective-permute-start.34 = (bf16[256,1536]{1,0:T(8,128)(2,1)}, bf16[256,1536]{1,0:T(8,128)(2,1)}, u32[]{:S(2)}, u32[]{:S(2)}) collective-permute-start(bf16[256,1536]{1,0:T(8,128)(2,1)} %fusion.28), channel_id=1, source_target_pairs={{0,8},{4,12},{8,0},{12,4},{16,24},{20,28},{24,16},{28,20},{1,9},{5... | collective-permute-start | bytes 2359304 | tf_op jit(solution)/shard_map/ppermute | solution.py:435
  (68 other events, 740.2 us)
Sparse Core Ops, SparseCore 0:
  10.9 100.7 all-gather.8
  113.8 44.2 all-gather.16
  160.0 43.7 all-gather.12
  205.8 45.9 all-gather.10
  253.2 44.6 all-gather.14
  299.9 44.6 all-gather.18
  346.9 42.5 reduce-scatter.9
  411.2 42.8 reduce-scatter.11
  517.0 26.5 reduce-scatter.19
  545.8 42.5 reduce-scatter.13
  590.7 43.1 reduce-scatter.7
  644.8 44.6 reduce-scatter.15
  705.6 44.2 reduce-scatter.17

commit v4 on v3

--- a/solution.py
+++ b/solution.py
@@ -10,18 +10,20 @@
 EPS = 1e-06
 SPAN = 64
 STEP = 8
-ROWS = 16
+ROWS = 64
 SUB, LANE = 8, 128
 BF, F32 = jnp.bfloat16, jnp.float32
 VMEM_LIMIT = 56 * 1024 * 1024
 
 
-def keep_rows(z_ref, rim_ref, zs_ref):
-    zs_ref[0:SUB, :] = rim_ref[...]
+def keep_rows(z_ref, rim_ref, zs_ref, streams=(0, 3)):
+    width = z_ref.shape[1] // 3
+    lanes = slice(streams[0] * width, streams[1] * width)
+    zs_ref[0:SUB, lanes] = rim_ref[:, lanes]
 
     def body(i, _):
         rows = pl.ds(pl.multiple_of(i * ROWS, ROWS), ROWS)
-        zs_ref[pl.ds(pl.multiple_of(i * ROWS + SUB, SUB), ROWS), :] = z_ref[rows, :].astype(F32)
+        zs_ref[pl.ds(pl.multiple_of(i * ROWS + SUB, SUB), ROWS), lanes] = z_ref[rows, lanes].astype(F32)
         return 0
 
     lax.fori_loop(0, z_ref.shape[0] // ROWS, body, 0)
@@ -76,11 +78,37 @@
         step(True)
 
 
-def front_kernel(keep_ref, flag_ref, z_ref, rim_ref, taps_ref, cols_ref, lam_ref,
+def eight_steps(values, powers, real, imag):
+    def join(earlier, later, n):
+        pr, pi = powers[n]
+        return pr * earlier[0] - pi * earlier[1] + later[0], pr * earlier[1] + pi * earlier[0] + later[1]
+
+    pr, pi = powers[0]
+    pairs = [(pr * values[j] + values[j + 1], pi * values[j]) for j in range(0, STEP, 2)]
+    fours = [join(pairs[j], pairs[j + 1], 1) for j in (0, 2)]
+    return join((real, imag), join(*fours, 2), 3)
+
+
+def end_scan(values, keep_of, masked, pow_ref, end_ref):
+    poles = end_ref.shape[0] // 2
+    for k in range(poles):
+        sr, si = end_ref[k], end_ref[poles + k]
+        if masked:
+            lr, li = pow_ref[k], pow_ref[poles + k]
+            for j in range(STEP):
+                keep = keep_of(j)
+                sr, si = sr * keep, si * keep
+                sr, si = lr * sr - li * si + values[j], lr * si + li * sr
+        else:
+            powers = [(pow_ref[2 * poles * n + k], pow_ref[2 * poles * n + poles + k]) for n in range(4)]
+            sr, si = eight_steps(values, powers, sr, si)
+        end_ref[k], end_ref[poles + k] = sr, si
+
+
+def front_kernel(keep_ref, flag_ref, z_ref, rim_ref, taps_ref, cols_ref, pow_ref,
                  u_ref, end_ref, zs_ref):
     count, width = z_ref.shape[0], z_ref.shape[1] // 3
-    poles = lam_ref.shape[0] // 2
-    keep_rows(z_ref, rim_ref, zs_ref)
+    keep_rows(z_ref, rim_ref, zs_ref, (1, 3))
 
     def natural(i, _):
         cols = chunk_cols(cols_ref, i)
@@ -95,15 +123,7 @@
     def scan(group, _):
         def step(masked):
             us = [u_ref[at(group, j), :] for j in range(STEP)]
-            for k in range(poles):
-                lr, li = lam_ref[k], lam_ref[poles + k]
-                sr, si = end_ref[k], end_ref[poles + k]
-                for j in range(STEP):
-                    if masked:
-                        keep = keep_ref[group * STEP + j]
-                        sr, si = sr * keep, si * keep
-                    sr, si = lr * sr - li * si + us[j], lr * si + li * sr
-                end_ref[k], end_ref[poles + k] = sr, si
+            end_scan(us, lambda j: keep_ref[group * STEP + j], masked, pow_ref, end_ref)
 
         by_flag(flag_ref[group], step)
         return 0
@@ -178,11 +198,10 @@
     lax.fori_loop(0, count // ROWS, natural, 0)
 
 
-def adjoint_kernel(keep_ref, flag_ref, z_ref, rim_ref, taps_ref, cols_ref, lam_ref, dmix_ref,
+def adjoint_kernel(keep_ref, flag_ref, z_ref, rim_ref, taps_ref, cols_ref, pow_ref, dmix_ref,
                    e_ref, end_ref, zs_ref):
     count, width = z_ref.shape[0], z_ref.shape[1] // 3
-    poles = lam_ref.shape[0] // 2
-    keep_rows(z_ref, rim_ref, zs_ref)
+    keep_rows(z_ref, rim_ref, zs_ref, (0, 1))
 
     def natural(i, _):
         rows = pl.ds(pl.multiple_of(i * ROWS, ROWS), ROWS)
@@ -197,16 +216,8 @@
         group = count // STEP - 1 - order
 
         def step(masked):
-            es = [e_ref[at(group, j), :] for j in range(STEP)]
-            for k in range(poles):
-                lr, li = lam_ref[k], lam_ref[poles + k]
-                br, bi = end_ref[k], end_ref[poles + k]
-                for j in reversed(range(STEP)):
-                    if masked:
-                        keep = keep_ref[group * STEP + j + 1]
-                        br, bi = br * keep, bi * keep
-                    br, bi = lr * br + li * bi + es[j], lr * bi - li * br
-                end_ref[k], end_ref[poles + k] = br, bi
+            es = [e_ref[at(group, STEP - 1 - j), :] for j in range(STEP)]
+            end_scan(es, lambda j: keep_ref[group * STEP + STEP - j], masked, pow_ref, end_ref)
 
         by_flag(flag_ref[group] + flag_ref[group + 1], step)
         return 0
@@ -368,7 +379,7 @@
     def without(*refs):
         kernel(*refs[:count], *refs[count + len(after) :])
 
-    vmem = pl.BlockSpec(memory_space=pltpu.VMEM)
+    local = pl.BlockSpec(memory_space=pltpu.VMEM)
     scalar = pl.BlockSpec(memory_space=pltpu.SMEM)
     moved = sum(a.size * a.dtype.itemsize for a in ins) + sum(
         functools.reduce(lambda x, y: x * y, s) * jnp.dtype(d).itemsize for s, d in outs
@@ -376,9 +387,9 @@
     return pl.pallas_call(
         without,
         out_shape=[jax.ShapeDtypeStruct(s, d) for s, d in outs],
-        in_specs=[scalar] * smem + [vmem] * (count - smem)
+        in_specs=[scalar] * smem + [local] * (count - smem)
         + [pl.BlockSpec(memory_space=pl.ANY)] * len(after),
-        out_specs=[vmem] * len(outs),
+        out_specs=[local] * len(outs),
         scratch_shapes=[pltpu.VMEM(s, d) for s, d in scratch],
         compiler_params=pltpu.CompilerParams(vmem_limit_bytes=VMEM_LIMIT),
         cost_estimate=pl.CostEstimate(flops=flops, bytes_accessed=moved, transcendentals=0),
@@ -630,6 +641,9 @@
     rate = jnp.exp(log_rate)
     lam_real, lam_imag = polar(1.0, rate, pole_angle)
     lam = packed(lam_real, lam_imag)
+    powers = [(lam_real, lam_imag)] + [polar(n, rate, pole_angle) for n in (2.0, 4.0, 8.0)]
+    pow_ahead = jnp.concatenate([packed(real, imag) for real, imag in powers])
+    pow_back = jnp.concatenate([packed(real, -imag) for real, imag in powers])
     lam_all = packed(*polar(float(count), rate, pole_angle))
     res = packed(residues[0], residues[1])
     taps = conv_taps.reshape(9, width)
@@ -664,7 +678,7 @@
     spans = [(v[1:] == v[:-1]).astype(F32) for v in last]
     spans_back = [(v[1:] == v[:-1]).astype(F32) for v in first]
     injects, ends = zip(*[
-        call(front_kernel, (*masks[m], *bases[m]), [(seq_shape, F32), (st_shape, F32)],
+        call(front_kernel, (*masks[m], *bases[m][:-1], pow_ahead), [(seq_shape, F32), (st_shape, F32)],
              [zs], 2, "mixer_front", 4 * work)
         for m in range(micros)
     ])
@@ -723,7 +737,7 @@
     down_chip, out_chip = grad_chip(down_halves), grad_chip(out_halves)
     down_far, out_far = grad_far(down_chip, Y), grad_far(out_chip, X)
     adjoints, ends = zip(*[
-        call(adjoint_kernel, (*masks[m], *bases[m], kept[m]["d_mixed"]),
+        call(adjoint_kernel, (*masks[m], *bases[m][:-1], pow_back, kept[m]["d_mixed"]),
              [(seq_shape, F32), (st_shape, F32)], [zs], 2, "mixer_adjoint", 4 * work,
              (down_chip, out_chip) if m else (*down_halves, *out_halves))
         for m in range(micros)

time: 786 us -> 777 us (0.989)
  Pallas kernels: 229 us -> 209 us
  waiting for transfers between devices: 122 us -> 132 us
  starting transfers between devices: 51 us -> 41.2 us
    pallas_call x8, Pallas kernels: 148 us -> 128 us  [call(): pl.pallas_call(without, out_shape=[jax.ShapeDtypeStruct(s, d) for s, d in...]
    all_gather x6, waiting for transfers between devices: 5.71 us -> 19.8 us  [gather(): return lax.all_gather(block, axis, axis=dim, tiled=True)]
    reduce_scatter x7, starting transfers between devices: 11.2 us -> 0.29 us  [scatter(): return lax.psum_scatter(block, axis, scatter_dimension=dim, tiled=True)]
    unnamed x171 -> x188, local copies, waits for them, and re-layouts: 27.5 us -> 32.1 us
  transfers between devices with their start and end apart: 53 -> 53, of which waited for: 13 -> 14; matrix products, arithmetic and copies ran while one was open for 36% -> 37% of each run, Pallas kernels for 30% -> 27%
where the time goes in v4:
time: 777 us; the launch traced here: 766 us
  Pallas kernels  209 us (27%)
  waiting for transfers between devices  132 us (17%)
  matrix products  132 us (17%)
  other arithmetic  109 us (14%)
  local copies, waits for them, and re-layouts  79.2 us (10%)
  starting transfers between devices  41.2 us (5%)
  blocking collectives  36.2 us (5%)
  between operations  27.4 us (4%)
    dot_general x15, matrix products, dot(): return lax.dot_general(a, b, (dims, ((), ())), preferred_element_type=F32)  132 us
    pallas_call x8, Pallas kernels, call(): pl.pallas_call(without, out_shape=[jax.ShapeDtypeStruct(s, d) for s, d in...  128 us
    ppermute x34, waiting for transfers between devices, over(): return lax.ppermute(value, 'seq', [(i, i ^ bit) for i in range(8)])  106 us
    pallas_call x4, Pallas kernels, grad_halves(): pl.pallas_call(functools.partial(halves_kernel, n), out_shape=[jax.ShapeD...  60.4 us
    unnamed x188, local copies, waits for them, and re-layouts  32.1 us
    ppermute x34, starting transfers between devices, over(): return lax.ppermute(value, 'seq', [(i, i ^ bit) for i in range(8)])  31.2 us
    pallas_call x3, Pallas kernels, place(): pl.pallas_call(functools.partial(place_kernel, plan, count), out_shape=ja...  21 us
    all_gather x6, waiting for transfers between devices, gather(): return lax.all_gather(block, axis, axis=dim, tiled=True)  19.8 us
  transfers between devices with their start and end apart: 53, of which 14 were waited for; matrix products, arithmetic and copies ran while one was open for 37% of the time, Pallas kernels for 27%

profile of v4, /device:TPU:0, one launch (start us, length us, event | category | flops | bytes accessed | tf_op | source)
XLA Modules:
  0.0 766.0 jit_solution(15373447176248398532)
XLA Ops:
  12.5 3.0 collective-permute-start.1
  21.5 42.6 %collective-permute-done.1.refs_2_ = bf16[256,4352]{1,0:T(8,128)(2,1)} collective-permute-done((bf16[256,4352]{1,0:T(8,128)(2,1)S(1)}, bf16[256,4352]{1,0:T(8,128)(2,1)}, u32[]{:S(2)}, u32[]{:S(2)}) %collective-permute-start.1) | collective-permute-done | bytes 2228256 | tf_op jit(solution)/shard_map/ppermute | solution.py:446
  64.1 2.6 slice.356
  77.8 14.7 %collective-permute-done.2.refs_3_ = bf16[256,1536]{1,0:T(8,128)(2,1)S(1)} collective-permute-done((bf16[256,1536]{1,0:T(8,128)(2,1)S(1)}, bf16[256,1536]{1,0:T(8,128)(2,1)S(1)}, u32[]{:S(2)}, u32[]{:S(2)}) %collective-permute-start.2) | collective-permute-done | bytes 786464 | tf_op jit(solution)/shard_map/ppermute | solution.py:446
  93.9 5.9 collective-permute-done.17.refs_3_
  109.2 5.5 place_in.1
  119.1 3.3 multiply_reduce_fusion
  122.5 3.4 slice_convert_fusion
  127.5 6.9 fusion.18
  138.8 9.0 %mixer_front.2 = (f32[4096,128]{1,0:T(8,128)}, f32[16,8,128]{2,1,0:T(8,128)}) custom-call(f32[520]{0:T(1024)} %get-tuple-element.158.refs_0_, s32[65]{0:T(128)} %get-tuple-element.238.refs_1_, bf16[512,1536]{1,0:T(8,128)(2,1)} %get-tuple-element.194.refs_2_.refs_4_, f32[8,1536]{1,0:T(8,128)} %get-tuple-element.202.refs_3_.refs_5_, ...), custom_call_target="tpu_custom_call" | custom-call | flops 13421772800 | bytes 4084260 | tf_op jit(solution)/shard_map/mixer_front/pallas_call | solution.py:387
  147.8 9.0 %mixer_front.3 = (f32[4096,128]{1,0:T(8,128)}, f32[16,8,128]{2,1,0:T(8,128)}) custom-call(f32[520]{0:T(1024)} %get-tuple-element.159.refs_0_, s32[65]{0:T(128)} %get-tuple-element.239.refs_1_, bf16[512,1536]{1,0:T(8,128)(2,1)} %get-tuple-element.195.refs_2_.refs_4_, f32[8,1536]{1,0:T(8,128)} %get-tuple-element.203.refs_3_.refs_5_, ...), custom_call_target="tpu_custom_call" | custom-call | flops 13421772800 | bytes 4084260 | tf_op jit(solution)/shard_map/mixer_front/pallas_call | solution.py:387
  160.1 16.2 %all_gather.31 = bf16[8,2,16,8,128]{4,3,2,1,0:T(8,128)(2,1)S(1)} all-gather(bf16[1,2,16,8,128]{4,3,2,1,0:T(8,128)(2,1)S(1)} %fusion.43), channel_id=1, replica_groups=mesh['seq'=8,'tp'=4] {'seq'}, dimensions={0}, use_global_device_ids=true | all-gather | bytes 589824 | tf_op jit(solution)/shard_map/all_gather | solution.py:685
  177.3 14.7 %mixer_finish.2 = (bf16[512,512]{1,0:T(8,128)(2,1)}, f32[512,512]{1,0:T(8,128)}, f32[8,16,8,128]{3,2,1,0:T(8,128)}) custom-call(f32[520]{0:T(1024)} %get-tuple-element.158.refs_0_, s32[65]{0:T(128)} %get-tuple-element.238.refs_1_, f32[8]{0:T(128)} %compare_convert_fusion.4.refs_2_, s32[1]{0:T(128)} %bitcast.5.me_ref.refs_3_, ...), custom_call_target="tpu_custom_call" | custom-call | flops 16777216000 | bytes 7101000 | tf_op jit(solution)/shard_map/mixer_finish/pallas_call | solution.py:387
  193.0 10.8 %all-gather.13.cloned.1.call-done.refs_15_ = bf16[2048,1408]{1,0:T(8,128)(2,1)} async-done(((bf16[256,1408]{1,0:T(8,128)(2,1)}), bf16[2048,1408]{1,0:T(8,128)(2,1)}) %all-gather.13.cloned.1.call-update) | async-done | bytes 5767184 | tf_op jit(solution)/shard_map/all_gather | solution.py:435
  203.8 14.4 %mixer_finish.3 = (bf16[512,512]{1,0:T(8,128)(2,1)}, f32[512,512]{1,0:T(8,128)}, f32[8,16,8,128]{3,2,1,0:T(8,128)}) custom-call(f32[520]{0:T(1024)} %get-tuple-element.159.refs_0_, s32[65]{0:T(128)} %get-tuple-element.239.refs_1_, f32[8]{0:T(128)} %compare_convert_fusion.2.refs_2_, s32[1]{0:T(128)} %bitcast.5.me_ref.refs_3_, ...), custom_call_target="tpu_custom_call" | custom-call | flops 16777216000 | bytes 7101000 | tf_op jit(solution)/shard_map/mixer_finish/pallas_call | solution.py:387
  221.6 11.3 %collective-permute-done.11.refs_4_ = bf16[256,1024]{1,0:T(8,128)(2,1)} collective-permute-done((bf16[256,1024]{1,0:T(8,128)(2,1)S(1)}, bf16[256,1024]{1,0:T(8,128)(2,1)}, u32[]{:S(2)}, u32[]{:S(2)}) %collective-permute-start.11) | collective-permute-done | bytes 524320 | tf_op jit(solution)/shard_map/ppermute | solution.py:446
  234.9 8.9 %place_gu.1 = bf16[2048,2816]{1,0:T(8,128)(2,1)} custom-call(s32[1]{0:T(128)} %bitcast.5.me_ref.refs_3_, bf16[256,4352]{1,0:T(8,128)(2,1)} %copy-done.3, bf16[256,4352]{1,0:T(8,128)(2,1)} %collective-permute-done.refs_1_, bf16[256,4352]{1,0:T(8,128)(2,1)} %collective-permute-done.1.refs_2_, bf16[256,2816]{1,0:T(8,128)(2,1)} %collective-permute-done.17.refs_3_, ...), custom_call_target="tpu_custom_call" | custom-call | bytes 23068672 | tf_op jit(solution)/shard_map/place_gu/pallas_call | solution.py:477
  243.9 6.5 place_out.1
  253.6 11.2 %multiply_reduce_fusion.6 = (f32[512]{0:T(512)S(1)}, f32[512,2048]{1,0:T(8,128)}) fusion(bf16[512,2048]{1,0:T(8,128)(2,1)} %all-gather.11.cloned.1.call-done.refs_2_, bf16[2048,2048]{1,0:T(8,128)(2,1)} %place_out.1, bf16[1280,2048]{1,0:T(8,128)(2,1)} %all-gather.9.cloned.1.call-done), kind=kOutput, calls=%fused_computation.42 | convolution fusion | flops 4299161088 | bytes 16779264 | tf_op jit(solution)/shard_map/dot_general | solution.py:620
  266.4 2.8 multiply_convert_fusion.2.refs_0_
  270.6 9.7 %fusion.78 = f32[512,2816]{1,0:T(8,128)S(1)} fusion(bf16[512,2048]{1,0:T(8,128)(2,1)S(1)} %multiply_convert_fusion.2.refs_0_, bf16[2048,2816]{1,0:T(8,128)(2,1)} %place_gu.1), kind=kOutput, calls=%fused_computation.250 | convolution fusion | flops 5905580032 | bytes 19398656 | tf_op jit(solution)/shard_map/dot_general | solution.py:620
  280.4 5.9 multiply_convert_fusion.7
  286.4 10.0 %multiply_reduce_fusion.2 = (f32[2048]{0:T(1024)}, f32[512]{0:T(512)}, f32[512,2048]{1,0:T(8,128)}) fusion(f32[512,2048]{1,0:T(8,128)S(1)} %copy-done, f32[512]{0:T(512)S(1)} %get-tuple-element.237, f32[2048]{0:T(1024)S(1)} %copy-done.44, bf16[2048,2816]{1,0:T(8,128)(2,1)S(1)} %bitcast.219, bf16[512,1408]{1,0:T(8,128)(2,1)} %get-tuple-element.189, ...), kind=kOutput, calls=%fused_computation.34 | convolution fusion | flops 5917636096 | bytes 22827008 | tf_op jit(solution)/shard_map/dot_general | solution.py:620
  297.1 4.6 fusion.71
  303.0 8.4 %convolution_convert_fusion.1 = bf16[512,2048]{1,0:T(8,128)(2,1)S(1)} fusion(bf16[512,2048]{1,0:T(8,128)(2,1)S(1)} %get-tuple-element.181.refs_0_, bf16[2048,2048]{1,0:T(8,128)(2,1)} %place_out.1), kind=kOutput, calls=%fused_computation.46 | convolution fusion | flops 4296015872 | bytes 12582912 | tf_op jit(solution)/shard_map/dot_general | solution.py:620
  312.9 9.3 %multiply_reduce_fusion.4 = (f32[512]{0:T(512)S(1)}, f32[512,2048]{1,0:T(8,128)S(1)}) fusion(bf16[512,2048]{1,0:T(8,128)(2,1)} %all-gather.15.cloned.1.call-done.refs_3_, bf16[2048,2048]{1,0:T(8,128)(2,1)} %place_out.1, f32[]{:T(128)} %bitcast.32, bf16[1280,2048]{1,0:T(8,128)(2,1)} %all-gather.9.cloned.1.call-done), kind=kOutput, calls=%fused_computation.38 | convolution fusion | flops 4300209664 | bytes 16779268 | tf_op jit(solution)/shard_map/dot_general | solution.py:620
  325.5 11.3 %fusion.79 = f32[512,2816]{1,0:T(8,128)} fusion(bf16[512,2048]{1,0:T(8,128)(2,1)S(1)} %multiply_convert_fusion.1.refs_1_, bf16[2048,2816]{1,0:T(8,128)(2,1)} %place_gu.1), kind=kOutput, calls=%fused_computation.251 | convolution fusion | flops 5905580032 | bytes 19398656 | tf_op jit(solution)/shard_map/dot_general | solution.py:620
  336.9 7.6 all-gather.19.cloned.1.call-done
  344.5 11.4 %multiply_convert_fusion.4 = (bf16[512,1408]{1,0:T(8,128)(2,1)}, bf16[512,1408]{1,0:T(8,128)(2,1)}, bf16[512,1408]{1,0:T(8,128)(2,1)}) fusion(f32[512,2816]{1,0:T(8,128)} %fusion.79, bf16[2048,1408]{1,0:T(8,128)(2,1)} %all-gather.13.cloned.1.call-done.refs_15_, bf16[1,512,2048]{2,1,0:T(8,128)(2,1)} %all-gather.19.cloned.1.call-done), kind=kOutput, calls=%fused_computation.57 | convolution fusion | flops 2964324352 | bytes 17956864 | tf_op jit(solution)/shard_map/dot_general | solution.py:620
  355.9 10.5 %multiply_reduce_fusion.1 = (f32[2048]{0:T(1024)S(1)}, f32[512]{0:T(512)S(1)}, f32[512,2048]{1,0:T(8,128)S(1)}) fusion(f32[512,2048]{1,0:T(8,128)S(1)} %copy-done.2, f32[512]{0:T(512)S(1)} %get-tuple-element.235, f32[2048]{0:T(1024)S(1)} %copy-done.44, bf16[2048,2816]{1,0:T(8,128)(2,1)} %place_gu.1, bf16[512,1408]{1,0:T(8,128)(2,1)} %get-tuple-element.187, ...), kind=kOutput, calls=%fused_computation.33 | convolution fusion | flops 5917636096 | bytes 22827008 | tf_op jit(solution)/shard_map/dot_general | solution.py:620
  366.4 4.3 fusion.66
  372.0 5.8 convolution_convert_fusion.refs_4_
  377.8 12.5 %grad_down.1 = (bf16[1024,1408]{1,0:T(8,128)(2,1)}, bf16[1024,1408]{1,0:T(8,128)(2,1)}) custom-call(s32[1]{0:T(128)} %bitcast.26.core_ref, bf16[512,2048]{1,0:T(8,128)(2,1)} %bitcast.233, bf16[512,2048]{1,0:T(8,128)(2,1)} %bitcast.234, bf16[512,1408]{1,0:T(8,128)(2,1)} %get-tuple-element.191.refs_2_, bf16[512,1408]{1,0:T(8,128)(2,1)} %get-tuple-element.190.refs_3_, ...), custom_call_target="tpu_custom_call" | custom-call | flops 5905580032 | bytes 12845056 | tf_op jit(solution)/shard_map/grad_down/pallas_call | solution.py:541
  390.3 15.4 %grad_out.1 = (bf16[1024,2048]{1,0:T(8,128)(2,1)}, bf16[1024,2048]{1,0:T(8,128)(2,1)}) custom-call(s32[1]{0:T(128)} %bitcast.26.core_ref, bf16[512,2048]{1,0:T(8,128)(2,1)} %copy-done.21, bf16[512,2048]{1,0:T(8,128)(2,1)} %copy-done.22, bf16[512,2048]{1,0:T(8,128)(2,1)} %all-gather.11.cloned.1.call-done.refs_2_, ...), custom_call_target="tpu_custom_call" | custom-call | flops 8589934592 | bytes 16777216 | tf_op jit(solution)/shard_map/grad_out/pallas_call | solution.py:541
  406.9 3.7 pad_maximum_fusion.refs_2_
  419.1 9.1 %mixer_adjoint.2 = (f32[4096,128]{1,0:T(8,128)}, f32[16,8,128]{2,1,0:T(8,128)}) custom-call(f32[520]{0:T(1024)} %get-tuple-element.158.refs_0_, s32[65]{0:T(128)} %get-tuple-element.238.refs_1_, bf16[512,1536]{1,0:T(8,128)(2,1)} %get-tuple-element.194.refs_2_.refs_4_, f32[8,1536]{1,0:T(8,128)} %get-tuple-element.202.refs_3_.refs_5_, ...), custom_call_target="tpu_custom_call" | custom-call | flops 13421772800 | bytes 4608548 | tf_op jit(solution)/shard_map/mixer_adjoint/pallas_call | solution.py:387
  428.1 7.9 %collective-permute-done.21 = bf16[256,1408]{1,0:T(8,128)(2,1)} collective-permute-done((bf16[256,1408]{1,0:T(8,128)(2,1)}, bf16[256,1408]{1,0:T(8,128)(2,1)}, u32[]{:S(2)}, u32[]{:S(2)}) %collective-permute-start.21) | collective-permute-done | bytes 720928 | tf_op jit(solution)/shard_map/ppermute | solution.py:446
  437.2 4.1 add_convert_fusion.1
  445.0 4.3 reduce-scatter.12.cloned.1.call-done.refs_7_.refs_14_
  449.3 8.8 %mixer_adjoint.3 = (f32[4096,128]{1,0:T(8,128)}, f32[16,8,128]{2,1,0:T(8,128)}) custom-call(f32[520]{0:T(1024)} %get-tuple-element.159.refs_0_, s32[65]{0:T(128)} %get-tuple-element.239.refs_1_, bf16[512,1536]{1,0:T(8,128)(2,1)} %get-tuple-element.195.refs_2_.refs_4_, f32[8,1536]{1,0:T(8,128)} %get-tuple-element.203.refs_3_.refs_5_, ...), custom_call_target="tpu_custom_call" | custom-call | flops 13421772800 | bytes 4608548 | tf_op jit(solution)/shard_map/mixer_adjoint/pallas_call | solution.py:387
  458.2 9.6 %collective-permute-done.22 = bf16[256,2048]{1,0:T(8,128)(2,1)S(1)} collective-permute-done((bf16[256,2048]{1,0:T(8,128)(2,1)S(1)}, bf16[256,2048]{1,0:T(8,128)(2,1)S(1)}, u32[]{:S(2)}, u32[]{:S(2)}) %collective-permute-start.22) | collective-permute-done | bytes 1048608 | tf_op jit(solution)/shard_map/ppermute | solution.py:446
  470.4 9.9 %all_gather.37 = bf16[8,2,16,8,128]{4,3,2,1,0:T(8,128)(2,1)S(1)} all-gather(bf16[1,2,16,8,128]{4,3,2,1,0:T(8,128)(2,1)S(1)} %fusion.44), channel_id=1, replica_groups=mesh['seq'=8,'tp'=4] {'seq'}, dimensions={0}, use_global_device_ids=true | all-gather | bytes 589824 | tf_op jit(solution)/shard_map/all_gather | solution.py:745
  486.3 19.5 %grad_gu.1 = (bf16[1024,2816]{1,0:T(8,128)(2,1)}, bf16[1024,2816]{1,0:T(8,128)(2,1)}) custom-call(s32[1]{0:T(128)} %bitcast.26.core_ref, bf16[512,2048]{1,0:T(8,128)(2,1)} %copy-done.19, bf16[512,2048]{1,0:T(8,128)(2,1)} %copy-done.20, bf16[512,2816]{1,0:T(8,128)(2,1)} %pad_maximum_fusion.refs_2_, bf16[512,2816]{1,0:T(8,128)(2,1)} %pad_maximum_fusion.1.refs_3_, ...), custom_call_target="tpu_custom_call" | custom-call | flops 11811160064 | bytes 21495808 | tf_op jit(solution)/shard_map/grad_gu/pallas_call | solution.py:541
  512.8 7.3 convolution_convert_fusion.2
  521.4 5.1 slice_bitcast_fusion
  526.5 7.7 %convolution_convert_fusion.3 = bf16[512,2048]{1,0:T(8,128)(2,1)} fusion(bf16[512,1408]{1,0:T(8,128)(2,1)S(1)} %copy-done.70, bf16[2048,1408]{1,0:T(8,128)(2,1)} %all-gather.13.cloned.1.call-done.refs_15_), kind=kOutput, calls=%fused_computation.48 | convolution fusion | flops 2953838592 | bytes 9306112 | tf_op jit(solution)/shard_map/dot_general | solution.py:620
  534.4 8.4 %add_convert_fusion = bf16[1024,2816]{1,0:T(8,128)(2,1)} fusion(bf16[1024,2816]{1,0:T(8,128)(2,1)} %collective-permute-done.23, bf16[1024,2816]{1,0:T(8,128)(2,1)} %get-tuple-element.65.refs_19_), kind=kLoop, calls=%fused_computation | loop fusion | flops 11534336 | bytes 17301504 | tf_op jit(solution)/shard_map/convert_element_type | solution.py:571
  545.7 31.4 %mixer_back.2 = (bf16[512,1536]{1,0:T(8,128)(2,1)}, f32[8,1536]{1,0:T(8,128)}, f32[64,1536]{1,0:T(8,128)}, f32[72,512]{1,0:T(8,128)}, f32[8,512]{1,0:T(8,128)}, ...) custom-call(f32[520]{0:T(1024)} %get-tuple-element.158.refs_0_, s32[65]{0:T(128)} %get-tuple-element.238.refs_1_, ...), custom_call_target="tpu_custom_call" | custom-call | flops 40265318400 | bytes 11508296 | tf_op jit(solution)/shard_map/mixer_back/pallas_call | solution.py:387
  581.3 3.2 collective-permute-start.39
  585.7 2.8 fusion.29.refs_19_
  590.2 2.9 fusion.22.refs_20_
  593.8 6.7 fusion.8
  603.0 31.3 %mixer_back.3 = (bf16[512,1536]{1,0:T(8,128)(2,1)}, f32[8,1536]{1,0:T(8,128)}, f32[64,1536]{1,0:T(8,128)}, f32[72,512]{1,0:T(8,128)}, f32[8,512]{1,0:T(8,128)}, ...) custom-call(f32[520]{0:T(1024)} %get-tuple-element.159.refs_0_, s32[65]{0:T(128)} %get-tuple-element.239.refs_1_, ...), custom_call_target="tpu_custom_call" | custom-call | flops 40265318400 | bytes 11508296 | tf_op jit(solution)/shard_map/mixer_back/pallas_call | solution.py:387
  643.8 12.9 %grad_in.1 = (bf16[1024,1536]{1,0:T(8,128)(2,1)}, bf16[1024,1536]{1,0:T(8,128)(2,1)}) custom-call(s32[1]{0:T(128)} %bitcast.26.core_ref, bf16[512,2048]{1,0:T(8,128)(2,1)} %get-tuple-element.193.refs_0_, bf16[512,2048]{1,0:T(8,128)(2,1)} %get-tuple-element.192.refs_1_, bf16[512,1536]{1,0:T(8,128)(2,1)} %copy-done.69, bf16[512,1536]{1,0:T(8,128)(2,1)} %fusion.42.refs_3_), custom_call_target="tpu_custom_call" | custom-call | flops 6442450944 | bytes 13631488 | tf_op jit(solution)/shard_map/grad_in/pallas_call | solution.py:541
  660.1 9.7 %fusion.17 = (f32[512]{0:T(512)S(1)}, f32[2048]{0:T(1024)S(1)}, f32[512,2048]{1,0:T(8,128)}) fusion(f32[2048]{0:T(1024)S(1)} %broadcast_add_fusion.1, bf16[1280,2048]{1,0:T(8,128)(2,1)} %all-gather.9.cloned.1.call-done, f32[512]{0:T(512)S(1)} %get-tuple-element.232, bf16[512,1536]{1,0:T(8,128)(2,1)} %fusion.42.refs_3_, bf16[2048,1536]{1,0:T(8,128)(2,1)} %place_in.1), kind=kOutput, calls=%fused_computation.31 | convolution fusion | flops 3228562944 | bytes 14176256 | tf_op jit(solution)/shard_map/dot_general | solution.py:620
  671.7 3.2 collective-permute-start.32
  678.8 10.1 %all_gather.38 = bf16[8,82,512]{2,1,0:T(8,128)(2,1)S(1)} all-gather(bf16[1,82,512]{2,1,0:T(8,128)(2,1)S(1)} %concatenate.98), channel_id=1, replica_groups=mesh['seq'=8,'tp'=4] {'seq'}, dimensions={0}, use_global_device_ids=true | all-gather | bytes 755712 | tf_op jit(solution)/shard_map/all_gather | solution.py:804
  690.1 5.7 fusion.16
  697.6 3.7 add_convert_fusion.2
  712.8 10.1 %collective-permute-done.33 = bf16[256,1536]{1,0:T(8,128)(2,1)} collective-permute-done((bf16[256,1536]{1,0:T(8,128)(2,1)}, bf16[256,1536]{1,0:T(8,128)(2,1)}, u32[]{:S(2)}, u32[]{:S(2)}) %collective-permute-start.33) | collective-permute-done | bytes 786464 | tf_op jit(solution)/shard_map/ppermute | solution.py:446
  728.6 2.9 fusion.32
  735.0 2.9 copy.78
  737.9 4.7 reshape.609
  753.0 2.8 fusion.27
  (448 shorter events, 156.3 us)
Async XLA Ops:
  7.2 107.6 %all-gather.9.cloned.1.call-start = ((), (), s32[]{:S(2)}) async-start(), calls=%async_computation.7 | async-start | bytes 6553600 | tf_op jit(solution)/shard_map/all_gather | solution.py:435
  10.8 166.6 %all-gather.17.cloned.1.call-start = ((), (), s32[]{:S(2)}) async-start(), calls=%async_computation.18 | async-start | bytes 2621440 | tf_op jit(solution)/shard_map/all_gather | solution.py:435
  12.5 54.2 %copy-start.3 = (bf16[256,4352]{1,0:T(8,128)(2,1)}, bf16[256,4352]{1,0:T(8,128)(2,1)S(1)}, u32[]{:S(2)}) copy-start(bf16[256,4352]{1,0:T(8,128)(2,1)S(1)} %pad_maximum_fusion.2.refs_0_) | copy-start | bytes 6684676
  12.5 51.6 %collective-permute-start.1 = (bf16[256,4352]{1,0:T(8,128)(2,1)S(1)}, bf16[256,4352]{1,0:T(8,128)(2,1)}, u32[]{:S(2)}, u32[]{:S(2)}) collective-permute-start(bf16[256,4352]{1,0:T(8,128)(2,1)S(1)} %pad_maximum_fusion.2.refs_0_), channel_id=1, source_target_pairs={{0,16},{4,20},{8,24},{12,28},{16,0},{20,4},{24,8},{28,12},{1,17},{... | collective-permute-start | bytes 6684680 | tf_op jit(solution)/shard_map/ppermute | solution.py:446
  15.6 92.8 %collective-permute-start.3 = (bf16[256,4352]{1,0:T(8,128)(2,1)S(1)}, bf16[256,4352]{1,0:T(8,128)(2,1)}, u32[]{:S(2)}, u32[]{:S(2)}) collective-permute-start(bf16[256,4352]{1,0:T(8,128)(2,1)S(1)} %pad_maximum_fusion.2.refs_0_), channel_id=1, source_target_pairs={{0,4},{4,0},{8,12},{12,8},{16,20},{20,16},{24,28},{28,24},{1,5},{5... | collective-permute-start | bytes 6684680 | tf_op jit(solution)/shard_map/ppermute | solution.py:446
  15.6 53.5 %collective-permute-start = (bf16[256,4352]{1,0:T(8,128)(2,1)S(1)}, bf16[256,4352]{1,0:T(8,128)(2,1)}, u32[]{:S(2)}, u32[]{:S(2)}) collective-permute-start(bf16[256,4352]{1,0:T(8,128)(2,1)S(1)} %pad_maximum_fusion.2.refs_0_), channel_id=1, source_target_pairs={{0,8},{4,12},{8,0},{12,4},{16,24},{20,28},{24,16},{28,20},{1,9},{5... | collective-permute-start | bytes 6684680 | tf_op jit(solution)/shard_map/ppermute | solution.py:446
  17.9 185.9 %all-gather.13.cloned.1.call-start = ((), (), s32[]{:S(2)}) async-start(), calls=%async_computation.9 | async-start | bytes 6488064 | tf_op jit(solution)/shard_map/all_gather | solution.py:435
  20.1 50.2 %copy-start.32 = (f32[16,512]{1,0:T(8,128)}, f32[16,512]{1,0:T(8,128)S(1)}, u32[]{:S(2)}) copy-start(f32[16,512]{1,0:T(8,128)S(1)} %get-tuple-element.214) | copy-start | bytes 98308
  20.1 50.2 %copy-start.34 = (f32[16,512]{1,0:T(8,128)}, f32[16,512]{1,0:T(8,128)S(1)}, u32[]{:S(2)}) copy-start(f32[16,512]{1,0:T(8,128)S(1)} %get-tuple-element.215) | copy-start | bytes 98308
  20.8 52.2 %copy-start.58 = (f32[16,8,128]{2,1,0:T(8,128)}, f32[16,8,128]{2,1,0:T(8,128)S(1)}, u32[]{:S(2)}) copy-start(f32[16,8,128]{2,1,0:T(8,128)S(1)} %get-tuple-element.227.refs_8_) | copy-start | bytes 196612
  20.9 49.4 %copy-start.41 = (f32[64,8,128]{2,1,0:T(8,128)}, f32[64,8,128]{2,1,0:T(8,128)S(1)}, u32[]{:S(2)}) copy-start(f32[64,8,128]{2,1,0:T(8,128)S(1)} %get-tuple-element.257) | copy-start | bytes 786436
  66.7 33.1 %collective-permute-start.17 = (bf16[256,2816]{1,0:T(8,128)(2,1)}, bf16[256,2816]{1,0:T(8,128)(2,1)}, u32[]{:S(2)}, u32[]{:S(2)}) collective-permute-start(bf16[256,2816]{1,0:T(8,128)(2,1)} %slice.356), channel_id=1, source_target_pairs={{0,8},{4,12},{8,0},{12,4},{16,24},{20,28},{24,16},{28,20},{1,9},{5... | collective-permute-start | bytes 4325384 | tf_op jit(solution)/shard_map/ppermute | solution.py:446
  69.1 39.3 %collective-permute-start.5 = (bf16[256,4352]{1,0:T(8,128)(2,1)}, bf16[256,4352]{1,0:T(8,128)(2,1)}, u32[]{:S(2)}, u32[]{:S(2)}) collective-permute-start(bf16[256,4352]{1,0:T(8,128)(2,1)} %collective-permute-done.1.refs_2_), channel_id=1, source_target_pairs={{0,4},{4,0},{8,12},{12,8},{16,20},{20,16},{24,28},{28,24},{1,5},{5... | collective-permute-start | bytes 6684680 | tf_op jit(solution)/shard_map/ppermute | solution.py:446
  69.1 39.3 %collective-permute-start.4 = (bf16[256,4352]{1,0:T(8,128)(2,1)}, bf16[256,4352]{1,0:T(8,128)(2,1)}, u32[]{:S(2)}, u32[]{:S(2)}) collective-permute-start(bf16[256,4352]{1,0:T(8,128)(2,1)} %collective-permute-done.refs_1_), channel_id=1, source_target_pairs={{0,4},{4,0},{8,12},{12,8},{16,20},{20,16},{24,28},{28,24},{1,5},{5... | collective-permute-start | bytes 6684680 | tf_op jit(solution)/shard_map/ppermute | solution.py:446
  73.0 19.5 %collective-permute-start.2 = (bf16[256,1536]{1,0:T(8,128)(2,1)S(1)}, bf16[256,1536]{1,0:T(8,128)(2,1)S(1)}, u32[]{:S(2)}, u32[]{:S(2)}) collective-permute-start(bf16[256,1536]{1,0:T(8,128)(2,1)S(1)} %slice.343), channel_id=1, source_target_pairs={{0,16},{4,20},{8,24},{12,28},{16,0},{20,4},{24,8},{28,12},{1,17},{... | collective-permute-start | bytes 2359304 | tf_op jit(solution)/shard_map/ppermute | solution.py:446
  77.1 37.7 %copy-start.38 = (f32[64,8,128]{2,1,0:T(8,128)}, f32[64,8,128]{2,1,0:T(8,128)S(1)}, u32[]{:S(2)}) copy-start(f32[64,8,128]{2,1,0:T(8,128)S(1)} %constant_dynamic-update-slice_fusion.6.refs_6_) | copy-start | bytes 786436
  103.2 148.5 %all-gather.11.cloned.1.call-start = ((), (), s32[]{:S(2)}) async-start(), calls=%async_computation.8 | async-start | bytes 2621440 | tf_op jit(solution)/shard_map/all_gather | solution.py:435
  105.0 3.3 collective-permute-start.6
  116.1 102.2 %copy-start.12 = (bf16[256,2048]{1,0:T(8,128)(2,1)}, bf16[256,2048]{1,0:T(8,128)(2,1)S(1)}, u32[]{:S(2)}) copy-start(bf16[256,2048]{1,0:T(8,128)(2,1)S(1)} %slice.351.refs_0_) | copy-start | bytes 3145732
  116.1 40.7 %collective-permute-start.9 = (bf16[256,2048]{1,0:T(8,128)(2,1)S(1)}, bf16[256,2048]{1,0:T(8,128)(2,1)S(1)}, u32[]{:S(2)}, u32[]{:S(2)}) collective-permute-start(bf16[256,2048]{1,0:T(8,128)(2,1)S(1)} %slice.351.refs_0_), channel_id=1, source_target_pairs={{0,16},{4,20},{8,24},{12,28},{16,0},{20,4},{24,8},{28,12},{1,17},{... | collective-permute-start | bytes 3145736 | tf_op jit(solution)/shard_map/ppermute | solution.py:446
  117.6 39.7 %collective-permute-start.8 = (bf16[256,2048]{1,0:T(8,128)(2,1)S(1)}, bf16[256,2048]{1,0:T(8,128)(2,1)S(1)}, u32[]{:S(2)}, u32[]{:S(2)}) collective-permute-start(bf16[256,2048]{1,0:T(8,128)(2,1)S(1)} %slice.351.refs_0_), channel_id=1, source_target_pairs={{0,8},{4,12},{8,0},{12,4},{16,24},{20,28},{24,16},{28,20},{1,9},{5... | collective-permute-start | bytes 3145736 | tf_op jit(solution)/shard_map/ppermute | solution.py:446
  134.4 3.7 collective-permute-start.7
  156.8 63.4 %copy-start.16 = (bf16[256,2048]{1,0:T(8,128)(2,1)}, bf16[256,2048]{1,0:T(8,128)(2,1)S(1)}, u32[]{:S(2)}) copy-start(bf16[256,2048]{1,0:T(8,128)(2,1)S(1)} %collective-permute-done.9.refs_2_) | copy-start | bytes 3145732
  157.3 62.9 %copy-start.17 = (bf16[256,2048]{1,0:T(8,128)(2,1)}, bf16[256,2048]{1,0:T(8,128)(2,1)S(1)}, u32[]{:S(2)}) copy-start(bf16[256,2048]{1,0:T(8,128)(2,1)S(1)} %collective-permute-done.8.refs_1_) | copy-start | bytes 3145732
  192.1 120.8 %all-gather.15.cloned.1.call-start = ((), (), s32[]{:S(2)}) async-start(), calls=%async_computation.12 | async-start | bytes 2621440 | tf_op jit(solution)/shard_map/all_gather | solution.py:435
  192.7 28.1 %collective-permute-start.18 = (bf16[256,2816]{1,0:T(8,128)(2,1)}, bf16[256,2816]{1,0:T(8,128)(2,1)}, u32[]{:S(2)}, u32[]{:S(2)}) collective-permute-start(bf16[256,2816]{1,0:T(8,128)(2,1)} %collective-permute-done.17.refs_3_), channel_id=1, source_target_pairs={{0,4},{4,0},{8,12},{12,8},{16,20},{20,16},{24,28},{28,24},{1,5},{5... | collective-permute-start | bytes 4325384 | tf_op jit(solution)/shard_map/ppermute | solution.py:446
  218.2 126.2 %all-gather.19.cloned.1.call-start = ((), (), s32[]{:S(2)}) async-start(), calls=%async_computation.19 | async-start | bytes 2621440 | tf_op jit(solution)/shard_map/all_gather | solution.py:435
  218.3 25.5 %collective-permute-start.12 = (bf16[256,2048]{1,0:T(8,128)(2,1)S(1)}, bf16[256,2048]{1,0:T(8,128)(2,1)}, u32[]{:S(2)}, u32[]{:S(2)}) collective-permute-start(bf16[256,2048]{1,0:T(8,128)(2,1)S(1)} %slice.351.refs_0_), channel_id=1, source_target_pairs={{0,4},{4,0},{8,12},{12,8},{16,20},{20,16},{24,28},{28,24},{1,5},{5... | collective-permute-start | bytes 3145736 | tf_op jit(solution)/shard_map/ppermute | solution.py:446
  218.6 14.3 %collective-permute-start.11 = (bf16[256,1024]{1,0:T(8,128)(2,1)S(1)}, bf16[256,1024]{1,0:T(8,128)(2,1)}, u32[]{:S(2)}, u32[]{:S(2)}) collective-permute-start(bf16[256,1024]{1,0:T(8,128)(2,1)S(1)} %slice.355), channel_id=1, source_target_pairs={{0,8},{4,12},{8,0},{12,4},{16,24},{20,28},{24,16},{28,20},{1,9},{5... | collective-permute-start | bytes 1572872 | tf_op jit(solution)/shard_map/ppermute | solution.py:446
  220.2 23.6 %collective-permute-start.14 = (bf16[256,2048]{1,0:T(8,128)(2,1)S(1)}, bf16[256,2048]{1,0:T(8,128)(2,1)}, u32[]{:S(2)}, u32[]{:S(2)}) collective-permute-start(bf16[256,2048]{1,0:T(8,128)(2,1)S(1)} %collective-permute-done.9.refs_2_), channel_id=1, source_target_pairs={{0,4},{4,0},{8,12},{12,8},{16,20},{20,16},{24,28},{28,24},{1,5},{5... | collective-permute-start | bytes 3145736 | tf_op jit(solution)/shard_map/ppermute | solution.py:446
  220.3 23.5 %collective-permute-start.13 = (bf16[256,2048]{1,0:T(8,128)(2,1)S(1)}, bf16[256,2048]{1,0:T(8,128)(2,1)}, u32[]{:S(2)}, u32[]{:S(2)}) collective-permute-start(bf16[256,2048]{1,0:T(8,128)(2,1)S(1)} %collective-permute-done.8.refs_1_), channel_id=1, source_target_pairs={{0,4},{4,0},{8,12},{12,8},{16,20},{20,16},{24,28},{28,24},{1,5},{5... | collective-permute-start | bytes 3145736 | tf_op jit(solution)/shard_map/ppermute | solution.py:446
  220.9 14.0 %collective-permute-start.10 = (bf16[256,1024]{1,0:T(8,128)(2,1)S(1)}, bf16[256,1024]{1,0:T(8,128)(2,1)}, u32[]{:S(2)}, u32[]{:S(2)}) collective-permute-start(bf16[256,1024]{1,0:T(8,128)(2,1)S(1)} %slice.354), channel_id=1, source_target_pairs={{0,16},{4,20},{8,24},{12,28},{16,0},{20,4},{24,8},{28,12},{1,17},{... | collective-permute-start | bytes 1572872 | tf_op jit(solution)/shard_map/ppermute | solution.py:446
  232.9 10.9 %collective-permute-start.16 = (bf16[256,1024]{1,0:T(8,128)(2,1)}, bf16[256,1024]{1,0:T(8,128)(2,1)}, u32[]{:S(2)}, u32[]{:S(2)}) collective-permute-start(bf16[256,1024]{1,0:T(8,128)(2,1)} %collective-permute-done.11.refs_4_), channel_id=1, source_target_pairs={{0,4},{4,0},{8,12},{12,8},{16,20},{20,16},{24,28},{28,24},{1,5},{5... | collective-permute-start | bytes 1572872 | tf_op jit(solution)/shard_map/ppermute | solution.py:446
  234.9 9.0 %collective-permute-start.15 = (bf16[256,1024]{1,0:T(8,128)(2,1)}, bf16[256,1024]{1,0:T(8,128)(2,1)}, u32[]{:S(2)}, u32[]{:S(2)}) collective-permute-start(bf16[256,1024]{1,0:T(8,128)(2,1)} %collective-permute-done.10.refs_3_), channel_id=1, source_target_pairs={{0,4},{4,0},{8,12},{12,8},{16,20},{20,16},{24,28},{28,24},{1,5},{5... | collective-permute-start | bytes 1572872 | tf_op jit(solution)/shard_map/ppermute | solution.py:446
  266.3 152.8 %reduce-scatter.10.cloned.1.call-start = ((), (), s32[]{:S(2)}) async-start(), calls=%async_computation.11 | async-start | bytes 2621440 | tf_op jit(solution)/shard_map/reduce_scatter | solution.py:439
  312.9 136.5 %reduce-scatter.12.cloned.1.call-start = ((), (), s32[]{:S(2)}) async-start(), calls=%async_computation.13 | async-start | bytes 2621440 | tf_op jit(solution)/shard_map/reduce_scatter | solution.py:439
  390.3 22.1 %collective-permute-start.19 = (bf16[1024,1408]{1,0:T(8,128)(2,1)}, bf16[1024,1408]{1,0:T(8,128)(2,1)S(1)}, u32[]{:S(2)}, u32[]{:S(2)}) collective-permute-start(bf16[1024,1408]{1,0:T(8,128)(2,1)} %get-tuple-element.55.refs_8_), channel_id=1, source_target_pairs={{0,4},{4,0},{8,12},{12,8},{16,20},{20,16},{24,28},{28,24},{1,5},{5... | collective-permute-start | bytes 8650760 | tf_op jit(solution)/shard_map/ppermute | solution.py:446
  405.7 31.5 %collective-permute-start.20 = (bf16[1024,2048]{1,0:T(8,128)(2,1)}, bf16[1024,2048]{1,0:T(8,128)(2,1)}, u32[]{:S(2)}, u32[]{:S(2)}) collective-permute-start(bf16[1024,2048]{1,0:T(8,128)(2,1)} %get-tuple-element.57.refs_10_), channel_id=1, source_target_pairs={{0,4},{4,0},{8,12},{12,8},{16,20},{20,16},{24,28},{28,24},{1,5},{5... | collective-permute-start | bytes 12582920 | tf_op jit(solution)/shard_map/ppermute | solution.py:446
  406.2 327.0 %reduce-scatter.20.cloned.1.call-start = ((), (), s32[]{:S(2)}) async-start(), calls=%async_computation.17 | async-start | bytes 1310720 | tf_op jit(solution)/shard_map/reduce_scatter | solution.py:439
  417.8 18.3 %collective-permute-start.21 = (bf16[256,1408]{1,0:T(8,128)(2,1)}, bf16[256,1408]{1,0:T(8,128)(2,1)}, u32[]{:S(2)}, u32[]{:S(2)}) collective-permute-start(bf16[256,1408]{1,0:T(8,128)(2,1)} %dynamic-slice_bitcast_fusion.2), channel_id=1, source_target_pairs={{0,16},{4,20},{8,24},{12,28},{16,0},{20,4},{24,8},{28,12},{1,17},{... | collective-permute-start | bytes 2162696 | tf_op jit(solution)/shard_map/ppermute | solution.py:446
  443.5 24.2 %collective-permute-start.22 = (bf16[256,2048]{1,0:T(8,128)(2,1)S(1)}, bf16[256,2048]{1,0:T(8,128)(2,1)S(1)}, u32[]{:S(2)}, u32[]{:S(2)}) collective-permute-start(bf16[256,2048]{1,0:T(8,128)(2,1)S(1)} %dynamic-slice_bitcast_fusion.1), channel_id=1, source_target_pairs={{0,8},{4,12},{8,0},{12,4},{16,24},{20,28},{24,16},{28,20},{1,9},{5... | collective-permute-start | bytes 3145736 | tf_op jit(solution)/shard_map/ppermute | solution.py:446
  483.8 25.6 %collective-permute-start.36 = (bf16[256,2048]{1,0:T(8,128)(2,1)}, bf16[256,2048]{1,0:T(8,128)(2,1)S(1)}, u32[]{:S(2)}, u32[]{:S(2)}) collective-permute-start(bf16[256,2048]{1,0:T(8,128)(2,1)} %fusion.34), channel_id=1, source_target_pairs={{0,8},{4,12},{8,0},{12,4},{16,24},{20,28},{24,16},{28,20},{1,9},{5... | collective-permute-start | bytes 3145736 | tf_op jit(solution)/shard_map/ppermute | solution.py:446
  485.8 25.2 %collective-permute-start.37 = (bf16[256,2048]{1,0:T(8,128)(2,1)S(1)}, bf16[256,2048]{1,0:T(8,128)(2,1)S(1)}, u32[]{:S(2)}, u32[]{:S(2)}) collective-permute-start(bf16[256,2048]{1,0:T(8,128)(2,1)S(1)} %fusion.26), channel_id=1, source_target_pairs={{0,16},{4,20},{8,24},{12,28},{16,0},{20,4},{24,8},{28,12},{1,17},{... | collective-permute-start | bytes 3145736 | tf_op jit(solution)/shard_map/ppermute | solution.py:446
  512.6 232.1 %reduce-scatter.14.cloned.1.call-start = ((), (), s32[]{:S(2)}) async-start(), calls=%async_computation.14 | async-start | bytes 2621440 | tf_op jit(solution)/shard_map/reduce_scatter | solution.py:439
  512.7 21.7 %collective-permute-start.23 = (bf16[1024,2816]{1,0:T(8,128)(2,1)}, bf16[1024,2816]{1,0:T(8,128)(2,1)}, u32[]{:S(2)}, u32[]{:S(2)}) collective-permute-start(bf16[1024,2816]{1,0:T(8,128)(2,1)} %get-tuple-element.64.refs_18_), channel_id=1, source_target_pairs={{0,4},{4,0},{8,12},{12,8},{16,20},{20,16},{24,28},{28,24},{1,5},{5... | collective-permute-start | bytes 17301512 | tf_op jit(solution)/shard_map/ppermute | solution.py:446
  520.1 227.0 %reduce-scatter.8.cloned.1.call-start = ((), (), s32[]{:S(2)}) async-start(), calls=%async_computation.10 | async-start | bytes 2621440 | tf_op jit(solution)/shard_map/reduce_scatter | solution.py:439
  534.3 216.4 %reduce-scatter.16.cloned.1.call-start = ((), (), s32[]{:S(2)}) async-start(), calls=%async_computation.15 | async-start | bytes 2621440 | tf_op jit(solution)/shard_map/reduce_scatter | solution.py:439
  534.4 59.3 %slice-start = ((s8[5242880]{0:T(1024)(128)(4,1)}), s8[4194304]{0:T(1024)(128)(4,1)S(1)}, s32[]{:S(2)}) async-start(s8[5242880]{0:T(1024)(128)(4,1)} %bitcast.201), calls=%async_computation.20 | async-start | bytes 8388608
  545.3 43.7 %collective-permute-start.24 = (bf16[256,2816]{1,0:T(8,128)(2,1)}, bf16[256,2816]{1,0:T(8,128)(2,1)S(1)}, u32[]{:S(2)}, u32[]{:S(2)}) collective-permute-start(bf16[256,2816]{1,0:T(8,128)(2,1)} %dynamic-slice_bitcast_fusion), channel_id=1, source_target_pairs={{0,8},{4,12},{8,0},{12,4},{16,24},{20,28},{24,16},{28,20},{1,9},{5... | collective-permute-start | bytes 4325384 | tf_op jit(solution)/shard_map/ppermute | solution.py:446
  545.7 48.0 %slice-start.1 = ((s8[5242880]{0:T(1024)(128)(4,1)}), s8[1048576]{0:T(1024)(128)(4,1)S(1)}, s32[]{:S(2)}) async-start(s8[5242880]{0:T(1024)(128)(4,1)} %bitcast.201), calls=%async_computation.21 | async-start | bytes 2097152
  577.9 6.6 collective-permute-start.25
  581.3 147.2 %collective-permute-start.39 = (bf16[256,1408]{1,0:T(8,128)(2,1)}, bf16[256,1408]{1,0:T(8,128)(2,1)}, u32[]{:S(2)}, u32[]{:S(2)}) collective-permute-start(bf16[256,1408]{1,0:T(8,128)(2,1)} %fusion.36), channel_id=1, source_target_pairs={{0,16},{4,20},{8,24},{12,28},{16,0},{20,4},{24,8},{28,12},{1,17},{... | collective-permute-start | bytes 2162696 | tf_op jit(solution)/shard_map/ppermute | solution.py:446
  588.5 49.9 %collective-permute-start.26 = (bf16[256,2816]{1,0:T(8,128)(2,1)}, bf16[256,2816]{1,0:T(8,128)(2,1)S(1)}, u32[]{:S(2)}, u32[]{:S(2)}) collective-permute-start(bf16[256,2816]{1,0:T(8,128)(2,1)} %fusion.29.refs_19_), channel_id=1, source_target_pairs={{0,8},{4,12},{8,0},{12,4},{16,24},{20,28},{24,16},{28,20},{1,9},{5... | collective-permute-start | bytes 4325384 | tf_op jit(solution)/shard_map/ppermute | solution.py:446
  593.1 45.2 %collective-permute-start.27 = (bf16[256,2816]{1,0:T(8,128)(2,1)}, bf16[256,2816]{1,0:T(8,128)(2,1)S(1)}, u32[]{:S(2)}, u32[]{:S(2)}) collective-permute-start(bf16[256,2816]{1,0:T(8,128)(2,1)} %fusion.22.refs_20_), channel_id=1, source_target_pairs={{0,16},{4,20},{8,24},{12,28},{16,0},{20,4},{24,8},{28,12},{1,17},{... | collective-permute-start | bytes 4325384 | tf_op jit(solution)/shard_map/ppermute | solution.py:446
  635.2 115.4 %reduce-scatter.18.cloned.1.call-start = ((), (), s32[]{:S(2)}) async-start(), calls=%async_computation.16 | async-start | bytes 2621440 | tf_op jit(solution)/shard_map/reduce_scatter | solution.py:439
  636.1 6.9 collective-permute-start.28
  656.7 39.2 %collective-permute-start.29 = (bf16[1024,1536]{1,0:T(8,128)(2,1)}, bf16[1024,1536]{1,0:T(8,128)(2,1)S(1)}, u32[]{:S(2)}, u32[]{:S(2)}) collective-permute-start(bf16[1024,1536]{1,0:T(8,128)(2,1)} %get-tuple-element.76), channel_id=1, source_target_pairs={{0,4},{4,0},{8,12},{12,8},{16,20},{20,16},{24,28},{28,24},{1,5},{5... | collective-permute-start | bytes 9437192 | tf_op jit(solution)/shard_map/ppermute | solution.py:446
  669.8 5.1 collective-permute-start.31
  671.1 5.8 collective-permute-start.30
  671.7 5.2 collective-permute-start.32
  702.2 20.7 %collective-permute-start.33 = (bf16[256,1536]{1,0:T(8,128)(2,1)}, bf16[256,1536]{1,0:T(8,128)(2,1)}, u32[]{:S(2)}, u32[]{:S(2)}) collective-permute-start(bf16[256,1536]{1,0:T(8,128)(2,1)} %add_bitcast_fusion), channel_id=1, source_target_pairs={{0,16},{4,20},{8,24},{12,28},{16,0},{20,4},{24,8},{28,12},{1,17},{... | collective-permute-start | bytes 2359304 | tf_op jit(solution)/shard_map/ppermute | solution.py:446
  706.0 22.5 %collective-permute-start.38 = (bf16[256,1408]{1,0:T(8,128)(2,1)}, bf16[256,1408]{1,0:T(8,128)(2,1)}, u32[]{:S(2)}, u32[]{:S(2)}) collective-permute-start(bf16[256,1408]{1,0:T(8,128)(2,1)} %fusion.33), channel_id=1, source_target_pairs={{0,8},{4,12},{8,0},{12,4},{16,24},{20,28},{24,16},{28,20},{1,9},{5... | collective-permute-start | bytes 2162696 | tf_op jit(solution)/shard_map/ppermute | solution.py:446
  711.4 41.6 %collective-permute-start.35 = (bf16[256,1536]{1,0:T(8,128)(2,1)}, bf16[256,1536]{1,0:T(8,128)(2,1)}, u32[]{:S(2)}, u32[]{:S(2)}) collective-permute-start(bf16[256,1536]{1,0:T(8,128)(2,1)} %fusion.35), channel_id=1, source_target_pairs={{0,16},{4,20},{8,24},{12,28},{16,0},{20,4},{24,8},{28,12},{1,17},{... | collective-permute-start | bytes 2359304 | tf_op jit(solution)/shard_map/ppermute | solution.py:446
  727.1 25.8 %collective-permute-start.34 = (bf16[256,1536]{1,0:T(8,128)(2,1)}, bf16[256,1536]{1,0:T(8,128)(2,1)}, u32[]{:S(2)}, u32[]{:S(2)}) collective-permute-start(bf16[256,1536]{1,0:T(8,128)(2,1)} %fusion.28), channel_id=1, source_target_pairs={{0,8},{4,12},{8,0},{12,4},{16,24},{20,28},{24,16},{28,20},{1,9},{5... | collective-permute-start | bytes 2359304 | tf_op jit(solution)/shard_map/ppermute | solution.py:446
  (72 other events, 679.9 us)
Sparse Core Ops, SparseCore 0:
  10.9 100.7 all-gather.8
  113.8 44.2 all-gather.16
  160.0 43.6 all-gather.12
  205.8 45.9 all-gather.10
  253.2 44.6 all-gather.14
  299.8 44.6 all-gather.18
  346.8 42.9 reduce-scatter.9
  406.4 42.9 reduce-scatter.11
  512.7 25.0 reduce-scatter.19
  540.1 42.5 reduce-scatter.13
  584.9 43.1 reduce-scatter.7
  635.4 43.2 reduce-scatter.15
  696.0 43.9 reduce-scatter.17

commit v5 on v4

--- a/solution.py
+++ b/solution.py
@@ -518,18 +518,21 @@
 
 def halves_kernel(micros, core_ref, *refs):
     lefts, rights, send_ref, keep_ref = refs[:micros], refs[micros : 2 * micros], refs[-2], refs[-1]
-    total = None
-    for left, right in zip(lefts, rights):
-        part = lax.dot_general(left[...], right[...], (((0,), (0,)), ((), ())), preferred_element_type=F32)
-        total = part if total is None else total + part
-
-    @pl.when(pl.program_id(0) < 4)
-    def _():
-        send_ref[...] = total.astype(BF)
-
-    @pl.when(pl.program_id(0) >= 4)
-    def _():
-        keep_ref[...] = total.astype(BF)
+    rows, width = send_ref.shape
+
+    def into(out_ref):
+        for start in range(0, width, 512):
+            lanes = slice(start, min(start + 512, width))
+            total = None
+            for left, right in zip(lefts, rights):
+                part = lax.dot_general(
+                    left[...], right[:, lanes], (((0,), (0,)), ((), ())), preferred_element_type=F32
+                )
+                total = part if total is None else total + part
+            out_ref[:, lanes] = total.astype(BF)
+
+    pl.when(pl.program_id(0) < 4)(lambda: into(send_ref))
+    pl.when(pl.program_id(0) >= 4)(lambda: into(keep_ref))
 
 
 def grad_halves(lefts, rights, name, after=()):
@@ -732,8 +735,8 @@
     def each(name):
         return [c[name] for c in kept]
 
-    down_halves = grad_halves(cot_full, each("act"), "grad_down", order)
     out_halves = grad_halves(each("d_low"), each("mixed"), "grad_out", order)
+    down_halves = grad_halves(cot_full, each("act"), "grad_down", out_halves)
     down_chip, out_chip = grad_chip(down_halves), grad_chip(out_halves)
     down_far, out_far = grad_far(down_chip, Y), grad_far(out_chip, X)
     adjoints, ends = zip(*[
@@ -742,7 +745,7 @@
              (down_chip, out_chip) if m else (*down_halves, *out_halves))
         for m in range(micros)
     ])
-    ends = lax.all_gather(tied(jnp.stack(ends), down_far, out_far).astype(BF), "seq").astype(F32)
+    ends = lax.all_gather(tied(jnp.stack(ends), down_far).astype(BF), "seq").astype(F32)
     gu_halves = grad_halves(each("h_mlp"), each("d_gu"), "grad_gu", (ends,))
     gu_chip = grad_chip(gu_halves)
     gu_far = grad_far(gu_chip, X)

time: 777 us -> 773 us (level)
  waiting for transfers between devices: 132 us -> 122 us
    all_gather x1, blocking collectives: 9.94 us -> 18 us  [shards(): lax.all_gather(tied(jnp.stack(ends), down_far).astype(BF), 'seq')]
  transfers between devices with their start and end apart: 53 -> 53, of which waited for: 14 -> 14; matrix products, arithmetic and copies ran while one was open for 37% -> 38% of each run, Pallas kernels for 27% -> 27%
where the time goes in v5:
time: 773 us; the launch traced here: 762 us
  Pallas kernels  207 us (27%)
  matrix products  132 us (17%)
  waiting for transfers between devices  122 us (16%)
  other arithmetic  110 us (14%)
  local copies, waits for them, and re-layouts  78.6 us (10%)
  blocking collectives  43.7 us (6%)
  starting transfers between devices  41.9 us (5%)
  between operations  26.8 us (3%)
    dot_general x15, matrix products, dot(): return lax.dot_general(a, b, (dims, ((), ())), preferred_element_type=F32)  132 us
    pallas_call x8, Pallas kernels, call(): pl.pallas_call(without, out_shape=[jax.ShapeDtypeStruct(s, d) for s, d in...  127 us
    ppermute x34, waiting for transfers between devices, over(): return lax.ppermute(value, 'seq', [(i, i ^ bit) for i in range(8)])  98.6 us
    pallas_call x4, Pallas kernels, grad_halves(): pl.pallas_call(functools.partial(halves_kernel, n), out_shape=[jax.ShapeD...  58.7 us
    ppermute x34, starting transfers between devices, over(): return lax.ppermute(value, 'seq', [(i, i ^ bit) for i in range(8)])  32 us
    unnamed x188, local copies, waits for them, and re-layouts  31.8 us
    pallas_call x3, Pallas kernels, place(): pl.pallas_call(functools.partial(place_kernel, plan, count), out_shape=ja...  20.9 us
    all_gather x6, waiting for transfers between devices, gather(): return lax.all_gather(block, axis, axis=dim, tiled=True)  20.1 us
  transfers between devices with their start and end apart: 53, of which 14 were waited for; matrix products, arithmetic and copies ran while one was open for 38% of the time, Pallas kernels for 27%

profile of v5, /device:TPU:0, one launch (start us, length us, event | category | flops | bytes accessed | tf_op | source)
XLA Modules:
  0.0 761.8 jit_solution(2729552641755966671)
XLA Ops:
  12.5 3.0 collective-permute-start.1
  21.5 42.6 %collective-permute-done.1.refs_2_ = bf16[256,4352]{1,0:T(8,128)(2,1)} collective-permute-done((bf16[256,4352]{1,0:T(8,128)(2,1)S(1)}, bf16[256,4352]{1,0:T(8,128)(2,1)}, u32[]{:S(2)}, u32[]{:S(2)}) %collective-permute-start.1) | collective-permute-done | bytes 2228256 | tf_op jit(solution)/shard_map/ppermute | solution.py:446
  64.1 2.6 slice.352
  77.8 14.7 %collective-permute-done.2.refs_3_ = bf16[256,1536]{1,0:T(8,128)(2,1)S(1)} collective-permute-done((bf16[256,1536]{1,0:T(8,128)(2,1)S(1)}, bf16[256,1536]{1,0:T(8,128)(2,1)S(1)}, u32[]{:S(2)}, u32[]{:S(2)}) %collective-permute-start.2) | collective-permute-done | bytes 786464 | tf_op jit(solution)/shard_map/ppermute | solution.py:446
  93.9 5.9 collective-permute-done.17.refs_3_
  109.4 5.5 place_in.1
  119.2 3.3 multiply_reduce_fusion
  122.6 3.4 slice_convert_fusion
  127.6 6.9 fusion.18
  139.0 8.9 %mixer_front.2 = (f32[4096,128]{1,0:T(8,128)}, f32[16,8,128]{2,1,0:T(8,128)}) custom-call(f32[520]{0:T(1024)} %get-tuple-element.158.refs_0_, s32[65]{0:T(128)} %get-tuple-element.238.refs_1_, bf16[512,1536]{1,0:T(8,128)(2,1)} %get-tuple-element.194.refs_2_.refs_4_, f32[8,1536]{1,0:T(8,128)} %get-tuple-element.202.refs_3_.refs_5_, ...), custom_call_target="tpu_custom_call" | custom-call | flops 13421772800 | bytes 4084260 | tf_op jit(solution)/shard_map/mixer_front/pallas_call | solution.py:387
  147.9 9.0 %mixer_front.3 = (f32[4096,128]{1,0:T(8,128)}, f32[16,8,128]{2,1,0:T(8,128)}) custom-call(f32[520]{0:T(1024)} %get-tuple-element.159.refs_0_, s32[65]{0:T(128)} %get-tuple-element.239.refs_1_, bf16[512,1536]{1,0:T(8,128)(2,1)} %get-tuple-element.195.refs_2_.refs_4_, f32[8,1536]{1,0:T(8,128)} %get-tuple-element.203.refs_3_.refs_5_, ...), custom_call_target="tpu_custom_call" | custom-call | flops 13421772800 | bytes 4084260 | tf_op jit(solution)/shard_map/mixer_front/pallas_call | solution.py:387
  160.2 16.1 %all_gather.31 = bf16[8,2,16,8,128]{4,3,2,1,0:T(8,128)(2,1)S(1)} all-gather(bf16[1,2,16,8,128]{4,3,2,1,0:T(8,128)(2,1)S(1)} %fusion.43), channel_id=1, replica_groups=mesh['seq'=8,'tp'=4] {'seq'}, dimensions={0}, use_global_device_ids=true | all-gather | bytes 589824 | tf_op jit(solution)/shard_map/all_gather | solution.py:688
  177.3 14.8 %mixer_finish.2 = (bf16[512,512]{1,0:T(8,128)(2,1)}, f32[512,512]{1,0:T(8,128)}, f32[8,16,8,128]{3,2,1,0:T(8,128)}) custom-call(f32[520]{0:T(1024)} %get-tuple-element.158.refs_0_, s32[65]{0:T(128)} %get-tuple-element.238.refs_1_, f32[8]{0:T(128)} %compare_convert_fusion.4.refs_2_, s32[1]{0:T(128)} %bitcast.5.me_ref.refs_3_, ...), custom_call_target="tpu_custom_call" | custom-call | flops 16777216000 | bytes 7101000 | tf_op jit(solution)/shard_map/mixer_finish/pallas_call | solution.py:387
  193.1 10.8 %all-gather.13.cloned.1.call-done.refs_15_ = bf16[2048,1408]{1,0:T(8,128)(2,1)} async-done(((bf16[256,1408]{1,0:T(8,128)(2,1)}), bf16[2048,1408]{1,0:T(8,128)(2,1)}) %all-gather.13.cloned.1.call-update) | async-done | bytes 5767184 | tf_op jit(solution)/shard_map/all_gather | solution.py:435
  203.9 14.4 %mixer_finish.3 = (bf16[512,512]{1,0:T(8,128)(2,1)}, f32[512,512]{1,0:T(8,128)}, f32[8,16,8,128]{3,2,1,0:T(8,128)}) custom-call(f32[520]{0:T(1024)} %get-tuple-element.159.refs_0_, s32[65]{0:T(128)} %get-tuple-element.239.refs_1_, f32[8]{0:T(128)} %compare_convert_fusion.2.refs_2_, s32[1]{0:T(128)} %bitcast.5.me_ref.refs_3_, ...), custom_call_target="tpu_custom_call" | custom-call | flops 16777216000 | bytes 7101000 | tf_op jit(solution)/shard_map/mixer_finish/pallas_call | solution.py:387
  221.5 11.4 %collective-permute-done.11.refs_4_ = bf16[256,1024]{1,0:T(8,128)(2,1)} collective-permute-done((bf16[256,1024]{1,0:T(8,128)(2,1)S(1)}, bf16[256,1024]{1,0:T(8,128)(2,1)}, u32[]{:S(2)}, u32[]{:S(2)}) %collective-permute-start.11) | collective-permute-done | bytes 524320 | tf_op jit(solution)/shard_map/ppermute | solution.py:446
  234.9 8.8 %place_gu.1 = bf16[2048,2816]{1,0:T(8,128)(2,1)} custom-call(s32[1]{0:T(128)} %bitcast.5.me_ref.refs_3_, bf16[256,4352]{1,0:T(8,128)(2,1)} %copy-done.3, bf16[256,4352]{1,0:T(8,128)(2,1)} %collective-permute-done.refs_1_, bf16[256,4352]{1,0:T(8,128)(2,1)} %collective-permute-done.1.refs_2_, bf16[256,2816]{1,0:T(8,128)(2,1)} %collective-permute-done.17.refs_3_, ...), custom_call_target="tpu_custom_call" | custom-call | bytes 23068672 | tf_op jit(solution)/shard_map/place_gu/pallas_call | solution.py:477
  243.7 6.5 place_out.1
  253.7 11.2 %multiply_reduce_fusion.6 = (f32[512]{0:T(512)S(1)}, f32[512,2048]{1,0:T(8,128)}) fusion(bf16[512,2048]{1,0:T(8,128)(2,1)} %all-gather.11.cloned.1.call-done.refs_2_, bf16[2048,2048]{1,0:T(8,128)(2,1)} %place_out.1, bf16[1280,2048]{1,0:T(8,128)(2,1)} %all-gather.9.cloned.1.call-done), kind=kOutput, calls=%fused_computation.42 | convolution fusion | flops 4299161088 | bytes 16779264 | tf_op jit(solution)/shard_map/dot_general | solution.py:623
  266.4 2.8 multiply_convert_fusion.2.refs_0_
  270.7 9.7 %fusion.78 = f32[512,2816]{1,0:T(8,128)S(1)} fusion(bf16[512,2048]{1,0:T(8,128)(2,1)S(1)} %multiply_convert_fusion.2.refs_0_, bf16[2048,2816]{1,0:T(8,128)(2,1)} %place_gu.1), kind=kOutput, calls=%fused_computation.250 | convolution fusion | flops 5905580032 | bytes 19398656 | tf_op jit(solution)/shard_map/dot_general | solution.py:623
  280.5 5.9 multiply_convert_fusion.7
  286.4 10.0 %multiply_reduce_fusion.2 = (f32[2048]{0:T(1024)}, f32[512]{0:T(512)}, f32[512,2048]{1,0:T(8,128)}) fusion(f32[512,2048]{1,0:T(8,128)S(1)} %copy-done, f32[512]{0:T(512)S(1)} %get-tuple-element.237, f32[2048]{0:T(1024)S(1)} %copy-done.44, bf16[2048,2816]{1,0:T(8,128)(2,1)S(1)} %bitcast.219, bf16[512,1408]{1,0:T(8,128)(2,1)} %get-tuple-element.189, ...), kind=kOutput, calls=%fused_computation.34 | convolution fusion | flops 5917636096 | bytes 22827008 | tf_op jit(solution)/shard_map/dot_general | solution.py:623
  297.1 4.6 fusion.71
  303.1 8.4 %convolution_convert_fusion.1 = bf16[512,2048]{1,0:T(8,128)(2,1)S(1)} fusion(bf16[512,2048]{1,0:T(8,128)(2,1)S(1)} %get-tuple-element.181.refs_0_, bf16[2048,2048]{1,0:T(8,128)(2,1)} %place_out.1), kind=kOutput, calls=%fused_computation.46 | convolution fusion | flops 4296015872 | bytes 12582912 | tf_op jit(solution)/shard_map/dot_general | solution.py:623
  313.1 9.3 %multiply_reduce_fusion.4 = (f32[512]{0:T(512)S(1)}, f32[512,2048]{1,0:T(8,128)S(1)}) fusion(bf16[512,2048]{1,0:T(8,128)(2,1)} %all-gather.15.cloned.1.call-done.refs_3_, bf16[2048,2048]{1,0:T(8,128)(2,1)} %place_out.1, f32[]{:T(128)} %bitcast.32, bf16[1280,2048]{1,0:T(8,128)(2,1)} %all-gather.9.cloned.1.call-done), kind=kOutput, calls=%fused_computation.38 | convolution fusion | flops 4300209664 | bytes 16779268 | tf_op jit(solution)/shard_map/dot_general | solution.py:623
  325.7 11.2 %fusion.79 = f32[512,2816]{1,0:T(8,128)} fusion(bf16[512,2048]{1,0:T(8,128)(2,1)S(1)} %multiply_convert_fusion.1.refs_1_, bf16[2048,2816]{1,0:T(8,128)(2,1)} %place_gu.1), kind=kOutput, calls=%fused_computation.251 | convolution fusion | flops 5905580032 | bytes 19398656 | tf_op jit(solution)/shard_map/dot_general | solution.py:623
  336.9 7.7 %all-gather.19.cloned.1.call-done = bf16[1,512,2048]{2,1,0:T(8,128)(2,1)} async-done(((bf16[1,512,512]{2,1,0:T(8,128)(2,1)}), bf16[1,512,2048]{2,1,0:T(8,128)(2,1)}) %all-gather.19.cloned.1.call-update) | async-done | bytes 2097168 | tf_op jit(solution)/shard_map/all_gather | solution.py:435
  344.6 11.4 %multiply_convert_fusion.4 = (bf16[512,1408]{1,0:T(8,128)(2,1)}, bf16[512,1408]{1,0:T(8,128)(2,1)}, bf16[512,1408]{1,0:T(8,128)(2,1)}) fusion(f32[512,2816]{1,0:T(8,128)} %fusion.79, bf16[2048,1408]{1,0:T(8,128)(2,1)} %all-gather.13.cloned.1.call-done.refs_15_, bf16[1,512,2048]{2,1,0:T(8,128)(2,1)} %all-gather.19.cloned.1.call-done), kind=kOutput, calls=%fused_computation.57 | convolution fusion | flops 2964324352 | bytes 17956864 | tf_op jit(solution)/shard_map/dot_general | solution.py:623
  356.0 10.5 %multiply_reduce_fusion.1 = (f32[2048]{0:T(1024)S(1)}, f32[512]{0:T(512)S(1)}, f32[512,2048]{1,0:T(8,128)S(1)}) fusion(f32[512,2048]{1,0:T(8,128)S(1)} %copy-done.2, f32[512]{0:T(512)S(1)} %get-tuple-element.235, f32[2048]{0:T(1024)S(1)} %copy-done.44, bf16[2048,2816]{1,0:T(8,128)(2,1)} %place_gu.1, bf16[512,1408]{1,0:T(8,128)(2,1)} %get-tuple-element.187, ...), kind=kOutput, calls=%fused_computation.33 | convolution fusion | flops 5917636096 | bytes 22827008 | tf_op jit(solution)/shard_map/dot_general | solution.py:623
  366.5 4.3 fusion.66
  372.1 5.8 convolution_convert_fusion.refs_4_
  377.9 14.8 %grad_out.1 = (bf16[1024,2048]{1,0:T(8,128)(2,1)}, bf16[1024,2048]{1,0:T(8,128)(2,1)}) custom-call(s32[1]{0:T(128)} %bitcast.26.core_ref, bf16[512,2048]{1,0:T(8,128)(2,1)} %copy-done.21, bf16[512,2048]{1,0:T(8,128)(2,1)} %copy-done.22, bf16[512,2048]{1,0:T(8,128)(2,1)} %all-gather.11.cloned.1.call-done.refs_2_, ...), custom_call_target="tpu_custom_call" | custom-call | flops 8589934592 | bytes 16777216 | tf_op jit(solution)/shard_map/grad_out/pallas_call | solution.py:544
  392.7 12.3 %grad_down.1 = (bf16[1024,1408]{1,0:T(8,128)(2,1)}, bf16[1024,1408]{1,0:T(8,128)(2,1)}) custom-call(s32[1]{0:T(128)} %bitcast.26.core_ref, bf16[512,2048]{1,0:T(8,128)(2,1)} %bitcast.233, bf16[512,2048]{1,0:T(8,128)(2,1)} %bitcast.234, bf16[512,1408]{1,0:T(8,128)(2,1)} %get-tuple-element.191.refs_2_, bf16[512,1408]{1,0:T(8,128)(2,1)} %get-tuple-element.190.refs_3_, ...), custom_call_target="tpu_custom_call" | custom-call | flops 5905580032 | bytes 12845056 | tf_op jit(solution)/shard_map/grad_down/pallas_call | solution.py:544
  406.2 3.7 pad_maximum_fusion.refs_2_
  415.6 2.5 add_convert_fusion.3
  420.6 8.8 %mixer_adjoint.2 = (f32[4096,128]{1,0:T(8,128)}, f32[16,8,128]{2,1,0:T(8,128)}) custom-call(f32[520]{0:T(1024)} %get-tuple-element.158.refs_0_, s32[65]{0:T(128)} %get-tuple-element.238.refs_1_, bf16[512,1536]{1,0:T(8,128)(2,1)} %get-tuple-element.194.refs_2_.refs_4_, f32[8,1536]{1,0:T(8,128)} %get-tuple-element.202.refs_3_.refs_5_, ...), custom_call_target="tpu_custom_call" | custom-call | flops 13421772800 | bytes 4608548 | tf_op jit(solution)/shard_map/mixer_adjoint/pallas_call | solution.py:387
  429.5 8.1 %collective-permute-done.21 = bf16[256,1408]{1,0:T(8,128)(2,1)} collective-permute-done((bf16[256,1408]{1,0:T(8,128)(2,1)}, bf16[256,1408]{1,0:T(8,128)(2,1)}, u32[]{:S(2)}, u32[]{:S(2)}) %collective-permute-start.21) | collective-permute-done | bytes 720928 | tf_op jit(solution)/shard_map/ppermute | solution.py:446
  439.5 4.1 add_convert_fusion.1
  448.3 8.9 %mixer_adjoint.3 = (f32[4096,128]{1,0:T(8,128)}, f32[16,8,128]{2,1,0:T(8,128)}) custom-call(f32[520]{0:T(1024)} %get-tuple-element.159.refs_0_, s32[65]{0:T(128)} %get-tuple-element.239.refs_1_, bf16[512,1536]{1,0:T(8,128)(2,1)} %get-tuple-element.195.refs_2_.refs_4_, f32[8,1536]{1,0:T(8,128)} %get-tuple-element.203.refs_3_.refs_5_, ...), custom_call_target="tpu_custom_call" | custom-call | flops 13421772800 | bytes 4608548 | tf_op jit(solution)/shard_map/mixer_adjoint/pallas_call | solution.py:387
  458.1 18.0 %all_gather.37 = bf16[8,2,16,8,128]{4,3,2,1,0:T(8,128)(2,1)S(1)} all-gather(bf16[1,2,16,8,128]{4,3,2,1,0:T(8,128)(2,1)S(1)} %fusion.44), channel_id=1, replica_groups=mesh['seq'=8,'tp'=4] {'seq'}, dimensions={0}, use_global_device_ids=true | all-gather | bytes 589824 | tf_op jit(solution)/shard_map/all_gather | solution.py:748
  482.9 19.1 %grad_gu.1 = (bf16[1024,2816]{1,0:T(8,128)(2,1)}, bf16[1024,2816]{1,0:T(8,128)(2,1)}) custom-call(s32[1]{0:T(128)} %bitcast.26.core_ref, bf16[512,2048]{1,0:T(8,128)(2,1)} %copy-done.19, bf16[512,2048]{1,0:T(8,128)(2,1)} %copy-done.20, bf16[512,2816]{1,0:T(8,128)(2,1)} %pad_maximum_fusion.refs_2_, bf16[512,2816]{1,0:T(8,128)(2,1)} %pad_maximum_fusion.1.refs_3_, ...), custom_call_target="tpu_custom_call" | custom-call | flops 11811160064 | bytes 21495808 | tf_op jit(solution)/shard_map/grad_gu/pallas_call | solution.py:544
  509.1 7.3 convolution_convert_fusion.2
  517.6 5.1 slice_bitcast_fusion
  522.7 7.3 convolution_convert_fusion.3
  530.2 8.4 %add_convert_fusion = bf16[1024,2816]{1,0:T(8,128)(2,1)} fusion(bf16[1024,2816]{1,0:T(8,128)(2,1)} %collective-permute-done.22, bf16[1024,2816]{1,0:T(8,128)(2,1)} %get-tuple-element.65.refs_19_), kind=kLoop, calls=%fused_computation | loop fusion | flops 11534336 | bytes 17301504 | tf_op jit(solution)/shard_map/convert_element_type | solution.py:574
  538.6 2.6 dynamic-slice_bitcast_fusion
  542.1 31.3 %mixer_back.2 = (bf16[512,1536]{1,0:T(8,128)(2,1)}, f32[8,1536]{1,0:T(8,128)}, f32[64,1536]{1,0:T(8,128)}, f32[72,512]{1,0:T(8,128)}, f32[8,512]{1,0:T(8,128)}, ...) custom-call(f32[520]{0:T(1024)} %get-tuple-element.158.refs_0_, s32[65]{0:T(128)} %get-tuple-element.238.refs_1_, ...), custom_call_target="tpu_custom_call" | custom-call | flops 40265318400 | bytes 11508296 | tf_op jit(solution)/shard_map/mixer_back/pallas_call | solution.py:387
  577.6 2.8 collective-permute-start.39
  581.6 2.8 fusion.29.refs_19_
  586.0 3.0 fusion.22.refs_20_
  590.2 7.0 fusion.8
  599.7 31.4 %mixer_back.3 = (bf16[512,1536]{1,0:T(8,128)(2,1)}, f32[8,1536]{1,0:T(8,128)}, f32[64,1536]{1,0:T(8,128)}, f32[72,512]{1,0:T(8,128)}, f32[8,512]{1,0:T(8,128)}, ...) custom-call(f32[520]{0:T(1024)} %get-tuple-element.159.refs_0_, s32[65]{0:T(128)} %get-tuple-element.239.refs_1_, ...), custom_call_target="tpu_custom_call" | custom-call | flops 40265318400 | bytes 11508296 | tf_op jit(solution)/shard_map/mixer_back/pallas_call | solution.py:387
  640.8 12.6 %grad_in.1 = (bf16[1024,1536]{1,0:T(8,128)(2,1)}, bf16[1024,1536]{1,0:T(8,128)(2,1)}) custom-call(s32[1]{0:T(128)} %bitcast.26.core_ref, bf16[512,2048]{1,0:T(8,128)(2,1)} %get-tuple-element.193.refs_0_, bf16[512,2048]{1,0:T(8,128)(2,1)} %get-tuple-element.192.refs_1_, bf16[512,1536]{1,0:T(8,128)(2,1)} %copy-done.69, bf16[512,1536]{1,0:T(8,128)(2,1)} %fusion.42.refs_3_), custom_call_target="tpu_custom_call" | custom-call | flops 6442450944 | bytes 13631488 | tf_op jit(solution)/shard_map/grad_in/pallas_call | solution.py:544
  656.3 9.7 %fusion.17 = (f32[512]{0:T(512)S(1)}, f32[2048]{0:T(1024)S(1)}, f32[512,2048]{1,0:T(8,128)}) fusion(f32[2048]{0:T(1024)S(1)} %broadcast_add_fusion.1, bf16[1280,2048]{1,0:T(8,128)(2,1)} %all-gather.9.cloned.1.call-done, f32[512]{0:T(512)S(1)} %get-tuple-element.232, bf16[512,1536]{1,0:T(8,128)(2,1)} %fusion.42.refs_3_, bf16[2048,1536]{1,0:T(8,128)(2,1)} %place_in.1), kind=kOutput, calls=%fused_computation.31 | convolution fusion | flops 3228562944 | bytes 14176256 | tf_op jit(solution)/shard_map/dot_general | solution.py:623
  667.2 3.7 collective-permute-start.31
  674.7 9.7 %all_gather.38 = bf16[8,82,512]{2,1,0:T(8,128)(2,1)S(1)} all-gather(bf16[1,82,512]{2,1,0:T(8,128)(2,1)S(1)} %concatenate.98), channel_id=1, replica_groups=mesh['seq'=8,'tp'=4] {'seq'}, dimensions={0}, use_global_device_ids=true | all-gather | bytes 755712 | tf_op jit(solution)/shard_map/all_gather | solution.py:807
  685.7 6.0 fusion.16
  693.4 3.7 add_convert_fusion.2
  708.6 10.1 %collective-permute-done.32 = bf16[256,1536]{1,0:T(8,128)(2,1)} collective-permute-done((bf16[256,1536]{1,0:T(8,128)(2,1)}, bf16[256,1536]{1,0:T(8,128)(2,1)}, u32[]{:S(2)}, u32[]{:S(2)}) %collective-permute-start.32) | collective-permute-done | bytes 786464 | tf_op jit(solution)/shard_map/ppermute | solution.py:446
  724.4 2.9 fusion.32
  730.9 2.9 copy.78
  733.8 4.7 reshape.605
  748.8 2.8 fusion.27
  (447 shorter events, 155.8 us)
Async XLA Ops:
  7.2 107.7 %all-gather.9.cloned.1.call-start = ((), (), s32[]{:S(2)}) async-start(), calls=%async_computation.7 | async-start | bytes 6553600 | tf_op jit(solution)/shard_map/all_gather | solution.py:435
  10.8 166.5 %all-gather.17.cloned.1.call-start = ((), (), s32[]{:S(2)}) async-start(), calls=%async_computation.18 | async-start | bytes 2621440 | tf_op jit(solution)/shard_map/all_gather | solution.py:435
  12.5 54.2 %copy-start.3 = (bf16[256,4352]{1,0:T(8,128)(2,1)}, bf16[256,4352]{1,0:T(8,128)(2,1)S(1)}, u32[]{:S(2)}) copy-start(bf16[256,4352]{1,0:T(8,128)(2,1)S(1)} %pad_maximum_fusion.2.refs_0_) | copy-start | bytes 6684676
  12.5 51.6 %collective-permute-start.1 = (bf16[256,4352]{1,0:T(8,128)(2,1)S(1)}, bf16[256,4352]{1,0:T(8,128)(2,1)}, u32[]{:S(2)}, u32[]{:S(2)}) collective-permute-start(bf16[256,4352]{1,0:T(8,128)(2,1)S(1)} %pad_maximum_fusion.2.refs_0_), channel_id=1, source_target_pairs={{0,16},{4,20},{8,24},{12,28},{16,0},{20,4},{24,8},{28,12},{1,17},{... | collective-permute-start | bytes 6684680 | tf_op jit(solution)/shard_map/ppermute | solution.py:446
  15.6 92.9 %collective-permute-start.3 = (bf16[256,4352]{1,0:T(8,128)(2,1)S(1)}, bf16[256,4352]{1,0:T(8,128)(2,1)}, u32[]{:S(2)}, u32[]{:S(2)}) collective-permute-start(bf16[256,4352]{1,0:T(8,128)(2,1)S(1)} %pad_maximum_fusion.2.refs_0_), channel_id=1, source_target_pairs={{0,4},{4,0},{8,12},{12,8},{16,20},{20,16},{24,28},{28,24},{1,5},{5... | collective-permute-start | bytes 6684680 | tf_op jit(solution)/shard_map/ppermute | solution.py:446
  15.6 53.5 %collective-permute-start = (bf16[256,4352]{1,0:T(8,128)(2,1)S(1)}, bf16[256,4352]{1,0:T(8,128)(2,1)}, u32[]{:S(2)}, u32[]{:S(2)}) collective-permute-start(bf16[256,4352]{1,0:T(8,128)(2,1)S(1)} %pad_maximum_fusion.2.refs_0_), channel_id=1, source_target_pairs={{0,8},{4,12},{8,0},{12,4},{16,24},{20,28},{24,16},{28,20},{1,9},{5... | collective-permute-start | bytes 6684680 | tf_op jit(solution)/shard_map/ppermute | solution.py:446
  17.9 186.0 %all-gather.13.cloned.1.call-start = ((), (), s32[]{:S(2)}) async-start(), calls=%async_computation.9 | async-start | bytes 6488064 | tf_op jit(solution)/shard_map/all_gather | solution.py:435
  20.1 50.2 %copy-start.32 = (f32[16,512]{1,0:T(8,128)}, f32[16,512]{1,0:T(8,128)S(1)}, u32[]{:S(2)}) copy-start(f32[16,512]{1,0:T(8,128)S(1)} %get-tuple-element.214) | copy-start | bytes 98308
  20.1 50.2 %copy-start.34 = (f32[16,512]{1,0:T(8,128)}, f32[16,512]{1,0:T(8,128)S(1)}, u32[]{:S(2)}) copy-start(f32[16,512]{1,0:T(8,128)S(1)} %get-tuple-element.215) | copy-start | bytes 98308
  20.8 52.2 %copy-start.58 = (f32[16,8,128]{2,1,0:T(8,128)}, f32[16,8,128]{2,1,0:T(8,128)S(1)}, u32[]{:S(2)}) copy-start(f32[16,8,128]{2,1,0:T(8,128)S(1)} %get-tuple-element.227.refs_8_) | copy-start | bytes 196612
  20.9 49.4 %copy-start.41 = (f32[64,8,128]{2,1,0:T(8,128)}, f32[64,8,128]{2,1,0:T(8,128)S(1)}, u32[]{:S(2)}) copy-start(f32[64,8,128]{2,1,0:T(8,128)S(1)} %get-tuple-element.257) | copy-start | bytes 786436
  66.7 33.1 %collective-permute-start.17 = (bf16[256,2816]{1,0:T(8,128)(2,1)}, bf16[256,2816]{1,0:T(8,128)(2,1)}, u32[]{:S(2)}, u32[]{:S(2)}) collective-permute-start(bf16[256,2816]{1,0:T(8,128)(2,1)} %slice.352), channel_id=1, source_target_pairs={{0,8},{4,12},{8,0},{12,4},{16,24},{20,28},{24,16},{28,20},{1,9},{5... | collective-permute-start | bytes 4325384 | tf_op jit(solution)/shard_map/ppermute | solution.py:446
  69.1 39.4 %collective-permute-start.5 = (bf16[256,4352]{1,0:T(8,128)(2,1)}, bf16[256,4352]{1,0:T(8,128)(2,1)}, u32[]{:S(2)}, u32[]{:S(2)}) collective-permute-start(bf16[256,4352]{1,0:T(8,128)(2,1)} %collective-permute-done.1.refs_2_), channel_id=1, source_target_pairs={{0,4},{4,0},{8,12},{12,8},{16,20},{20,16},{24,28},{28,24},{1,5},{5... | collective-permute-start | bytes 6684680 | tf_op jit(solution)/shard_map/ppermute | solution.py:446
  69.1 39.4 %collective-permute-start.4 = (bf16[256,4352]{1,0:T(8,128)(2,1)}, bf16[256,4352]{1,0:T(8,128)(2,1)}, u32[]{:S(2)}, u32[]{:S(2)}) collective-permute-start(bf16[256,4352]{1,0:T(8,128)(2,1)} %collective-permute-done.refs_1_), channel_id=1, source_target_pairs={{0,4},{4,0},{8,12},{12,8},{16,20},{20,16},{24,28},{28,24},{1,5},{5... | collective-permute-start | bytes 6684680 | tf_op jit(solution)/shard_map/ppermute | solution.py:446
  73.0 19.5 %collective-permute-start.2 = (bf16[256,1536]{1,0:T(8,128)(2,1)S(1)}, bf16[256,1536]{1,0:T(8,128)(2,1)S(1)}, u32[]{:S(2)}, u32[]{:S(2)}) collective-permute-start(bf16[256,1536]{1,0:T(8,128)(2,1)S(1)} %slice.339), channel_id=1, source_target_pairs={{0,16},{4,20},{8,24},{12,28},{16,0},{20,4},{24,8},{28,12},{1,17},{... | collective-permute-start | bytes 2359304 | tf_op jit(solution)/shard_map/ppermute | solution.py:446
  77.1 37.8 %copy-start.38 = (f32[64,8,128]{2,1,0:T(8,128)}, f32[64,8,128]{2,1,0:T(8,128)S(1)}, u32[]{:S(2)}) copy-start(f32[64,8,128]{2,1,0:T(8,128)S(1)} %constant_dynamic-update-slice_fusion.6.refs_6_) | copy-start | bytes 786436
  103.2 148.6 %all-gather.11.cloned.1.call-start = ((), (), s32[]{:S(2)}) async-start(), calls=%async_computation.8 | async-start | bytes 2621440 | tf_op jit(solution)/shard_map/all_gather | solution.py:435
  105.0 3.5 collective-permute-start.6
  116.2 102.1 %copy-start.12 = (bf16[256,2048]{1,0:T(8,128)(2,1)}, bf16[256,2048]{1,0:T(8,128)(2,1)S(1)}, u32[]{:S(2)}) copy-start(bf16[256,2048]{1,0:T(8,128)(2,1)S(1)} %slice.347.refs_0_) | copy-start | bytes 3145732
  116.2 40.7 %collective-permute-start.9 = (bf16[256,2048]{1,0:T(8,128)(2,1)S(1)}, bf16[256,2048]{1,0:T(8,128)(2,1)S(1)}, u32[]{:S(2)}, u32[]{:S(2)}) collective-permute-start(bf16[256,2048]{1,0:T(8,128)(2,1)S(1)} %slice.347.refs_0_), channel_id=1, source_target_pairs={{0,16},{4,20},{8,24},{12,28},{16,0},{20,4},{24,8},{28,12},{1,17},{... | collective-permute-start | bytes 3145736 | tf_op jit(solution)/shard_map/ppermute | solution.py:446
  117.7 39.7 %collective-permute-start.8 = (bf16[256,2048]{1,0:T(8,128)(2,1)S(1)}, bf16[256,2048]{1,0:T(8,128)(2,1)S(1)}, u32[]{:S(2)}, u32[]{:S(2)}) collective-permute-start(bf16[256,2048]{1,0:T(8,128)(2,1)S(1)} %slice.347.refs_0_), channel_id=1, source_target_pairs={{0,8},{4,12},{8,0},{12,4},{16,24},{20,28},{24,16},{28,20},{1,9},{5... | collective-permute-start | bytes 3145736 | tf_op jit(solution)/shard_map/ppermute | solution.py:446
  134.5 3.8 collective-permute-start.7
  156.9 63.3 %copy-start.16 = (bf16[256,2048]{1,0:T(8,128)(2,1)}, bf16[256,2048]{1,0:T(8,128)(2,1)S(1)}, u32[]{:S(2)}) copy-start(bf16[256,2048]{1,0:T(8,128)(2,1)S(1)} %collective-permute-done.9.refs_2_) | copy-start | bytes 3145732
  157.5 62.8 %copy-start.17 = (bf16[256,2048]{1,0:T(8,128)(2,1)}, bf16[256,2048]{1,0:T(8,128)(2,1)S(1)}, u32[]{:S(2)}) copy-start(bf16[256,2048]{1,0:T(8,128)(2,1)S(1)} %collective-permute-done.8.refs_1_) | copy-start | bytes 3145732
  192.1 120.9 %all-gather.15.cloned.1.call-start = ((), (), s32[]{:S(2)}) async-start(), calls=%async_computation.12 | async-start | bytes 2621440 | tf_op jit(solution)/shard_map/all_gather | solution.py:435
  192.7 28.1 %collective-permute-start.18 = (bf16[256,2816]{1,0:T(8,128)(2,1)}, bf16[256,2816]{1,0:T(8,128)(2,1)}, u32[]{:S(2)}, u32[]{:S(2)}) collective-permute-start(bf16[256,2816]{1,0:T(8,128)(2,1)} %collective-permute-done.17.refs_3_), channel_id=1, source_target_pairs={{0,4},{4,0},{8,12},{12,8},{16,20},{20,16},{24,28},{28,24},{1,5},{5... | collective-permute-start | bytes 4325384 | tf_op jit(solution)/shard_map/ppermute | solution.py:446
  218.2 126.3 %all-gather.19.cloned.1.call-start = ((), (), s32[]{:S(2)}) async-start(), calls=%async_computation.19 | async-start | bytes 2621440 | tf_op jit(solution)/shard_map/all_gather | solution.py:435
  218.3 25.4 %collective-permute-start.12 = (bf16[256,2048]{1,0:T(8,128)(2,1)S(1)}, bf16[256,2048]{1,0:T(8,128)(2,1)}, u32[]{:S(2)}, u32[]{:S(2)}) collective-permute-start(bf16[256,2048]{1,0:T(8,128)(2,1)S(1)} %slice.347.refs_0_), channel_id=1, source_target_pairs={{0,4},{4,0},{8,12},{12,8},{16,20},{20,16},{24,28},{28,24},{1,5},{5... | collective-permute-start | bytes 3145736 | tf_op jit(solution)/shard_map/ppermute | solution.py:446
  218.6 14.3 %collective-permute-start.11 = (bf16[256,1024]{1,0:T(8,128)(2,1)S(1)}, bf16[256,1024]{1,0:T(8,128)(2,1)}, u32[]{:S(2)}, u32[]{:S(2)}) collective-permute-start(bf16[256,1024]{1,0:T(8,128)(2,1)S(1)} %slice.351), channel_id=1, source_target_pairs={{0,8},{4,12},{8,0},{12,4},{16,24},{20,28},{24,16},{28,20},{1,9},{5... | collective-permute-start | bytes 1572872 | tf_op jit(solution)/shard_map/ppermute | solution.py:446
  220.2 23.5 %collective-permute-start.14 = (bf16[256,2048]{1,0:T(8,128)(2,1)S(1)}, bf16[256,2048]{1,0:T(8,128)(2,1)}, u32[]{:S(2)}, u32[]{:S(2)}) collective-permute-start(bf16[256,2048]{1,0:T(8,128)(2,1)S(1)} %collective-permute-done.9.refs_2_), channel_id=1, source_target_pairs={{0,4},{4,0},{8,12},{12,8},{16,20},{20,16},{24,28},{28,24},{1,5},{5... | collective-permute-start | bytes 3145736 | tf_op jit(solution)/shard_map/ppermute | solution.py:446
  220.3 23.4 %collective-permute-start.13 = (bf16[256,2048]{1,0:T(8,128)(2,1)S(1)}, bf16[256,2048]{1,0:T(8,128)(2,1)}, u32[]{:S(2)}, u32[]{:S(2)}) collective-permute-start(bf16[256,2048]{1,0:T(8,128)(2,1)S(1)} %collective-permute-done.8.refs_1_), channel_id=1, source_target_pairs={{0,4},{4,0},{8,12},{12,8},{16,20},{20,16},{24,28},{28,24},{1,5},{5... | collective-permute-start | bytes 3145736 | tf_op jit(solution)/shard_map/ppermute | solution.py:446
  220.8 14.0 %collective-permute-start.10 = (bf16[256,1024]{1,0:T(8,128)(2,1)S(1)}, bf16[256,1024]{1,0:T(8,128)(2,1)}, u32[]{:S(2)}, u32[]{:S(2)}) collective-permute-start(bf16[256,1024]{1,0:T(8,128)(2,1)S(1)} %slice.350), channel_id=1, source_target_pairs={{0,16},{4,20},{8,24},{12,28},{16,0},{20,4},{24,8},{28,12},{1,17},{... | collective-permute-start | bytes 1572872 | tf_op jit(solution)/shard_map/ppermute | solution.py:446
  232.9 10.8 %collective-permute-start.16 = (bf16[256,1024]{1,0:T(8,128)(2,1)}, bf16[256,1024]{1,0:T(8,128)(2,1)}, u32[]{:S(2)}, u32[]{:S(2)}) collective-permute-start(bf16[256,1024]{1,0:T(8,128)(2,1)} %collective-permute-done.11.refs_4_), channel_id=1, source_target_pairs={{0,4},{4,0},{8,12},{12,8},{16,20},{20,16},{24,28},{28,24},{1,5},{5... | collective-permute-start | bytes 1572872 | tf_op jit(solution)/shard_map/ppermute | solution.py:446
  234.9 8.9 %collective-permute-start.15 = (bf16[256,1024]{1,0:T(8,128)(2,1)}, bf16[256,1024]{1,0:T(8,128)(2,1)}, u32[]{:S(2)}, u32[]{:S(2)}) collective-permute-start(bf16[256,1024]{1,0:T(8,128)(2,1)} %collective-permute-done.10.refs_3_), channel_id=1, source_target_pairs={{0,4},{4,0},{8,12},{12,8},{16,20},{20,16},{24,28},{28,24},{1,5},{5... | collective-permute-start | bytes 1572872 | tf_op jit(solution)/shard_map/ppermute | solution.py:446
  266.4 154.3 %reduce-scatter.10.cloned.1.call-start = ((), (), s32[]{:S(2)}) async-start(), calls=%async_computation.11 | async-start | bytes 2621440 | tf_op jit(solution)/shard_map/reduce_scatter | solution.py:439
  312.8 135.5 %reduce-scatter.12.cloned.1.call-start = ((), (), s32[]{:S(2)}) async-start(), calls=%async_computation.13 | async-start | bytes 2621440 | tf_op jit(solution)/shard_map/reduce_scatter | solution.py:439
  405.0 9.0 %collective-permute-start.19 = (bf16[1024,1408]{1,0:T(8,128)(2,1)}, bf16[1024,1408]{1,0:T(8,128)(2,1)S(1)}, u32[]{:S(2)}, u32[]{:S(2)}) collective-permute-start(bf16[1024,1408]{1,0:T(8,128)(2,1)} %get-tuple-element.57.refs_8_), channel_id=1, source_target_pairs={{0,4},{4,0},{8,12},{12,8},{16,20},{20,16},{24,28},{28,24},{1,5},{5... | collective-permute-start | bytes 8650760 | tf_op jit(solution)/shard_map/ppermute | solution.py:446
  405.0 34.5 %collective-permute-start.20 = (bf16[1024,2048]{1,0:T(8,128)(2,1)}, bf16[1024,2048]{1,0:T(8,128)(2,1)}, u32[]{:S(2)}, u32[]{:S(2)}) collective-permute-start(bf16[1024,2048]{1,0:T(8,128)(2,1)} %get-tuple-element.55.refs_4_.refs_10_), channel_id=1, source_target_pairs={{0,4},{4,0},{8,12},{12,8},{16,20},{20,16},{24,28},{28,24},{1,5},{5... | collective-permute-start | bytes 12582920 | tf_op jit(solution)/shard_map/ppermute | solution.py:446
  405.5 323.5 %reduce-scatter.20.cloned.1.call-start = ((), (), s32[]{:S(2)}) async-start(), calls=%async_computation.17 | async-start | bytes 1310720 | tf_op jit(solution)/shard_map/reduce_scatter | solution.py:439
  419.1 18.5 %collective-permute-start.21 = (bf16[256,1408]{1,0:T(8,128)(2,1)}, bf16[256,1408]{1,0:T(8,128)(2,1)}, u32[]{:S(2)}, u32[]{:S(2)}) collective-permute-start(bf16[256,1408]{1,0:T(8,128)(2,1)} %dynamic-slice_bitcast_fusion.2), channel_id=1, source_target_pairs={{0,16},{4,20},{8,24},{12,28},{16,0},{20,4},{24,8},{28,12},{1,17},{... | collective-permute-start | bytes 2162696 | tf_op jit(solution)/shard_map/ppermute | solution.py:446
  445.8 34.8 %collective-permute-start.36 = (bf16[256,2048]{1,0:T(8,128)(2,1)S(1)}, bf16[256,2048]{1,0:T(8,128)(2,1)S(1)}, u32[]{:S(2)}, u32[]{:S(2)}) collective-permute-start(bf16[256,2048]{1,0:T(8,128)(2,1)S(1)} %dynamic-slice_bitcast_fusion.1), channel_id=1, source_target_pairs={{0,8},{4,12},{8,0},{12,4},{16,24},{20,28},{24,16},{28,20},{1,9},{5... | collective-permute-start | bytes 3145736 | tf_op jit(solution)/shard_map/ppermute | solution.py:446
  479.5 26.2 %collective-permute-start.35 = (bf16[256,2048]{1,0:T(8,128)(2,1)}, bf16[256,2048]{1,0:T(8,128)(2,1)S(1)}, u32[]{:S(2)}, u32[]{:S(2)}) collective-permute-start(bf16[256,2048]{1,0:T(8,128)(2,1)} %fusion.34), channel_id=1, source_target_pairs={{0,8},{4,12},{8,0},{12,4},{16,24},{20,28},{24,16},{28,20},{1,9},{5... | collective-permute-start | bytes 3145736 | tf_op jit(solution)/shard_map/ppermute | solution.py:446
  481.9 25.3 %collective-permute-start.37 = (bf16[256,2048]{1,0:T(8,128)(2,1)}, bf16[256,2048]{1,0:T(8,128)(2,1)S(1)}, u32[]{:S(2)}, u32[]{:S(2)}) collective-permute-start(bf16[256,2048]{1,0:T(8,128)(2,1)} %fusion.26), channel_id=1, source_target_pairs={{0,16},{4,20},{8,24},{12,28},{16,0},{20,4},{24,8},{28,12},{1,17},{... | collective-permute-start | bytes 3145736 | tf_op jit(solution)/shard_map/ppermute | solution.py:446
  508.9 231.5 %reduce-scatter.14.cloned.1.call-start = ((), (), s32[]{:S(2)}) async-start(), calls=%async_computation.14 | async-start | bytes 2621440 | tf_op jit(solution)/shard_map/reduce_scatter | solution.py:439
  509.0 21.2 %collective-permute-start.22 = (bf16[1024,2816]{1,0:T(8,128)(2,1)}, bf16[1024,2816]{1,0:T(8,128)(2,1)}, u32[]{:S(2)}, u32[]{:S(2)}) collective-permute-start(bf16[1024,2816]{1,0:T(8,128)(2,1)} %get-tuple-element.64.refs_18_), channel_id=1, source_target_pairs={{0,4},{4,0},{8,12},{12,8},{16,20},{20,16},{24,28},{28,24},{1,5},{5... | collective-permute-start | bytes 17301512 | tf_op jit(solution)/shard_map/ppermute | solution.py:446
  516.4 226.4 %reduce-scatter.8.cloned.1.call-start = ((), (), s32[]{:S(2)}) async-start(), calls=%async_computation.10 | async-start | bytes 2621440 | tf_op jit(solution)/shard_map/reduce_scatter | solution.py:439
  530.1 216.4 %reduce-scatter.16.cloned.1.call-start = ((), (), s32[]{:S(2)}) async-start(), calls=%async_computation.15 | async-start | bytes 2621440 | tf_op jit(solution)/shard_map/reduce_scatter | solution.py:439
  530.2 60.0 %slice-start = ((s8[5242880]{0:T(1024)(128)(4,1)}), s8[4194304]{0:T(1024)(128)(4,1)S(1)}, s32[]{:S(2)}) async-start(s8[5242880]{0:T(1024)(128)(4,1)} %bitcast.201), calls=%async_computation.20 | async-start | bytes 8388608
  541.2 43.7 %collective-permute-start.23 = (bf16[256,2816]{1,0:T(8,128)(2,1)}, bf16[256,2816]{1,0:T(8,128)(2,1)S(1)}, u32[]{:S(2)}, u32[]{:S(2)}) collective-permute-start(bf16[256,2816]{1,0:T(8,128)(2,1)} %dynamic-slice_bitcast_fusion), channel_id=1, source_target_pairs={{0,8},{4,12},{8,0},{12,4},{16,24},{20,28},{24,16},{28,20},{1,9},{5... | collective-permute-start | bytes 4325384 | tf_op jit(solution)/shard_map/ppermute | solution.py:446
  542.1 48.1 %slice-start.1 = ((s8[5242880]{0:T(1024)(128)(4,1)}), s8[1048576]{0:T(1024)(128)(4,1)S(1)}, s32[]{:S(2)}) async-start(s8[5242880]{0:T(1024)(128)(4,1)} %bitcast.201), calls=%async_computation.21 | async-start | bytes 2097152
  574.2 6.2 collective-permute-start.24
  577.6 146.8 %collective-permute-start.39 = (bf16[256,1408]{1,0:T(8,128)(2,1)}, bf16[256,1408]{1,0:T(8,128)(2,1)}, u32[]{:S(2)}, u32[]{:S(2)}) collective-permute-start(bf16[256,1408]{1,0:T(8,128)(2,1)} %fusion.36), channel_id=1, source_target_pairs={{0,16},{4,20},{8,24},{12,28},{16,0},{20,4},{24,8},{28,12},{1,17},{... | collective-permute-start | bytes 2162696 | tf_op jit(solution)/shard_map/ppermute | solution.py:446
  584.3 50.8 %collective-permute-start.25 = (bf16[256,2816]{1,0:T(8,128)(2,1)}, bf16[256,2816]{1,0:T(8,128)(2,1)S(1)}, u32[]{:S(2)}, u32[]{:S(2)}) collective-permute-start(bf16[256,2816]{1,0:T(8,128)(2,1)} %fusion.29.refs_19_), channel_id=1, source_target_pairs={{0,8},{4,12},{8,0},{12,4},{16,24},{20,28},{24,16},{28,20},{1,9},{5... | collective-permute-start | bytes 4325384 | tf_op jit(solution)/shard_map/ppermute | solution.py:446
  589.0 46.2 %collective-permute-start.26 = (bf16[256,2816]{1,0:T(8,128)(2,1)}, bf16[256,2816]{1,0:T(8,128)(2,1)S(1)}, u32[]{:S(2)}, u32[]{:S(2)}) collective-permute-start(bf16[256,2816]{1,0:T(8,128)(2,1)} %fusion.22.refs_20_), channel_id=1, source_target_pairs={{0,16},{4,20},{8,24},{12,28},{16,0},{20,4},{24,8},{28,12},{1,17},{... | collective-permute-start | bytes 4325384 | tf_op jit(solution)/shard_map/ppermute | solution.py:446
  632.0 114.5 %reduce-scatter.18.cloned.1.call-start = ((), (), s32[]{:S(2)}) async-start(), calls=%async_computation.16 | async-start | bytes 2621440 | tf_op jit(solution)/shard_map/reduce_scatter | solution.py:439
  632.9 7.2 collective-permute-start.27
  653.4 38.3 %collective-permute-start.28 = (bf16[1024,1536]{1,0:T(8,128)(2,1)}, bf16[1024,1536]{1,0:T(8,128)(2,1)S(1)}, u32[]{:S(2)}, u32[]{:S(2)}) collective-permute-start(bf16[1024,1536]{1,0:T(8,128)(2,1)} %get-tuple-element.76), channel_id=1, source_target_pairs={{0,4},{4,0},{8,12},{12,8},{16,20},{20,16},{24,28},{28,24},{1,5},{5... | collective-permute-start | bytes 9437192 | tf_op jit(solution)/shard_map/ppermute | solution.py:446
  666.1 4.8 collective-permute-start.30
  667.1 5.8 collective-permute-start.29
  667.2 5.7 collective-permute-start.31
  698.0 20.7 %collective-permute-start.32 = (bf16[256,1536]{1,0:T(8,128)(2,1)}, bf16[256,1536]{1,0:T(8,128)(2,1)}, u32[]{:S(2)}, u32[]{:S(2)}) collective-permute-start(bf16[256,1536]{1,0:T(8,128)(2,1)} %add_bitcast_fusion), channel_id=1, source_target_pairs={{0,16},{4,20},{8,24},{12,28},{16,0},{20,4},{24,8},{28,12},{1,17},{... | collective-permute-start | bytes 2359304 | tf_op jit(solution)/shard_map/ppermute | solution.py:446
  701.8 22.5 %collective-permute-start.38 = (bf16[256,1408]{1,0:T(8,128)(2,1)}, bf16[256,1408]{1,0:T(8,128)(2,1)}, u32[]{:S(2)}, u32[]{:S(2)}) collective-permute-start(bf16[256,1408]{1,0:T(8,128)(2,1)} %fusion.33), channel_id=1, source_target_pairs={{0,8},{4,12},{8,0},{12,4},{16,24},{20,28},{24,16},{28,20},{1,9},{5... | collective-permute-start | bytes 2162696 | tf_op jit(solution)/shard_map/ppermute | solution.py:446
  707.2 41.6 %collective-permute-start.34 = (bf16[256,1536]{1,0:T(8,128)(2,1)}, bf16[256,1536]{1,0:T(8,128)(2,1)}, u32[]{:S(2)}, u32[]{:S(2)}) collective-permute-start(bf16[256,1536]{1,0:T(8,128)(2,1)} %fusion.35), channel_id=1, source_target_pairs={{0,16},{4,20},{8,24},{12,28},{16,0},{20,4},{24,8},{28,12},{1,17},{... | collective-permute-start | bytes 2359304 | tf_op jit(solution)/shard_map/ppermute | solution.py:446
  722.9 25.9 %collective-permute-start.33 = (bf16[256,1536]{1,0:T(8,128)(2,1)}, bf16[256,1536]{1,0:T(8,128)(2,1)}, u32[]{:S(2)}, u32[]{:S(2)}) collective-permute-start(bf16[256,1536]{1,0:T(8,128)(2,1)} %fusion.28), channel_id=1, source_target_pairs={{0,8},{4,12},{8,0},{12,4},{16,24},{20,28},{24,16},{28,20},{1,9},{5... | collective-permute-start | bytes 2359304 | tf_op jit(solution)/shard_map/ppermute | solution.py:446
  (72 other events, 666.1 us)
Sparse Core Ops, SparseCore 0:
  10.9 100.7 all-gather.8
  113.8 44.2 all-gather.16
  160.0 43.7 all-gather.12
  205.9 45.9 all-gather.10
  253.2 44.6 all-gather.14
  299.9 44.6 all-gather.18
  346.9 42.6 reduce-scatter.9
  405.6 42.6 reduce-scatter.11
  509.0 24.8 reduce-scatter.19
  536.1 42.5 reduce-scatter.13
  581.0 43.1 reduce-scatter.7
  632.1 42.4 reduce-scatter.15
  691.8 43.9 reduce-scatter.17

commit v6 on v5

--- a/solution.py
+++ b/solution.py
@@ -782,29 +782,29 @@
             gain = tied(gain_in, in_halves[0])
         d_h_in = dot(d_z, in_full, ((1,), (1,)))
         d_norm, d_gain_in = norm_back(x_full[m].astype(F32), scale_in[m], gain, d_h_in)
+        smalls.append((d_taps, d_lam, d_res, d_skip))
         gains = [d_gain_in, c["d_gain_mlp"]] if m == 0 else [gains[0] + d_gain_in, gains[1] + c["d_gain_mlp"]]
         if m == micros - 1:
             gains = tp_sum(jnp.concatenate(gains).reshape(-1, width).astype(BF))
-            d_norm = tied(d_norm, gains)
+            d_taps, d_lam, d_res, d_skip = (sum(parts) for parts in zip(*smalls))
+            g_real, g_imag = unpacked(d_lam, log_rate.shape)
+            s_real, s_imag = unpacked(d_res, log_rate.shape)
+            h_real = residues[0] * g_real + residues[1] * g_imag
+            h_imag = residues[0] * g_imag - residues[1] * g_real
+            small = jnp.concatenate([
+                jnp.sum(d_taps.reshape(9, SUB, width), axis=1),
+                -rate * (lam_real * h_real + lam_imag * h_imag),
+                lam_real * h_imag - lam_imag * h_real,
+                s_real, -s_imag,
+                jnp.sum(d_skip, axis=0, keepdims=True),
+                gains,
+            ])
+            small = jnp.sum(lax.all_gather(small.astype(BF), "seq").astype(F32), axis=0)
+            d_norm = tied(d_norm, small)
         partial_grads.append((c["d_mid"] + d_norm).astype(BF))
         token_grads.append(scatter(partial_grads[m], "tp", 1))
-        smalls.append((d_taps, d_lam, d_res, d_skip))
 
     in_chip = grad_chip(in_halves)
-    d_taps, d_lam, d_res, d_skip = (sum(parts) for parts in zip(*smalls))
-    g_real, g_imag = unpacked(d_lam, log_rate.shape)
-    s_real, s_imag = unpacked(d_res, log_rate.shape)
-    h_real = residues[0] * g_real + residues[1] * g_imag
-    h_imag = residues[0] * g_imag - residues[1] * g_real
-    small = jnp.concatenate([
-        jnp.sum(d_taps.reshape(9, SUB, width), axis=1),
-        -rate * (lam_real * h_real + lam_imag * h_imag),
-        lam_real * h_imag - lam_imag * h_real,
-        s_real, -s_imag,
-        jnp.sum(d_skip, axis=0, keepdims=True),
-        gains,
-    ])
-    small = jnp.sum(lax.all_gather(small.astype(BF), "seq").astype(F32), axis=0)
     in_far = grad_far(in_chip, Y, (small,))
     g_in = grad_own(in_chip, grad_turn(in_chip, in_far, Y, (small,)))
     g_down = grad_own(down_chip, down_turn, (in_far,))

time: 773 us -> 772 us (level)
  transfers between devices with their start and end apart: 53 -> 53, of which waited for: 14 -> 15; matrix products, arithmetic and copies ran while one was open for 38% -> 38% of each run, Pallas kernels for 27% -> 27%
where the time goes in v6:
time: 772 us; the launch traced here: 761 us
  Pallas kernels  207 us (27%)
  matrix products  132 us (17%)
  waiting for transfers between devices  122 us (16%)
  other arithmetic  110 us (14%)
  local copies, waits for them, and re-layouts  78.3 us (10%)
  blocking collectives  43.8 us (6%)
  starting transfers between devices  41.3 us (5%)
  between operations  26.2 us (3%)
    dot_general x15, matrix products, dot(): return lax.dot_general(a, b, (dims, ((), ())), preferred_element_type=F32)  132 us
    pallas_call x8, Pallas kernels, call(): pl.pallas_call(without, out_shape=[jax.ShapeDtypeStruct(s, d) for s, d in...  128 us
    ppermute x34, waiting for transfers between devices, over(): return lax.ppermute(value, 'seq', [(i, i ^ bit) for i in range(8)])  98.9 us
    pallas_call x4, Pallas kernels, grad_halves(): pl.pallas_call(functools.partial(halves_kernel, n), out_shape=[jax.ShapeD...  58.7 us
    unnamed x188, local copies, waits for them, and re-layouts  31.8 us
    ppermute x34, starting transfers between devices, over(): return lax.ppermute(value, 'seq', [(i, i ^ bit) for i in range(8)])  31.4 us
    pallas_call x3, Pallas kernels, place(): pl.pallas_call(functools.partial(place_kernel, plan, count), out_shape=ja...  20.9 us
    all_gather x6, waiting for transfers between devices, gather(): return lax.all_gather(block, axis, axis=dim, tiled=True)  20.1 us
  transfers between devices with their start and end apart: 53, of which 15 were waited for; matrix products, arithmetic and copies ran while one was open for 38% of the time, Pallas kernels for 27%

profile of v6, /device:TPU:0, one launch (start us, length us, event | category | flops | bytes accessed | tf_op | source)
XLA Modules:
  0.0 760.8 jit_solution(16110530792698757115)
XLA Ops:
  12.5 3.0 collective-permute-start.1
  21.5 42.6 %collective-permute-done.1.refs_2_ = bf16[256,4352]{1,0:T(8,128)(2,1)} collective-permute-done((bf16[256,4352]{1,0:T(8,128)(2,1)S(1)}, bf16[256,4352]{1,0:T(8,128)(2,1)}, u32[]{:S(2)}, u32[]{:S(2)}) %collective-permute-start.1) | collective-permute-done | bytes 2228256 | tf_op jit(solution)/shard_map/ppermute | solution.py:446
  64.1 2.6 slice.349
  77.8 14.7 %collective-permute-done.2.refs_3_ = bf16[256,1536]{1,0:T(8,128)(2,1)S(1)} collective-permute-done((bf16[256,1536]{1,0:T(8,128)(2,1)S(1)}, bf16[256,1536]{1,0:T(8,128)(2,1)S(1)}, u32[]{:S(2)}, u32[]{:S(2)}) %collective-permute-start.2) | collective-permute-done | bytes 786464 | tf_op jit(solution)/shard_map/ppermute | solution.py:446
  93.9 5.9 collective-permute-done.17.refs_3_
  109.3 5.5 place_in.1
  119.2 3.3 multiply_reduce_fusion
  122.6 3.4 slice_convert_fusion
  127.6 6.9 fusion.18
  138.9 9.0 %mixer_front.2 = (f32[4096,128]{1,0:T(8,128)}, f32[16,8,128]{2,1,0:T(8,128)}) custom-call(f32[520]{0:T(1024)} %get-tuple-element.158.refs_0_, s32[65]{0:T(128)} %get-tuple-element.236.refs_1_, bf16[512,1536]{1,0:T(8,128)(2,1)} %get-tuple-element.192.refs_2_.refs_4_, f32[8,1536]{1,0:T(8,128)} %get-tuple-element.200.refs_3_.refs_5_, ...), custom_call_target="tpu_custom_call" | custom-call | flops 13421772800 | bytes 4084260 | tf_op jit(solution)/shard_map/mixer_front/pallas_call | solution.py:387
  148.0 9.0 %mixer_front.3 = (f32[4096,128]{1,0:T(8,128)}, f32[16,8,128]{2,1,0:T(8,128)}) custom-call(f32[520]{0:T(1024)} %get-tuple-element.159.refs_0_, s32[65]{0:T(128)} %get-tuple-element.237.refs_1_, bf16[512,1536]{1,0:T(8,128)(2,1)} %get-tuple-element.193.refs_2_.refs_4_, f32[8,1536]{1,0:T(8,128)} %get-tuple-element.201.refs_3_.refs_5_, ...), custom_call_target="tpu_custom_call" | custom-call | flops 13421772800 | bytes 4084260 | tf_op jit(solution)/shard_map/mixer_front/pallas_call | solution.py:387
  160.2 16.1 %all_gather.31 = bf16[8,2,16,8,128]{4,3,2,1,0:T(8,128)(2,1)S(1)} all-gather(bf16[1,2,16,8,128]{4,3,2,1,0:T(8,128)(2,1)S(1)} %fusion.43), channel_id=1, replica_groups=mesh['seq'=8,'tp'=4] {'seq'}, dimensions={0}, use_global_device_ids=true | all-gather | bytes 589824 | tf_op jit(solution)/shard_map/all_gather | solution.py:688
  177.3 14.8 %mixer_finish.2 = (bf16[512,512]{1,0:T(8,128)(2,1)}, f32[512,512]{1,0:T(8,128)}, f32[8,16,8,128]{3,2,1,0:T(8,128)}) custom-call(f32[520]{0:T(1024)} %get-tuple-element.158.refs_0_, s32[65]{0:T(128)} %get-tuple-element.236.refs_1_, f32[8]{0:T(128)} %compare_convert_fusion.4.refs_2_, s32[1]{0:T(128)} %bitcast.5.me_ref.refs_3_, ...), custom_call_target="tpu_custom_call" | custom-call | flops 16777216000 | bytes 7101000 | tf_op jit(solution)/shard_map/mixer_finish/pallas_call | solution.py:387
  193.1 10.8 %all-gather.13.cloned.1.call-done.refs_15_ = bf16[2048,1408]{1,0:T(8,128)(2,1)} async-done(((bf16[256,1408]{1,0:T(8,128)(2,1)}), bf16[2048,1408]{1,0:T(8,128)(2,1)}) %all-gather.13.cloned.1.call-update) | async-done | bytes 5767184 | tf_op jit(solution)/shard_map/all_gather | solution.py:435
  203.9 14.3 %mixer_finish.3 = (bf16[512,512]{1,0:T(8,128)(2,1)}, f32[512,512]{1,0:T(8,128)}, f32[8,16,8,128]{3,2,1,0:T(8,128)}) custom-call(f32[520]{0:T(1024)} %get-tuple-element.159.refs_0_, s32[65]{0:T(128)} %get-tuple-element.237.refs_1_, f32[8]{0:T(128)} %compare_convert_fusion.2.refs_2_, s32[1]{0:T(128)} %bitcast.5.me_ref.refs_3_, ...), custom_call_target="tpu_custom_call" | custom-call | flops 16777216000 | bytes 7101000 | tf_op jit(solution)/shard_map/mixer_finish/pallas_call | solution.py:387
  221.6 11.3 %collective-permute-done.11.refs_4_ = bf16[256,1024]{1,0:T(8,128)(2,1)} collective-permute-done((bf16[256,1024]{1,0:T(8,128)(2,1)S(1)}, bf16[256,1024]{1,0:T(8,128)(2,1)}, u32[]{:S(2)}, u32[]{:S(2)}) %collective-permute-start.11) | collective-permute-done | bytes 524320 | tf_op jit(solution)/shard_map/ppermute | solution.py:446
  234.9 8.8 %place_gu.1 = bf16[2048,2816]{1,0:T(8,128)(2,1)} custom-call(s32[1]{0:T(128)} %bitcast.5.me_ref.refs_3_, bf16[256,4352]{1,0:T(8,128)(2,1)} %copy-done.3, bf16[256,4352]{1,0:T(8,128)(2,1)} %collective-permute-done.refs_1_, bf16[256,4352]{1,0:T(8,128)(2,1)} %collective-permute-done.1.refs_2_, bf16[256,2816]{1,0:T(8,128)(2,1)} %collective-permute-done.17.refs_3_, ...), custom_call_target="tpu_custom_call" | custom-call | bytes 23068672 | tf_op jit(solution)/shard_map/place_gu/pallas_call | solution.py:477
  243.8 6.5 place_out.1
  253.6 11.2 %multiply_reduce_fusion.6 = (f32[512]{0:T(512)S(1)}, f32[512,2048]{1,0:T(8,128)}) fusion(bf16[512,2048]{1,0:T(8,128)(2,1)} %all-gather.11.cloned.1.call-done.refs_2_, bf16[2048,2048]{1,0:T(8,128)(2,1)} %place_out.1, bf16[1280,2048]{1,0:T(8,128)(2,1)} %all-gather.9.cloned.1.call-done), kind=kOutput, calls=%fused_computation.42 | convolution fusion | flops 4299161088 | bytes 16779264 | tf_op jit(solution)/shard_map/dot_general | solution.py:623
  266.4 2.8 multiply_convert_fusion.2.refs_0_
  270.7 9.7 %fusion.79 = f32[512,2816]{1,0:T(8,128)S(1)} fusion(bf16[512,2048]{1,0:T(8,128)(2,1)S(1)} %multiply_convert_fusion.2.refs_0_, bf16[2048,2816]{1,0:T(8,128)(2,1)} %place_gu.1), kind=kOutput, calls=%fused_computation.250 | convolution fusion | flops 5905580032 | bytes 19398656 | tf_op jit(solution)/shard_map/dot_general | solution.py:623
  280.4 5.9 multiply_convert_fusion.7
  286.4 10.0 %multiply_reduce_fusion.2 = (f32[2048]{0:T(1024)}, f32[512]{0:T(512)}, f32[512,2048]{1,0:T(8,128)}) fusion(f32[512,2048]{1,0:T(8,128)S(1)} %copy-done, f32[512]{0:T(512)S(1)} %get-tuple-element.235, f32[2048]{0:T(1024)S(1)} %copy-done.44, bf16[2048,2816]{1,0:T(8,128)(2,1)S(1)} %bitcast.218, bf16[512,1408]{1,0:T(8,128)(2,1)} %get-tuple-element.187, ...), kind=kOutput, calls=%fused_computation.34 | convolution fusion | flops 5917636096 | bytes 22827008 | tf_op jit(solution)/shard_map/dot_general | solution.py:623
  297.1 4.6 fusion.72
  303.0 8.4 %convolution_convert_fusion.1 = bf16[512,2048]{1,0:T(8,128)(2,1)S(1)} fusion(bf16[512,2048]{1,0:T(8,128)(2,1)S(1)} %get-tuple-element.179.refs_0_, bf16[2048,2048]{1,0:T(8,128)(2,1)} %place_out.1), kind=kOutput, calls=%fused_computation.46 | convolution fusion | flops 4296015872 | bytes 12582912 | tf_op jit(solution)/shard_map/dot_general | solution.py:623
  313.0 9.3 %multiply_reduce_fusion.4 = (f32[512]{0:T(512)S(1)}, f32[512,2048]{1,0:T(8,128)S(1)}) fusion(bf16[512,2048]{1,0:T(8,128)(2,1)} %all-gather.15.cloned.1.call-done.refs_3_, bf16[2048,2048]{1,0:T(8,128)(2,1)} %place_out.1, f32[]{:T(128)} %bitcast.32, bf16[1280,2048]{1,0:T(8,128)(2,1)} %all-gather.9.cloned.1.call-done), kind=kOutput, calls=%fused_computation.38 | convolution fusion | flops 4300209664 | bytes 16779268 | tf_op jit(solution)/shard_map/dot_general | solution.py:623
  325.5 11.2 %fusion.80 = f32[512,2816]{1,0:T(8,128)} fusion(bf16[512,2048]{1,0:T(8,128)(2,1)S(1)} %multiply_convert_fusion.1.refs_1_, bf16[2048,2816]{1,0:T(8,128)(2,1)} %place_gu.1), kind=kOutput, calls=%fused_computation.251 | convolution fusion | flops 5905580032 | bytes 19398656 | tf_op jit(solution)/shard_map/dot_general | solution.py:623
  336.7 7.9 %all-gather.19.cloned.1.call-done = bf16[1,512,2048]{2,1,0:T(8,128)(2,1)} async-done(((bf16[1,512,512]{2,1,0:T(8,128)(2,1)}), bf16[1,512,2048]{2,1,0:T(8,128)(2,1)}) %all-gather.19.cloned.1.call-update) | async-done | bytes 2097168 | tf_op jit(solution)/shard_map/all_gather | solution.py:435
  344.6 11.4 %multiply_convert_fusion.4 = (bf16[512,1408]{1,0:T(8,128)(2,1)}, bf16[512,1408]{1,0:T(8,128)(2,1)}, bf16[512,1408]{1,0:T(8,128)(2,1)}) fusion(f32[512,2816]{1,0:T(8,128)} %fusion.80, bf16[2048,1408]{1,0:T(8,128)(2,1)} %all-gather.13.cloned.1.call-done.refs_15_, bf16[1,512,2048]{2,1,0:T(8,128)(2,1)} %all-gather.19.cloned.1.call-done), kind=kOutput, calls=%fused_computation.57 | convolution fusion | flops 2964324352 | bytes 17956864 | tf_op jit(solution)/shard_map/dot_general | solution.py:623
  356.0 10.5 %multiply_reduce_fusion.1 = (f32[2048]{0:T(1024)S(1)}, f32[512]{0:T(512)S(1)}, f32[512,2048]{1,0:T(8,128)S(1)}) fusion(f32[512,2048]{1,0:T(8,128)S(1)} %copy-done.2, f32[512]{0:T(512)S(1)} %get-tuple-element.233, f32[2048]{0:T(1024)S(1)} %copy-done.44, bf16[2048,2816]{1,0:T(8,128)(2,1)} %place_gu.1, bf16[512,1408]{1,0:T(8,128)(2,1)} %get-tuple-element.185, ...), kind=kOutput, calls=%fused_computation.33 | convolution fusion | flops 5917636096 | bytes 22827008 | tf_op jit(solution)/shard_map/dot_general | solution.py:623
  366.6 4.3 fusion.67
  372.2 5.7 convolution_convert_fusion.refs_4_
  377.9 14.8 %grad_out.1 = (bf16[1024,2048]{1,0:T(8,128)(2,1)}, bf16[1024,2048]{1,0:T(8,128)(2,1)}) custom-call(s32[1]{0:T(128)} %bitcast.26.core_ref, bf16[512,2048]{1,0:T(8,128)(2,1)} %copy-done.21, bf16[512,2048]{1,0:T(8,128)(2,1)} %copy-done.22, bf16[512,2048]{1,0:T(8,128)(2,1)} %all-gather.11.cloned.1.call-done.refs_2_, ...), custom_call_target="tpu_custom_call" | custom-call | flops 8589934592 | bytes 16777216 | tf_op jit(solution)/shard_map/grad_out/pallas_call | solution.py:544
  392.8 12.3 %grad_down.1 = (bf16[1024,1408]{1,0:T(8,128)(2,1)}, bf16[1024,1408]{1,0:T(8,128)(2,1)}) custom-call(s32[1]{0:T(128)} %bitcast.26.core_ref, bf16[512,2048]{1,0:T(8,128)(2,1)} %bitcast.232, bf16[512,2048]{1,0:T(8,128)(2,1)} %bitcast.233, bf16[512,1408]{1,0:T(8,128)(2,1)} %get-tuple-element.189.refs_2_, bf16[512,1408]{1,0:T(8,128)(2,1)} %get-tuple-element.188.refs_3_, ...), custom_call_target="tpu_custom_call" | custom-call | flops 5905580032 | bytes 12845056 | tf_op jit(solution)/shard_map/grad_down/pallas_call | solution.py:544
  406.2 3.7 pad_maximum_fusion.refs_2_
  415.6 2.5 add_convert_fusion.3
  420.5 9.0 %mixer_adjoint.2 = (f32[4096,128]{1,0:T(8,128)}, f32[16,8,128]{2,1,0:T(8,128)}) custom-call(f32[520]{0:T(1024)} %get-tuple-element.158.refs_0_, s32[65]{0:T(128)} %get-tuple-element.236.refs_1_, bf16[512,1536]{1,0:T(8,128)(2,1)} %get-tuple-element.192.refs_2_.refs_4_, f32[8,1536]{1,0:T(8,128)} %get-tuple-element.200.refs_3_.refs_5_, ...), custom_call_target="tpu_custom_call" | custom-call | flops 13421772800 | bytes 4608548 | tf_op jit(solution)/shard_map/mixer_adjoint/pallas_call | solution.py:387
  429.6 8.1 %collective-permute-done.21 = bf16[256,1408]{1,0:T(8,128)(2,1)} collective-permute-done((bf16[256,1408]{1,0:T(8,128)(2,1)}, bf16[256,1408]{1,0:T(8,128)(2,1)}, u32[]{:S(2)}, u32[]{:S(2)}) %collective-permute-start.21) | collective-permute-done | bytes 720928 | tf_op jit(solution)/shard_map/ppermute | solution.py:446
  439.6 4.1 add_convert_fusion.1
  448.3 8.8 %mixer_adjoint.3 = (f32[4096,128]{1,0:T(8,128)}, f32[16,8,128]{2,1,0:T(8,128)}) custom-call(f32[520]{0:T(1024)} %get-tuple-element.159.refs_0_, s32[65]{0:T(128)} %get-tuple-element.237.refs_1_, bf16[512,1536]{1,0:T(8,128)(2,1)} %get-tuple-element.193.refs_2_.refs_4_, f32[8,1536]{1,0:T(8,128)} %get-tuple-element.201.refs_3_.refs_5_, ...), custom_call_target="tpu_custom_call" | custom-call | flops 13421772800 | bytes 4608548 | tf_op jit(solution)/shard_map/mixer_adjoint/pallas_call | solution.py:387
  458.0 17.7 %all_gather.37 = bf16[8,2,16,8,128]{4,3,2,1,0:T(8,128)(2,1)S(1)} all-gather(bf16[1,2,16,8,128]{4,3,2,1,0:T(8,128)(2,1)S(1)} %fusion.44), channel_id=1, replica_groups=mesh['seq'=8,'tp'=4] {'seq'}, dimensions={0}, use_global_device_ids=true | all-gather | bytes 589824 | tf_op jit(solution)/shard_map/all_gather | solution.py:748
  482.6 19.1 %grad_gu.1 = (bf16[1024,2816]{1,0:T(8,128)(2,1)}, bf16[1024,2816]{1,0:T(8,128)(2,1)}) custom-call(s32[1]{0:T(128)} %bitcast.26.core_ref, bf16[512,2048]{1,0:T(8,128)(2,1)} %copy-done.19, bf16[512,2048]{1,0:T(8,128)(2,1)} %copy-done.20, bf16[512,2816]{1,0:T(8,128)(2,1)} %pad_maximum_fusion.refs_2_, bf16[512,2816]{1,0:T(8,128)(2,1)} %pad_maximum_fusion.1.refs_3_, ...), custom_call_target="tpu_custom_call" | custom-call | flops 11811160064 | bytes 21495808 | tf_op jit(solution)/shard_map/grad_gu/pallas_call | solution.py:544
  509.1 7.3 convolution_convert_fusion.2
  517.6 5.1 slice_bitcast_fusion
  522.8 7.3 convolution_convert_fusion.3
  530.2 8.4 %add_convert_fusion = bf16[1024,2816]{1,0:T(8,128)(2,1)} fusion(bf16[1024,2816]{1,0:T(8,128)(2,1)} %collective-permute-done.22, bf16[1024,2816]{1,0:T(8,128)(2,1)} %get-tuple-element.65.refs_19_), kind=kLoop, calls=%fused_computation | loop fusion | flops 11534336 | bytes 17301504 | tf_op jit(solution)/shard_map/convert_element_type | solution.py:574
  538.6 2.6 dynamic-slice_bitcast_fusion
  541.8 31.4 %mixer_back.2 = (bf16[512,1536]{1,0:T(8,128)(2,1)}, f32[8,1536]{1,0:T(8,128)}, f32[64,1536]{1,0:T(8,128)}, f32[72,512]{1,0:T(8,128)}, f32[8,512]{1,0:T(8,128)}, ...) custom-call(f32[520]{0:T(1024)} %get-tuple-element.158.refs_0_, s32[65]{0:T(128)} %get-tuple-element.236.refs_1_, ...), custom_call_target="tpu_custom_call" | custom-call | flops 40265318400 | bytes 11508296 | tf_op jit(solution)/shard_map/mixer_back/pallas_call | solution.py:387
  577.4 3.0 collective-permute-start.39
  581.6 2.8 fusion.29.refs_19_
  586.1 3.0 fusion.22.refs_20_
  589.8 7.0 fusion.8
  599.2 31.3 %mixer_back.3 = (bf16[512,1536]{1,0:T(8,128)(2,1)}, f32[8,1536]{1,0:T(8,128)}, f32[64,1536]{1,0:T(8,128)}, f32[72,512]{1,0:T(8,128)}, f32[8,512]{1,0:T(8,128)}, ...) custom-call(f32[520]{0:T(1024)} %get-tuple-element.159.refs_0_, s32[65]{0:T(128)} %get-tuple-element.237.refs_1_, ...), custom_call_target="tpu_custom_call" | custom-call | flops 40265318400 | bytes 11508296 | tf_op jit(solution)/shard_map/mixer_back/pallas_call | solution.py:387
  640.1 12.6 %grad_in.1 = (bf16[1024,1536]{1,0:T(8,128)(2,1)}, bf16[1024,1536]{1,0:T(8,128)(2,1)}) custom-call(s32[1]{0:T(128)} %bitcast.26.core_ref, bf16[512,2048]{1,0:T(8,128)(2,1)} %get-tuple-element.191.refs_0_, bf16[512,2048]{1,0:T(8,128)(2,1)} %get-tuple-element.190.refs_1_, bf16[512,1536]{1,0:T(8,128)(2,1)} %copy-done.69, bf16[512,1536]{1,0:T(8,128)(2,1)} %fusion.42.refs_3_), custom_call_target="tpu_custom_call" | custom-call | flops 6442450944 | bytes 13631488 | tf_op jit(solution)/shard_map/grad_in/pallas_call | solution.py:544
  656.1 9.7 %fusion.17 = (f32[512]{0:T(512)S(1)}, f32[2048]{0:T(1024)S(1)}, f32[512,2048]{1,0:T(8,128)}) fusion(f32[2048]{0:T(1024)S(1)} %broadcast_add_fusion.1, bf16[1280,2048]{1,0:T(8,128)(2,1)} %all-gather.9.cloned.1.call-done, f32[512]{0:T(512)S(1)} %get-tuple-element.230, bf16[512,1536]{1,0:T(8,128)(2,1)} %fusion.42.refs_3_, bf16[2048,1536]{1,0:T(8,128)(2,1)} %place_in.1), kind=kOutput, calls=%fused_computation.31 | convolution fusion | flops 3228562944 | bytes 14176256 | tf_op jit(solution)/shard_map/dot_general | solution.py:623
  667.2 3.5 collective-permute-start.31
  673.4 10.0 %all_gather.38 = bf16[8,82,512]{2,1,0:T(8,128)(2,1)S(1)} all-gather(bf16[1,82,512]{2,1,0:T(8,128)(2,1)S(1)} %concatenate.98), channel_id=1, replica_groups=mesh['seq'=8,'tp'=4] {'seq'}, dimensions={0}, use_global_device_ids=true | all-gather | bytes 755712 | tf_op jit(solution)/shard_map/all_gather | solution.py:802
  684.6 6.0 fusion.16
  692.3 3.7 add_convert_fusion.2
  707.6 10.1 %collective-permute-done.32 = bf16[256,1536]{1,0:T(8,128)(2,1)} collective-permute-done((bf16[256,1536]{1,0:T(8,128)(2,1)}, bf16[256,1536]{1,0:T(8,128)(2,1)}, u32[]{:S(2)}, u32[]{:S(2)}) %collective-permute-start.32) | collective-permute-done | bytes 786464 | tf_op jit(solution)/shard_map/ppermute | solution.py:446
  723.4 2.9 fusion.32
  729.9 2.9 copy.78
  732.8 4.7 reshape.603
  747.8 2.8 fusion.27
  (446 shorter events, 155.1 us)
Async XLA Ops:
  7.2 107.7 %all-gather.9.cloned.1.call-start = ((), (), s32[]{:S(2)}) async-start(), calls=%async_computation.7 | async-start | bytes 6553600 | tf_op jit(solution)/shard_map/all_gather | solution.py:435
  10.8 166.5 %all-gather.17.cloned.1.call-start = ((), (), s32[]{:S(2)}) async-start(), calls=%async_computation.18 | async-start | bytes 2621440 | tf_op jit(solution)/shard_map/all_gather | solution.py:435
  12.5 54.2 %copy-start.3 = (bf16[256,4352]{1,0:T(8,128)(2,1)}, bf16[256,4352]{1,0:T(8,128)(2,1)S(1)}, u32[]{:S(2)}) copy-start(bf16[256,4352]{1,0:T(8,128)(2,1)S(1)} %pad_maximum_fusion.2.refs_0_) | copy-start | bytes 6684676
  12.5 51.6 %collective-permute-start.1 = (bf16[256,4352]{1,0:T(8,128)(2,1)S(1)}, bf16[256,4352]{1,0:T(8,128)(2,1)}, u32[]{:S(2)}, u32[]{:S(2)}) collective-permute-start(bf16[256,4352]{1,0:T(8,128)(2,1)S(1)} %pad_maximum_fusion.2.refs_0_), channel_id=1, source_target_pairs={{0,16},{4,20},{8,24},{12,28},{16,0},{20,4},{24,8},{28,12},{1,17},{... | collective-permute-start | bytes 6684680 | tf_op jit(solution)/shard_map/ppermute | solution.py:446
  15.6 92.9 %collective-permute-start.3 = (bf16[256,4352]{1,0:T(8,128)(2,1)S(1)}, bf16[256,4352]{1,0:T(8,128)(2,1)}, u32[]{:S(2)}, u32[]{:S(2)}) collective-permute-start(bf16[256,4352]{1,0:T(8,128)(2,1)S(1)} %pad_maximum_fusion.2.refs_0_), channel_id=1, source_target_pairs={{0,4},{4,0},{8,12},{12,8},{16,20},{20,16},{24,28},{28,24},{1,5},{5... | collective-permute-start | bytes 6684680 | tf_op jit(solution)/shard_map/ppermute | solution.py:446
  15.6 53.5 %collective-permute-start = (bf16[256,4352]{1,0:T(8,128)(2,1)S(1)}, bf16[256,4352]{1,0:T(8,128)(2,1)}, u32[]{:S(2)}, u32[]{:S(2)}) collective-permute-start(bf16[256,4352]{1,0:T(8,128)(2,1)S(1)} %pad_maximum_fusion.2.refs_0_), channel_id=1, source_target_pairs={{0,8},{4,12},{8,0},{12,4},{16,24},{20,28},{24,16},{28,20},{1,9},{5... | collective-permute-start | bytes 6684680 | tf_op jit(solution)/shard_map/ppermute | solution.py:446
  17.9 186.0 %all-gather.13.cloned.1.call-start = ((), (), s32[]{:S(2)}) async-start(), calls=%async_computation.9 | async-start | bytes 6488064 | tf_op jit(solution)/shard_map/all_gather | solution.py:435
  20.1 50.2 %copy-start.32 = (f32[16,512]{1,0:T(8,128)}, f32[16,512]{1,0:T(8,128)S(1)}, u32[]{:S(2)}) copy-start(f32[16,512]{1,0:T(8,128)S(1)} %get-tuple-element.212) | copy-start | bytes 98308
  20.1 50.2 %copy-start.34 = (f32[16,512]{1,0:T(8,128)}, f32[16,512]{1,0:T(8,128)S(1)}, u32[]{:S(2)}) copy-start(f32[16,512]{1,0:T(8,128)S(1)} %get-tuple-element.213) | copy-start | bytes 98308
  20.8 52.2 %copy-start.58 = (f32[16,8,128]{2,1,0:T(8,128)}, f32[16,8,128]{2,1,0:T(8,128)S(1)}, u32[]{:S(2)}) copy-start(f32[16,8,128]{2,1,0:T(8,128)S(1)} %get-tuple-element.225.refs_8_) | copy-start | bytes 196612
  20.9 49.4 %copy-start.41 = (f32[64,8,128]{2,1,0:T(8,128)}, f32[64,8,128]{2,1,0:T(8,128)S(1)}, u32[]{:S(2)}) copy-start(f32[64,8,128]{2,1,0:T(8,128)S(1)} %get-tuple-element.255) | copy-start | bytes 786436
  66.7 33.1 %collective-permute-start.17 = (bf16[256,2816]{1,0:T(8,128)(2,1)}, bf16[256,2816]{1,0:T(8,128)(2,1)}, u32[]{:S(2)}, u32[]{:S(2)}) collective-permute-start(bf16[256,2816]{1,0:T(8,128)(2,1)} %slice.349), channel_id=1, source_target_pairs={{0,8},{4,12},{8,0},{12,4},{16,24},{20,28},{24,16},{28,20},{1,9},{5... | collective-permute-start | bytes 4325384 | tf_op jit(solution)/shard_map/ppermute | solution.py:446
  69.1 39.4 %collective-permute-start.5 = (bf16[256,4352]{1,0:T(8,128)(2,1)}, bf16[256,4352]{1,0:T(8,128)(2,1)}, u32[]{:S(2)}, u32[]{:S(2)}) collective-permute-start(bf16[256,4352]{1,0:T(8,128)(2,1)} %collective-permute-done.1.refs_2_), channel_id=1, source_target_pairs={{0,4},{4,0},{8,12},{12,8},{16,20},{20,16},{24,28},{28,24},{1,5},{5... | collective-permute-start | bytes 6684680 | tf_op jit(solution)/shard_map/ppermute | solution.py:446
  69.1 39.4 %collective-permute-start.4 = (bf16[256,4352]{1,0:T(8,128)(2,1)}, bf16[256,4352]{1,0:T(8,128)(2,1)}, u32[]{:S(2)}, u32[]{:S(2)}) collective-permute-start(bf16[256,4352]{1,0:T(8,128)(2,1)} %collective-permute-done.refs_1_), channel_id=1, source_target_pairs={{0,4},{4,0},{8,12},{12,8},{16,20},{20,16},{24,28},{28,24},{1,5},{5... | collective-permute-start | bytes 6684680 | tf_op jit(solution)/shard_map/ppermute | solution.py:446
  73.0 19.5 %collective-permute-start.2 = (bf16[256,1536]{1,0:T(8,128)(2,1)S(1)}, bf16[256,1536]{1,0:T(8,128)(2,1)S(1)}, u32[]{:S(2)}, u32[]{:S(2)}) collective-permute-start(bf16[256,1536]{1,0:T(8,128)(2,1)S(1)} %slice.336), channel_id=1, source_target_pairs={{0,16},{4,20},{8,24},{12,28},{16,0},{20,4},{24,8},{28,12},{1,17},{... | collective-permute-start | bytes 2359304 | tf_op jit(solution)/shard_map/ppermute | solution.py:446
  77.1 37.8 %copy-start.38 = (f32[64,8,128]{2,1,0:T(8,128)}, f32[64,8,128]{2,1,0:T(8,128)S(1)}, u32[]{:S(2)}) copy-start(f32[64,8,128]{2,1,0:T(8,128)S(1)} %constant_dynamic-update-slice_fusion.6.refs_6_) | copy-start | bytes 786436
  103.2 148.5 %all-gather.11.cloned.1.call-start = ((), (), s32[]{:S(2)}) async-start(), calls=%async_computation.8 | async-start | bytes 2621440 | tf_op jit(solution)/shard_map/all_gather | solution.py:435
  105.0 3.5 collective-permute-start.6
  116.2 102.1 %copy-start.12 = (bf16[256,2048]{1,0:T(8,128)(2,1)}, bf16[256,2048]{1,0:T(8,128)(2,1)S(1)}, u32[]{:S(2)}) copy-start(bf16[256,2048]{1,0:T(8,128)(2,1)S(1)} %slice.344.refs_0_) | copy-start | bytes 3145732
  116.2 40.7 %collective-permute-start.9 = (bf16[256,2048]{1,0:T(8,128)(2,1)S(1)}, bf16[256,2048]{1,0:T(8,128)(2,1)S(1)}, u32[]{:S(2)}, u32[]{:S(2)}) collective-permute-start(bf16[256,2048]{1,0:T(8,128)(2,1)S(1)} %slice.344.refs_0_), channel_id=1, source_target_pairs={{0,16},{4,20},{8,24},{12,28},{16,0},{20,4},{24,8},{28,12},{1,17},{... | collective-permute-start | bytes 3145736 | tf_op jit(solution)/shard_map/ppermute | solution.py:446
  117.7 39.8 %collective-permute-start.8 = (bf16[256,2048]{1,0:T(8,128)(2,1)S(1)}, bf16[256,2048]{1,0:T(8,128)(2,1)S(1)}, u32[]{:S(2)}, u32[]{:S(2)}) collective-permute-start(bf16[256,2048]{1,0:T(8,128)(2,1)S(1)} %slice.344.refs_0_), channel_id=1, source_target_pairs={{0,8},{4,12},{8,0},{12,4},{16,24},{20,28},{24,16},{28,20},{1,9},{5... | collective-permute-start | bytes 3145736 | tf_op jit(solution)/shard_map/ppermute | solution.py:446
  134.5 3.8 collective-permute-start.7
  156.9 63.3 %copy-start.16 = (bf16[256,2048]{1,0:T(8,128)(2,1)}, bf16[256,2048]{1,0:T(8,128)(2,1)S(1)}, u32[]{:S(2)}) copy-start(bf16[256,2048]{1,0:T(8,128)(2,1)S(1)} %collective-permute-done.9.refs_2_) | copy-start | bytes 3145732
  157.5 62.8 %copy-start.17 = (bf16[256,2048]{1,0:T(8,128)(2,1)}, bf16[256,2048]{1,0:T(8,128)(2,1)S(1)}, u32[]{:S(2)}) copy-start(bf16[256,2048]{1,0:T(8,128)(2,1)S(1)} %collective-permute-done.8.refs_1_) | copy-start | bytes 3145732
  192.2 120.7 %all-gather.15.cloned.1.call-start = ((), (), s32[]{:S(2)}) async-start(), calls=%async_computation.12 | async-start | bytes 2621440 | tf_op jit(solution)/shard_map/all_gather | solution.py:435
  192.8 28.0 %collective-permute-start.18 = (bf16[256,2816]{1,0:T(8,128)(2,1)}, bf16[256,2816]{1,0:T(8,128)(2,1)}, u32[]{:S(2)}, u32[]{:S(2)}) collective-permute-start(bf16[256,2816]{1,0:T(8,128)(2,1)} %collective-permute-done.17.refs_3_), channel_id=1, source_target_pairs={{0,4},{4,0},{8,12},{12,8},{16,20},{20,16},{24,28},{28,24},{1,5},{5... | collective-permute-start | bytes 4325384 | tf_op jit(solution)/shard_map/ppermute | solution.py:446
  218.2 126.4 %all-gather.19.cloned.1.call-start = ((), (), s32[]{:S(2)}) async-start(), calls=%async_computation.19 | async-start | bytes 2621440 | tf_op jit(solution)/shard_map/all_gather | solution.py:435
  218.3 25.4 %collective-permute-start.12 = (bf16[256,2048]{1,0:T(8,128)(2,1)S(1)}, bf16[256,2048]{1,0:T(8,128)(2,1)}, u32[]{:S(2)}, u32[]{:S(2)}) collective-permute-start(bf16[256,2048]{1,0:T(8,128)(2,1)S(1)} %slice.344.refs_0_), channel_id=1, source_target_pairs={{0,4},{4,0},{8,12},{12,8},{16,20},{20,16},{24,28},{28,24},{1,5},{5... | collective-permute-start | bytes 3145736 | tf_op jit(solution)/shard_map/ppermute | solution.py:446
  218.6 14.3 %collective-permute-start.11 = (bf16[256,1024]{1,0:T(8,128)(2,1)S(1)}, bf16[256,1024]{1,0:T(8,128)(2,1)}, u32[]{:S(2)}, u32[]{:S(2)}) collective-permute-start(bf16[256,1024]{1,0:T(8,128)(2,1)S(1)} %slice.348), channel_id=1, source_target_pairs={{0,8},{4,12},{8,0},{12,4},{16,24},{20,28},{24,16},{28,20},{1,9},{5... | collective-permute-start | bytes 1572872 | tf_op jit(solution)/shard_map/ppermute | solution.py:446
  220.2 23.5 %collective-permute-start.14 = (bf16[256,2048]{1,0:T(8,128)(2,1)S(1)}, bf16[256,2048]{1,0:T(8,128)(2,1)}, u32[]{:S(2)}, u32[]{:S(2)}) collective-permute-start(bf16[256,2048]{1,0:T(8,128)(2,1)S(1)} %collective-permute-done.9.refs_2_), channel_id=1, source_target_pairs={{0,4},{4,0},{8,12},{12,8},{16,20},{20,16},{24,28},{28,24},{1,5},{5... | collective-permute-start | bytes 3145736 | tf_op jit(solution)/shard_map/ppermute | solution.py:446
  220.3 23.4 %collective-permute-start.13 = (bf16[256,2048]{1,0:T(8,128)(2,1)S(1)}, bf16[256,2048]{1,0:T(8,128)(2,1)}, u32[]{:S(2)}, u32[]{:S(2)}) collective-permute-start(bf16[256,2048]{1,0:T(8,128)(2,1)S(1)} %collective-permute-done.8.refs_1_), channel_id=1, source_target_pairs={{0,4},{4,0},{8,12},{12,8},{16,20},{20,16},{24,28},{28,24},{1,5},{5... | collective-permute-start | bytes 3145736 | tf_op jit(solution)/shard_map/ppermute | solution.py:446
  220.9 14.0 %collective-permute-start.10 = (bf16[256,1024]{1,0:T(8,128)(2,1)S(1)}, bf16[256,1024]{1,0:T(8,128)(2,1)}, u32[]{:S(2)}, u32[]{:S(2)}) collective-permute-start(bf16[256,1024]{1,0:T(8,128)(2,1)S(1)} %slice.347), channel_id=1, source_target_pairs={{0,16},{4,20},{8,24},{12,28},{16,0},{20,4},{24,8},{28,12},{1,17},{... | collective-permute-start | bytes 1572872 | tf_op jit(solution)/shard_map/ppermute | solution.py:446
  232.9 10.8 %collective-permute-start.16 = (bf16[256,1024]{1,0:T(8,128)(2,1)}, bf16[256,1024]{1,0:T(8,128)(2,1)}, u32[]{:S(2)}, u32[]{:S(2)}) collective-permute-start(bf16[256,1024]{1,0:T(8,128)(2,1)} %collective-permute-done.11.refs_4_), channel_id=1, source_target_pairs={{0,4},{4,0},{8,12},{12,8},{16,20},{20,16},{24,28},{28,24},{1,5},{5... | collective-permute-start | bytes 1572872 | tf_op jit(solution)/shard_map/ppermute | solution.py:446
  234.9 8.9 %collective-permute-start.15 = (bf16[256,1024]{1,0:T(8,128)(2,1)}, bf16[256,1024]{1,0:T(8,128)(2,1)}, u32[]{:S(2)}, u32[]{:S(2)}) collective-permute-start(bf16[256,1024]{1,0:T(8,128)(2,1)} %collective-permute-done.10.refs_3_), channel_id=1, source_target_pairs={{0,4},{4,0},{8,12},{12,8},{16,20},{20,16},{24,28},{28,24},{1,5},{5... | collective-permute-start | bytes 1572872 | tf_op jit(solution)/shard_map/ppermute | solution.py:446
  266.3 154.2 %reduce-scatter.10.cloned.1.call-start = ((), (), s32[]{:S(2)}) async-start(), calls=%async_computation.11 | async-start | bytes 2621440 | tf_op jit(solution)/shard_map/reduce_scatter | solution.py:439
  312.7 135.6 %reduce-scatter.12.cloned.1.call-start = ((), (), s32[]{:S(2)}) async-start(), calls=%async_computation.13 | async-start | bytes 2621440 | tf_op jit(solution)/shard_map/reduce_scatter | solution.py:439
  405.0 9.0 %collective-permute-start.19 = (bf16[1024,1408]{1,0:T(8,128)(2,1)}, bf16[1024,1408]{1,0:T(8,128)(2,1)S(1)}, u32[]{:S(2)}, u32[]{:S(2)}) collective-permute-start(bf16[1024,1408]{1,0:T(8,128)(2,1)} %get-tuple-element.57.refs_8_), channel_id=1, source_target_pairs={{0,4},{4,0},{8,12},{12,8},{16,20},{20,16},{24,28},{28,24},{1,5},{5... | collective-permute-start | bytes 8650760 | tf_op jit(solution)/shard_map/ppermute | solution.py:446
  405.0 34.5 %collective-permute-start.20 = (bf16[1024,2048]{1,0:T(8,128)(2,1)}, bf16[1024,2048]{1,0:T(8,128)(2,1)}, u32[]{:S(2)}, u32[]{:S(2)}) collective-permute-start(bf16[1024,2048]{1,0:T(8,128)(2,1)} %get-tuple-element.55.refs_4_.refs_10_), channel_id=1, source_target_pairs={{0,4},{4,0},{8,12},{12,8},{16,20},{20,16},{24,28},{28,24},{1,5},{5... | collective-permute-start | bytes 12582920 | tf_op jit(solution)/shard_map/ppermute | solution.py:446
  405.6 322.5 %reduce-scatter.20.cloned.1.call-start = ((), (), s32[]{:S(2)}) async-start(), calls=%async_computation.17 | async-start | bytes 1310720 | tf_op jit(solution)/shard_map/reduce_scatter | solution.py:439
  419.2 18.5 %collective-permute-start.21 = (bf16[256,1408]{1,0:T(8,128)(2,1)}, bf16[256,1408]{1,0:T(8,128)(2,1)}, u32[]{:S(2)}, u32[]{:S(2)}) collective-permute-start(bf16[256,1408]{1,0:T(8,128)(2,1)} %dynamic-slice_bitcast_fusion.2), channel_id=1, source_target_pairs={{0,16},{4,20},{8,24},{12,28},{16,0},{20,4},{24,8},{28,12},{1,17},{... | collective-permute-start | bytes 2162696 | tf_op jit(solution)/shard_map/ppermute | solution.py:446
  445.8 34.8 %collective-permute-start.36 = (bf16[256,2048]{1,0:T(8,128)(2,1)S(1)}, bf16[256,2048]{1,0:T(8,128)(2,1)S(1)}, u32[]{:S(2)}, u32[]{:S(2)}) collective-permute-start(bf16[256,2048]{1,0:T(8,128)(2,1)S(1)} %dynamic-slice_bitcast_fusion.1), channel_id=1, source_target_pairs={{0,8},{4,12},{8,0},{12,4},{16,24},{20,28},{24,16},{28,20},{1,9},{5... | collective-permute-start | bytes 3145736 | tf_op jit(solution)/shard_map/ppermute | solution.py:446
  479.2 26.2 %collective-permute-start.35 = (bf16[256,2048]{1,0:T(8,128)(2,1)}, bf16[256,2048]{1,0:T(8,128)(2,1)S(1)}, u32[]{:S(2)}, u32[]{:S(2)}) collective-permute-start(bf16[256,2048]{1,0:T(8,128)(2,1)} %fusion.34), channel_id=1, source_target_pairs={{0,8},{4,12},{8,0},{12,4},{16,24},{20,28},{24,16},{28,20},{1,9},{5... | collective-permute-start | bytes 3145736 | tf_op jit(solution)/shard_map/ppermute | solution.py:446
  482.0 25.3 %collective-permute-start.37 = (bf16[256,2048]{1,0:T(8,128)(2,1)}, bf16[256,2048]{1,0:T(8,128)(2,1)S(1)}, u32[]{:S(2)}, u32[]{:S(2)}) collective-permute-start(bf16[256,2048]{1,0:T(8,128)(2,1)} %fusion.26), channel_id=1, source_target_pairs={{0,16},{4,20},{8,24},{12,28},{16,0},{20,4},{24,8},{28,12},{1,17},{... | collective-permute-start | bytes 3145736 | tf_op jit(solution)/shard_map/ppermute | solution.py:446
  508.9 230.5 %reduce-scatter.14.cloned.1.call-start = ((), (), s32[]{:S(2)}) async-start(), calls=%async_computation.14 | async-start | bytes 2621440 | tf_op jit(solution)/shard_map/reduce_scatter | solution.py:439
  509.0 21.2 %collective-permute-start.22 = (bf16[1024,2816]{1,0:T(8,128)(2,1)}, bf16[1024,2816]{1,0:T(8,128)(2,1)}, u32[]{:S(2)}, u32[]{:S(2)}) collective-permute-start(bf16[1024,2816]{1,0:T(8,128)(2,1)} %get-tuple-element.64.refs_18_), channel_id=1, source_target_pairs={{0,4},{4,0},{8,12},{12,8},{16,20},{20,16},{24,28},{28,24},{1,5},{5... | collective-permute-start | bytes 17301512 | tf_op jit(solution)/shard_map/ppermute | solution.py:446
  516.4 225.5 %reduce-scatter.8.cloned.1.call-start = ((), (), s32[]{:S(2)}) async-start(), calls=%async_computation.10 | async-start | bytes 2621440 | tf_op jit(solution)/shard_map/reduce_scatter | solution.py:439
  530.1 215.4 %reduce-scatter.16.cloned.1.call-start = ((), (), s32[]{:S(2)}) async-start(), calls=%async_computation.15 | async-start | bytes 2621440 | tf_op jit(solution)/shard_map/reduce_scatter | solution.py:439
  530.2 59.5 %slice-start = ((s8[5242880]{0:T(1024)(128)(4,1)}), s8[4194304]{0:T(1024)(128)(4,1)S(1)}, s32[]{:S(2)}) async-start(s8[5242880]{0:T(1024)(128)(4,1)} %bitcast.200), calls=%async_computation.20 | async-start | bytes 8388608
  541.2 43.7 %collective-permute-start.23 = (bf16[256,2816]{1,0:T(8,128)(2,1)}, bf16[256,2816]{1,0:T(8,128)(2,1)S(1)}, u32[]{:S(2)}, u32[]{:S(2)}) collective-permute-start(bf16[256,2816]{1,0:T(8,128)(2,1)} %dynamic-slice_bitcast_fusion), channel_id=1, source_target_pairs={{0,8},{4,12},{8,0},{12,4},{16,24},{20,28},{24,16},{28,20},{1,9},{5... | collective-permute-start | bytes 4325384 | tf_op jit(solution)/shard_map/ppermute | solution.py:446
  541.8 48.0 %slice-start.1 = ((s8[5242880]{0:T(1024)(128)(4,1)}), s8[1048576]{0:T(1024)(128)(4,1)S(1)}, s32[]{:S(2)}) async-start(s8[5242880]{0:T(1024)(128)(4,1)} %bitcast.200), calls=%async_computation.21 | async-start | bytes 2097152
  574.0 6.4 collective-permute-start.24
  577.4 146.0 %collective-permute-start.39 = (bf16[256,1408]{1,0:T(8,128)(2,1)}, bf16[256,1408]{1,0:T(8,128)(2,1)}, u32[]{:S(2)}, u32[]{:S(2)}) collective-permute-start(bf16[256,1408]{1,0:T(8,128)(2,1)} %fusion.36), channel_id=1, source_target_pairs={{0,16},{4,20},{8,24},{12,28},{16,0},{20,4},{24,8},{28,12},{1,17},{... | collective-permute-start | bytes 2162696 | tf_op jit(solution)/shard_map/ppermute | solution.py:446
  584.4 50.3 %collective-permute-start.25 = (bf16[256,2816]{1,0:T(8,128)(2,1)}, bf16[256,2816]{1,0:T(8,128)(2,1)S(1)}, u32[]{:S(2)}, u32[]{:S(2)}) collective-permute-start(bf16[256,2816]{1,0:T(8,128)(2,1)} %fusion.29.refs_19_), channel_id=1, source_target_pairs={{0,8},{4,12},{8,0},{12,4},{16,24},{20,28},{24,16},{28,20},{1,9},{5... | collective-permute-start | bytes 4325384 | tf_op jit(solution)/shard_map/ppermute | solution.py:446
  589.0 45.6 %collective-permute-start.26 = (bf16[256,2816]{1,0:T(8,128)(2,1)}, bf16[256,2816]{1,0:T(8,128)(2,1)S(1)}, u32[]{:S(2)}, u32[]{:S(2)}) collective-permute-start(bf16[256,2816]{1,0:T(8,128)(2,1)} %fusion.22.refs_20_), channel_id=1, source_target_pairs={{0,16},{4,20},{8,24},{12,28},{16,0},{20,4},{24,8},{28,12},{1,17},{... | collective-permute-start | bytes 4325384 | tf_op jit(solution)/shard_map/ppermute | solution.py:446
  631.5 114.0 %reduce-scatter.18.cloned.1.call-start = ((), (), s32[]{:S(2)}) async-start(), calls=%async_computation.16 | async-start | bytes 2621440 | tf_op jit(solution)/shard_map/reduce_scatter | solution.py:439
  632.4 6.9 collective-permute-start.27
  652.6 38.0 %collective-permute-start.28 = (bf16[1024,1536]{1,0:T(8,128)(2,1)}, bf16[1024,1536]{1,0:T(8,128)(2,1)S(1)}, u32[]{:S(2)}, u32[]{:S(2)}) collective-permute-start(bf16[1024,1536]{1,0:T(8,128)(2,1)} %get-tuple-element.76), channel_id=1, source_target_pairs={{0,4},{4,0},{8,12},{12,8},{16,20},{20,16},{24,28},{28,24},{1,5},{5... | collective-permute-start | bytes 9437192 | tf_op jit(solution)/shard_map/ppermute | solution.py:446
  665.8 4.9 collective-permute-start.30
  666.8 5.9 collective-permute-start.29
  667.2 5.5 collective-permute-start.31
  697.0 20.7 %collective-permute-start.32 = (bf16[256,1536]{1,0:T(8,128)(2,1)}, bf16[256,1536]{1,0:T(8,128)(2,1)}, u32[]{:S(2)}, u32[]{:S(2)}) collective-permute-start(bf16[256,1536]{1,0:T(8,128)(2,1)} %add_bitcast_fusion), channel_id=1, source_target_pairs={{0,16},{4,20},{8,24},{12,28},{16,0},{20,4},{24,8},{28,12},{1,17},{... | collective-permute-start | bytes 2359304 | tf_op jit(solution)/shard_map/ppermute | solution.py:446
  700.8 22.6 %collective-permute-start.38 = (bf16[256,1408]{1,0:T(8,128)(2,1)}, bf16[256,1408]{1,0:T(8,128)(2,1)}, u32[]{:S(2)}, u32[]{:S(2)}) collective-permute-start(bf16[256,1408]{1,0:T(8,128)(2,1)} %fusion.33), channel_id=1, source_target_pairs={{0,8},{4,12},{8,0},{12,4},{16,24},{20,28},{24,16},{28,20},{1,9},{5... | collective-permute-start | bytes 2162696 | tf_op jit(solution)/shard_map/ppermute | solution.py:446
  706.1 41.6 %collective-permute-start.34 = (bf16[256,1536]{1,0:T(8,128)(2,1)}, bf16[256,1536]{1,0:T(8,128)(2,1)}, u32[]{:S(2)}, u32[]{:S(2)}) collective-permute-start(bf16[256,1536]{1,0:T(8,128)(2,1)} %fusion.35), channel_id=1, source_target_pairs={{0,16},{4,20},{8,24},{12,28},{16,0},{20,4},{24,8},{28,12},{1,17},{... | collective-permute-start | bytes 2359304 | tf_op jit(solution)/shard_map/ppermute | solution.py:446
  721.9 25.9 %collective-permute-start.33 = (bf16[256,1536]{1,0:T(8,128)(2,1)}, bf16[256,1536]{1,0:T(8,128)(2,1)}, u32[]{:S(2)}, u32[]{:S(2)}) collective-permute-start(bf16[256,1536]{1,0:T(8,128)(2,1)} %fusion.28), channel_id=1, source_target_pairs={{0,8},{4,12},{8,0},{12,4},{16,24},{20,28},{24,16},{28,20},{1,9},{5... | collective-permute-start | bytes 2359304 | tf_op jit(solution)/shard_map/ppermute | solution.py:446
  (72 other events, 666.0 us)
Sparse Core Ops, SparseCore 0:
  10.9 100.7 all-gather.8
  113.8 44.2 all-gather.16
  160.0 43.7 all-gather.12
  205.9 45.8 all-gather.10
  253.1 44.7 all-gather.14
  299.9 44.6 all-gather.18
  346.9 42.5 reduce-scatter.9
  405.7 42.5 reduce-scatter.11
  509.0 24.8 reduce-scatter.19
  536.1 42.4 reduce-scatter.13
  581.0 43.1 reduce-scatter.7
  631.6 42.9 reduce-scatter.15
  690.7 43.9 reduce-scatter.17
